TPU v7x, 32 devices: a whole 2x2x4 slice. The times are simulated.
32 devices in a mesh: section: 2 (over core), tile: 16 (over z, y, x).
Axes of the slice: x: 2, y: 2, z: 4, core: 2. Of those that a mesh axis runs over, the one named last changes fastest.
Arguments:
- aerial_patch_grid: bfloat16 [384, 384, 768], P('tile'), may hold values from -6 to 6
- patch_conv_weight: bfloat16 [3, 4, 4, 96], replicated, may hold values from -0.875 to 0.875
- patch_bias: float32 [96], replicated, may hold values from -3 to 3
- merging_conv_weight: bfloat16 [2, 2, 96, 192], replicated, may hold values from -0.3125 to 0.3125
- merge_bias: float32 [192], replicated, may hold values from -3 to 3
- down_weight: bfloat16 [3, 3, 192, 384], replicated, may hold values from -0.15625 to 0.15625
- down_bias: float32 [384], replicated, may hold values from -3 to 3
- norm_gain: float32 [384], replicated, may hold values from 0.1 to 1.9
- spectral_filter: bfloat16 [384, 2, 384, 384], P('tile'), may hold values from -6 to 6
Outputs:
- block_output: bfloat16 [384, 384, 384], P('section', 'tile')
All inputs are finite; a program needn't handle non-finite values.
Results may differ from a plain program's by a relative error of at most 0.015.
Values may be sent and summed in bfloat16 or wider, within the bound.
No kernel may reach another device: no remote copies, remote signals or barrier semaphores. Data moves between devices by JAX's collectives and lax.ppermute only.
A program may use at most 192 MiB of HBM per device.

v0:
```python
import math

import jax
import jax.numpy as jnp
from jax import lax
from jax.sharding import PartitionSpec as P

EPSILON = 1e-05


def from_behind(block, axis, distance):
    devices = range(lax.axis_size(axis))
    route = [(i - distance, i) for i in devices if i - distance in devices]
    return lax.ppermute(block, axis, route)


def fourier_tables(length):
    indices = jnp.arange(length, dtype=jnp.int32)
    product = indices[:, None] * indices[None, :] % length
    angles = product.astype(jnp.float32) * (2.0 * math.pi / length)
    return (jnp.cos(angles).astype(jnp.bfloat16), jnp.sin(angles).astype(jnp.bfloat16))


def patch_kernel_matrix(patch_conv_weight):
    identity = jnp.eye(4, dtype=jnp.float32)
    larger = jnp.einsum(
        "baqk,xy,uv->bxauqyvk", patch_conv_weight.astype(jnp.float32), identity, identity
    )
    band_count = patch_conv_weight.shape[0]
    width = patch_conv_weight.shape[3]
    return larger.reshape(band_count * 256, 16 * width).astype(jnp.bfloat16)


def merging_kernel_matrix(merging_conv_weight):
    identity = jnp.eye(2, dtype=jnp.float32)
    larger = jnp.einsum(
        "aqjk,xy,uv->xauqjyvk", merging_conv_weight.astype(jnp.float32), identity, identity
    )
    in_width = merging_conv_weight.shape[2]
    out_width = merging_conv_weight.shape[3]
    return larger.reshape(16 * in_width, 4 * out_width).astype(jnp.bfloat16)


def down_matrices(down_weight):
    nothing = jnp.zeros_like(down_weight[0, 0])
    in_width = down_weight.shape[2]
    out_width = down_weight.shape[3]

    def arrange(entries):
        return jnp.stack(
            [jnp.stack(entries[0], axis=0), jnp.stack(entries[1], axis=0)], axis=0
        ).reshape(4 * in_width, out_width)

    own_taps = arrange(
        [[down_weight[1, 1], down_weight[1, 2]], [down_weight[2, 1], down_weight[2, 2]]]
    )
    upper_taps = arrange([[nothing, nothing], [down_weight[0, 1], down_weight[0, 2]]])
    left_taps = arrange([[nothing, down_weight[1, 0]], [nothing, down_weight[2, 0]]])
    corner_taps = arrange([[nothing, nothing], [nothing, down_weight[0, 0]]])
    return (own_taps, upper_taps, left_taps, corner_taps)


def stem_layers(aerial_patch_grid, patch_conv_weight, patch_bias, merging_conv_weight, merge_bias):
    initial_layer = jnp.einsum(
        "zji,if->zjf",
        aerial_patch_grid,
        patch_kernel_matrix(patch_conv_weight),
        preferred_element_type=jnp.float32,
    )
    initial_layer = jax.nn.gelu(initial_layer + jnp.tile(patch_bias, 16), approximate=True).astype(
        jnp.bfloat16
    )
    layer_two = jnp.einsum(
        "zji,if->zjf",
        initial_layer,
        merging_kernel_matrix(merging_conv_weight),
        preferred_element_type=jnp.float32,
    )
    return jax.nn.gelu(layer_two + jnp.tile(merge_bias, 4), approximate=True).astype(jnp.bfloat16)


def rim_above(extended):
    return from_behind(extended[-1:], "tile", 1)


def down_conv(upper_rim, extended, down_weight, down_bias):
    stacked = jnp.concatenate([upper_rim, extended], axis=0)
    own_taps, upper_taps, left_taps, corner_taps = down_matrices(down_weight)
    summed = jnp.einsum(
        "rwk,kc->crw", stacked[1:, 1:], own_taps, preferred_element_type=jnp.float32
    )
    summed = summed + jnp.einsum(
        "rwk,kc->crw", stacked[:-1, 1:], upper_taps, preferred_element_type=jnp.float32
    )
    summed = summed + jnp.einsum(
        "rwk,kc->crw", stacked[1:, :-1], left_taps, preferred_element_type=jnp.float32
    )
    summed = summed + jnp.einsum(
        "rwk,kc->crw", stacked[:-1, :-1], corner_taps, preferred_element_type=jnp.float32
    )
    return (summed + down_bias[:, None, None]).astype(jnp.bfloat16)


def layer_norm(features, norm_gain):
    values = features.astype(jnp.float32)
    mean_value = jnp.mean(values, axis=0, keepdims=True)
    centered = values - mean_value
    variance = jnp.mean(centered * centered, axis=0, keepdims=True)
    return (norm_gain[:, None, None] * centered * lax.rsqrt(variance + EPSILON)).astype(
        jnp.bfloat16
    )


def filter_columns(row_spectrum, kernel, forward_h, inverse_h):
    spectrum = jnp.einsum(
        "puqh,chqw->cpuw", forward_h, row_spectrum, preferred_element_type=jnp.float32
    ).astype(jnp.bfloat16)
    spec_real = spectrum[:, 0].astype(jnp.float32)
    spec_imag = spectrum[:, 1].astype(jnp.float32)
    filter_real = kernel[:, 0].astype(jnp.float32)
    filter_imag = kernel[:, 1].astype(jnp.float32)
    weighted = jnp.stack(
        [
            filter_real * spec_real - filter_imag * spec_imag,
            filter_real * spec_imag + filter_imag * spec_real,
        ],
        axis=1,
    ).astype(jnp.bfloat16)
    return jnp.einsum(
        "qhpu,cpuw->chqw", inverse_h, weighted, preferred_element_type=jnp.float32
    ).astype(jnp.bfloat16)


def local(
    aerial_patch_grid,
    patch_conv_weight,
    patch_bias,
    merging_conv_weight,
    merge_bias,
    down_weight,
    down_bias,
    norm_gain,
    spectral_filter,
):
    section_index = lax.axis_index("section")
    first_section = section_index == 0
    field_cols = aerial_patch_grid.shape[1]
    channels = down_weight.shape[3]
    group_width = spectral_filter.shape[0]
    full_rows = spectral_filter.shape[2]
    half_channels = channels // 2
    cell_half = field_cols // 2
    image_part = lax.dynamic_slice_in_dim(
        aerial_patch_grid, section_index * cell_half, cell_half, 1
    )
    layer_two = stem_layers(
        image_part, patch_conv_weight, patch_bias, merging_conv_weight, merge_bias
    )
    left_column = from_behind(layer_two[:, -1:], "section", 1)
    extended = jnp.concatenate([left_column, layer_two], axis=1)
    upper_rim = rim_above(extended)
    feature_half = down_conv(upper_rim, extended, down_weight, down_bias)
    features = lax.all_gather(feature_half, "section", axis=2, tiled=True)
    normed = layer_norm(features, norm_gain)
    cos_h, sin_h = fourier_tables(full_rows)
    cos_w, sin_w = fourier_tables(field_cols)
    forward_table = jnp.stack([cos_w, -sin_w], axis=1)
    forward_h = jnp.stack(
        [jnp.stack([cos_h, sin_h], axis=1), jnp.stack([-sin_h, cos_h], axis=1)], axis=0
    )
    inverse_h = jnp.stack(
        [jnp.stack([cos_h, -sin_h], axis=1), jnp.stack([sin_h, cos_h], axis=1)], axis=0
    )
    inverse_table = jnp.stack([cos_w, -sin_w], axis=0)
    norm_scale = 1.0 / (full_rows * field_cols)
    fields = lax.all_to_all(normed, "tile", split_axis=0, concat_axis=1, tiled=True)

    def whole_filter():
        frequency_rows = jnp.einsum(
            "chx,xqw->chqw", fields, forward_table, preferred_element_type=jnp.float32
        ).astype(jnp.bfloat16)
        back_rows = filter_columns(frequency_rows, spectral_filter, forward_h, inverse_h)
        result = jnp.einsum(
            "chqw,qwv->chv", back_rows, inverse_table, preferred_element_type=jnp.float32
        )
        return (result * norm_scale).astype(jnp.bfloat16)

    def empty_fields():
        return jnp.zeros((group_width, full_rows, field_cols), jnp.bfloat16)

    filtered_fields = lax.cond(first_section, empty_fields, whole_filter)
    rows_back = lax.all_to_all(filtered_fields, "tile", split_axis=1, concat_axis=0, tiled=True)
    returned = from_behind(rows_back[:half_channels], "section", -1)
    filtered = jnp.where(first_section, returned, rows_back[half_channels:])
    own_part = lax.dynamic_slice_in_dim(features, section_index * half_channels, half_channels, 0)
    return (own_part.astype(jnp.float32) + filtered.astype(jnp.float32)).astype(jnp.bfloat16)


def solution(mesh):
    return jax.shard_map(
        local,
        mesh=mesh,
        in_specs=(
            P("tile", None, None),
            P(),
            P(),
            P(),
            P(),
            P(),
            P(),
            P(),
            P("tile", None, None, None),
        ),
        out_specs=P("section", "tile", None),
        check_vma=False,
    )
```

profile of v0, /device:TPU:0, one launch (start us, length us, event | category | flops | bytes accessed | tf_op | source)
XLA Modules:
  0.0 556.5 jit_solution(13284753169762362883)
XLA Ops:
  6.6 0.1 broadcast_multiply_fusion.2
  6.6 0.7 tile.5
  7.3 0.1 add.146
  7.4 0.7 tile.4
  8.0 0.1 add.140
  8.1 0.7 convert.21
  8.8 0.1 broadcast_multiply_fusion.1
  8.9 1.0 convert.23
  9.9 2.7 fusion.58
  12.6 3.5 reshape.179
  16.0 1.7 fusion.57
  17.7 4.5 reshape.178
  22.2 33.1 %fusion.49 = bf16[24,192,768]{2,1,0:T(8,128)(2,1)} fusion(bf16[1536,768,1]{1,0,2:T(8,128)(2,1)} %reshape.179, f32[768]{0:T(1024)S(1)} %add.146, bf16[768,1536,1]{1,0,2:T(8,128)(2,1)} %reshape.178, f32[1536]{0:T(1024)S(1)} %add.140, bf16[24,384,768]{2,1,0:T(8,128)(2,1)} %param.11, s32[]{:T(128)S(6)} %select_n.65), kind=kOutput, calls=%fused_computation.52 | convolution fusion | flops 21849440256 | bytes 18883588 | tf_op jit(solution)/shard_map/zji,if->zjf/dot_general | solution.py:73
  55.4 1.0 slice.88
  56.4 2.9 collective-permute-start
  59.3 0.1 slice_bitcast_fusion.4
  59.5 0.1 maximum_bitcast_fusion.6
  59.5 0.1 pad_maximum_fusion.8
  59.6 0.0 slice-start.1
  59.6 9.9 %fusion.79 = f32[384,24,192]{0,2,1:T(8,128)} fusion(bf16[768,384,1]{1,0,2:T(8,128)(2,1)S(1)} %bitcast.143, bf16[24,192,768]{2,1,0:T(8,128)(2,1)} %fusion.49), kind=kOutput, calls=%fused_computation.127 | convolution fusion | flops 2717908992 | bytes 14745600 | tf_op jit(solution)/shard_map/rwk,kc->crw/dot_general | solution.py:89
  69.6 0.1 pad_bitcast_fusion.1
  69.6 0.1 pad_maximum_fusion.9
  69.7 0.1 maximum_bitcast_fusion.8
  69.8 0.1 stack.107
  69.8 0.1 stack.115
  69.9 0.1 pad_maximum_fusion.11
  70.0 4.2 collective-permute-start.1
  74.2 5.8 %fusion.52 = f32[384,24,192]{0,2,1:T(8,128)} fusion(bf16[768,384,1]{1,0,2:T(8,128)(2,1)S(1)} %bitcast.141, bf16[24,192,768]{2,1,0:T(8,128)(2,1)S(1)} %bitcast.136, bf16[24,1,768]{2,1,0:T(2,128)(2,1)S(1)} %collective-permute-done), kind=kOutput, calls=%fused_computation.58 | convolution fusion | flops 2732064768 | bytes 14782464 | tf_op jit(solution)/shard_map/rwk,kc->crw/dot_general | solution.py:95
  80.1 0.4 collective-permute-done.1
  80.5 4.7 maximum_maximum_fusion
  85.1 9.8 %fusion.54 = f32[384,24,192]{0,2,1:T(8,128)} fusion(bf16[768,384,1]{1,0,2:T(8,128)(2,1)S(1)} %bitcast.142, bf16[25,193,768]{2,1,0:T(8,128)(2,1)} %maximum_maximum_fusion), kind=kOutput, calls=%fused_computation.60 | convolution fusion | flops 2717908992 | bytes 14745600 | tf_op jit(solution)/shard_map/rwk,kc->crw/dot_general | solution.py:92
  95.0 14.9 %add_convert_fusion.1 = bf16[384,24,192]{0,2,1:T(8,128)(2,1)} fusion(f32[384,24,192]{0,2,1:T(8,128)} %fusion.52, f32[384,24,192]{0,2,1:T(8,128)} %fusion.79, f32[384,24,192]{0,2,1:T(8,128)} %fusion.54, f32[384]{0:T(512)S(1)} %copy-done.2, bf16[768,384,1]{1,0,2:T(8,128)(2,1)S(1)} %bitcast.140, bf16[25,193,768]{2,1,0:T(8,128)(2,1)} %maximum_maximum_fusion), kind=kOutput, calls=%fused_computation.62 | convolution fusion | flops 2726756352 | bytes 32441856 | tf_op jit(solution)/shard_map/rwk,kc->crw/dot_general | solution.py:98
  109.9 0.0 all-gather.2.cloned.1.call-update
  109.9 0.0 copy-start.3
  109.9 20.3 %all-gather.2.cloned.1.call-done = bf16[384,24,384]{0,2,1:T(8,128)(2,1)} async-done(((bf16[384,24,192]{0,2,1:T(8,128)(2,1)}), bf16[384,24,384]{0,2,1:T(8,128)(2,1)}) %all-gather.2.cloned.1.call-update) | async-done | bytes 7077904 | tf_op jit(solution)/shard_map/all_gather | solution.py:163
  130.3 4.4 convert_reduce_fusion
  134.7 0.6 copy-done
  135.3 3.5 fusion.41
  138.9 4.6 fusion.40
  143.5 10.3 %copy.35 = bf16[384,24,384]{2,1,0:T(8,128)(2,1)} copy(bf16[384,24,384]{0,2,1:T(8,128)(2,1)} %fusion.40) | data formatting | bytes 14155776 | tf_op jit(solution)/shard_map/convert_element_type | solution.py:109
  153.8 6.8 %all-to-all-start = ((bf16[384,24,384]{2,1,0:T(8,128)(2,1)}), bf16[384,24,384]{2,1,0:T(8,128)(2,1)}, u32[]{:S(2)}, u32[]{:S(2)}) async-start(bf16[384,24,384]{2,1,0:T(8,128)(2,1)} %copy.35), calls=%async_computation | async-start | bytes 14155776 | tf_op jit(solution)/shard_map/all_to_all | solution.py:176
  160.6 2.3 fusion.73
  163.0 2.3 fusion.72
  165.3 2.3 cosine_convert_fusion.1
  167.6 2.3 sine_convert_fusion.1
  169.9 2.3 cosine_convert_fusion
  172.2 0.1 pad_maximum_fusion.10
  172.3 0.3 fusion.77
  172.6 0.3 pad_maximum_fusion.2
  172.8 122.5 %all-to-all-done = bf16[384,24,384]{2,1,0:T(8,128)(2,1)} async-done(((bf16[384,24,384]{2,1,0:T(8,128)(2,1)}), bf16[384,24,384]{2,1,0:T(8,128)(2,1)}, u32[]{:S(2)}, u32[]{:S(2)}) %all-to-all-start) | async-done | bytes 7077920 | tf_op jit(solution)/shard_map/all_to_all | solution.py:176
  295.4 9.7 %conditional.1 = (bf16[24,384,384]{2,1,0:T(8,128)(2,1)}) conditional(s32[]{:T(128)} %convert_element_type.202, (bf16[24,2,384,384]{3,2,1,0:T(8,128)(2,1)}, bf16[24,16,24,384]{3,2,0,1:T(8,128)(2,1)}, bf16[384,2,384]{2,0,1:T(8,128)(2,1)S(1)}, bf16[2,384,2,384]{3,1,2,0:T(8,128)(2,1)S(1)}, bf16[2,384,2,384]{3,1,2,0:T(8,128)(2,1)S(1)}, ...), branch_computations={%region_2.3_spmd, %region_3.4_spmd} | conditional | flops 32713998336 | bytes 130940936 | solution.py:191
  301.2 3.9 broadcast.196
  305.1 7.2 %copy.38 = bf16[24,384,384]{2,0,1:T(8,128)(2,1)S(1)} copy(bf16[24,384,384]{2,1,0:T(8,128)(2,1)} %get-tuple-element.81) | data formatting | bytes 14155776 | tf_op jit(solution)/shard_map/cond | solution.py:191
  312.3 114.2 %all_to_all.33 = bf16[24,384,384]{2,0,1:T(8,128)(2,1)S(1)} all-to-all(bf16[24,384,384]{2,0,1:T(8,128)(2,1)S(1)} %copy.38), channel_id=1, replica_groups=mesh['section'=2,'tile'=16] {'tile'}, dimensions={1} | all-to-all | bytes 14155776 | tf_op jit(solution)/shard_map/all_to_all | solution.py:192
  426.4 1.3 copy.39
  427.7 0.7 fusion.78
  428.4 2.3 copy.40
  430.7 1.6 collective-permute-start.2
  432.3 0.5 copy.41
  432.8 4.9 copy.43
  437.7 87.6 %collective-permute-done.2 = bf16[192,24,384]{2,1,0:T(8,128)(2,1)} collective-permute-done((bf16[192,24,384]{2,1,0:T(8,128)(2,1)}, bf16[192,24,384]{2,1,0:T(8,128)(2,1)}, u32[]{:S(2)}, u32[]{:S(2)}) %collective-permute-start.2) | collective-permute-done | bytes 3538976 | tf_op jit(solution)/shard_map/ppermute | solution.py:14
  525.3 7.1 %copy.42 = bf16[192,24,384]{0,2,1:T(8,128)(2,1)} copy(bf16[192,24,384]{2,1,0:T(8,128)(2,1)} %collective-permute-done.2) | data formatting | bytes 7077888 | tf_op jit(solution)/shard_map/ppermute | solution.py:14
  532.4 10.1 %add_convert_fusion = bf16[192,24,384]{0,2,1:T(8,128)(2,1)} fusion(bf16[192,24,384]{0,2,1:T(8,128)(2,1)} %copy.42, bf16[192,24,384]{0,2,1:T(8,128)(2,1)} %copy.43, bf16[384,24,384]{0,2,1:T(8,128)(2,1)} %all-gather.2.cloned.1.call-done, s32[]{:T(128)S(6)} %select_n.65, pred[]{:T(512)S(6)} %eq.14), kind=kLoop, calls=%fused_computation.53 | loop fusion | flops 8847360 | bytes 14155781 | tf_op jit(solution)/shard_map/convert_element_type | solution.py:196
  542.5 6.8 %copy.44 = bf16[192,24,384]{2,1,0:T(8,128)(2,1)} copy(bf16[192,24,384]{0,2,1:T(8,128)(2,1)} %add_convert_fusion) | data formatting | bytes 7077888 | tf_op jit(solution)/shard_map/convert_element_type | solution.py:196
  (16 shorter events, 0.1 us)
Async XLA Ops:
  6.5 123.7 %all-gather.2.cloned.1.call-start = ((), (), s32[]{:S(2)}) async-start(), calls=%async_computation.2 | async-start | bytes 10616832 | tf_op jit(solution)/shard_map/all_gather | solution.py:163
  22.2 37.1 %copy-start.1 = (bf16[3,3,192,384]{3,2,1,0:T(8,128)(2,1)S(1)}, bf16[3,3,192,384]{3,2,1,0:T(8,128)(2,1)}, u32[]{:S(2)}) copy-start(bf16[3,3,192,384]{3,2,1,0:T(8,128)(2,1)} %param.16) | copy-start | bytes 3981316
  56.4 13.5 %collective-permute-start = (bf16[24,1,768]{2,1,0:T(2,128)(2,1)S(1)}, bf16[24,1,768]{2,1,0:T(2,128)(2,1)S(1)}, u32[]{:S(2)}, u32[]{:S(2)}) collective-permute-start(bf16[24,1,768]{2,1,0:T(2,128)(2,1)S(1)} %slice.88), channel_id=1, source_target_pairs={{0,16},{1,17},{2,18},{3,19},{4,20},{5,21},{6,22},{7,23},{8,24},{9,... | collective-permute-start | bytes 110600 | tf_op jit(solution)/shard_map/ppermute | solution.py:14
  59.6 10.3 %slice-start = ((s8[7077888]{0:T(1024)(128)(4,1)}), s8[4194304]{0:T(1024)(128)(4,1)S(1)}, s32[]{:S(2)}) async-start(s8[7077888]{0:T(1024)(128)(4,1)} %bitcast.135), calls=%async_computation.3 | async-start | bytes 8388608
  59.6 10.3 %slice-start.1 = ((s8[7077888]{0:T(1024)(128)(4,1)}), s8[2883584]{0:T(1024)(128)(4,1)S(1)}, s32[]{:S(2)}) async-start(s8[7077888]{0:T(1024)(128)(4,1)} %bitcast.135), calls=%async_computation.4 | async-start | bytes 5767168
  70.0 10.5 %collective-permute-start.1 = (bf16[1,193,768]{2,1,0:T(8,128)(2,1)S(1)}, bf16[1,193,768]{2,1,0:T(8,128)(2,1)S(1)}, u32[]{:S(2)}, u32[]{:S(2)}) collective-permute-start(bf16[1,193,768]{2,1,0:T(8,128)(2,1)S(1)} %pad_maximum_fusion.11), channel_id=1, source_target_pairs={{0,1},{1,2},{2,3},{3,4},{4,5},{5,6},{6,7},{7,8},{8,9},{9,10},{10,1... | collective-permute-start | bytes 889352 | tf_op jit(solution)/shard_map/ppermute | solution.py:14
  85.1 9.8 %copy-start.2 = (f32[384]{0:T(512)S(1)}, f32[384]{0:T(512)}, u32[]{:S(2)}) copy-start(f32[384]{0:T(512)} %param.17) | copy-start | bytes 4612
  109.9 28.9 %copy-start.3 = (f32[384]{0:T(512)S(1)}, f32[384]{0:T(512)}, u32[]{:S(2)}) copy-start(f32[384]{0:T(512)} %param.18) | copy-start | bytes 4612
  130.3 5.0 copy-start
  153.8 141.6 %all-to-all-start = ((bf16[384,24,384]{2,1,0:T(8,128)(2,1)}), bf16[384,24,384]{2,1,0:T(8,128)(2,1)}, u32[]{:S(2)}, u32[]{:S(2)}) async-start(bf16[384,24,384]{2,1,0:T(8,128)(2,1)} %copy.35), calls=%async_computation | async-start | bytes 14155776 | tf_op jit(solution)/shard_map/all_to_all | solution.py:176
  430.7 94.5 %collective-permute-start.2 = (bf16[192,24,384]{2,1,0:T(8,128)(2,1)}, bf16[192,24,384]{2,1,0:T(8,128)(2,1)}, u32[]{:S(2)}, u32[]{:S(2)}) collective-permute-start(bf16[192,24,384]{2,1,0:T(8,128)(2,1)} %bitcast.51), channel_id=1, source_target_pairs={{16,0},{17,1},{18,2},{19,3},{20,4},{21,5},{22,6},{23,7},{24,8},{25... | collective-permute-start | bytes 10616840 | tf_op jit(solution)/shard_map/ppermute | solution.py:14
Sparse Core Ops, SparseCore 0:
  110.0 20.1 all-gather.1
where the time goes:
time: 560 us; the launch traced here: 557 us
  waiting for transfers between devices  231 us (41%)
  blocking collectives  114 us (20%)
  matrix products  73.6 us (13%)
  local copies, waits for them, and re-layouts  56.4 us (10%)
  other arithmetic  46.2 us (8%)
  starting transfers between devices  15.5 us (3%)
  between operations  14 us (2%)
  loops' own time  5.79 us (1%)
    all_to_all x1, waiting for transfers between devices, local(): lax.all_to_all(normed, 'tile', split_axis=0, concat_axis=1, tiled=True)  123 us
    all_to_all x1, blocking collectives, local(): lax.all_to_all(filtered_fields, 'tile', split_axis=1, concat_axis=0, tile...  114 us
    ppermute x3, waiting for transfers between devices, from_behind(): return lax.ppermute(block, axis, route)  88 us
    dot_general x1, matrix products, stem_layers(): jnp.einsum('zji,if->zjf', initial_layer, merging_kernel_matrix(merging_co...  33.1 us
    all_gather x1, waiting for transfers between devices, local(): features = lax.all_gather(feature_half, 'section', axis=2, tiled=True)  20.3 us
    dot_general x1, matrix products, down_conv(): jnp.einsum('rwk,kc->crw', stacked[:-1, :-1], corner_taps, preferred_eleme...  14.9 us
  transfers between devices with their start and end apart: 5, of which 4 were waited for; matrix products, arithmetic and copies ran while one was open for 6% of the time, Pallas kernels for 0%

commit v1 on v0

--- a/solution.py
+++ b/solution.py
@@ -1,8 +1,11 @@
+import functools
 import math
 
 import jax
 import jax.numpy as jnp
 from jax import lax
+from jax.experimental import pallas as pl
+from jax.experimental.pallas import tpu as pltpu
 from jax.sharding import PartitionSpec as P
 
 EPSILON = 1e-05
@@ -131,7 +134,7 @@
     ).astype(jnp.bfloat16)
 
 
-def local(
+def general_local(
     aerial_patch_grid,
     patch_conv_weight,
     patch_bias,
@@ -196,6 +199,489 @@
     return (own_part.astype(jnp.float32) + filtered.astype(jnp.float32)).astype(jnp.bfloat16)
 
 
+DEVICES = ("tile", "section")
+GELU_LINEAR = 2.0 * math.sqrt(2.0 / math.pi)
+GELU_CUBIC = 4.0 * 0.044715 * GELU_LINEAR
+ONES = 16
+
+
+def split_bias(bias):
+    parts = []
+    left = bias
+    for _ in range(3):
+        part = left.astype(jnp.bfloat16)
+        parts.append(part)
+        left = left - part.astype(jnp.float32)
+    parts += [jnp.zeros_like(parts[0])] * (ONES - 3)
+    return jnp.stack(parts, axis=1)
+
+
+def stem_weights(
+    patch_conv_weight, patch_bias, merging_conv_weight, merge_bias, down_weight, down_bias
+):
+    half = jnp.asarray(0.5, jnp.bfloat16)
+    width = patch_conv_weight.shape[3]
+    bands = patch_conv_weight.shape[0]
+    identity = jnp.eye(4, dtype=jnp.bfloat16)
+    first = jnp.einsum("baqk,vw->vkbawq", patch_conv_weight, identity)
+    first = first.reshape(4 * width, bands * 64) * half
+    first = jnp.concatenate([first, split_bias(jnp.tile(0.5 * patch_bias, 4))], axis=1)
+    merged = merging_conv_weight.shape[3]
+    second = merging_conv_weight.reshape(4 * width, merged).T * half
+    second = jnp.concatenate([second, split_bias(0.5 * merge_bias)], axis=1)
+    taps = [(1, 1), (1, 2), (2, 1), (2, 2), (1, 0), (2, 0), (0, 1), (0, 2), (0, 0)]
+    third = jnp.concatenate([down_weight[a, q] for a, q in taps], axis=0).T
+    third = jnp.concatenate([third, split_bias(down_bias)], axis=1)
+    return first, second, third
+
+
+def half_gelu(h):
+    return h + h * jnp.tanh(h * (GELU_LINEAR + GELU_CUBIC * (h * h)))
+
+
+def stem_kernel(
+    place_ref, x_ref, halo_ref, w1_ref, w2_ref, w3_ref, gain_ref, normed_ref, feat_ref, field
+):
+    step = pl.program_id(0)
+    rows, cols, depth = x_ref.shape
+    bands = depth // 256
+    channels = w3_ref.shape[0]
+    merged = w2_ref.shape[0]
+    group = normed_ref.shape[2] // rows
+    cells = rows * cols
+    w1 = w1_ref[...]
+    w2 = w2_ref[...]
+
+    def ones(n):
+        return jnp.where(lax.broadcasted_iota(jnp.int32, (ONES, n), 0) < 3, 1.0, 0.0).astype(
+            jnp.bfloat16
+        )
+
+    def layer_one(turned, offsets):
+        n = turned.shape[1]
+        parts = [turned[o : o + 64] for o in offsets] + [ones(n)]
+        h = jnp.dot(w1, jnp.concatenate(parts, axis=0), preferred_element_type=jnp.float32)
+        return half_gelu(h).astype(jnp.bfloat16)
+
+    def layer_two(upper, lower, y):
+        n = upper.shape[1]
+        span = slice(2 * y * (w1.shape[0] // 4), 2 * (y + 1) * (w1.shape[0] // 4))
+        stacked = jnp.concatenate([upper[span], lower[span], ones(n)], axis=0)
+        return half_gelu(jnp.dot(w2, stacked, preferred_element_type=jnp.float32))
+
+    def shifted(values):
+        lanes = lax.broadcasted_iota(jnp.int32, values.shape, 1)
+        moved = pltpu.roll(values, 1, 1)
+        return jnp.where(lax.rem(lanes, cols) == 0, 0.0, moved)
+
+    def put(block, lanes, values):
+        field[block * merged : (block + 1) * merged, lanes] = values.astype(jnp.bfloat16)
+
+    first_row = slice(0, cols)
+    last_row = slice(cells - cols, cells)
+    later_rows = slice(cols, cells)
+    earlier_rows = slice(0, cells - cols)
+
+    @pl.when(step == 0)
+    def _():
+        field[9 * merged : 9 * merged + ONES, :] = ones(cells)
+        turned = halo_ref[...].T
+        keep = place_ref[1].astype(jnp.float32)
+        upper, lower = (
+            layer_one(turned, [128 * b + 64 * a for b in range(bands)]) for a in range(2)
+        )
+        put(6, first_row, layer_two(upper, lower, 0) * keep)
+        right = layer_two(upper, lower, 1) * keep
+        put(7, first_row, right)
+        put(8, first_row, shifted(right))
+
+    @pl.when(step > 0)
+    def _():
+        for source, target in ((2, 6), (3, 7), (5, 8)):
+            field[target * merged : (target + 1) * merged, first_row] = field[
+                source * merged : (source + 1) * merged, last_row
+            ]
+
+    turned = x_ref[...].reshape(cells, depth).T
+    for x in range(2):
+        upper, lower = (
+            layer_one(turned, [256 * b + 64 * (2 * x + a) for b in range(bands)])
+            for a in range(2)
+        )
+        left = layer_two(upper, lower, 0)
+        right = layer_two(upper, lower, 1)
+        put(2 * x, slice(None), left)
+        put(2 * x + 1, slice(None), right)
+        moved = shifted(right)
+        put(4 + x, slice(None), moved)
+        if x == 1:
+            put(6, later_rows, left[:, earlier_rows])
+            put(7, later_rows, right[:, earlier_rows])
+            put(8, later_rows, moved[:, earlier_rows])
+
+    features = jnp.dot(w3_ref[...], field[...], preferred_element_type=jnp.float32).astype(
+        jnp.bfloat16
+    )
+    for r in range(rows):
+        feat_ref[r] = features[:, r * cols : (r + 1) * cols]
+    values = features.astype(jnp.float32)
+    centered = values - jnp.mean(values, axis=0, keepdims=True)
+    variance = jnp.mean(centered * centered, axis=0, keepdims=True)
+    normed = gain_ref[...] * (centered * lax.rsqrt(variance + EPSILON))
+    pair = 2 * group
+    index = lax.broadcasted_iota(jnp.int32, (pair, cols), 0)
+    for t in range(channels // pair):
+        one = normed[pair * t : pair * (t + 1), :cols]
+        two = normed[pair * t : pair * (t + 1), cols:]
+        normed_ref[2 * t, 0] = jnp.where(index < group, one, pltpu.roll(two, group, 0)).astype(
+            jnp.bfloat16
+        )
+        normed_ref[2 * t + 1, 0] = jnp.where(
+            index < group, pltpu.roll(one, group, 0), two
+        ).astype(jnp.bfloat16)
+
+
+def stem(image, halo, place, weights, norm_gain, devices):
+    tile_rows, cols, depth = image.shape
+    rows = tile_rows // 2
+    first, second, third = weights
+    channels = third.shape[0]
+    merged = second.shape[0]
+    steps = rows // 2
+    group = channels // devices
+    gain = jnp.broadcast_to(norm_gain[:, None], (channels, 2 * cols)).astype(jnp.float32)
+
+    def whole(array):
+        return pl.BlockSpec(array.shape, lambda i, place: (0,) * array.ndim)
+
+    operands = (halo, first, second, third, gain)
+    macs = rows * cols * (16 * 208 * 96 + 4 * 400 * merged + third.shape[1] * channels)
+    return pl.pallas_call(
+        stem_kernel,
+        grid_spec=pltpu.PrefetchScalarGridSpec(
+            num_scalar_prefetch=1,
+            grid=(steps,),
+            in_specs=[pl.BlockSpec((2, cols, depth), lambda i, place: (place[0] + i, 0, 0))]
+            + [whole(a) for a in operands],
+            out_specs=[
+                pl.BlockSpec((devices, 1, 2 * group, cols), lambda i, place: (0, i, 0, 0)),
+                pl.BlockSpec((2, channels, cols), lambda i, place: (i, 0, 0)),
+            ],
+            scratch_shapes=[pltpu.VMEM((9 * merged + ONES, 2 * cols), jnp.bfloat16)],
+        ),
+        out_shape=[
+            jax.ShapeDtypeStruct((devices, steps, 2 * group, cols), jnp.bfloat16),
+            jax.ShapeDtypeStruct((rows, channels, cols), jnp.bfloat16),
+        ],
+        compiler_params=pltpu.CompilerParams(vmem_limit_bytes=56 * 1024 * 1024),
+        cost_estimate=pl.CostEstimate(
+            flops=2 * macs, bytes_accessed=rows * cols * 3000, transcendentals=0
+        ),
+        name="stem",
+    )(place, image, *operands)
+
+
+def symmetric_kernel(place_ref, f_ref, turn_w_ref, turn_u_ref, g_ref):
+    width = g_ref.shape[3]
+    for part in range(2):
+        block = f_ref[0, part]
+        across = jnp.dot(block, turn_w_ref[...], preferred_element_type=jnp.float32)
+        turned = jnp.dot(
+            turn_u_ref[...], across.astype(jnp.bfloat16), preferred_element_type=jnp.float32
+        )
+        own = block[:, :width].astype(jnp.float32)
+        g_ref[0, part] = 0.5 * (own + turned if part == 0 else own - turned)
+
+
+def symmetric_filter(spectral_filter, place, group, width):
+    full_rows, full_cols = spectral_filter.shape[2:]
+    u = jnp.arange(full_rows, dtype=jnp.int32)
+    w = jnp.arange(full_cols, dtype=jnp.int32)
+    turn_u = ((u[:, None] + u[None, :]) % full_rows == 0).astype(jnp.bfloat16)
+    turn_w = ((w[:, None] + w[None, :width]) % full_cols == 0).astype(jnp.bfloat16)
+    return pl.pallas_call(
+        symmetric_kernel,
+        grid_spec=pltpu.PrefetchScalarGridSpec(
+            num_scalar_prefetch=1,
+            grid=(group,),
+            in_specs=[
+                pl.BlockSpec(
+                    (1, 2, full_rows, full_cols), lambda i, place: (place[0] + i, 0, 0, 0)
+                ),
+                pl.BlockSpec(turn_w.shape, lambda i, place: (0, 0)),
+                pl.BlockSpec(turn_u.shape, lambda i, place: (0, 0)),
+            ],
+            out_specs=pl.BlockSpec((1, 2, full_rows, width), lambda i, place: (i, 0, 0, 0)),
+        ),
+        out_shape=jax.ShapeDtypeStruct((group, 2, full_rows, width), jnp.float32),
+        compiler_params=pltpu.CompilerParams(vmem_limit_bytes=32 * 1024 * 1024),
+        cost_estimate=pl.CostEstimate(
+            flops=8 * group * full_rows * full_cols * width,
+            bytes_accessed=group * full_rows * width * 14,
+            transcendentals=0,
+        ),
+        name="symmetric_filter",
+    )(place, spectral_filter, turn_w, turn_u)
+
+
+def to_lane_tiles(target, rows, values):
+    for j in range(target.shape[0]):
+        target[j, rows, :] = values[:, 128 * j : 128 * (j + 1)]
+
+
+def from_lane_tiles(source, rows):
+    return jnp.concatenate([source[j, rows, :] for j in range(source.shape[0])], axis=1)
+
+
+def filter_kernel(
+    first, norm_scale, fields_ref, g_ref, row_table_ref, fwd_ref, inv_ref, back_ref, out_ref, held, made
+):
+    step = pl.program_id(0)
+    full_rows = fwd_ref.shape[0] // 2
+    width = g_ref.shape[3]
+    group = held.shape[1] // full_rows
+    count = made.shape[1] // full_rows
+    per_step = g_ref.shape[0]
+
+    @pl.when(step == 0)
+    def _():
+        to_lane_tiles(held, slice(None), fields_ref[...].astype(jnp.float32))
+
+    blocks = []
+    for k in range(per_step):
+        rows = pl.ds(first + step * per_step + k, full_rows, stride=group)
+        field = from_lane_tiles(held, rows)
+        spread = jnp.dot(
+            field.astype(jnp.bfloat16), row_table_ref[...], preferred_element_type=jnp.float32
+        ).astype(jnp.bfloat16)
+        blocks.append(jnp.concatenate([spread[:, :width], spread[:, width:]], axis=0))
+    spectrum = jnp.dot(
+        fwd_ref[...], jnp.concatenate(blocks, axis=1), preferred_element_type=jnp.float32
+    )
+    blocks = []
+    for k in range(per_step):
+        real = spectrum[:full_rows, k * width : (k + 1) * width]
+        imag = spectrum[full_rows:, k * width : (k + 1) * width]
+        g_real = g_ref[k, 0]
+        g_imag = g_ref[k, 1]
+        blocks.append(
+            jnp.concatenate(
+                [g_real * real - g_imag * imag, g_real * imag + g_imag * real], axis=0
+            ).astype(jnp.bfloat16)
+        )
+    back = jnp.dot(
+        inv_ref[...], jnp.concatenate(blocks, axis=1), preferred_element_type=jnp.float32
+    ).astype(jnp.bfloat16)
+    for k in range(per_step):
+        lanes = slice(k * width, (k + 1) * width)
+        both = jnp.concatenate([back[:full_rows, lanes], back[full_rows:, lanes]], axis=1)
+        result = jnp.dot(both, back_ref[...], preferred_element_type=jnp.float32)
+        rows = pl.ds(step * per_step + k, full_rows, stride=count)
+        to_lane_tiles(made, rows, result * norm_scale)
+
+    @pl.when(step == pl.num_programs(0) - 1)
+    def _():
+        out_ref[...] = from_lane_tiles(made, slice(None)).astype(jnp.bfloat16)
+
+
+def filter_tables(full_rows, field_cols, width):
+    cos_h, sin_h = fourier_tables(full_rows)
+    cos_w, sin_w = fourier_tables(field_cols)
+    fwd = jnp.concatenate(
+        [jnp.concatenate([cos_h, sin_h], 1), jnp.concatenate([-sin_h, cos_h], 1)], 0
+    )
+    inv = jnp.concatenate(
+        [jnp.concatenate([cos_h, -sin_h], 1), jnp.concatenate([sin_h, cos_h], 1)], 0
+    )
+    w = jnp.arange(width, dtype=jnp.int32)
+    half = field_cols // 2
+    valid = (w <= half).astype(jnp.bfloat16)
+    times = jnp.where((w == 0) | (w == half), 1.0, 2.0).astype(jnp.bfloat16) * valid
+    row_table = jnp.concatenate([cos_w[:, :width] * valid, -sin_w[:, :width] * valid], 1)
+    back_table = jnp.concatenate(
+        [cos_w[:width] * times[:, None], -sin_w[:width] * times[:, None]], 0
+    )
+    return row_table, fwd, inv, back_table
+
+
+def filter_channels(fields, symmetric, tables, first, count, per_step, devices):
+    row_table, fwd, inv, back_table = tables
+    full_rows = fwd.shape[0] // 2
+    cols = fields.shape[1]
+    group = fields.shape[0] // full_rows
+    width = symmetric.shape[3]
+
+    def whole(array):
+        return pl.BlockSpec(array.shape, lambda i: (0,) * array.ndim)
+
+    macs = count * (2 * 4 * full_rows * full_rows * width + 4 * full_rows * cols * width)
+    made = pl.pallas_call(
+        functools.partial(filter_kernel, first, 1.0 / (full_rows * cols)),
+        grid=(count // per_step,),
+        in_specs=[
+            whole(fields),
+            pl.BlockSpec(
+                (per_step, 2, full_rows, width), lambda i: (first // per_step + i, 0, 0, 0)
+            ),
+            whole(row_table),
+            whole(fwd),
+            whole(inv),
+            whole(back_table),
+        ],
+        out_specs=pl.BlockSpec((full_rows * count, cols), lambda i: (0, 0)),
+        out_shape=jax.ShapeDtypeStruct((full_rows * count, cols), jnp.bfloat16),
+        scratch_shapes=[
+            pltpu.VMEM((cols // 128, full_rows * group, 128), jnp.float32),
+            pltpu.VMEM((cols // 128, full_rows * count, 128), jnp.float32),
+        ],
+        compiler_params=pltpu.CompilerParams(vmem_limit_bytes=56 * 1024 * 1024),
+        cost_estimate=pl.CostEstimate(
+            flops=2 * macs, bytes_accessed=count * full_rows * cols * 8, transcendentals=0
+        ),
+        name="spectral_filter",
+    )(fields, symmetric, row_table, fwd, inv, back_table)
+    return made.reshape(devices, full_rows // devices * count, cols)
+
+
+def residual_kernel(count, place_ref, kept_ref, other_ref, feat_ref, *refs):
+    out_ref, held = refs[-2:]
+    span = kept_ref.shape[1]
+    rows = held.shape[1] // count
+    own = pl.multiple_of(place_ref[0] * span, 8)
+    far = pl.multiple_of((1 - place_ref[0]) * span, 8)
+    to_lane_tiles(held, pl.ds(own, span), kept_ref[0].astype(jnp.float32))
+    to_lane_tiles(held, pl.ds(far, span), other_ref[0].astype(jnp.float32))
+    for k in range(count):
+        filtered = from_lane_tiles(held, pl.ds(k, rows, stride=count))
+        out_ref[0, k] = (feat_ref[0, k].astype(jnp.float32) + filtered).astype(jnp.bfloat16)
+
+
+def add_residual(place, returned, other, features, previous, part, parts):
+    halves, span, cols = other.shape
+    group, rows = features.shape[1:3]
+    count = group // parts
+    block = pl.BlockSpec((1, count, rows, cols), lambda i, place: (i, part, 0, 0))
+    operands = [returned, other, features]
+    in_specs = [
+        pl.BlockSpec((1, span, cols), lambda i, place: (place[0] * halves + i, 0, 0)),
+        pl.BlockSpec((1, span, cols), lambda i, place: (i, 0, 0)),
+        block,
+    ]
+    aliases = {}
+    if previous is not None:
+        operands.append(previous)
+        in_specs.append(pl.BlockSpec(memory_space=pl.ANY))
+        aliases = {4: 0}
+    return pl.pallas_call(
+        functools.partial(residual_kernel, count),
+        grid_spec=pltpu.PrefetchScalarGridSpec(
+            num_scalar_prefetch=1,
+            grid=(halves,),
+            in_specs=in_specs,
+            out_specs=block,
+            scratch_shapes=[pltpu.VMEM((cols // 128, rows * count, 128), jnp.float32)],
+        ),
+        out_shape=jax.ShapeDtypeStruct(features.shape, jnp.bfloat16),
+        input_output_aliases=aliases,
+        compiler_params=pltpu.CompilerParams(vmem_limit_bytes=32 * 1024 * 1024),
+        cost_estimate=pl.CostEstimate(
+            flops=halves * count * rows * cols,
+            bytes_accessed=halves * count * rows * cols * 8,
+            transcendentals=0,
+        ),
+        name="residual",
+    )(place, *operands)
+
+
+def swap(block):
+    return lax.ppermute(block, "section", [(0, 1), (1, 0)])
+
+
+def local(
+    aerial_patch_grid,
+    patch_conv_weight,
+    patch_bias,
+    merging_conv_weight,
+    merge_bias,
+    down_weight,
+    down_bias,
+    norm_gain,
+    spectral_filter,
+):
+    tile_rows, field_cols, depth = aerial_patch_grid.shape
+    channels = down_weight.shape[3]
+    tile_channels = spectral_filter.shape[0]
+    full_rows = spectral_filter.shape[2]
+    sections = lax.axis_size("section")
+    devices = sections * lax.axis_size("tile")
+    suits = (
+        sections == 2
+        and tile_rows % 4 == 0
+        and tile_channels % 4 == 0
+        and (tile_rows // 2) * (tile_channels // 4) % 8 == 0
+        and field_cols % 128 == 0
+        and full_rows % 128 == 0
+        and tile_channels % 8 == 0
+    )
+    arguments = (
+        aerial_patch_grid,
+        patch_conv_weight,
+        patch_bias,
+        merging_conv_weight,
+        merge_bias,
+        down_weight,
+        down_bias,
+        norm_gain,
+        spectral_filter,
+    )
+    if not suits:
+        return general_local(*arguments)
+    section = lax.axis_index("section")
+    tile = lax.axis_index("tile")
+    rows = tile_rows // 2
+    group = tile_channels // 2
+    half_channels = channels // 2
+    width = -(-(field_cols // 2 + 1) // 128) * 128
+
+    def lower_half(row):
+        return jnp.concatenate(
+            [row[:, 256 * b + 128 : 256 * b + 256] for b in range(depth // 256)], axis=1
+        )
+
+    arriving = from_behind(lower_half(aerial_patch_grid[-1]), "tile", 1)
+    halo = jnp.where(section == 0, arriving, lower_half(aerial_patch_grid[rows - 1]))
+    inside = ((section > 0) | (tile > 0)).astype(jnp.int32)
+    weights = stem_weights(*arguments[1:7])
+    place = jnp.stack([section * (rows // 2), inside]).astype(jnp.int32)
+    normed, features = stem(aerial_patch_grid, halo, place, weights, norm_gain, devices)
+    fields = lax.all_to_all(normed, DEVICES, split_axis=0, concat_axis=0, tiled=True)
+    fields = fields.reshape(full_rows * group, field_cols)
+
+    channel_place = jnp.reshape(section * group, (1,)).astype(jnp.int32)
+    symmetric = symmetric_filter(spectral_filter, channel_place, group, width)
+    tables = filter_tables(full_rows, field_cols, width)
+
+    own = lax.dynamic_slice_in_dim(features, section * half_channels, half_channels, 1)
+    sent = lax.dynamic_slice_in_dim(features, (1 - section) * half_channels, half_channels, 1)
+    arrived = swap(sent)
+    low = jnp.where(section == 0, own, arrived)
+    high = jnp.where(section == 0, arrived, own)
+    residual = jnp.transpose(jnp.concatenate([low, high], axis=0), (1, 0, 2))
+    residual = residual.reshape(half_channels // group, group, tile_rows, field_cols)
+
+    parts = 2
+    count = group // parts
+    section_place = jnp.reshape(section, (1,)).astype(jnp.int32)
+    output = None
+    for part in range(parts):
+        made = filter_channels(fields, symmetric, tables, part * count, count, 2, devices)
+        returned = lax.all_to_all(made, DEVICES, split_axis=0, concat_axis=0, tiled=True)
+        halves = devices // 2
+        other = swap(lax.dynamic_slice_in_dim(returned, (1 - section) * halves, halves, 0))
+        output = add_residual(section_place, returned, other, residual, output, part, parts)
+    return output.reshape(half_channels, tile_rows, field_cols)
+
+
 def solution(mesh):
     return jax.shard_map(
         local,

time: 560 us -> 276 us (0.49)
  blocking collectives: 114 us -> 0 us
  waiting for transfers between devices: 231 us -> 121 us
  Pallas kernels: 0 us -> 83.7 us
  matrix products: 73.6 us -> 0 us
  other arithmetic: 46.2 us -> 15.4 us
  local copies, waits for them, and re-layouts: 56.4 us -> 34.3 us
  between operations: 14 us -> 0.5 us
  loops' own time: 5.79 us -> 0 us
    all_to_all x1 -> x0, blocking collectives: 114 us -> none  [local(): lax.all_to_all(filtered_fields, 'tile', split_axis=1, concat_axis=0, tile...]
    ppermute x3 -> x1, waiting for transfers between devices: 88 us -> 0.01 us  [from_behind(): return lax.ppermute(block, axis, route)]
    pallas_call x0 -> x6, Pallas kernels: none -> 83.7 us  [the longest x1 28 us: stem(): pl.pallas_call(stem_kernel, grid_spec=pltpu.PrefetchScalarGridSpec(num_sc...]
    dot_general x5 -> x0, matrix products: 73.6 us -> none  [the longest x1 33.1 us: stem_layers(): jnp.einsum('zji,if->zjf', initial_layer, merging_kernel_matrix(merging_co...]
    convert_element_type x4 -> x2, local copies, waits for them, and re-layouts: 25.1 us -> 1.62 us  [the longest x1 0.83 us: split_bias(): left = left - part.astype(jnp.float32)]
    convert_element_type x6 -> x7, other arithmetic: 23.7 us -> 0.6 us  [the longest x1 0.29 us: symmetric_filter(): turn_u = ((u[:, None] + u[None, :]) % full_rows == 0).astype(jnp.bfloat16)]
    all_gather x1 -> x0, waiting for transfers between devices: 20.3 us -> none  [local(): features = lax.all_gather(feature_half, 'section', axis=2, tiled=True)]
    slice x5, local copies, waits for them, and re-layouts: 9.45 us -> 1.05 us  [the longest x1 0.94 us: stem_weights(): third = jnp.concatenate([down_weight[a, q] for a, q in taps], axis=0).T]
  transfers between devices with their start and end apart: 5 -> 7, of which waited for: 4 -> 3; matrix products, arithmetic and copies ran while one was open for 6% -> 14% of each run, Pallas kernels for 0% -> 12%
where the time goes in v1:
time: 276 us; the launch traced here: 274 us
  waiting for transfers between devices  121 us (44%)
  Pallas kernels  83.7 us (30%)
  local copies, waits for them, and re-layouts  34.3 us (12%)
  starting transfers between devices  18.6 us (7%)
  other arithmetic  15.4 us (6%)
    all_to_all x2, waiting for transfers between devices, local(): lax.all_to_all(made, DEVICES, split_axis=0, concat_axis=0, tiled=True)  66.5 us
    all_to_all x1, waiting for transfers between devices, local(): lax.all_to_all(normed, DEVICES, split_axis=0, concat_axis=0, tiled=True)  54.7 us
    pallas_call x1, Pallas kernels, stem(): pl.pallas_call(stem_kernel, grid_spec=pltpu.PrefetchScalarGridSpec(num_sc...  28 us
    pallas_call x2, Pallas kernels, filter_channels(): pl.pallas_call(functools.partial(filter_kernel, first, 1.0 / (full_rows *...  25.1 us
    pallas_call x2, Pallas kernels, add_residual(): pl.pallas_call(functools.partial(residual_kernel, count), grid_spec=pltpu...  18.1 us
    pallas_call x1, Pallas kernels, symmetric_filter(): pl.pallas_call(symmetric_kernel, grid_spec=pltpu.PrefetchScalarGridSpec(n...  12.6 us
    unnamed x51, local copies, waits for them, and re-layouts  8.94 us
    all_to_all x2, starting transfers between devices, local(): lax.all_to_all(made, DEVICES, split_axis=0, concat_axis=0, tiled=True)  8.12 us
  transfers between devices with their start and end apart: 7, of which 3 were waited for; matrix products, arithmetic and copies ran while one was open for 14% of the time, Pallas kernels for 12%

profile of v1, /device:TPU:0, one launch (start us, length us, event | category | flops | bytes accessed | tf_op | source)
XLA Modules:
  0.0 273.8 jit_solution(2182490461024913362)
XLA Ops:
  0.0 1.4 slice_bitcast_fusion
  1.5 0.8 pad_maximum_fusion.6
  2.2 5.6 %collective-permute-start = (bf16[384,384]{1,0:T(8,128)(2,1)}, bf16[384,384]{1,0:T(8,128)(2,1)}, u32[]{:S(2)}, u32[]{:S(2)}) collective-permute-start(bf16[384,384]{1,0:T(8,128)(2,1)} %pad_maximum_fusion.6), channel_id=1, source_target_pairs={{0,1},{1,2},{2,3},{3,4},{4,5},{5,6},{6,7},{7,8},{8,9},{9,10},{10,1... | collective-permute-start | bytes 884744 | tf_op jit(solution)/shard_map/ppermute | solution.py:17
  7.8 0.1 tile.10
  7.9 0.1 copy.43
  8.1 0.7 stack.46
  8.8 0.7 stack.45
  9.5 0.7 stack.44
  10.2 0.1 stack.49
  10.4 0.8 copy.46
  11.2 0.7 stack.48
  11.9 0.7 stack.47
  12.7 0.8 copy.44
  13.5 0.1 multiply_bitcast_fusion
  13.6 0.2 mul.157
  13.8 0.8 copy.45
  14.7 0.8 copy.64
  15.4 0.9 fusion.26
  16.4 0.1 copy.73
  16.6 0.1 copy.72
  16.7 0.1 copy.71
  16.9 0.1 copy.70
  17.0 0.1 copy.69
  17.1 0.1 copy-done.9
  17.3 0.1 copy.68
  17.4 0.8 copy.67
  18.3 0.8 copy.66
  19.1 0.8 copy.65
  20.0 0.9 concatenate.53.w1_ref
  21.0 2.2 concatenate.57
  23.3 3.3 %concatenate.58.w3_ref = bf16[384,1744]{1,0:T(8,128)(2,1)} concatenate(bf16[384,1728]{1,0:T(8,128)(2,1)S(1)} %bitcast.33, bf16[384,1]{1,0:T(8,128)(2,1)} %stack.47, bf16[384,1]{1,0:T(8,128)(2,1)} %stack.48, bf16[384,1]{1,0:T(8,128)(2,1)S(1)} %stack.49, bf16[384,1]{1,0:T(8,128)(2,1)S(1)} %broadcast.65, bf16[384,4]{1,0:T(8,128)(2,1)S(1)} %broadcast.66, bf16[384,8]{1,0:T(8,128)(2,1)S(1)} %broadcast.67), dimensions={1} | concatenate | bytes 2678784 | tf_op jit(solution)/shard_map/concatenate | solution.py:234
  26.7 0.8 concatenate.56.w2_ref
  27.5 0.6 pad_add_fusion.place_ref
  28.2 1.8 maximum_select_fusion.halo_ref
  30.0 1.2 broadcast_in_dim.8.gain_ref
  31.2 28.0 %stem.1 = (bf16[32,6,24,384]{3,2,1,0:T(8,128)(2,1)}, bf16[12,384,384]{2,1,0:T(8,128)(2,1)}) custom-call(s32[2]{0:T(128)} %pad_add_fusion.place_ref, bf16[24,384,768]{2,1,0:T(8,128)(2,1)} %x_ref.1, bf16[384,384]{1,0:T(8,128)(2,1)} %maximum_select_fusion.halo_ref, bf16[384,208]{1,0:T(8,128)(2,1)} %concatenate.53.w1_ref, bf16[192,400]{1,0:T(8,128)(2,1)} %concatenate.56.w2_ref, ...), custom_call_target="tpu_custom_call" | custom-call | flops 11947474944 | bytes 13824000 | tf_op jit(solution)/shard_map/stem/pallas_call | solution.py:359
  59.2 4.4 %all-to-all-start = ((bf16[32,6,24,384]{3,2,1,0:T(8,128)(2,1)}), bf16[32,6,24,384]{3,2,1,0:T(8,128)(2,1)S(1)}, u32[]{:S(2)}, u32[]{:S(2)}) async-start(bf16[32,6,24,384]{3,2,1,0:T(8,128)(2,1)} %get-tuple-element.7), calls=%async_computation | async-start | bytes 7077888 | tf_op jit(solution)/shard_map/all_to_all | solution.py:657
  63.6 2.3 fusion.19
  66.0 0.3 fusion.10.turn_u_ref
  66.3 2.6 sine_convert_fusion
  68.8 0.1 slice_multiply_fusion
  68.9 0.8 pad_maximum_fusion.5.back_ref
  69.8 0.8 pad_maximum_fusion.4.row_table_ref
  70.6 1.6 fusion.1
  72.1 0.3 fusion.16.turn_w_ref
  72.4 12.6 %symmetric_filter.1.g_ref = f32[12,2,384,256]{3,2,1,0:T(8,128)S(1)} custom-call(s32[1]{0:T(128)} %bitcast.19.place_ref, bf16[24,2,384,384]{3,2,1,0:T(8,128)(2,1)} %f_ref.1, bf16[384,256]{1,0:T(8,128)(2,1)S(1)} %fusion.16.turn_w_ref, bf16[384,384]{1,0:T(8,128)(2,1)S(1)} %fusion.10.turn_u_ref), custom_call_target="tpu_custom_call" | custom-call | flops 3623878656 | bytes 16515072 | tf_op jit(solution)/shard_map/symmetric_filter/pallas_call | solution.py:402
  85.0 3.6 %copy-done = f32[12,2,384,256]{3,2,1,0:T(8,128)} copy-done((f32[12,2,384,256]{3,2,1,0:T(8,128)}, f32[12,2,384,256]{3,2,1,0:T(8,128)S(1)}, u32[]{:S(2)}) %copy-start) | copy-done | bytes 9437208
  88.6 54.7 %all-to-all-done = bf16[32,6,24,384]{3,2,1,0:T(8,128)(2,1)S(1)} async-done(((bf16[32,6,24,384]{3,2,1,0:T(8,128)(2,1)}), bf16[32,6,24,384]{3,2,1,0:T(8,128)(2,1)S(1)}, u32[]{:S(2)}, u32[]{:S(2)}) %all-to-all-start) | async-done | bytes 3538976 | tf_op jit(solution)/shard_map/all_to_all | solution.py:657
  143.3 1.8 copy-done.1
  145.1 12.6 %spectral_filter.3 = bf16[2304,384]{1,0:T(8,128)(2,1)} custom-call(bf16[4608,384]{1,0:T(8,128)(2,1)} %bitcast.34, f32[12,2,384,256]{3,2,1,0:T(8,128)} %copy-done, bf16[384,512]{1,0:T(8,128)(2,1)} %pad_maximum_fusion.4.row_table_ref, bf16[768,768]{1,0:T(8,128)(2,1)} %get-tuple-element.23.fwd_ref, bf16[768,768]{1,0:T(8,128)(2,1)} %get-tuple-element.22.inv_ref, ...), custom_call_target="tpu_custom_call" | custom-call | flops 5435817984 | bytes 7077888 | tf_op jit(solution)/shard_map/spectral_filter/pallas_call | solution.py:518
  157.7 3.9 %all-to-all-start.2 = ((bf16[32,72,384]{2,1,0:T(8,128)(2,1)}), bf16[32,72,384]{2,1,0:T(8,128)(2,1)S(1)}, u32[]{:S(2)}, u32[]{:S(2)}) async-start(bf16[32,72,384]{2,1,0:T(8,128)(2,1)} %bitcast.37), calls=%async_computation.2 | async-start | bytes 3538944 | tf_op jit(solution)/shard_map/all_to_all | solution.py:678
  161.6 12.6 %spectral_filter.2 = bf16[2304,384]{1,0:T(8,128)(2,1)} custom-call(bf16[4608,384]{1,0:T(8,128)(2,1)} %bitcast.35, f32[12,2,384,256]{3,2,1,0:T(8,128)} %copy-done, bf16[384,512]{1,0:T(8,128)(2,1)} %pad_maximum_fusion.4.row_table_ref, bf16[768,768]{1,0:T(8,128)(2,1)} %get-tuple-element.23.fwd_ref, bf16[768,768]{1,0:T(8,128)(2,1)} %get-tuple-element.22.inv_ref, ...), custom_call_target="tpu_custom_call" | custom-call | flops 5435817984 | bytes 7077888 | tf_op jit(solution)/shard_map/spectral_filter/pallas_call | solution.py:518
  174.2 29.2 %all-to-all-done.2.kept_ref = bf16[32,72,384]{2,1,0:T(8,128)(2,1)S(1)} async-done(((bf16[32,72,384]{2,1,0:T(8,128)(2,1)}), bf16[32,72,384]{2,1,0:T(8,128)(2,1)S(1)}, u32[]{:S(2)}, u32[]{:S(2)}) %all-to-all-start.2) | async-done | bytes 1769504 | tf_op jit(solution)/shard_map/all_to_all | solution.py:678
  203.4 4.2 %all-to-all-start.1 = ((bf16[32,72,384]{2,1,0:T(8,128)(2,1)}), bf16[32,72,384]{2,1,0:T(8,128)(2,1)S(1)}, u32[]{:S(2)}, u32[]{:S(2)}) async-start(bf16[32,72,384]{2,1,0:T(8,128)(2,1)} %bitcast.36), calls=%async_computation.1 | async-start | bytes 3538944 | tf_op jit(solution)/shard_map/all_to_all | solution.py:678
  207.6 2.9 %constant_dynamic-slice_fusion.1 = bf16[12,192,384]{2,1,0:T(8,128)(2,1)} fusion(bf16[12,384,384]{2,1,0:T(8,128)(2,1)} %get-tuple-element.8, s32[]{:T(128)S(6)} %select_n.90), kind=kLoop, calls=%fused_computation.62 | loop fusion | bytes 3538948 | tf_op jit(solution)/shard_map/dynamic_slice | solution.py:665
  210.5 1.0 constant_dynamic-slice_fusion
  211.6 0.5 collective-permute-start.3
  212.0 37.3 %all-to-all-done.1.kept_ref = bf16[32,72,384]{2,1,0:T(8,128)(2,1)S(1)} async-done(((bf16[32,72,384]{2,1,0:T(8,128)(2,1)}), bf16[32,72,384]{2,1,0:T(8,128)(2,1)S(1)}, u32[]{:S(2)}, u32[]{:S(2)}) %all-to-all-start.1) | async-done | bytes 1769504 | tf_op jit(solution)/shard_map/all_to_all | solution.py:678
  249.3 1.0 constant_dynamic-slice_fusion.2
  250.4 2.9 %broadcast_select_fusion.1 = (bf16[12,192,384]{2,1,0:T(8,128)(2,1)S(1)}, bf16[12,192,384]{2,1,0:T(8,128)(2,1)S(1)}) fusion(bf16[12,192,384]{2,1,0:T(8,128)(2,1)} %collective-permute-done.2, pred[]{:T(512)S(6)} %eq.43, bf16[12,384,384]{2,1,0:T(8,128)(2,1)} %get-tuple-element.8, s32[]{:T(128)S(6)} %select_n.89), kind=kLoop, calls=%fused_computation.2 | loop fusion | flops 1769472 | bytes 7077893 | tf_op jit(solution)/shard_map/jit(_where)/select_n | solution.py:667
  253.2 0.4 maximum_bitcast_fusion
  253.6 2.1 copy.63
  255.8 9.0 %residual.2.refs_0_ = bf16[16,12,24,384]{3,2,1,0:T(8,128)(2,1)} custom-call(s32[1]{0:T(128)} %bitcast.place_ref, bf16[32,72,384]{2,1,0:T(8,128)(2,1)S(1)} %all-to-all-done.2.kept_ref, bf16[16,72,384]{2,1,0:T(8,128)(2,1)} %collective-permute-done.3.other_ref, bf16[16,12,24,384]{3,2,1,0:T(8,128)(2,1)S(1)} %bitcast.31), custom_call_target="tpu_custom_call" | custom-call | flops 884736 | bytes 7077888 | tf_op jit(solution)/shard_map/residual/pallas_call | solution.py:575
  264.8 9.0 %residual.3 = bf16[16,12,24,384]{3,2,1,0:T(8,128)(2,1)} custom-call(s32[1]{0:T(128)} %bitcast.place_ref, bf16[32,72,384]{2,1,0:T(8,128)(2,1)S(1)} %all-to-all-done.1.kept_ref, bf16[16,72,384]{2,1,0:T(8,128)(2,1)} %collective-permute-done.1.other_ref, bf16[16,12,24,384]{3,2,1,0:T(8,128)(2,1)S(1)} %bitcast.32, ...), custom_call_target="tpu_custom_call", output_to_operand_aliasing={{}: (4, {})} | custom-call | flops 884736 | bytes 7077888 | tf_op jit(solution)/shard_map/residual/pallas_call | solution.py:575
  (67 shorter events, 0.4 us)
Async XLA Ops:
  0.0 7.8 %copy-start.20 = (f32[96]{0:T(128)S(1)}, f32[96]{0:T(128)}, u32[]{:S(2)}) copy-start(f32[96]{0:T(128)} %param.11) | copy-start | bytes 1156
  0.0 8.1 %copy-start.19 = (f32[192]{0:T(256)S(1)}, f32[192]{0:T(256)}, u32[]{:S(2)}) copy-start(f32[192]{0:T(256)} %param.13) | copy-start | bytes 2308
  0.0 8.1 %copy-start.18 = (f32[384]{0:T(512)S(1)}, f32[384]{0:T(512)}, u32[]{:S(2)}) copy-start(f32[384]{0:T(512)} %param.15) | copy-start | bytes 4612
  0.0 13.5 %copy-start.15 = (bf16[3,4,4,96]{3,2,1,0:T(4,128)(2,1)S(1)}, bf16[3,4,4,96]{3,2,1,0:T(4,128)(2,1)}, u32[]{:S(2)}) copy-start(bf16[3,4,4,96]{3,2,1,0:T(4,128)(2,1)} %param.10) | copy-start | bytes 27652
  1.4 13.2 %copy-start.14 = (bf16[2,2,96,192]{3,2,1,0:T(8,128)(2,1)S(1)}, bf16[2,2,96,192]{3,2,1,0:T(8,128)(2,1)}, u32[]{:S(2)}) copy-start(bf16[2,2,96,192]{3,2,1,0:T(8,128)(2,1)} %param.12) | copy-start | bytes 442372
  1.4 14.0 %copy-start.2 = (bf16[3,3,192,384]{3,2,1,0:T(8,128)(2,1)S(1)}, bf16[3,3,192,384]{3,2,1,0:T(8,128)(2,1)}, u32[]{:S(2)}) copy-start(bf16[3,3,192,384]{3,2,1,0:T(8,128)(2,1)} %param.14) | copy-start | bytes 3981316
  2.2 26.0 %collective-permute-start = (bf16[384,384]{1,0:T(8,128)(2,1)}, bf16[384,384]{1,0:T(8,128)(2,1)}, u32[]{:S(2)}, u32[]{:S(2)}) collective-permute-start(bf16[384,384]{1,0:T(8,128)(2,1)} %pad_maximum_fusion.6), channel_id=1, source_target_pairs={{0,1},{1,2},{2,3},{3,4},{4,5},{5,6},{6,7},{7,8},{8,9},{9,10},{10,1... | collective-permute-start | bytes 884744 | tf_op jit(solution)/shard_map/ppermute | solution.py:17
  16.4 0.9 copy-start.9
  16.4 1.1 copy-start.8
  16.4 1.9 copy-start.7
  16.4 2.7 copy-start.6
  16.4 3.5 %copy-start.3 = (f32[384,1]{1,0:T(8,128)S(1)}, f32[384,1]{1,0:T(8,128)}, u32[]{:S(2)}) copy-start(f32[384,1]{1,0:T(8,128)} %copy.44) | copy-start | bytes 4612
  16.5 3.5 %copy-start.4 = (bf16[384,192]{1,0:T(8,128)(2,1)S(1)}, bf16[384,192]{1,0:T(8,128)(2,1)}, u32[]{:S(2)}) copy-start(bf16[384,192]{1,0:T(8,128)(2,1)} %copy.45) | copy-start | bytes 442372
  16.5 3.5 %copy-start.10 = (bf16[384,1]{1,0:T(8,128)(2,1)S(1)}, bf16[384,1]{1,0:T(8,128)(2,1)}, u32[]{:S(2)}) copy-start(bf16[384,1]{1,0:T(8,128)(2,1)} %copy.46) | copy-start | bytes 2308
  23.2 3.4 %copy-start.5 = (bf16[384,192]{0,1:T(8,128)(2,1)S(1)}, bf16[384,192]{0,1:T(8,128)(2,1)}, u32[]{:S(2)}) copy-start(bf16[384,192]{0,1:T(8,128)(2,1)} %copy.64) | copy-start | bytes 442372
  23.3 3.4 %copy-start.11 = (bf16[192,1]{1,0:T(8,128)(2,1)S(1)}, bf16[192,1]{1,0:T(8,128)(2,1)}, u32[]{:S(2)}) copy-start(bf16[192,1]{1,0:T(8,128)(2,1)} %stack.46) | copy-start | bytes 1156
  23.3 3.4 %copy-start.12 = (bf16[192,1]{1,0:T(8,128)(2,1)S(1)}, bf16[192,1]{1,0:T(8,128)(2,1)}, u32[]{:S(2)}) copy-start(bf16[192,1]{1,0:T(8,128)(2,1)} %stack.45) | copy-start | bytes 1156
  23.3 3.4 %copy-start.13 = (bf16[192,1]{1,0:T(8,128)(2,1)S(1)}, bf16[192,1]{1,0:T(8,128)(2,1)}, u32[]{:S(2)}) copy-start(bf16[192,1]{1,0:T(8,128)(2,1)} %stack.44) | copy-start | bytes 1156
  26.6 3.4 %copy-start.17 = (f32[384]{0:T(512)S(1)}, f32[384]{0:T(512)}, u32[]{:S(2)}) copy-start(f32[384]{0:T(512)} %param.16) | copy-start | bytes 4612
  59.2 84.1 %all-to-all-start = ((bf16[32,6,24,384]{3,2,1,0:T(8,128)(2,1)}), bf16[32,6,24,384]{3,2,1,0:T(8,128)(2,1)S(1)}, u32[]{:S(2)}, u32[]{:S(2)}) async-start(bf16[32,6,24,384]{3,2,1,0:T(8,128)(2,1)} %get-tuple-element.7), calls=%async_computation | async-start | bytes 7077888 | tf_op jit(solution)/shard_map/all_to_all | solution.py:657
  63.6 6.2 %copy-start.16 = (s32[384]{0:T(512)}, s32[384]{0:T(512)S(1)}, u32[]{:S(2)}) copy-start(s32[384]{0:T(512)S(1)} %iota.42) | copy-start | bytes 4612
  70.6 1.6 slice-start
  85.0 3.6 %copy-start = (f32[12,2,384,256]{3,2,1,0:T(8,128)}, f32[12,2,384,256]{3,2,1,0:T(8,128)S(1)}, u32[]{:S(2)}) copy-start(f32[12,2,384,256]{3,2,1,0:T(8,128)S(1)} %symmetric_filter.1.g_ref) | copy-start | bytes 28311556
  143.3 1.8 copy-start.1
  157.7 45.7 %all-to-all-start.2 = ((bf16[32,72,384]{2,1,0:T(8,128)(2,1)}), bf16[32,72,384]{2,1,0:T(8,128)(2,1)S(1)}, u32[]{:S(2)}, u32[]{:S(2)}) async-start(bf16[32,72,384]{2,1,0:T(8,128)(2,1)} %bitcast.37), calls=%async_computation.2 | async-start | bytes 3538944 | tf_op jit(solution)/shard_map/all_to_all | solution.py:678
  203.4 46.0 %all-to-all-start.1 = ((bf16[32,72,384]{2,1,0:T(8,128)(2,1)}), bf16[32,72,384]{2,1,0:T(8,128)(2,1)S(1)}, u32[]{:S(2)}, u32[]{:S(2)}) async-start(bf16[32,72,384]{2,1,0:T(8,128)(2,1)} %bitcast.36), calls=%async_computation.1 | async-start | bytes 3538944 | tf_op jit(solution)/shard_map/all_to_all | solution.py:678
  210.5 39.9 %collective-permute-start.2 = (bf16[12,192,384]{2,1,0:T(8,128)(2,1)}, bf16[12,192,384]{2,1,0:T(8,128)(2,1)}, u32[]{:S(2)}, u32[]{:S(2)}) collective-permute-start(bf16[12,192,384]{2,1,0:T(8,128)(2,1)} %constant_dynamic-slice_fusion.1), channel_id=1, source_target_pairs={{0,16},{16,0},{1,17},{17,1},{2,18},{18,2},{3,19},{19,3},{4,20},{20... | collective-permute-start | bytes 5308424 | tf_op jit(solution)/shard_map/ppermute | solution.py:597
  211.6 44.2 %collective-permute-start.3 = (bf16[16,72,384]{2,1,0:T(8,128)(2,1)}, bf16[16,72,384]{2,1,0:T(8,128)(2,1)}, u32[]{:S(2)}, u32[]{:S(2)}) collective-permute-start(bf16[16,72,384]{2,1,0:T(8,128)(2,1)} %constant_dynamic-slice_fusion), channel_id=1, source_target_pairs={{0,16},{16,0},{1,17},{17,1},{2,18},{18,2},{3,19},{19,3},{4,20},{20... | collective-permute-start | bytes 2654216 | tf_op jit(solution)/shard_map/ppermute | solution.py:597
  250.4 14.4 %collective-permute-start.1 = (bf16[16,72,384]{2,1,0:T(8,128)(2,1)}, bf16[16,72,384]{2,1,0:T(8,128)(2,1)}, u32[]{:S(2)}, u32[]{:S(2)}) collective-permute-start(bf16[16,72,384]{2,1,0:T(8,128)(2,1)} %constant_dynamic-slice_fusion.2), channel_id=1, source_target_pairs={{0,16},{16,0},{1,17},{17,1},{2,18},{18,2},{3,19},{19,3},{4,20},{20... | collective-permute-start | bytes 2654216 | tf_op jit(solution)/shard_map/ppermute | solution.py:597

commit v2 on v1

--- a/solution.py
+++ b/solution.py
@@ -3,6 +3,7 @@
 
 import jax
 import jax.numpy as jnp
+import numpy as np
 from jax import lax
 from jax.experimental import pallas as pl
 from jax.experimental.pallas import tpu as pltpu
@@ -17,9 +18,10 @@
     return lax.ppermute(block, axis, route)
 
 
-def fourier_tables(length):
+def fourier_tables(length, columns=None):
     indices = jnp.arange(length, dtype=jnp.int32)
-    product = indices[:, None] * indices[None, :] % length
+    columns = indices if columns is None else jnp.asarray(columns, jnp.int32)
+    product = indices[:, None] * columns[None, :] % length
     angles = product.astype(jnp.float32) * (2.0 * math.pi / length)
     return (jnp.cos(angles).astype(jnp.bfloat16), jnp.sin(angles).astype(jnp.bfloat16))
 
@@ -200,48 +202,107 @@
 
 
 DEVICES = ("tile", "section")
+VMEM_BYTES = 60 * 1024 * 1024
 GELU_LINEAR = 2.0 * math.sqrt(2.0 / math.pi)
 GELU_CUBIC = 4.0 * 0.044715 * GELU_LINEAR
-ONES = 16
-
-
-def split_bias(bias):
-    parts = []
-    left = bias
+ONES = (64, 128, 64)
+TAPS = ((1, 1), (1, 2), (2, 1), (2, 2), (1, 0), (2, 0), (0, 1), (0, 2), (0, 0))
+
+
+def bias_rows(bias, count):
+    high = bias.astype(jnp.bfloat16)
+    rest = bias - high.astype(jnp.float32)
+    middle = rest.astype(jnp.bfloat16)
+    low = (rest - middle.astype(jnp.float32)).astype(jnp.bfloat16)
+    shape = (count, bias.shape[1])
+    row = lax.broadcasted_iota(jnp.int32, shape, 0)
+    rows = jnp.zeros(shape, jnp.float32)
+    for k, part in enumerate((high, middle, low)):
+        rows = jnp.where(row == k, jnp.broadcast_to(part.astype(jnp.float32), shape), rows)
+    return rows.astype(jnp.bfloat16)
+
+
+def weights_kernel(
+    patch_ref, patch_bias_ref, merge_ref, merge_bias_ref, down_ref, down_bias_ref, gain_ref,
+    w1_ref, w2_ref, w3_ref, column_ref,
+):
+    def exact(a, b):
+        return jnp.dot(
+            a.astype(jnp.bfloat16), b.astype(jnp.bfloat16), preferred_element_type=jnp.float32
+        )
+
+    taps, width = patch_ref.shape
+    row = lax.broadcasted_iota(jnp.int32, (4 * taps, taps), 0)
+    col = lax.broadcasted_iota(jnp.int32, (4 * taps, taps), 1)
+    pick = jnp.where(row // 16 * 4 + row % 4 == col, 1.0, 0.0)
+    row = lax.broadcasted_iota(jnp.int32, (width, 4 * width), 0)
+    col = lax.broadcasted_iota(jnp.int32, (width, 4 * width), 1)
+    repeat = jnp.where(col % width == row, 1.0, 0.0)
+    spread = exact(pick, exact(patch_ref[...], repeat))
+    row = lax.broadcasted_iota(jnp.int32, spread.shape, 0)
+    col = lax.broadcasted_iota(jnp.int32, spread.shape, 1)
+    spread = jnp.where(row // 4 % 4 == col // width, 0.5 * spread, 0.0).astype(jnp.bfloat16)
+    bias = jnp.broadcast_to(0.5 * patch_bias_ref[...], (8, width))
+    tiled = jnp.zeros((8, 4 * width), jnp.float32)
     for _ in range(3):
-        part = left.astype(jnp.bfloat16)
-        parts.append(part)
-        left = left - part.astype(jnp.float32)
-    parts += [jnp.zeros_like(parts[0])] * (ONES - 3)
-    return jnp.stack(parts, axis=1)
+        part = bias.astype(jnp.bfloat16).astype(jnp.float32)
+        tiled = tiled + exact(part, repeat)
+        bias = bias - part
+    first = jnp.concatenate([spread, bias_rows(tiled[:1], ONES[0])], axis=0)
+    w1_ref[...] = first.T
+    half = (merge_ref[...].astype(jnp.float32) * 0.5).astype(jnp.bfloat16)
+    second = jnp.concatenate([half, bias_rows(0.5 * merge_bias_ref[...], ONES[1])], axis=0)
+    w2_ref[...] = second.T
+    third = [down_ref[3 * a + q] for a, q in TAPS]
+    third = jnp.concatenate(third + [bias_rows(down_bias_ref[...], ONES[2])], axis=0)
+    w3_ref[...] = third.T
+    column_ref[...] = jnp.broadcast_to(gain_ref[...], (128, gain_ref.shape[1])).T
 
 
 def stem_weights(
-    patch_conv_weight, patch_bias, merging_conv_weight, merge_bias, down_weight, down_bias
+    patch_conv_weight, patch_bias, merging_conv_weight, merge_bias, down_weight, down_bias,
+    norm_gain,
 ):
-    half = jnp.asarray(0.5, jnp.bfloat16)
     width = patch_conv_weight.shape[3]
-    bands = patch_conv_weight.shape[0]
-    identity = jnp.eye(4, dtype=jnp.bfloat16)
-    first = jnp.einsum("baqk,vw->vkbawq", patch_conv_weight, identity)
-    first = first.reshape(4 * width, bands * 64) * half
-    first = jnp.concatenate([first, split_bias(jnp.tile(0.5 * patch_bias, 4))], axis=1)
     merged = merging_conv_weight.shape[3]
-    second = merging_conv_weight.reshape(4 * width, merged).T * half
-    second = jnp.concatenate([second, split_bias(0.5 * merge_bias)], axis=1)
-    taps = [(1, 1), (1, 2), (2, 1), (2, 2), (1, 0), (2, 0), (0, 1), (0, 2), (0, 0)]
-    third = jnp.concatenate([down_weight[a, q] for a, q in taps], axis=0).T
-    third = jnp.concatenate([third, split_bias(down_bias)], axis=1)
-    return first, second, third
+    channels = down_weight.shape[3]
+    patch = patch_conv_weight.reshape(-1, width)
+    depths = (4 * patch.shape[0] + ONES[0], 4 * width + ONES[1], 9 * merged + ONES[2])
+    return pl.pallas_call(
+        weights_kernel,
+        out_shape=[
+            jax.ShapeDtypeStruct((4 * width, depths[0]), jnp.bfloat16),
+            jax.ShapeDtypeStruct((merged, depths[1]), jnp.bfloat16),
+            jax.ShapeDtypeStruct((channels, depths[2]), jnp.bfloat16),
+            jax.ShapeDtypeStruct((channels, 128), jnp.float32),
+        ],
+        compiler_params=pltpu.CompilerParams(vmem_limit_bytes=VMEM_BYTES),
+        cost_estimate=pl.CostEstimate(flops=1000000, bytes_accessed=4000000, transcendentals=0),
+        name="stem_weights",
+    )(
+        patch,
+        patch_bias[None],
+        merging_conv_weight.reshape(-1, merged),
+        merge_bias[None],
+        down_weight.reshape(9, merged, channels),
+        down_bias[None],
+        norm_gain[None],
+    )
 
 
 def half_gelu(h):
     return h + h * jnp.tanh(h * (GELU_LINEAR + GELU_CUBIC * (h * h)))
 
 
-def stem_kernel(
-    place_ref, x_ref, halo_ref, w1_ref, w2_ref, w3_ref, gain_ref, normed_ref, feat_ref, field
-):
+def lower_half(row):
+    depth = row.shape[1]
+    return jnp.concatenate(
+        [row[:, 256 * b + 128 : 256 * b + 256] for b in range(depth // 256)], axis=1
+    )
+
+
+def stem_kernel(place_ref, x_ref, above_ref, *refs):
+    w1_ref, w2_ref, w3_ref, gain_ref, normed_ref, feat_ref, field = refs[-7:]
     step = pl.program_id(0)
     rows, cols, depth = x_ref.shape
     bands = depth // 256
@@ -252,21 +313,21 @@
     w1 = w1_ref[...]
     w2 = w2_ref[...]
 
-    def ones(n):
-        return jnp.where(lax.broadcasted_iota(jnp.int32, (ONES, n), 0) < 3, 1.0, 0.0).astype(
+    def ones(count, n):
+        return jnp.where(lax.broadcasted_iota(jnp.int32, (count, n), 0) < 3, 1.0, 0.0).astype(
             jnp.bfloat16
         )
 
     def layer_one(turned, offsets):
         n = turned.shape[1]
-        parts = [turned[o : o + 64] for o in offsets] + [ones(n)]
+        parts = [turned[o : o + 64] for o in offsets] + [ones(ONES[0], n)]
         h = jnp.dot(w1, jnp.concatenate(parts, axis=0), preferred_element_type=jnp.float32)
         return half_gelu(h).astype(jnp.bfloat16)
 
     def layer_two(upper, lower, y):
         n = upper.shape[1]
         span = slice(2 * y * (w1.shape[0] // 4), 2 * (y + 1) * (w1.shape[0] // 4))
-        stacked = jnp.concatenate([upper[span], lower[span], ones(n)], axis=0)
+        stacked = jnp.concatenate([upper[span], lower[span], ones(ONES[1], n)], axis=0)
         return half_gelu(jnp.dot(w2, stacked, preferred_element_type=jnp.float32))
 
     def shifted(values):
@@ -284,9 +345,13 @@
 
     @pl.when(step == 0)
     def _():
-        field[9 * merged : 9 * merged + ONES, :] = ones(cells)
-        turned = halo_ref[...].T
-        keep = place_ref[1].astype(jnp.float32)
+        field[9 * merged :, :] = ones(ONES[2], cells)
+        above = lower_half(above_ref[0])
+        keep = 1.0
+        if len(refs) > 7:
+            keep = place_ref[1].astype(jnp.float32)
+            above = jnp.where(place_ref[2] > 0, refs[0][...], above)
+        turned = above.T
         upper, lower = (
             layer_one(turned, [128 * b + 64 * a for b in range(bands)]) for a in range(2)
         )
@@ -327,7 +392,8 @@
     values = features.astype(jnp.float32)
     centered = values - jnp.mean(values, axis=0, keepdims=True)
     variance = jnp.mean(centered * centered, axis=0, keepdims=True)
-    normed = gain_ref[...] * (centered * lax.rsqrt(variance + EPSILON))
+    gain = jnp.concatenate([gain_ref[...]] * (cells // 128), axis=1)
+    normed = gain * (centered * lax.rsqrt(variance + EPSILON))
     pair = 2 * group
     index = lax.broadcasted_iota(jnp.int32, (pair, cols), 0)
     for t in range(channels // pair):
@@ -341,44 +407,49 @@
         ).astype(jnp.bfloat16)
 
 
-def stem(image, halo, place, weights, norm_gain, devices):
-    tile_rows, cols, depth = image.shape
-    rows = tile_rows // 2
-    first, second, third = weights
-    channels = third.shape[0]
-    merged = second.shape[0]
-    steps = rows // 2
+def stem(image, arriving, place, weights, first, steps, devices):
+    cols, depth = image.shape[1:]
+    rows = 2 * steps
+    channels, third_depth = weights[2].shape
+    merged = weights[1].shape[0]
     group = channels // devices
-    gain = jnp.broadcast_to(norm_gain[:, None], (channels, 2 * cols)).astype(jnp.float32)
 
     def whole(array):
         return pl.BlockSpec(array.shape, lambda i, place: (0,) * array.ndim)
 
-    operands = (halo, first, second, third, gain)
-    macs = rows * cols * (16 * 208 * 96 + 4 * 400 * merged + third.shape[1] * channels)
+    operands = list(weights)
+    if arriving is not None:
+        operands = [arriving] + operands
+    macs = rows * cols * (16 * 208 * 96 + 4 * 400 * merged + third_depth * channels)
     return pl.pallas_call(
         stem_kernel,
         grid_spec=pltpu.PrefetchScalarGridSpec(
             num_scalar_prefetch=1,
             grid=(steps,),
-            in_specs=[pl.BlockSpec((2, cols, depth), lambda i, place: (place[0] + i, 0, 0))]
+            in_specs=[
+                pl.BlockSpec((2, cols, depth), lambda i, place: (place[0] + first + i, 0, 0)),
+                pl.BlockSpec(
+                    (1, cols, depth),
+                    lambda i, place: (jnp.maximum(2 * (place[0] + first) - 1, 0), 0, 0),
+                ),
+            ]
             + [whole(a) for a in operands],
             out_specs=[
                 pl.BlockSpec((devices, 1, 2 * group, cols), lambda i, place: (0, i, 0, 0)),
                 pl.BlockSpec((2, channels, cols), lambda i, place: (i, 0, 0)),
             ],
-            scratch_shapes=[pltpu.VMEM((9 * merged + ONES, 2 * cols), jnp.bfloat16)],
+            scratch_shapes=[pltpu.VMEM((third_depth, 2 * cols), jnp.bfloat16)],
         ),
         out_shape=[
             jax.ShapeDtypeStruct((devices, steps, 2 * group, cols), jnp.bfloat16),
             jax.ShapeDtypeStruct((rows, channels, cols), jnp.bfloat16),
         ],
-        compiler_params=pltpu.CompilerParams(vmem_limit_bytes=56 * 1024 * 1024),
+        compiler_params=pltpu.CompilerParams(vmem_limit_bytes=VMEM_BYTES),
         cost_estimate=pl.CostEstimate(
-            flops=2 * macs, bytes_accessed=rows * cols * 3000, transcendentals=0
+            flops=4 * macs, bytes_accessed=rows * cols * 3000, transcendentals=0
         ),
         name="stem",
-    )(place, image, *operands)
+    )(place, image, image, *operands)
 
 
 def symmetric_kernel(place_ref, f_ref, turn_w_ref, turn_u_ref, g_ref):
@@ -414,7 +485,7 @@
             out_specs=pl.BlockSpec((1, 2, full_rows, width), lambda i, place: (i, 0, 0, 0)),
         ),
         out_shape=jax.ShapeDtypeStruct((group, 2, full_rows, width), jnp.float32),
-        compiler_params=pltpu.CompilerParams(vmem_limit_bytes=32 * 1024 * 1024),
+        compiler_params=pltpu.CompilerParams(vmem_limit_bytes=VMEM_BYTES),
         cost_estimate=pl.CostEstimate(
             flops=8 * group * full_rows * full_cols * width,
             bytes_accessed=group * full_rows * width * 14,
@@ -434,8 +505,9 @@
 
 
 def filter_kernel(
-    first, norm_scale, fields_ref, g_ref, row_table_ref, fwd_ref, inv_ref, back_ref, out_ref, held, made
+    first, norm_scale, *refs
 ):
+    *pieces, g_ref, row_table_ref, fwd_ref, inv_ref, back_ref, out_ref, held, made = refs
     step = pl.program_id(0)
     full_rows = fwd_ref.shape[0] // 2
     width = g_ref.shape[3]
@@ -445,7 +517,11 @@
 
     @pl.when(step == 0)
     def _():
-        to_lane_tiles(held, slice(None), fields_ref[...].astype(jnp.float32))
+        begin = 0
+        for piece in pieces:
+            end = begin + piece.shape[0]
+            to_lane_tiles(held, slice(begin, end), piece[...].astype(jnp.float32))
+            begin = end
 
     blocks = []
     for k in range(per_step):
@@ -484,11 +560,12 @@
         out_ref[...] = from_lane_tiles(made, slice(None)).astype(jnp.bfloat16)
 
 
-def filter_tables(full_rows, field_cols, width):
+def filter_tables(full_rows, field_cols, width, row_order):
     cos_h, sin_h = fourier_tables(full_rows)
+    cos_f, sin_f = fourier_tables(full_rows, row_order)
     cos_w, sin_w = fourier_tables(field_cols)
     fwd = jnp.concatenate(
-        [jnp.concatenate([cos_h, sin_h], 1), jnp.concatenate([-sin_h, cos_h], 1)], 0
+        [jnp.concatenate([cos_f, sin_f], 1), jnp.concatenate([-sin_f, cos_f], 1)], 0
     )
     inv = jnp.concatenate(
         [jnp.concatenate([cos_h, -sin_h], 1), jnp.concatenate([sin_h, cos_h], 1)], 0
@@ -504,11 +581,11 @@
     return row_table, fwd, inv, back_table
 
 
-def filter_channels(fields, symmetric, tables, first, count, per_step, devices):
+def filter_channels(pieces, symmetric, tables, first, count, per_step, devices):
     row_table, fwd, inv, back_table = tables
     full_rows = fwd.shape[0] // 2
-    cols = fields.shape[1]
-    group = fields.shape[0] // full_rows
+    cols = pieces[0].shape[1]
+    group = sum(piece.shape[0] for piece in pieces) // full_rows
     width = symmetric.shape[3]
 
     def whole(array):
@@ -519,7 +596,7 @@
         functools.partial(filter_kernel, first, 1.0 / (full_rows * cols)),
         grid=(count // per_step,),
         in_specs=[
-            whole(fields),
+            *[whole(piece) for piece in pieces],
             pl.BlockSpec(
                 (per_step, 2, full_rows, width), lambda i: (first // per_step + i, 0, 0, 0)
             ),
@@ -534,38 +611,42 @@
             pltpu.VMEM((cols // 128, full_rows * group, 128), jnp.float32),
             pltpu.VMEM((cols // 128, full_rows * count, 128), jnp.float32),
         ],
-        compiler_params=pltpu.CompilerParams(vmem_limit_bytes=56 * 1024 * 1024),
+        compiler_params=pltpu.CompilerParams(vmem_limit_bytes=VMEM_BYTES),
         cost_estimate=pl.CostEstimate(
             flops=2 * macs, bytes_accessed=count * full_rows * cols * 8, transcendentals=0
         ),
         name="spectral_filter",
-    )(fields, symmetric, row_table, fwd, inv, back_table)
+    )(*pieces, symmetric, row_table, fwd, inv, back_table)
     return made.reshape(devices, full_rows // devices * count, cols)
 
 
 def residual_kernel(count, place_ref, kept_ref, other_ref, feat_ref, *refs):
     out_ref, held = refs[-2:]
-    span = kept_ref.shape[1]
+    groups, span, cols = kept_ref.shape
     rows = held.shape[1] // count
     own = pl.multiple_of(place_ref[0] * span, 8)
     far = pl.multiple_of((1 - place_ref[0]) * span, 8)
-    to_lane_tiles(held, pl.ds(own, span), kept_ref[0].astype(jnp.float32))
-    to_lane_tiles(held, pl.ds(far, span), other_ref[0].astype(jnp.float32))
-    for k in range(count):
-        filtered = from_lane_tiles(held, pl.ds(k, rows, stride=count))
-        out_ref[0, k] = (feat_ref[0, k].astype(jnp.float32) + filtered).astype(jnp.bfloat16)
-
-
-def add_residual(place, returned, other, features, previous, part, parts):
+    for g in range(groups):
+        to_lane_tiles(held, pl.ds(own, span), kept_ref[g].astype(jnp.float32))
+        to_lane_tiles(held, pl.ds(far, span), other_ref[g].astype(jnp.float32))
+        for k in range(count):
+            filtered = from_lane_tiles(held, pl.ds(k, rows, stride=count))
+            out_ref[g, k] = (feat_ref[g, k].astype(jnp.float32) + filtered).astype(jnp.bfloat16)
+
+
+def add_residual(place, returned, other, features, previous, first, count):
     halves, span, cols = other.shape
     group, rows = features.shape[1:3]
-    count = group // parts
-    block = pl.BlockSpec((1, count, rows, cols), lambda i, place: (i, part, 0, 0))
+    groups = 4 if halves % 4 == 0 else 1
+    steps = halves // groups
     operands = [returned, other, features]
     in_specs = [
-        pl.BlockSpec((1, span, cols), lambda i, place: (place[0] * halves + i, 0, 0)),
-        pl.BlockSpec((1, span, cols), lambda i, place: (i, 0, 0)),
-        block,
+        pl.BlockSpec((groups, span, cols), lambda i, place: (place[0] * steps + i, 0, 0)),
+        pl.BlockSpec((groups, span, cols), lambda i, place: (i, 0, 0)),
+        pl.BlockSpec(
+            (groups, count, rows, cols),
+            lambda i, place: (i, first // count, 0, 0),
+        ),
     ]
     aliases = {}
     if previous is not None:
@@ -576,14 +657,14 @@
         functools.partial(residual_kernel, count),
         grid_spec=pltpu.PrefetchScalarGridSpec(
             num_scalar_prefetch=1,
-            grid=(halves,),
+            grid=(steps,),
             in_specs=in_specs,
-            out_specs=block,
+            out_specs=in_specs[2],
             scratch_shapes=[pltpu.VMEM((cols // 128, rows * count, 128), jnp.float32)],
         ),
         out_shape=jax.ShapeDtypeStruct(features.shape, jnp.bfloat16),
         input_output_aliases=aliases,
-        compiler_params=pltpu.CompilerParams(vmem_limit_bytes=32 * 1024 * 1024),
+        compiler_params=pltpu.CompilerParams(vmem_limit_bytes=VMEM_BYTES),
         cost_estimate=pl.CostEstimate(
             flops=halves * count * rows * cols,
             bytes_accessed=halves * count * rows * cols * 8,
@@ -643,23 +724,38 @@
     half_channels = channels // 2
     width = -(-(field_cols // 2 + 1) // 128) * 128
 
-    def lower_half(row):
-        return jnp.concatenate(
-            [row[:, 256 * b + 128 : 256 * b + 256] for b in range(depth // 256)], axis=1
+    arriving = from_behind(lower_half(aerial_patch_grid[-1]), "tile", 1)
+    inside = (section > 0) | (tile > 0)
+    place = jnp.stack([section * (rows // 2), inside, section == 0]).astype(jnp.int32)
+    weights = stem_weights(*arguments[1:8])
+    pairs = rows // 2
+    early = max(pairs // 3, 1)
+    spans = [(pairs - early, early), (0, pairs - early)]
+    pieces = []
+    features = []
+    row_order = []
+    for first, steps in spans:
+        normed, part = stem(
+            aerial_patch_grid,
+            arriving if first == 0 else None,
+            place,
+            weights,
+            first,
+            steps,
+            devices,
         )
-
-    arriving = from_behind(lower_half(aerial_patch_grid[-1]), "tile", 1)
-    halo = jnp.where(section == 0, arriving, lower_half(aerial_patch_grid[rows - 1]))
-    inside = ((section > 0) | (tile > 0)).astype(jnp.int32)
-    weights = stem_weights(*arguments[1:7])
-    place = jnp.stack([section * (rows // 2), inside]).astype(jnp.int32)
-    normed, features = stem(aerial_patch_grid, halo, place, weights, norm_gain, devices)
-    fields = lax.all_to_all(normed, DEVICES, split_axis=0, concat_axis=0, tiled=True)
-    fields = fields.reshape(full_rows * group, field_cols)
+        normed, arriving = lax.optimization_barrier((normed, arriving))
+        normed = lax.all_to_all(normed, DEVICES, split_axis=0, concat_axis=0, tiled=True)
+        pieces.append(normed.reshape(2 * steps * devices * group, field_cols))
+        features.insert(0, part)
+        own_rows = np.arange(2 * first, 2 * (first + steps))
+        row_order.append((rows * np.arange(devices)[:, None] + own_rows).reshape(-1))
+    features = jnp.concatenate(features, axis=0)
+    row_order = np.concatenate(row_order).astype(np.int32)
 
     channel_place = jnp.reshape(section * group, (1,)).astype(jnp.int32)
     symmetric = symmetric_filter(spectral_filter, channel_place, group, width)
-    tables = filter_tables(full_rows, field_cols, width)
+    tables = filter_tables(full_rows, field_cols, width, row_order)
 
     own = lax.dynamic_slice_in_dim(features, section * half_channels, half_channels, 1)
     sent = lax.dynamic_slice_in_dim(features, (1 - section) * half_channels, half_channels, 1)
@@ -668,17 +764,20 @@
     high = jnp.where(section == 0, arrived, own)
     residual = jnp.transpose(jnp.concatenate([low, high], axis=0), (1, 0, 2))
     residual = residual.reshape(half_channels // group, group, tile_rows, field_cols)
-
-    parts = 2
-    count = group // parts
+    pieces, residual, symmetric, tables = lax.optimization_barrier(
+        (pieces, residual, symmetric, tables)
+    )
+
     section_place = jnp.reshape(section, (1,)).astype(jnp.int32)
+    halves = devices // 2
     output = None
-    for part in range(parts):
-        made = filter_channels(fields, symmetric, tables, part * count, count, 2, devices)
+    for first, count in ((group - 2, 2), (0, group - 2)):
+        made = filter_channels(pieces, symmetric, tables, first, count, 2, devices)
         returned = lax.all_to_all(made, DEVICES, split_axis=0, concat_axis=0, tiled=True)
-        halves = devices // 2
+        if output is not None:
+            returned, output = lax.optimization_barrier((returned, output))
         other = swap(lax.dynamic_slice_in_dim(returned, (1 - section) * halves, halves, 0))
-        output = add_residual(section_place, returned, other, residual, output, part, parts)
+        output = add_residual(section_place, returned, other, residual, output, first, count)
     return output.reshape(half_channels, tile_rows, field_cols)
 
 

time: 276 us -> 229 us (0.83)
  waiting for transfers between devices: 121 us -> 88 us
  local copies, waits for them, and re-layouts: 34.3 us -> 11.9 us
  starting transfers between devices: 18.6 us -> 23.9 us
  other arithmetic: 15.4 us -> 19.1 us
    all_to_all x1 -> x2, waiting for transfers between devices: 54.7 us -> 21.9 us  [local(): lax.all_to_all(normed, DEVICES, split_axis=0, concat_axis=0, tiled=True)]
    pallas_call x2, Pallas kernels: 18.1 us -> 8.52 us  [add_residual(): pl.pallas_call(functools.partial(residual_kernel, count), grid_spec=pltpu...]
    concatenate x6 -> x1, local copies, waits for them, and re-layouts: 7.36 us -> 0.24 us  [local(): features = jnp.concatenate(features, axis=0)]
    unnamed x51 -> x21, local copies, waits for them, and re-layouts: 8.94 us -> 3.78 us
    all_to_all x2, waiting for transfers between devices: 66.5 us -> 61.4 us  [local(): lax.all_to_all(made, DEVICES, split_axis=0, concat_axis=0, tiled=True)]
    ppermute x3, waiting for transfers between devices: 0.01 us -> 4.72 us  [swap(): return lax.ppermute(block, 'section', [(0, 1), (1, 0)])]
    pallas_call x1 -> x2, Pallas kernels: 28 us -> 32.7 us  [stem(): pl.pallas_call(stem_kernel, grid_spec=pltpu.PrefetchScalarGridSpec(num_sc...]
    all_to_all x1 -> x2, starting transfers between devices: 4.4 us -> 8.86 us  [local(): lax.all_to_all(normed, DEVICES, split_axis=0, concat_axis=0, tiled=True)]
  transfers between devices with their start and end apart: 7 -> 8, of which waited for: 3 -> 5; matrix products, arithmetic and copies ran while one was open for 14% -> 12% of each run, Pallas kernels for 12% -> 32%
where the time goes in v2:
time: 229 us; the launch traced here: 228 us
  waiting for transfers between devices  88 us (38%)
  Pallas kernels  84.4 us (37%)
  starting transfers between devices  23.9 us (10%)
  other arithmetic  19.1 us (8%)
  local copies, waits for them, and re-layouts  11.9 us (5%)
    all_to_all x2, waiting for transfers between devices, local(): lax.all_to_all(made, DEVICES, split_axis=0, concat_axis=0, tiled=True)  61.4 us
    pallas_call x2, Pallas kernels, stem(): pl.pallas_call(stem_kernel, grid_spec=pltpu.PrefetchScalarGridSpec(num_sc...  32.7 us
    pallas_call x2, Pallas kernels, filter_channels(): pl.pallas_call(functools.partial(filter_kernel, first, 1.0 / (full_rows *...  24.9 us
    all_to_all x2, waiting for transfers between devices, local(): lax.all_to_all(normed, DEVICES, split_axis=0, concat_axis=0, tiled=True)  21.9 us
    pallas_call x1, Pallas kernels, symmetric_filter(): pl.pallas_call(symmetric_kernel, grid_spec=pltpu.PrefetchScalarGridSpec(n...  15.1 us
    all_to_all x2, starting transfers between devices, local(): lax.all_to_all(made, DEVICES, split_axis=0, concat_axis=0, tiled=True)  9.79 us
    all_to_all x2, starting transfers between devices, local(): lax.all_to_all(normed, DEVICES, split_axis=0, concat_axis=0, tiled=True)  8.86 us
    pallas_call x2, Pallas kernels, add_residual(): pl.pallas_call(functools.partial(residual_kernel, count), grid_spec=pltpu...  8.52 us
  transfers between devices with their start and end apart: 8, of which 5 were waited for; matrix products, arithmetic and copies ran while one was open for 12% of the time, Pallas kernels for 32%

profile of v2, /device:TPU:0, one launch (start us, length us, event | category | flops | bytes accessed | tf_op | source)
XLA Modules:
  0.0 227.6 jit_solution(11341267221486440161)
XLA Ops:
  0.0 0.0 copy-start.7
  0.0 0.0 copy-start.8
  0.0 1.1 slice_bitcast_fusion
  1.1 0.1 fusion.27
  1.2 4.9 %collective-permute-start = (bf16[384,384]{1,0:T(8,128)(2,1)S(1)}, bf16[384,384]{1,0:T(8,128)(2,1)S(1)}, u32[]{:S(2)}, u32[]{:S(2)}) collective-permute-start(bf16[384,384]{1,0:T(8,128)(2,1)S(1)} %pad_maximum_fusion.2), channel_id=1, source_target_pairs={{0,1},{1,2},{2,3},{3,4},{4,5},{5,6},{6,7},{7,8},{8,9},{9,10},{10,1... | collective-permute-start | bytes 884744 | tf_op jit(solution)/shard_map/ppermute | solution.py:18
  6.1 0.0 copy-done.7
  6.1 0.6 broadcast_in_dim.18.down_bias_ref
  6.7 0.0 copy-done.8
  6.7 0.6 broadcast_in_dim.19.gain_ref
  7.3 0.6 pad_add_fusion.place_ref
  7.9 3.2 %stem_weights.1 = (bf16[384,256]{1,0:T(8,128)(2,1)}, bf16[192,512]{1,0:T(8,128)(2,1)}, bf16[384,1792]{1,0:T(8,128)(2,1)}, f32[384,128]{1,0:T(8,128)}) custom-call(bf16[48,96]{1,0:T(8,128)(2,1)} %bitcast.28, f32[1,96]{1,0:T(1,128)} %bitcast.30, bf16[384,192]{1,0:T(8,128)(2,1)} %bitcast.27, f32[1,192]{1,0:T(1,128)} %bitcast.29, bf16[9,192,384]{2,1,0:T(8,128)(2,1)} %bitcast.26, ...), custom_call_target="tpu_custom_call" | custom-call | flops 1000000 | bytes 4000000 | tf_op jit(solution)/shard_map/stem_weights/pallas_call | solution.py:271
  11.1 12.3 %stem.2 = (bf16[32,2,24,384]{3,2,1,0:T(8,128)(2,1)}, bf16[4,384,384]{2,1,0:T(8,128)(2,1)}) custom-call(s32[3]{0:T(128)} %pad_add_fusion.place_ref, bf16[24,384,768]{2,1,0:T(8,128)(2,1)} %above_ref.3, bf16[24,384,768]{2,1,0:T(8,128)(2,1)} %above_ref.3, bf16[384,256]{1,0:T(8,128)(2,1)} %get-tuple-element.26.refs_0_.refs_1_, ...), custom_call_target="tpu_custom_call" | custom-call | flops 8078229504 | bytes 4608000 | tf_op jit(solution)/shard_map/stem/pallas_call | solution.py:424
  23.5 0.0 collective-permute-done.refs_0_
  23.5 4.9 %all-to-all-start = ((bf16[32,2,24,384]{3,2,1,0:T(8,128)(2,1)}), bf16[32,2,24,384]{3,2,1,0:T(8,128)(2,1)S(1)}, u32[]{:S(2)}, u32[]{:S(2)}) async-start(bf16[32,2,24,384]{3,2,1,0:T(8,128)(2,1)} %get-tuple-element.31), calls=%async_computation | async-start | bytes 2359296 | tf_op jit(solution)/shard_map/all_to_all | solution.py:748
  28.4 0.0 copy-done.9
  28.4 20.3 %stem.3 = (bf16[32,4,24,384]{3,2,1,0:T(8,128)(2,1)}, bf16[8,384,384]{2,1,0:T(8,128)(2,1)}) custom-call(s32[3]{0:T(128)} %pad_add_fusion.place_ref, bf16[24,384,768]{2,1,0:T(8,128)(2,1)} %above_ref.3, bf16[24,384,768]{2,1,0:T(8,128)(2,1)} %above_ref.3, bf16[384,384]{1,0:T(8,128)(2,1)} %copy-done.9, bf16[384,256]{1,0:T(8,128)(2,1)} %get-tuple-element.26.refs_0_.refs_1_, ...), custom_call_target="tpu_custom_call" | custom-call | flops 16156459008 | bytes 9216000 | tf_op jit(solution)/shard_map/stem/pallas_call | solution.py:424
  48.8 8.7 %all-to-all-done = bf16[32,2,24,384]{3,2,1,0:T(8,128)(2,1)S(1)} async-done(((bf16[32,2,24,384]{3,2,1,0:T(8,128)(2,1)}), bf16[32,2,24,384]{3,2,1,0:T(8,128)(2,1)S(1)}, u32[]{:S(2)}, u32[]{:S(2)}) %all-to-all-start) | async-done | bytes 1179680 | tf_op jit(solution)/shard_map/all_to_all | solution.py:748
  57.5 0.0 copy-start.1
  57.5 1.0 copy-done.1
  58.5 3.9 %all-to-all-start.1 = ((bf16[32,4,24,384]{3,2,1,0:T(8,128)(2,1)}), bf16[32,4,24,384]{3,2,1,0:T(8,128)(2,1)}, u32[]{:S(2)}, u32[]{:S(2)}) async-start(bf16[32,4,24,384]{3,2,1,0:T(8,128)(2,1)} %get-tuple-element.34), calls=%async_computation.1 | async-start | bytes 4718592 | tf_op jit(solution)/shard_map/all_to_all | solution.py:748
  62.5 0.0 copy-start.6
  62.5 2.3 %fusion.22 = bf16[384,384]{1,0:T(8,128)(2,1)S(1)} fusion(), kind=kLoop, calls=%fused_computation.47 | loop fusion | flops 1916928 | bytes 294912 | tf_op jit(solution)/shard_map/neg | solution.py:571
  64.9 1.0 fusion.12.turn_u_ref
  65.9 2.5 %sine_convert_fusion.1 = (bf16[384,384]{1,0:T(8,128)(2,1)S(1)}, bf16[384,384]{1,0:T(8,128)(2,1)S(1)}) fusion(), kind=kLoop, calls=%fused_computation.19 | loop fusion | flops 1622016 | bytes 589824 | tf_op jit(solution)/shard_map/convert_element_type | solution.py:26
  68.4 0.1 slice_multiply_fusion
  68.6 0.8 pad_maximum_fusion.1.refs_6_
  69.4 2.0 constant_dynamic-update-slice_fusion.1
  71.4 0.0 copy-done.6
  71.4 0.0 copy-done.3
  71.4 0.2 constant_dynamic-update-slice_fusion
  71.6 1.4 constant_dynamic-slice_fusion.2
  73.1 0.0 copy-start.5
  73.1 0.0 collective-permute-start.1
  73.1 0.8 pad_maximum_fusion.refs_3_
  73.9 0.0 slice-start
  73.9 1.1 maximum_maximum_fusion.1.refs_5_
  75.0 0.0 copy-done.5
  75.0 2.3 %fusion.23 = bf16[384,384]{1,0:T(8,128)(2,1)S(1)} fusion(s32[384]{0:T(512)S(1)} %copy-done.5), kind=kLoop, calls=%fused_computation.48 | loop fusion | flops 1916928 | bytes 296448 | tf_op jit(solution)/shard_map/neg | solution.py:568
  77.4 2.5 %sine_convert_fusion = (bf16[384,384]{1,0:T(8,128)(2,1)S(1)}, bf16[384,384]{1,0:T(8,128)(2,1)S(1)}) fusion(s32[384]{0:T(512)S(1)} %copy-done.5), kind=kLoop, calls=%fused_computation.14 | loop fusion | flops 1622016 | bytes 591360 | tf_op jit(solution)/shard_map/convert_element_type | solution.py:26
  79.9 1.1 maximum_maximum_fusion.refs_4_
  81.0 0.0 slice-done
  81.1 0.9 fusion.19.turn_w_ref
  82.0 15.1 %symmetric_filter.1.refs_2_ = f32[12,2,384,256]{3,2,1,0:T(8,128)} custom-call(s32[1]{0:T(128)} %bitcast.14.place_ref, bf16[24,2,384,384]{3,2,1,0:T(8,128)(2,1)} %f_ref.1, bf16[384,256]{1,0:T(8,128)(2,1)} %fusion.19.turn_w_ref, bf16[384,384]{1,0:T(8,128)(2,1)} %fusion.12.turn_u_ref), custom_call_target="tpu_custom_call" | custom-call | flops 3623878656 | bytes 16515072 | tf_op jit(solution)/shard_map/symmetric_filter/pallas_call | solution.py:473
  97.1 0.0 collective-permute-done.1
  97.1 2.3 %broadcast_select_fusion.1 = (bf16[12,192,384]{2,1,0:T(8,128)(2,1)S(1)}, bf16[12,192,384]{2,1,0:T(8,128)(2,1)S(1)}) fusion(bf16[12,192,384]{2,1,0:T(8,128)(2,1)} %collective-permute-done.1, pred[]{:T(512)S(6)} %eq.41, bf16[12,384,384]{2,1,0:T(8,128)(2,1)S(1)} %constant_dynamic-update-slice_fusion, s32[]{:T(128)S(6)} %select_n.70), kind=kLoop, calls=%fused_computation.2 | loop fusion | flops 1769472 | bytes 7077893 | tf_op jit(solution)/shard_map/jit(_where)/select_n | solution.py:763
  99.4 0.4 maximum_bitcast_fusion
  99.8 4.0 %copy.12 = bf16[192,24,384]{2,1,0:T(8,128)(2,1)} copy(bf16[192,24,384]{2,0,1:T(8,128)(2,1)S(1)} %maximum_bitcast_fusion) | data formatting | bytes 7077888 | tf_op jit(solution)/shard_map/transpose | solution.py:765
  103.8 13.1 %all-to-all-done.1 = bf16[32,4,24,384]{3,2,1,0:T(8,128)(2,1)} async-done(((bf16[32,4,24,384]{3,2,1,0:T(8,128)(2,1)}), bf16[32,4,24,384]{3,2,1,0:T(8,128)(2,1)}, u32[]{:S(2)}, u32[]{:S(2)}) %all-to-all-start.1) | async-done | bytes 2359328 | tf_op jit(solution)/shard_map/all_to_all | solution.py:748
  116.9 6.9 %spectral_filter.3 = bf16[768,384]{1,0:T(8,128)(2,1)} custom-call(bf16[1536,384]{1,0:T(8,128)(2,1)} %bitcast.22, bf16[3072,384]{1,0:T(8,128)(2,1)} %bitcast.11.refs_1_, f32[12,2,384,256]{3,2,1,0:T(8,128)} %symmetric_filter.1.refs_2_, bf16[384,512]{1,0:T(8,128)(2,1)} %pad_maximum_fusion.refs_3_, bf16[768,768]{1,0:T(8,128)(2,1)} %maximum_maximum_fusion.refs_4_, ...), custom_call_target="tpu_custom_call" | custom-call | flops 1811939328 | bytes 2359296 | tf_op jit(solution)/shard_map/spectral_filter/pallas_call | solution.py:595
  123.7 4.2 %all-to-all-start.3 = ((bf16[32,24,384]{2,1,0:T(8,128)(2,1)}), bf16[32,24,384]{2,1,0:T(8,128)(2,1)S(1)}, u32[]{:S(2)}, u32[]{:S(2)}) async-start(bf16[32,24,384]{2,1,0:T(8,128)(2,1)} %bitcast.25), calls=%async_computation.3 | async-start | bytes 1179648 | tf_op jit(solution)/shard_map/all_to_all | solution.py:776
  127.9 18.1 %spectral_filter.2 = bf16[3840,384]{1,0:T(8,128)(2,1)} custom-call(bf16[1536,384]{1,0:T(8,128)(2,1)} %bitcast.23, bf16[3072,384]{1,0:T(8,128)(2,1)} %bitcast.11.refs_1_, f32[12,2,384,256]{3,2,1,0:T(8,128)} %symmetric_filter.1.refs_2_, bf16[384,512]{1,0:T(8,128)(2,1)} %pad_maximum_fusion.refs_3_, bf16[768,768]{1,0:T(8,128)(2,1)} %maximum_maximum_fusion.refs_4_, ...), custom_call_target="tpu_custom_call" | custom-call | flops 9059696640 | bytes 11796480 | tf_op jit(solution)/shard_map/spectral_filter/pallas_call | solution.py:595
  146.0 0.0 all-to-all-done.3.kept_ref
  146.0 5.6 %all-to-all-start.2 = ((bf16[32,120,384]{2,1,0:T(8,128)(2,1)}), bf16[32,120,384]{2,1,0:T(8,128)(2,1)S(1)}, u32[]{:S(2)}, u32[]{:S(2)}) async-start(bf16[32,120,384]{2,1,0:T(8,128)(2,1)} %bitcast.24), calls=%async_computation.2 | async-start | bytes 5898240 | tf_op jit(solution)/shard_map/all_to_all | solution.py:776
  151.6 0.0 copy-done.2
  151.7 0.3 collective-permute-start.2
  152.0 1.3 collective-permute-done.2.other_ref
  153.3 0.7 copy-done.4
  154.0 3.4 %residual.2.refs_0_ = bf16[16,12,24,384]{3,2,1,0:T(8,128)(2,1)} custom-call(s32[1]{0:T(128)} %bitcast.place_ref, bf16[32,24,384]{2,1,0:T(8,128)(2,1)} %copy-done.2, bf16[16,24,384]{2,1,0:T(8,128)(2,1)} %copy-done.4, bf16[16,12,24,384]{3,2,1,0:T(8,128)(2,1)} %bitcast.20), custom_call_target="tpu_custom_call" | custom-call | flops 294912 | bytes 2359296 | tf_op jit(solution)/shard_map/residual/pallas_call | solution.py:656
  157.5 61.4 %all-to-all-done.2.kept_ref = bf16[32,120,384]{2,1,0:T(8,128)(2,1)S(1)} async-done(((bf16[32,120,384]{2,1,0:T(8,128)(2,1)}), bf16[32,120,384]{2,1,0:T(8,128)(2,1)S(1)}, u32[]{:S(2)}, u32[]{:S(2)}) %all-to-all-start.2) | async-done | bytes 2949152 | tf_op jit(solution)/shard_map/all_to_all | solution.py:776
  218.9 0.1 constant_dynamic-slice_fusion
  219.0 0.1 collective-permute-start.3
  219.1 3.4 %collective-permute-done.3.other_ref = bf16[16,120,384]{2,1,0:T(8,128)(2,1)} collective-permute-done((bf16[16,120,384]{2,1,0:T(8,128)(2,1)S(1)}, bf16[16,120,384]{2,1,0:T(8,128)(2,1)}, u32[]{:S(2)}, u32[]{:S(2)}) %collective-permute-start.3) | collective-permute-done | bytes 1474592 | tf_op jit(solution)/shard_map/ppermute | solution.py:678
  222.5 0.0 copy-done
  222.5 5.1 %residual.3 = bf16[16,12,24,384]{3,2,1,0:T(8,128)(2,1)} custom-call(s32[1]{0:T(128)} %bitcast.place_ref, bf16[32,120,384]{2,1,0:T(8,128)(2,1)} %copy-done, bf16[16,120,384]{2,1,0:T(8,128)(2,1)} %collective-permute-done.3.other_ref, bf16[16,12,24,384]{3,2,1,0:T(8,128)(2,1)} %bitcast.21, ...), custom_call_target="tpu_custom_call", output_to_operand_aliasing={{}: (4, {})} | custom-call | flops 1474560 | bytes 11796480 | tf_op jit(solution)/shard_map/residual/pallas_call | solution.py:656
  (11 shorter events, 0.1 us)
Async XLA Ops:
  0.0 6.1 %copy-start.7 = (f32[384]{0:T(512)S(1)}, f32[384]{0:T(512)}, u32[]{:S(2)}) copy-start(f32[384]{0:T(512)} %param.16) | copy-start | bytes 4612
  0.0 6.7 %copy-start.8 = (f32[384]{0:T(512)S(1)}, f32[384]{0:T(512)}, u32[]{:S(2)}) copy-start(f32[384]{0:T(512)} %param.17) | copy-start | bytes 4612
  1.2 22.2 %collective-permute-start = (bf16[384,384]{1,0:T(8,128)(2,1)S(1)}, bf16[384,384]{1,0:T(8,128)(2,1)S(1)}, u32[]{:S(2)}, u32[]{:S(2)}) collective-permute-start(bf16[384,384]{1,0:T(8,128)(2,1)S(1)} %pad_maximum_fusion.2), channel_id=1, source_target_pairs={{0,1},{1,2},{2,3},{3,4},{4,5},{5,6},{6,7},{7,8},{8,9},{9,10},{10,1... | collective-permute-start | bytes 884744 | tf_op jit(solution)/shard_map/ppermute | solution.py:18
  23.5 4.9 %copy-start.9 = (bf16[384,384]{1,0:T(8,128)(2,1)}, bf16[384,384]{1,0:T(8,128)(2,1)S(1)}, u32[]{:S(2)}) copy-start(bf16[384,384]{1,0:T(8,128)(2,1)S(1)} %collective-permute-done.refs_0_) | copy-start | bytes 884740
  23.5 34.0 %all-to-all-start = ((bf16[32,2,24,384]{3,2,1,0:T(8,128)(2,1)}), bf16[32,2,24,384]{3,2,1,0:T(8,128)(2,1)S(1)}, u32[]{:S(2)}, u32[]{:S(2)}) async-start(bf16[32,2,24,384]{3,2,1,0:T(8,128)(2,1)} %get-tuple-element.31), calls=%async_computation | async-start | bytes 2359296 | tf_op jit(solution)/shard_map/all_to_all | solution.py:748
  57.5 1.0 copy-start.1
  58.5 58.4 %all-to-all-start.1 = ((bf16[32,4,24,384]{3,2,1,0:T(8,128)(2,1)}), bf16[32,4,24,384]{3,2,1,0:T(8,128)(2,1)}, u32[]{:S(2)}, u32[]{:S(2)}) async-start(bf16[32,4,24,384]{3,2,1,0:T(8,128)(2,1)} %get-tuple-element.34), calls=%async_computation.1 | async-start | bytes 4718592 | tf_op jit(solution)/shard_map/all_to_all | solution.py:748
  62.5 8.9 %copy-start.6 = (s32[384]{0:T(512)}, s32[384]{0:T(512)S(1)}, u32[]{:S(2)}) copy-start(s32[384]{0:T(512)S(1)} %iota.31) | copy-start | bytes 4612
  69.4 2.0 copy-start.3
  73.1 2.0 copy-start.5
  73.1 24.0 %collective-permute-start.1 = (bf16[12,192,384]{2,1,0:T(8,128)(2,1)}, bf16[12,192,384]{2,1,0:T(8,128)(2,1)}, u32[]{:S(2)}, u32[]{:S(2)}) collective-permute-start(bf16[12,192,384]{2,1,0:T(8,128)(2,1)} %constant_dynamic-slice_fusion.2), channel_id=1, source_target_pairs={{0,16},{16,0},{1,17},{17,1},{2,18},{18,2},{3,19},{19,3},{4,20},{20... | collective-permute-start | bytes 5308424 | tf_op jit(solution)/shard_map/ppermute | solution.py:678
  73.9 7.1 %slice-start = ((s32[384]{0:T(512)}), s32[256]{0:T(256)S(1)}, s32[]{:S(2)}) async-start(s32[384]{0:T(512)} %copy-done.6), calls=%async_computation.4 | async-start | bytes 2048 | tf_op jit(solution)/shard_map/slice | solution.py:472
  123.7 22.2 %all-to-all-start.3 = ((bf16[32,24,384]{2,1,0:T(8,128)(2,1)}), bf16[32,24,384]{2,1,0:T(8,128)(2,1)S(1)}, u32[]{:S(2)}, u32[]{:S(2)}) async-start(bf16[32,24,384]{2,1,0:T(8,128)(2,1)} %bitcast.25), calls=%async_computation.3 | async-start | bytes 1179648 | tf_op jit(solution)/shard_map/all_to_all | solution.py:776
  146.0 5.6 %copy-start.2 = (bf16[32,24,384]{2,1,0:T(8,128)(2,1)}, bf16[32,24,384]{2,1,0:T(8,128)(2,1)S(1)}, u32[]{:S(2)}) copy-start(bf16[32,24,384]{2,1,0:T(8,128)(2,1)S(1)} %all-to-all-done.3.kept_ref) | copy-start | bytes 1769476
  146.0 72.9 %all-to-all-start.2 = ((bf16[32,120,384]{2,1,0:T(8,128)(2,1)}), bf16[32,120,384]{2,1,0:T(8,128)(2,1)S(1)}, u32[]{:S(2)}, u32[]{:S(2)}) async-start(bf16[32,120,384]{2,1,0:T(8,128)(2,1)} %bitcast.24), calls=%async_computation.2 | async-start | bytes 5898240 | tf_op jit(solution)/shard_map/all_to_all | solution.py:776
  151.7 1.6 collective-permute-start.2
  153.3 0.7 copy-start.4
  218.9 3.6 %copy-start = (bf16[32,120,384]{2,1,0:T(8,128)(2,1)}, bf16[32,120,384]{2,1,0:T(8,128)(2,1)S(1)}, u32[]{:S(2)}) copy-start(bf16[32,120,384]{2,1,0:T(8,128)(2,1)S(1)} %all-to-all-done.2.kept_ref) | copy-start | bytes 8847364
  219.0 3.5 %collective-permute-start.3 = (bf16[16,120,384]{2,1,0:T(8,128)(2,1)S(1)}, bf16[16,120,384]{2,1,0:T(8,128)(2,1)}, u32[]{:S(2)}, u32[]{:S(2)}) collective-permute-start(bf16[16,120,384]{2,1,0:T(8,128)(2,1)S(1)} %constant_dynamic-slice_fusion), channel_id=1, source_target_pairs={{0,16},{16,0},{1,17},{17,1},{2,18},{18,2},{3,19},{19,3},{4,20},{20... | collective-permute-start | bytes 4423688 | tf_op jit(solution)/shard_map/ppermute | solution.py:678

commit v3 on v2

--- a/solution.py
+++ b/solution.py
@@ -222,10 +222,10 @@
     return rows.astype(jnp.bfloat16)
 
 
-def weights_kernel(
-    patch_ref, patch_bias_ref, merge_ref, merge_bias_ref, down_ref, down_bias_ref, gain_ref,
-    w1_ref, w2_ref, w3_ref, column_ref,
-):
+def build_weights(sources, targets):
+    patch_ref, patch_bias_ref, merge_ref, merge_bias_ref, down_ref, down_bias_ref, gain_ref = sources
+    w1_ref, w2_ref, w3_ref, column_ref = targets
+
     def exact(a, b):
         return jnp.dot(
             a.astype(jnp.bfloat16), b.astype(jnp.bfloat16), preferred_element_type=jnp.float32
@@ -259,35 +259,32 @@
     column_ref[...] = jnp.broadcast_to(gain_ref[...], (128, gain_ref.shape[1])).T
 
 
-def stem_weights(
+def weight_sources(
     patch_conv_weight, patch_bias, merging_conv_weight, merge_bias, down_weight, down_bias,
     norm_gain,
 ):
     width = patch_conv_weight.shape[3]
     merged = merging_conv_weight.shape[3]
-    channels = down_weight.shape[3]
-    patch = patch_conv_weight.reshape(-1, width)
-    depths = (4 * patch.shape[0] + ONES[0], 4 * width + ONES[1], 9 * merged + ONES[2])
-    return pl.pallas_call(
-        weights_kernel,
-        out_shape=[
-            jax.ShapeDtypeStruct((4 * width, depths[0]), jnp.bfloat16),
-            jax.ShapeDtypeStruct((merged, depths[1]), jnp.bfloat16),
-            jax.ShapeDtypeStruct((channels, depths[2]), jnp.bfloat16),
-            jax.ShapeDtypeStruct((channels, 128), jnp.float32),
-        ],
-        compiler_params=pltpu.CompilerParams(vmem_limit_bytes=VMEM_BYTES),
-        cost_estimate=pl.CostEstimate(flops=1000000, bytes_accessed=4000000, transcendentals=0),
-        name="stem_weights",
-    )(
-        patch,
+    return [
+        patch_conv_weight.reshape(-1, width),
         patch_bias[None],
         merging_conv_weight.reshape(-1, merged),
         merge_bias[None],
-        down_weight.reshape(9, merged, channels),
+        down_weight.reshape(-1, merged, down_weight.shape[3]),
         down_bias[None],
         norm_gain[None],
-    )
+    ]
+
+
+def weight_shapes(sources):
+    taps, width = sources[0].shape
+    merged, channels = sources[4].shape[1:]
+    return [
+        jax.ShapeDtypeStruct((4 * width, 4 * taps + ONES[0]), jnp.bfloat16),
+        jax.ShapeDtypeStruct((merged, 4 * width + ONES[1]), jnp.bfloat16),
+        jax.ShapeDtypeStruct((channels, 9 * merged + ONES[2]), jnp.bfloat16),
+        jax.ShapeDtypeStruct((channels, 128), jnp.float32),
+    ]
 
 
 def half_gelu(h):
@@ -301,8 +298,13 @@
     )
 
 
-def stem_kernel(place_ref, x_ref, above_ref, *refs):
-    w1_ref, w2_ref, w3_ref, gain_ref, normed_ref, feat_ref, field = refs[-7:]
+def stem_kernel(kind, place_ref, x_ref, above_ref, *refs):
+    if kind == "first":
+        sources = refs[:7]
+        normed_ref, feat_ref, w1_ref, w2_ref, w3_ref, gain_ref, field = refs[7:]
+    else:
+        w1_ref, w2_ref, w3_ref, gain_ref = refs[:4]
+        normed_ref, feat_ref, field = refs[-3:]
     step = pl.program_id(0)
     rows, cols, depth = x_ref.shape
     bands = depth // 256
@@ -310,6 +312,13 @@
     merged = w2_ref.shape[0]
     group = normed_ref.shape[2] // rows
     cells = rows * cols
+
+    if kind == "first":
+
+        @pl.when(step == 0)
+        def _():
+            build_weights(sources, (w1_ref, w2_ref, w3_ref, gain_ref))
+
     w1 = w1_ref[...]
     w2 = w2_ref[...]
 
@@ -348,9 +357,9 @@
         field[9 * merged :, :] = ones(ONES[2], cells)
         above = lower_half(above_ref[0])
         keep = 1.0
-        if len(refs) > 7:
+        if kind == "last":
             keep = place_ref[1].astype(jnp.float32)
-            above = jnp.where(place_ref[2] > 0, refs[0][...], above)
+            above = jnp.where(place_ref[2] > 0, refs[4][...], above)
         turned = above.T
         upper, lower = (
             layer_one(turned, [128 * b + 64 * a for b in range(bands)]) for a in range(2)
@@ -407,22 +416,39 @@
         ).astype(jnp.bfloat16)
 
 
-def stem(image, arriving, place, weights, first, steps, devices):
+def stem(kind, image, place, weights, first, steps, base, pairs, devices, extra=()):
     cols, depth = image.shape[1:]
     rows = 2 * steps
-    channels, third_depth = weights[2].shape
-    merged = weights[1].shape[0]
+    shapes = weight_shapes(weights) if kind == "first" else weights
+    channels, third_depth = shapes[2].shape
+    merged = shapes[1].shape[0]
     group = channels // devices
 
     def whole(array):
-        return pl.BlockSpec(array.shape, lambda i, place: (0,) * array.ndim)
-
-    operands = list(weights)
-    if arriving is not None:
-        operands = [arriving] + operands
+        return pl.BlockSpec(array.shape, lambda i, place: (0,) * len(array.shape))
+
+    operands = list(weights) + list(extra)
+    in_specs = [whole(a) for a in weights]
+    out_specs = [
+        pl.BlockSpec(
+            (devices, 1, 2 * group, cols), lambda i, place: (0, first - base + i, 0, 0)
+        ),
+        pl.BlockSpec((2, channels, cols), lambda i, place: (first - base + i, 0, 0)),
+    ]
+    out_shape = [
+        jax.ShapeDtypeStruct((devices, pairs, 2 * group, cols), jnp.bfloat16),
+        jax.ShapeDtypeStruct((2 * pairs, channels, cols), jnp.bfloat16),
+    ]
+    aliases = {}
+    if kind == "first":
+        out_specs += [whole(a) for a in shapes]
+        out_shape += shapes
+    if kind == "last":
+        in_specs += [whole(extra[0])] + [pl.BlockSpec(memory_space=pl.ANY)] * 2
+        aliases = {8: 0, 9: 1}
     macs = rows * cols * (16 * 208 * 96 + 4 * 400 * merged + third_depth * channels)
     return pl.pallas_call(
-        stem_kernel,
+        functools.partial(stem_kernel, kind),
         grid_spec=pltpu.PrefetchScalarGridSpec(
             num_scalar_prefetch=1,
             grid=(steps,),
@@ -433,17 +459,12 @@
                     lambda i, place: (jnp.maximum(2 * (place[0] + first) - 1, 0), 0, 0),
                 ),
             ]
-            + [whole(a) for a in operands],
-            out_specs=[
-                pl.BlockSpec((devices, 1, 2 * group, cols), lambda i, place: (0, i, 0, 0)),
-                pl.BlockSpec((2, channels, cols), lambda i, place: (i, 0, 0)),
-            ],
+            + in_specs,
+            out_specs=out_specs,
             scratch_shapes=[pltpu.VMEM((third_depth, 2 * cols), jnp.bfloat16)],
         ),
-        out_shape=[
-            jax.ShapeDtypeStruct((devices, steps, 2 * group, cols), jnp.bfloat16),
-            jax.ShapeDtypeStruct((rows, channels, cols), jnp.bfloat16),
-        ],
+        out_shape=out_shape,
+        input_output_aliases=aliases,
         compiler_params=pltpu.CompilerParams(vmem_limit_bytes=VMEM_BYTES),
         cost_estimate=pl.CostEstimate(
             flops=4 * macs, bytes_accessed=rows * cols * 3000, transcendentals=0
@@ -611,7 +632,7 @@
             pltpu.VMEM((cols // 128, full_rows * group, 128), jnp.float32),
             pltpu.VMEM((cols // 128, full_rows * count, 128), jnp.float32),
         ],
-        compiler_params=pltpu.CompilerParams(vmem_limit_bytes=VMEM_BYTES),
+        compiler_params=pltpu.CompilerParams(vmem_limit_bytes=VMEM_BYTES * 2 // 3),
         cost_estimate=pl.CostEstimate(
             flops=2 * macs, bytes_accessed=count * full_rows * cols * 8, transcendentals=0
         ),
@@ -664,7 +685,7 @@
         ),
         out_shape=jax.ShapeDtypeStruct(features.shape, jnp.bfloat16),
         input_output_aliases=aliases,
-        compiler_params=pltpu.CompilerParams(vmem_limit_bytes=VMEM_BYTES),
+        compiler_params=pltpu.CompilerParams(vmem_limit_bytes=VMEM_BYTES // 3),
         cost_estimate=pl.CostEstimate(
             flops=halves * count * rows * cols,
             bytes_accessed=halves * count * rows * cols * 8,
@@ -697,9 +718,8 @@
     devices = sections * lax.axis_size("tile")
     suits = (
         sections == 2
-        and tile_rows % 4 == 0
-        and tile_channels % 4 == 0
-        and (tile_rows // 2) * (tile_channels // 4) % 8 == 0
+        and tile_rows % 8 == 0
+        and tile_rows >= 16
         and field_cols % 128 == 0
         and full_rows % 128 == 0
         and tile_channels % 8 == 0
@@ -727,29 +747,27 @@
     arriving = from_behind(lower_half(aerial_patch_grid[-1]), "tile", 1)
     inside = (section > 0) | (tile > 0)
     place = jnp.stack([section * (rows // 2), inside, section == 0]).astype(jnp.int32)
-    weights = stem_weights(*arguments[1:8])
+    sources = weight_sources(*arguments[1:8])
     pairs = rows // 2
     early = max(pairs // 3, 1)
-    spans = [(pairs - early, early), (0, pairs - early)]
+    late = pairs - early
+    normed_early, feat_early, *weights = stem(
+        "first", aerial_patch_grid, place, sources, late, early, late, early, devices
+    )
+    normed_late = stem(
+        "middle", aerial_patch_grid, place, weights, 1, late - 1, 0, late, devices
+    )
+    normed_late, feat_late = stem(
+        "last", aerial_patch_grid, place, weights, 0, 1, 0, late, devices, (arriving, *normed_late)
+    )
     pieces = []
-    features = []
     row_order = []
-    for first, steps in spans:
-        normed, part = stem(
-            aerial_patch_grid,
-            arriving if first == 0 else None,
-            place,
-            weights,
-            first,
-            steps,
-            devices,
-        )
-        normed, arriving = lax.optimization_barrier((normed, arriving))
+    for normed, first, count in ((normed_early, late, early), (normed_late, 0, late)):
         normed = lax.all_to_all(normed, DEVICES, split_axis=0, concat_axis=0, tiled=True)
-        pieces.append(normed.reshape(2 * steps * devices * group, field_cols))
-        features.insert(0, part)
-        own_rows = np.arange(2 * first, 2 * (first + steps))
+        pieces.append(normed.reshape(2 * count * devices * group, field_cols))
+        own_rows = np.arange(2 * first, 2 * (first + count))
         row_order.append((rows * np.arange(devices)[:, None] + own_rows).reshape(-1))
+    features = [feat_late, feat_early]
     features = jnp.concatenate(features, axis=0)
     row_order = np.concatenate(row_order).astype(np.int32)
 

time: 229 us -> 249 us (1.087)
  local copies, waits for them, and re-layouts: 11.9 us -> 27.8 us
  starting transfers between devices: 23.9 us -> 38.6 us
  waiting for transfers between devices: 88 us -> 81.1 us
  Pallas kernels: 84.4 us -> 80.7 us
    all_to_all x2, starting transfers between devices: 8.86 us -> 24.6 us  [local(): lax.all_to_all(normed, DEVICES, split_axis=0, concat_axis=0, tiled=True)]
    unnamed x21 -> x35, local copies, waits for them, and re-layouts: 3.78 us -> 17.8 us
    all_to_all x2, waiting for transfers between devices: 21.9 us -> 15.1 us  [local(): lax.all_to_all(normed, DEVICES, split_axis=0, concat_axis=0, tiled=True)]
    pallas_call x2, Pallas kernels: 24.9 us -> 20.1 us  [filter_channels(): pl.pallas_call(functools.partial(filter_kernel, first, 1.0 / (full_rows *...]
  transfers between devices with their start and end apart: 8 -> 8, of which waited for: 5 -> 4; matrix products, arithmetic and copies ran while one was open for 12% -> 11% of each run, Pallas kernels for 32% -> 23%
where the time goes in v3:
time: 249 us; the launch traced here: 248 us
  waiting for transfers between devices  81.1 us (33%)
  Pallas kernels  80.7 us (32%)
  starting transfers between devices  38.6 us (16%)
  local copies, waits for them, and re-layouts  27.8 us (11%)
  other arithmetic  19 us (8%)
    all_to_all x2, waiting for transfers between devices, local(): lax.all_to_all(made, DEVICES, split_axis=0, concat_axis=0, tiled=True)  61.4 us
    pallas_call x3, Pallas kernels, stem(): pl.pallas_call(functools.partial(stem_kernel, kind), grid_spec=pltpu.Pref...  38.2 us
    all_to_all x2, starting transfers between devices, local(): lax.all_to_all(normed, DEVICES, split_axis=0, concat_axis=0, tiled=True)  24.6 us
    pallas_call x2, Pallas kernels, filter_channels(): pl.pallas_call(functools.partial(filter_kernel, first, 1.0 / (full_rows *...  20.1 us
    unnamed x35, local copies, waits for them, and re-layouts  17.8 us
    all_to_all x2, waiting for transfers between devices, local(): lax.all_to_all(normed, DEVICES, split_axis=0, concat_axis=0, tiled=True)  15.1 us
    pallas_call x1, Pallas kernels, symmetric_filter(): pl.pallas_call(symmetric_kernel, grid_spec=pltpu.PrefetchScalarGridSpec(n...  15 us
    all_to_all x2, starting transfers between devices, local(): lax.all_to_all(made, DEVICES, split_axis=0, concat_axis=0, tiled=True)  9.87 us
  transfers between devices with their start and end apart: 8, of which 4 were waited for; matrix products, arithmetic and copies ran while one was open for 11% of the time, Pallas kernels for 23%

profile of v3, /device:TPU:0, one launch (start us, length us, event | category | flops | bytes accessed | tf_op | source)
XLA Modules:
  0.0 247.5 jit_solution(18415737322219705845)
XLA Ops:
  0.0 1.2 broadcast_in_dim.18.refs_5_
  1.2 1.3 broadcast_in_dim.19.refs_6_
  2.5 0.6 pad_add_fusion.place_ref
  3.1 13.6 %stem.3 = (bf16[32,2,24,384]{3,2,1,0:T(8,128)(2,1)}, bf16[4,384,384]{2,1,0:T(8,128)(2,1)}, bf16[384,256]{1,0:T(8,128)(2,1)}, bf16[192,512]{1,0:T(8,128)(2,1)}, b...) custom-call(s32[3]{0:T(128)} %pad_add_fusion.place_ref, bf16[24,384,768]{2,1,0:T(8,128)(2,1)} %above_ref.5, ...), custom_call_target="tpu_custom_call" | custom-call | flops 8078229504 | bytes 4608000 | tf_op jit(solution)/shard_map/stem/pallas_call | solution.py:450
  16.7 7.3 %all-to-all-start = ((bf16[32,2,24,384]{3,2,1,0:T(8,128)(2,1)}), bf16[32,2,24,384]{3,2,1,0:T(8,128)(2,1)S(1)}, u32[]{:S(2)}, u32[]{:S(2)}) async-start(bf16[32,2,24,384]{3,2,1,0:T(8,128)(2,1)} %get-tuple-element.25), calls=%async_computation | async-start | bytes 2359296 | tf_op jit(solution)/shard_map/all_to_all | solution.py:766
  24.0 1.1 slice_bitcast_fusion
  25.1 0.1 fusion.27
  25.2 3.9 %collective-permute-start = (bf16[384,384]{1,0:T(8,128)(2,1)S(1)}, bf16[384,384]{1,0:T(8,128)(2,1)S(1)}, u32[]{:S(2)}, u32[]{:S(2)}) collective-permute-start(bf16[384,384]{1,0:T(8,128)(2,1)S(1)} %pad_maximum_fusion.2), channel_id=1, source_target_pairs={{0,1},{1,2},{2,3},{3,4},{4,5},{5,6},{6,7},{7,8},{8,9},{9,10},{10,1... | collective-permute-start | bytes 884744 | tf_op jit(solution)/shard_map/ppermute | solution.py:18
  29.1 16.2 %stem.4 = (bf16[32,4,24,384]{3,2,1,0:T(8,128)(2,1)}, bf16[8,384,384]{2,1,0:T(8,128)(2,1)}) custom-call(s32[3]{0:T(128)} %pad_add_fusion.place_ref, bf16[24,384,768]{2,1,0:T(8,128)(2,1)} %above_ref.5, bf16[24,384,768]{2,1,0:T(8,128)(2,1)} %above_ref.5, bf16[384,256]{1,0:T(8,128)(2,1)} %get-tuple-element.26.refs_0_, ...), custom_call_target="tpu_custom_call" | custom-call | flops 12117344256 | bytes 6912000 | tf_op jit(solution)/shard_map/stem/pallas_call | solution.py:450
  45.3 0.0 collective-permute-done.refs_4_
  45.3 0.7 copy-done.14
  46.0 8.5 %stem.5 = (bf16[32,4,24,384]{3,2,1,0:T(8,128)(2,1)}, bf16[8,384,384]{2,1,0:T(8,128)(2,1)}) custom-call(s32[3]{0:T(128)} %pad_add_fusion.place_ref, bf16[24,384,768]{2,1,0:T(8,128)(2,1)} %above_ref.5, bf16[24,384,768]{2,1,0:T(8,128)(2,1)} %above_ref.5, bf16[384,256]{1,0:T(8,128)(2,1)} %get-tuple-element.26.refs_0_, ...), custom_call_target="tpu_custom_call", output_to_operand_aliasing={{0}: (8, {}), {1}: (9, {})} | custom-call | flops 4039114752 | bytes 2304000 | tf_op jit(solution)/shard_map/stem/pallas_call | solution.py:450
  54.4 0.0 all-to-all-done
  54.4 1.0 copy-done
  55.5 17.3 %all-to-all-start.1 = ((bf16[32,4,24,384]{3,2,1,0:T(8,128)(2,1)}), bf16[32,4,24,384]{3,2,1,0:T(8,128)(2,1)}, u32[]{:S(2)}, u32[]{:S(2)}) async-start(bf16[32,4,24,384]{3,2,1,0:T(8,128)(2,1)} %get-tuple-element.32), calls=%async_computation.1 | async-start | bytes 4718592 | tf_op jit(solution)/shard_map/all_to_all | solution.py:766
  72.8 0.0 copy-start.16
  72.8 2.3 fusion.22
  75.1 1.0 fusion.12.turn_u_ref
  76.1 2.5 %sine_convert_fusion.1 = (bf16[384,384]{1,0:T(8,128)(2,1)S(1)}, bf16[384,384]{1,0:T(8,128)(2,1)S(1)}) fusion(), kind=kLoop, calls=%fused_computation.19 | loop fusion | flops 1622016 | bytes 589824 | tf_op jit(solution)/shard_map/convert_element_type | solution.py:26
  78.7 0.1 slice_multiply_fusion
  78.8 0.8 pad_maximum_fusion.1.refs_6_
  79.6 2.0 constant_dynamic-update-slice_fusion.1
  81.6 0.2 constant_dynamic-update-slice_fusion
  81.9 1.5 constant_dynamic-slice_fusion.2
  83.4 0.0 collective-permute-start.1
  83.4 0.8 pad_maximum_fusion.refs_3_
  84.2 1.1 maximum_maximum_fusion.1.refs_5_
  85.3 2.3 fusion.23
  87.6 2.5 %sine_convert_fusion = (bf16[384,384]{1,0:T(8,128)(2,1)S(1)}, bf16[384,384]{1,0:T(8,128)(2,1)S(1)}) fusion(s32[384]{0:T(512)S(1)} %copy-done.15), kind=kLoop, calls=%fused_computation.14 | loop fusion | flops 1622016 | bytes 591360 | tf_op jit(solution)/shard_map/convert_element_type | solution.py:26
  90.2 1.1 maximum_maximum_fusion.refs_4_
  91.3 0.9 fusion.19.turn_w_ref
  92.2 15.0 %symmetric_filter.1.refs_2_ = f32[12,2,384,256]{3,2,1,0:T(8,128)} custom-call(s32[1]{0:T(128)} %bitcast.14.place_ref, bf16[24,2,384,384]{3,2,1,0:T(8,128)(2,1)} %f_ref.1, bf16[384,256]{1,0:T(8,128)(2,1)} %fusion.19.turn_w_ref, bf16[384,384]{1,0:T(8,128)(2,1)} %fusion.12.turn_u_ref), custom_call_target="tpu_custom_call" | custom-call | flops 3623878656 | bytes 16515072 | tf_op jit(solution)/shard_map/symmetric_filter/pallas_call | solution.py:494
  107.3 0.0 collective-permute-done.1
  107.3 2.3 broadcast_select_fusion.1
  109.6 0.4 maximum_bitcast_fusion
  110.0 2.1 copy.14
  112.1 15.1 %all-to-all-done.1 = bf16[32,4,24,384]{3,2,1,0:T(8,128)(2,1)} async-done(((bf16[32,4,24,384]{3,2,1,0:T(8,128)(2,1)}), bf16[32,4,24,384]{3,2,1,0:T(8,128)(2,1)}, u32[]{:S(2)}, u32[]{:S(2)}) %all-to-all-start.1) | async-done | bytes 2359328 | tf_op jit(solution)/shard_map/all_to_all | solution.py:766
  127.2 1.3 copy-done.1
  128.5 1.3 copy-done.3
  129.7 1.3 copy-done.5
  131.0 1.0 copy-done.9
  132.0 1.0 copy-done.11
  133.0 4.8 %spectral_filter.3 = bf16[768,384]{1,0:T(8,128)(2,1)S(1)} custom-call(bf16[1536,384]{1,0:T(8,128)(2,1)S(1)} %bitcast.22, bf16[3072,384]{1,0:T(8,128)(2,1)} %bitcast.11.refs_1_, f32[12,2,384,256]{3,2,1,0:T(8,128)} %symmetric_filter.1.refs_2_, bf16[384,512]{1,0:T(8,128)(2,1)S(1)} %copy-done.11, bf16[768,768]{1,0:T(8,128)(2,1)S(1)} %copy-done.5, ...), custom_call_target="tpu_custom_call" | custom-call | flops 1811939328 | bytes 2359296 | tf_op jit(solution)/shard_map/spectral_filter/pallas_call | solution.py:616
  137.9 0.0 copy-start.8
  137.9 0.8 copy-done.8
  138.7 4.2 %all-to-all-start.3 = ((bf16[32,24,384]{2,1,0:T(8,128)(2,1)}), bf16[32,24,384]{2,1,0:T(8,128)(2,1)}, u32[]{:S(2)}, u32[]{:S(2)}) async-start(bf16[32,24,384]{2,1,0:T(8,128)(2,1)} %bitcast.25), calls=%async_computation.3 | async-start | bytes 1179648 | tf_op jit(solution)/shard_map/all_to_all | solution.py:794
  142.9 1.3 copy-done.2
  144.2 1.3 copy-done.4
  145.5 1.3 copy-done.6
  146.7 1.0 copy-done.10
  147.7 1.0 copy-done.12
  148.7 15.2 %spectral_filter.2 = bf16[3840,384]{1,0:T(8,128)(2,1)S(1)} custom-call(bf16[1536,384]{1,0:T(8,128)(2,1)S(1)} %bitcast.23, bf16[3072,384]{1,0:T(8,128)(2,1)} %bitcast.11.refs_1_, f32[12,2,384,256]{3,2,1,0:T(8,128)} %symmetric_filter.1.refs_2_, bf16[384,512]{1,0:T(8,128)(2,1)S(1)} %copy-done.12, bf16[768,768]{1,0:T(8,128)(2,1)S(1)} %copy-done.6, ...), custom_call_target="tpu_custom_call" | custom-call | flops 9059696640 | bytes 11796480 | tf_op jit(solution)/shard_map/spectral_filter/pallas_call | solution.py:616
  164.0 1.6 copy-done.7
  165.6 0.0 all-to-all-done.3.kept_ref
  165.6 5.6 %all-to-all-start.2 = ((bf16[32,120,384]{2,1,0:T(8,128)(2,1)}), bf16[32,120,384]{2,1,0:T(8,128)(2,1)}, u32[]{:S(2)}, u32[]{:S(2)}) async-start(bf16[32,120,384]{2,1,0:T(8,128)(2,1)} %bitcast.24), calls=%async_computation.2 | async-start | bytes 5898240 | tf_op jit(solution)/shard_map/all_to_all | solution.py:794
  171.2 1.0 constant_dynamic-slice_fusion.1
  172.2 0.3 collective-permute-start.2
  172.5 1.4 collective-permute-done.2.other_ref
  173.9 3.2 %residual.2.refs_0_ = bf16[16,12,24,384]{3,2,1,0:T(8,128)(2,1)} custom-call(s32[1]{0:T(128)} %bitcast.place_ref, bf16[32,24,384]{2,1,0:T(8,128)(2,1)} %all-to-all-done.3.kept_ref, bf16[16,24,384]{2,1,0:T(8,128)(2,1)S(1)} %collective-permute-done.2.other_ref, bf16[16,12,24,384]{3,2,1,0:T(8,128)(2,1)S(1)} %bitcast.20), custom_call_target="tpu_custom_call" | custom-call | flops 294912 | bytes 2359296 | tf_op jit(solution)/shard_map/residual/pallas_call | solution.py:677
  177.1 61.4 %all-to-all-done.2.kept_ref = bf16[32,120,384]{2,1,0:T(8,128)(2,1)} async-done(((bf16[32,120,384]{2,1,0:T(8,128)(2,1)}), bf16[32,120,384]{2,1,0:T(8,128)(2,1)}, u32[]{:S(2)}, u32[]{:S(2)}) %all-to-all-start.2) | async-done | bytes 2949152 | tf_op jit(solution)/shard_map/all_to_all | solution.py:794
  238.4 1.5 constant_dynamic-slice_fusion
  240.0 0.1 collective-permute-start.3
  240.0 3.3 %collective-permute-done.3.other_ref = bf16[16,120,384]{2,1,0:T(8,128)(2,1)S(1)} collective-permute-done((bf16[16,120,384]{2,1,0:T(8,128)(2,1)S(1)}, bf16[16,120,384]{2,1,0:T(8,128)(2,1)S(1)}, u32[]{:S(2)}, u32[]{:S(2)}) %collective-permute-start.3) | collective-permute-done | bytes 1474592 | tf_op jit(solution)/shard_map/ppermute | solution.py:699
  243.3 4.2 %residual.3 = bf16[16,12,24,384]{3,2,1,0:T(8,128)(2,1)} custom-call(s32[1]{0:T(128)} %bitcast.place_ref, bf16[32,120,384]{2,1,0:T(8,128)(2,1)} %all-to-all-done.2.kept_ref, bf16[16,120,384]{2,1,0:T(8,128)(2,1)S(1)} %collective-permute-done.3.other_ref, bf16[16,12,24,384]{3,2,1,0:T(8,128)(2,1)S(1)} %bitcast.21, ...), custom_call_target="tpu_custom_call", output_to_operand_aliasing={{}: (4, {})} | custom-call | flops 1474560 | bytes 11796480 | tf_op jit(solution)/shard_map/residual/pallas_call | solution.py:677
  (25 shorter events, 0.1 us)
Async XLA Ops:
  16.7 37.8 %all-to-all-start = ((bf16[32,2,24,384]{3,2,1,0:T(8,128)(2,1)}), bf16[32,2,24,384]{3,2,1,0:T(8,128)(2,1)S(1)}, u32[]{:S(2)}, u32[]{:S(2)}) async-start(bf16[32,2,24,384]{3,2,1,0:T(8,128)(2,1)} %get-tuple-element.25), calls=%async_computation | async-start | bytes 2359296 | tf_op jit(solution)/shard_map/all_to_all | solution.py:766
  25.2 20.0 %collective-permute-start = (bf16[384,384]{1,0:T(8,128)(2,1)S(1)}, bf16[384,384]{1,0:T(8,128)(2,1)S(1)}, u32[]{:S(2)}, u32[]{:S(2)}) collective-permute-start(bf16[384,384]{1,0:T(8,128)(2,1)S(1)} %pad_maximum_fusion.2), channel_id=1, source_target_pairs={{0,1},{1,2},{2,3},{3,4},{4,5},{5,6},{6,7},{7,8},{8,9},{9,10},{10,1... | collective-permute-start | bytes 884744 | tf_op jit(solution)/shard_map/ppermute | solution.py:18
  45.3 0.7 copy-start.14
  54.4 1.0 copy-start
  55.5 71.7 %all-to-all-start.1 = ((bf16[32,4,24,384]{3,2,1,0:T(8,128)(2,1)}), bf16[32,4,24,384]{3,2,1,0:T(8,128)(2,1)}, u32[]{:S(2)}, u32[]{:S(2)}) async-start(bf16[32,4,24,384]{3,2,1,0:T(8,128)(2,1)} %get-tuple-element.32), calls=%async_computation.1 | async-start | bytes 4718592 | tf_op jit(solution)/shard_map/all_to_all | solution.py:766
  72.8 8.8 %copy-start.16 = (s32[384]{0:T(512)}, s32[384]{0:T(512)S(1)}, u32[]{:S(2)}) copy-start(s32[384]{0:T(512)S(1)} %iota.31) | copy-start | bytes 4612
  79.6 2.0 copy-start.13
  83.4 1.9 copy-start.15
  83.4 23.9 %collective-permute-start.1 = (bf16[12,192,384]{2,1,0:T(8,128)(2,1)}, bf16[12,192,384]{2,1,0:T(8,128)(2,1)}, u32[]{:S(2)}, u32[]{:S(2)}) collective-permute-start(bf16[12,192,384]{2,1,0:T(8,128)(2,1)} %constant_dynamic-slice_fusion.2), channel_id=1, source_target_pairs={{0,16},{16,0},{1,17},{17,1},{2,18},{18,2},{3,19},{19,3},{4,20},{20... | collective-permute-start | bytes 5308424 | tf_op jit(solution)/shard_map/ppermute | solution.py:699
  84.2 7.1 %slice-start = ((s32[384]{0:T(512)}), s32[256]{0:T(256)S(1)}, s32[]{:S(2)}) async-start(s32[384]{0:T(512)} %copy-done.16), calls=%async_computation.4 | async-start | bytes 2048 | tf_op jit(solution)/shard_map/slice | solution.py:493
  127.2 1.3 copy-start.1
  128.5 1.3 copy-start.3
  129.7 1.3 copy-start.5
  131.0 1.0 copy-start.9
  132.0 1.0 copy-start.11
  137.9 0.8 copy-start.8
  138.7 26.9 %all-to-all-start.3 = ((bf16[32,24,384]{2,1,0:T(8,128)(2,1)}), bf16[32,24,384]{2,1,0:T(8,128)(2,1)}, u32[]{:S(2)}, u32[]{:S(2)}) async-start(bf16[32,24,384]{2,1,0:T(8,128)(2,1)} %bitcast.25), calls=%async_computation.3 | async-start | bytes 1179648 | tf_op jit(solution)/shard_map/all_to_all | solution.py:794
  142.9 1.3 copy-start.2
  144.2 1.3 copy-start.4
  145.5 1.3 copy-start.6
  146.7 1.0 copy-start.10
  147.7 1.0 copy-start.12
  164.0 1.6 copy-start.7
  165.6 72.9 %all-to-all-start.2 = ((bf16[32,120,384]{2,1,0:T(8,128)(2,1)}), bf16[32,120,384]{2,1,0:T(8,128)(2,1)}, u32[]{:S(2)}, u32[]{:S(2)}) async-start(bf16[32,120,384]{2,1,0:T(8,128)(2,1)} %bitcast.24), calls=%async_computation.2 | async-start | bytes 5898240 | tf_op jit(solution)/shard_map/all_to_all | solution.py:794
  172.2 1.6 collective-permute-start.2
  240.0 3.3 %collective-permute-start.3 = (bf16[16,120,384]{2,1,0:T(8,128)(2,1)S(1)}, bf16[16,120,384]{2,1,0:T(8,128)(2,1)S(1)}, u32[]{:S(2)}, u32[]{:S(2)}) collective-permute-start(bf16[16,120,384]{2,1,0:T(8,128)(2,1)S(1)} %constant_dynamic-slice_fusion), channel_id=1, source_target_pairs={{0,16},{16,0},{1,17},{17,1},{2,18},{18,2},{3,19},{19,3},{4,20},{20... | collective-permute-start | bytes 4423688 | tf_op jit(solution)/shard_map/ppermute | solution.py:699

commit v4 on v3

--- a/solution.py
+++ b/solution.py
@@ -242,7 +242,7 @@
     row = lax.broadcasted_iota(jnp.int32, spread.shape, 0)
     col = lax.broadcasted_iota(jnp.int32, spread.shape, 1)
     spread = jnp.where(row // 4 % 4 == col // width, 0.5 * spread, 0.0).astype(jnp.bfloat16)
-    bias = jnp.broadcast_to(0.5 * patch_bias_ref[...], (8, width))
+    bias = jnp.broadcast_to(0.5 * patch_bias_ref[...][None], (8, width))
     tiled = jnp.zeros((8, 4 * width), jnp.float32)
     for _ in range(3):
         part = bias.astype(jnp.bfloat16).astype(jnp.float32)
@@ -251,12 +251,12 @@
     first = jnp.concatenate([spread, bias_rows(tiled[:1], ONES[0])], axis=0)
     w1_ref[...] = first.T
     half = (merge_ref[...].astype(jnp.float32) * 0.5).astype(jnp.bfloat16)
-    second = jnp.concatenate([half, bias_rows(0.5 * merge_bias_ref[...], ONES[1])], axis=0)
+    second = jnp.concatenate([half, bias_rows(0.5 * merge_bias_ref[...][None], ONES[1])], axis=0)
     w2_ref[...] = second.T
     third = [down_ref[3 * a + q] for a, q in TAPS]
-    third = jnp.concatenate(third + [bias_rows(down_bias_ref[...], ONES[2])], axis=0)
+    third = jnp.concatenate(third + [bias_rows(down_bias_ref[...][None], ONES[2])], axis=0)
     w3_ref[...] = third.T
-    column_ref[...] = jnp.broadcast_to(gain_ref[...], (128, gain_ref.shape[1])).T
+    column_ref[...] = jnp.broadcast_to(gain_ref[...][None], (128, gain_ref.shape[0])).T
 
 
 def weight_sources(
@@ -267,12 +267,12 @@
     merged = merging_conv_weight.shape[3]
     return [
         patch_conv_weight.reshape(-1, width),
-        patch_bias[None],
+        patch_bias,
         merging_conv_weight.reshape(-1, merged),
-        merge_bias[None],
+        merge_bias,
         down_weight.reshape(-1, merged, down_weight.shape[3]),
-        down_bias[None],
-        norm_gain[None],
+        down_bias,
+        norm_gain,
     ]
 
 
@@ -416,7 +416,7 @@
         ).astype(jnp.bfloat16)
 
 
-def stem(kind, image, place, weights, first, steps, base, pairs, devices, extra=()):
+def stem(kind, image, place, weights, first, steps, devices, extra=()):
     cols, depth = image.shape[1:]
     rows = 2 * steps
     shapes = weight_shapes(weights) if kind == "first" else weights
@@ -430,22 +430,18 @@
     operands = list(weights) + list(extra)
     in_specs = [whole(a) for a in weights]
     out_specs = [
-        pl.BlockSpec(
-            (devices, 1, 2 * group, cols), lambda i, place: (0, first - base + i, 0, 0)
-        ),
-        pl.BlockSpec((2, channels, cols), lambda i, place: (first - base + i, 0, 0)),
+        pl.BlockSpec((devices, 1, 2 * group, cols), lambda i, place: (0, i, 0, 0)),
+        pl.BlockSpec((2, channels, cols), lambda i, place: (i, 0, 0)),
     ]
     out_shape = [
-        jax.ShapeDtypeStruct((devices, pairs, 2 * group, cols), jnp.bfloat16),
-        jax.ShapeDtypeStruct((2 * pairs, channels, cols), jnp.bfloat16),
+        jax.ShapeDtypeStruct((devices, steps, 2 * group, cols), jnp.bfloat16),
+        jax.ShapeDtypeStruct((rows, channels, cols), jnp.bfloat16),
     ]
-    aliases = {}
     if kind == "first":
         out_specs += [whole(a) for a in shapes]
         out_shape += shapes
     if kind == "last":
-        in_specs += [whole(extra[0])] + [pl.BlockSpec(memory_space=pl.ANY)] * 2
-        aliases = {8: 0, 9: 1}
+        in_specs += [whole(extra[0])]
     macs = rows * cols * (16 * 208 * 96 + 4 * 400 * merged + third_depth * channels)
     return pl.pallas_call(
         functools.partial(stem_kernel, kind),
@@ -464,7 +460,6 @@
             scratch_shapes=[pltpu.VMEM((third_depth, 2 * cols), jnp.bfloat16)],
         ),
         out_shape=out_shape,
-        input_output_aliases=aliases,
         compiler_params=pltpu.CompilerParams(vmem_limit_bytes=VMEM_BYTES),
         cost_estimate=pl.CostEstimate(
             flops=4 * macs, bytes_accessed=rows * cols * 3000, transcendentals=0
@@ -632,7 +627,7 @@
             pltpu.VMEM((cols // 128, full_rows * group, 128), jnp.float32),
             pltpu.VMEM((cols // 128, full_rows * count, 128), jnp.float32),
         ],
-        compiler_params=pltpu.CompilerParams(vmem_limit_bytes=VMEM_BYTES * 2 // 3),
+        compiler_params=pltpu.CompilerParams(vmem_limit_bytes=VMEM_BYTES),
         cost_estimate=pl.CostEstimate(
             flops=2 * macs, bytes_accessed=count * full_rows * cols * 8, transcendentals=0
         ),
@@ -685,7 +680,7 @@
         ),
         out_shape=jax.ShapeDtypeStruct(features.shape, jnp.bfloat16),
         input_output_aliases=aliases,
-        compiler_params=pltpu.CompilerParams(vmem_limit_bytes=VMEM_BYTES // 3),
+        compiler_params=pltpu.CompilerParams(vmem_limit_bytes=VMEM_BYTES),
         cost_estimate=pl.CostEstimate(
             flops=halves * count * rows * cols,
             bytes_accessed=halves * count * rows * cols * 8,
@@ -752,13 +747,11 @@
     early = max(pairs // 3, 1)
     late = pairs - early
     normed_early, feat_early, *weights = stem(
-        "first", aerial_patch_grid, place, sources, late, early, late, early, devices
-    )
-    normed_late = stem(
-        "middle", aerial_patch_grid, place, weights, 1, late - 1, 0, late, devices
-    )
+        "first", aerial_patch_grid, place, sources, late, early, devices
+    )
+    normed_early, arriving = lax.optimization_barrier((normed_early, arriving))
     normed_late, feat_late = stem(
-        "last", aerial_patch_grid, place, weights, 0, 1, 0, late, devices, (arriving, *normed_late)
+        "last", aerial_patch_grid, place, weights, 0, late, devices, (arriving,)
     )
     pieces = []
     row_order = []

time: 249 us -> 225 us (0.904)
  local copies, waits for them, and re-layouts: 27.8 us -> 10.7 us
  starting transfers between devices: 38.6 us -> 23.9 us
  waiting for transfers between devices: 81.1 us -> 88 us
    all_to_all x2, starting transfers between devices: 24.6 us -> 8.87 us  [local(): lax.all_to_all(normed, DEVICES, split_axis=0, concat_axis=0, tiled=True)]
    unnamed x35 -> x17, local copies, waits for them, and re-layouts: 17.8 us -> 3.77 us
    all_to_all x2, waiting for transfers between devices: 15.1 us -> 21.9 us  [local(): lax.all_to_all(normed, DEVICES, split_axis=0, concat_axis=0, tiled=True)]
    pallas_call x2, Pallas kernels: 20.1 us -> 24.9 us  [filter_channels(): pl.pallas_call(functools.partial(filter_kernel, first, 1.0 / (full_rows *...]
    pallas_call x3 -> x2, Pallas kernels: 38.2 us -> 33.9 us  [stem(): pl.pallas_call(functools.partial(stem_kernel, kind), grid_spec=pltpu.Pref...]
    broadcast_in_dim x2 -> x0, local copies, waits for them, and re-layouts: 2.51 us -> none  [the longest x1 1.27 us: weight_sources(): norm_gain[None]]
  transfers between devices with their start and end apart: 8 -> 8, of which waited for: 4 -> 5; matrix products, arithmetic and copies ran while one was open for 11% -> 12% of each run, Pallas kernels for 23% -> 31%
where the time goes in v4:
time: 225 us; the launch traced here: 224 us
  waiting for transfers between devices  88 us (39%)
  Pallas kernels  82.4 us (37%)
  starting transfers between devices  23.9 us (11%)
  other arithmetic  19.1 us (8%)
  local copies, waits for them, and re-layouts  10.7 us (5%)
    all_to_all x2, waiting for transfers between devices, local(): lax.all_to_all(made, DEVICES, split_axis=0, concat_axis=0, tiled=True)  61.4 us
    pallas_call x2, Pallas kernels, stem(): pl.pallas_call(functools.partial(stem_kernel, kind), grid_spec=pltpu.Pref...  33.9 us
    pallas_call x2, Pallas kernels, filter_channels(): pl.pallas_call(functools.partial(filter_kernel, first, 1.0 / (full_rows *...  24.9 us
    all_to_all x2, waiting for transfers between devices, local(): lax.all_to_all(normed, DEVICES, split_axis=0, concat_axis=0, tiled=True)  21.9 us
    pallas_call x1, Pallas kernels, symmetric_filter(): pl.pallas_call(symmetric_kernel, grid_spec=pltpu.PrefetchScalarGridSpec(n...  15.1 us
    all_to_all x2, starting transfers between devices, local(): lax.all_to_all(made, DEVICES, split_axis=0, concat_axis=0, tiled=True)  9.79 us
    all_to_all x2, starting transfers between devices, local(): lax.all_to_all(normed, DEVICES, split_axis=0, concat_axis=0, tiled=True)  8.87 us
    pallas_call x2, Pallas kernels, add_residual(): pl.pallas_call(functools.partial(residual_kernel, count), grid_spec=pltpu...  8.52 us
  transfers between devices with their start and end apart: 8, of which 5 were waited for; matrix products, arithmetic and copies ran while one was open for 12% of the time, Pallas kernels for 31%

profile of v4, /device:TPU:0, one launch (start us, length us, event | category | flops | bytes accessed | tf_op | source)
XLA Modules:
  0.0 224.4 jit_solution(2227177089988234533)
XLA Ops:
  0.0 1.1 slice_bitcast_fusion
  1.1 0.1 fusion.27
  1.2 4.9 %collective-permute-start = (bf16[384,384]{1,0:T(8,128)(2,1)S(1)}, bf16[384,384]{1,0:T(8,128)(2,1)S(1)}, u32[]{:S(2)}, u32[]{:S(2)}) collective-permute-start(bf16[384,384]{1,0:T(8,128)(2,1)S(1)} %pad_maximum_fusion.2), channel_id=1, source_target_pairs={{0,1},{1,2},{2,3},{3,4},{4,5},{5,6},{6,7},{7,8},{8,9},{9,10},{10,1... | collective-permute-start | bytes 884744 | tf_op jit(solution)/shard_map/ppermute | solution.py:18
  6.1 0.7 pad_add_fusion.place_ref
  6.8 13.5 %stem.2 = (bf16[32,2,24,384]{3,2,1,0:T(8,128)(2,1)}, bf16[4,384,384]{2,1,0:T(8,128)(2,1)}, bf16[384,256]{1,0:T(8,128)(2,1)}, bf16[192,512]{1,0:T(8,128)(2,1)}, b...) custom-call(s32[3]{0:T(128)} %pad_add_fusion.place_ref, bf16[24,384,768]{2,1,0:T(8,128)(2,1)} %above_ref.3, ...), custom_call_target="tpu_custom_call" | custom-call | flops 8078229504 | bytes 4608000 | tf_op jit(solution)/shard_map/stem/pallas_call | solution.py:446
  20.3 0.0 collective-permute-done.refs_4_
  20.3 0.0 copy-start.7
  20.3 4.9 %all-to-all-start = ((bf16[32,2,24,384]{3,2,1,0:T(8,128)(2,1)}), bf16[32,2,24,384]{3,2,1,0:T(8,128)(2,1)S(1)}, u32[]{:S(2)}, u32[]{:S(2)}) async-start(bf16[32,2,24,384]{3,2,1,0:T(8,128)(2,1)} %get-tuple-element.26), calls=%async_computation | async-start | bytes 2359296 | tf_op jit(solution)/shard_map/all_to_all | solution.py:759
  25.2 0.0 copy-done.7
  25.3 20.4 %stem.3 = (bf16[32,4,24,384]{3,2,1,0:T(8,128)(2,1)}, bf16[8,384,384]{2,1,0:T(8,128)(2,1)}) custom-call(s32[3]{0:T(128)} %pad_add_fusion.place_ref, bf16[24,384,768]{2,1,0:T(8,128)(2,1)} %above_ref.3, bf16[24,384,768]{2,1,0:T(8,128)(2,1)} %above_ref.3, bf16[384,256]{1,0:T(8,128)(2,1)} %get-tuple-element.27.refs_0_, ...), custom_call_target="tpu_custom_call" | custom-call | flops 16156459008 | bytes 9216000 | tf_op jit(solution)/shard_map/stem/pallas_call | solution.py:446
  45.6 8.7 %all-to-all-done = bf16[32,2,24,384]{3,2,1,0:T(8,128)(2,1)S(1)} async-done(((bf16[32,2,24,384]{3,2,1,0:T(8,128)(2,1)}), bf16[32,2,24,384]{3,2,1,0:T(8,128)(2,1)S(1)}, u32[]{:S(2)}, u32[]{:S(2)}) %all-to-all-start) | async-done | bytes 1179680 | tf_op jit(solution)/shard_map/all_to_all | solution.py:759
  54.3 0.0 copy-start.1
  54.3 1.0 copy-done.1
  55.4 3.9 %all-to-all-start.1 = ((bf16[32,4,24,384]{3,2,1,0:T(8,128)(2,1)}), bf16[32,4,24,384]{3,2,1,0:T(8,128)(2,1)}, u32[]{:S(2)}, u32[]{:S(2)}) async-start(bf16[32,4,24,384]{3,2,1,0:T(8,128)(2,1)} %get-tuple-element.32), calls=%async_computation.1 | async-start | bytes 4718592 | tf_op jit(solution)/shard_map/all_to_all | solution.py:759
  59.3 0.0 copy-start.6
  59.4 2.3 %fusion.22 = bf16[384,384]{1,0:T(8,128)(2,1)S(1)} fusion(), kind=kLoop, calls=%fused_computation.47 | loop fusion | flops 1916928 | bytes 294912 | tf_op jit(solution)/shard_map/neg | solution.py:587
  61.7 1.0 fusion.12.turn_u_ref
  62.7 2.5 %sine_convert_fusion.1 = (bf16[384,384]{1,0:T(8,128)(2,1)S(1)}, bf16[384,384]{1,0:T(8,128)(2,1)S(1)}) fusion(), kind=kLoop, calls=%fused_computation.19 | loop fusion | flops 1622016 | bytes 589824 | tf_op jit(solution)/shard_map/convert_element_type | solution.py:26
  65.3 0.1 slice_multiply_fusion
  65.4 0.8 pad_maximum_fusion.1.refs_6_
  66.2 0.0 copy-start.3
  66.2 2.0 constant_dynamic-update-slice_fusion.1
  68.2 0.0 copy-done.6
  68.2 0.0 copy-done.3
  68.2 0.2 constant_dynamic-update-slice_fusion
  68.5 1.4 constant_dynamic-slice_fusion.2
  69.9 0.0 copy-start.5
  69.9 0.0 collective-permute-start.1
  70.0 0.8 pad_maximum_fusion.refs_3_
  70.7 0.0 slice-start
  70.7 1.1 maximum_maximum_fusion.1.refs_5_
  71.9 0.0 copy-done.5
  71.9 2.3 %fusion.23 = bf16[384,384]{1,0:T(8,128)(2,1)S(1)} fusion(s32[384]{0:T(512)S(1)} %copy-done.5), kind=kLoop, calls=%fused_computation.48 | loop fusion | flops 1916928 | bytes 296448 | tf_op jit(solution)/shard_map/neg | solution.py:584
  74.2 2.5 %sine_convert_fusion = (bf16[384,384]{1,0:T(8,128)(2,1)S(1)}, bf16[384,384]{1,0:T(8,128)(2,1)S(1)}) fusion(s32[384]{0:T(512)S(1)} %copy-done.5), kind=kLoop, calls=%fused_computation.14 | loop fusion | flops 1622016 | bytes 591360 | tf_op jit(solution)/shard_map/convert_element_type | solution.py:26
  76.7 1.1 maximum_maximum_fusion.refs_4_
  77.9 0.0 slice-done
  77.9 0.9 fusion.19.turn_w_ref
  78.8 15.1 %symmetric_filter.1.refs_2_ = f32[12,2,384,256]{3,2,1,0:T(8,128)} custom-call(s32[1]{0:T(128)} %bitcast.12.place_ref, bf16[24,2,384,384]{3,2,1,0:T(8,128)(2,1)} %f_ref.1, bf16[384,256]{1,0:T(8,128)(2,1)} %fusion.19.turn_w_ref, bf16[384,384]{1,0:T(8,128)(2,1)} %fusion.12.turn_u_ref), custom_call_target="tpu_custom_call" | custom-call | flops 3623878656 | bytes 16515072 | tf_op jit(solution)/shard_map/symmetric_filter/pallas_call | solution.py:489
  93.9 0.0 collective-permute-done.1
  93.9 2.3 %broadcast_select_fusion.1 = (bf16[12,192,384]{2,1,0:T(8,128)(2,1)S(1)}, bf16[12,192,384]{2,1,0:T(8,128)(2,1)S(1)}) fusion(bf16[12,192,384]{2,1,0:T(8,128)(2,1)} %collective-permute-done.1, pred[]{:T(512)S(6)} %eq.41, bf16[12,384,384]{2,1,0:T(8,128)(2,1)S(1)} %constant_dynamic-update-slice_fusion, s32[]{:T(128)S(6)} %select_n.70), kind=kLoop, calls=%fused_computation.2 | loop fusion | flops 1769472 | bytes 7077893 | tf_op jit(solution)/shard_map/jit(_where)/select_n | solution.py:774
  96.2 0.4 maximum_bitcast_fusion
  96.6 4.0 %copy.12 = bf16[192,24,384]{2,1,0:T(8,128)(2,1)} copy(bf16[192,24,384]{2,0,1:T(8,128)(2,1)S(1)} %maximum_bitcast_fusion) | data formatting | bytes 7077888 | tf_op jit(solution)/shard_map/transpose | solution.py:776
  100.6 13.1 %all-to-all-done.1 = bf16[32,4,24,384]{3,2,1,0:T(8,128)(2,1)} async-done(((bf16[32,4,24,384]{3,2,1,0:T(8,128)(2,1)}), bf16[32,4,24,384]{3,2,1,0:T(8,128)(2,1)}, u32[]{:S(2)}, u32[]{:S(2)}) %all-to-all-start.1) | async-done | bytes 2359328 | tf_op jit(solution)/shard_map/all_to_all | solution.py:759
  113.7 6.9 %spectral_filter.3 = bf16[768,384]{1,0:T(8,128)(2,1)} custom-call(bf16[1536,384]{1,0:T(8,128)(2,1)} %bitcast.20, bf16[3072,384]{1,0:T(8,128)(2,1)} %bitcast.9.refs_1_, f32[12,2,384,256]{3,2,1,0:T(8,128)} %symmetric_filter.1.refs_2_, bf16[384,512]{1,0:T(8,128)(2,1)} %pad_maximum_fusion.refs_3_, bf16[768,768]{1,0:T(8,128)(2,1)} %maximum_maximum_fusion.refs_4_, ...), custom_call_target="tpu_custom_call" | custom-call | flops 1811939328 | bytes 2359296 | tf_op jit(solution)/shard_map/spectral_filter/pallas_call | solution.py:611
  120.6 4.2 %all-to-all-start.3 = ((bf16[32,24,384]{2,1,0:T(8,128)(2,1)}), bf16[32,24,384]{2,1,0:T(8,128)(2,1)S(1)}, u32[]{:S(2)}, u32[]{:S(2)}) async-start(bf16[32,24,384]{2,1,0:T(8,128)(2,1)} %bitcast.23), calls=%async_computation.3 | async-start | bytes 1179648 | tf_op jit(solution)/shard_map/all_to_all | solution.py:787
  124.8 18.0 %spectral_filter.2 = bf16[3840,384]{1,0:T(8,128)(2,1)} custom-call(bf16[1536,384]{1,0:T(8,128)(2,1)} %bitcast.21, bf16[3072,384]{1,0:T(8,128)(2,1)} %bitcast.9.refs_1_, f32[12,2,384,256]{3,2,1,0:T(8,128)} %symmetric_filter.1.refs_2_, bf16[384,512]{1,0:T(8,128)(2,1)} %pad_maximum_fusion.refs_3_, bf16[768,768]{1,0:T(8,128)(2,1)} %maximum_maximum_fusion.refs_4_, ...), custom_call_target="tpu_custom_call" | custom-call | flops 9059696640 | bytes 11796480 | tf_op jit(solution)/shard_map/spectral_filter/pallas_call | solution.py:611
  142.8 0.0 all-to-all-done.3.kept_ref
  142.8 0.0 copy-start.2
  142.8 5.6 %all-to-all-start.2 = ((bf16[32,120,384]{2,1,0:T(8,128)(2,1)}), bf16[32,120,384]{2,1,0:T(8,128)(2,1)S(1)}, u32[]{:S(2)}, u32[]{:S(2)}) async-start(bf16[32,120,384]{2,1,0:T(8,128)(2,1)} %bitcast.22), calls=%async_computation.2 | async-start | bytes 5898240 | tf_op jit(solution)/shard_map/all_to_all | solution.py:787
  148.5 0.0 copy-done.2
  148.5 0.3 collective-permute-start.2
  148.9 1.3 collective-permute-done.2.other_ref
  150.2 0.0 copy-start.4
  150.2 0.7 copy-done.4
  150.9 3.4 %residual.2.refs_0_ = bf16[16,12,24,384]{3,2,1,0:T(8,128)(2,1)} custom-call(s32[1]{0:T(128)} %bitcast.place_ref, bf16[32,24,384]{2,1,0:T(8,128)(2,1)} %copy-done.2, bf16[16,24,384]{2,1,0:T(8,128)(2,1)} %copy-done.4, bf16[16,12,24,384]{3,2,1,0:T(8,128)(2,1)} %bitcast.18), custom_call_target="tpu_custom_call" | custom-call | flops 294912 | bytes 2359296 | tf_op jit(solution)/shard_map/residual/pallas_call | solution.py:672
  154.3 61.4 %all-to-all-done.2.kept_ref = bf16[32,120,384]{2,1,0:T(8,128)(2,1)S(1)} async-done(((bf16[32,120,384]{2,1,0:T(8,128)(2,1)}), bf16[32,120,384]{2,1,0:T(8,128)(2,1)S(1)}, u32[]{:S(2)}, u32[]{:S(2)}) %all-to-all-start.2) | async-done | bytes 2949152 | tf_op jit(solution)/shard_map/all_to_all | solution.py:787
  215.7 0.0 copy-start
  215.7 0.1 constant_dynamic-slice_fusion
  215.9 0.1 collective-permute-start.3
  216.0 3.4 %collective-permute-done.3.other_ref = bf16[16,120,384]{2,1,0:T(8,128)(2,1)} collective-permute-done((bf16[16,120,384]{2,1,0:T(8,128)(2,1)S(1)}, bf16[16,120,384]{2,1,0:T(8,128)(2,1)}, u32[]{:S(2)}, u32[]{:S(2)}) %collective-permute-start.3) | collective-permute-done | bytes 1474592 | tf_op jit(solution)/shard_map/ppermute | solution.py:694
  219.3 0.0 copy-done
  219.3 5.1 %residual.3 = bf16[16,12,24,384]{3,2,1,0:T(8,128)(2,1)} custom-call(s32[1]{0:T(128)} %bitcast.place_ref, bf16[32,120,384]{2,1,0:T(8,128)(2,1)} %copy-done, bf16[16,120,384]{2,1,0:T(8,128)(2,1)} %collective-permute-done.3.other_ref, bf16[16,12,24,384]{3,2,1,0:T(8,128)(2,1)} %bitcast.19, ...), custom_call_target="tpu_custom_call", output_to_operand_aliasing={{}: (4, {})} | custom-call | flops 1474560 | bytes 11796480 | tf_op jit(solution)/shard_map/residual/pallas_call | solution.py:672
  (6 shorter events, 0.1 us)
Async XLA Ops:
  1.2 19.1 %collective-permute-start = (bf16[384,384]{1,0:T(8,128)(2,1)S(1)}, bf16[384,384]{1,0:T(8,128)(2,1)S(1)}, u32[]{:S(2)}, u32[]{:S(2)}) collective-permute-start(bf16[384,384]{1,0:T(8,128)(2,1)S(1)} %pad_maximum_fusion.2), channel_id=1, source_target_pairs={{0,1},{1,2},{2,3},{3,4},{4,5},{5,6},{6,7},{7,8},{8,9},{9,10},{10,1... | collective-permute-start | bytes 884744 | tf_op jit(solution)/shard_map/ppermute | solution.py:18
  20.3 4.9 %copy-start.7 = (bf16[384,384]{1,0:T(8,128)(2,1)}, bf16[384,384]{1,0:T(8,128)(2,1)S(1)}, u32[]{:S(2)}) copy-start(bf16[384,384]{1,0:T(8,128)(2,1)S(1)} %collective-permute-done.refs_4_) | copy-start | bytes 884740
  20.3 34.0 %all-to-all-start = ((bf16[32,2,24,384]{3,2,1,0:T(8,128)(2,1)}), bf16[32,2,24,384]{3,2,1,0:T(8,128)(2,1)S(1)}, u32[]{:S(2)}, u32[]{:S(2)}) async-start(bf16[32,2,24,384]{3,2,1,0:T(8,128)(2,1)} %get-tuple-element.26), calls=%async_computation | async-start | bytes 2359296 | tf_op jit(solution)/shard_map/all_to_all | solution.py:759
  54.3 1.0 copy-start.1
  55.4 58.4 %all-to-all-start.1 = ((bf16[32,4,24,384]{3,2,1,0:T(8,128)(2,1)}), bf16[32,4,24,384]{3,2,1,0:T(8,128)(2,1)}, u32[]{:S(2)}, u32[]{:S(2)}) async-start(bf16[32,4,24,384]{3,2,1,0:T(8,128)(2,1)} %get-tuple-element.32), calls=%async_computation.1 | async-start | bytes 4718592 | tf_op jit(solution)/shard_map/all_to_all | solution.py:759
  59.3 8.9 %copy-start.6 = (s32[384]{0:T(512)}, s32[384]{0:T(512)S(1)}, u32[]{:S(2)}) copy-start(s32[384]{0:T(512)S(1)} %iota.31) | copy-start | bytes 4612
  66.2 2.0 copy-start.3
  69.9 2.0 copy-start.5
  69.9 24.0 %collective-permute-start.1 = (bf16[12,192,384]{2,1,0:T(8,128)(2,1)}, bf16[12,192,384]{2,1,0:T(8,128)(2,1)}, u32[]{:S(2)}, u32[]{:S(2)}) collective-permute-start(bf16[12,192,384]{2,1,0:T(8,128)(2,1)} %constant_dynamic-slice_fusion.2), channel_id=1, source_target_pairs={{0,16},{16,0},{1,17},{17,1},{2,18},{18,2},{3,19},{19,3},{4,20},{20... | collective-permute-start | bytes 5308424 | tf_op jit(solution)/shard_map/ppermute | solution.py:694
  70.7 7.1 %slice-start = ((s32[384]{0:T(512)}), s32[256]{0:T(256)S(1)}, s32[]{:S(2)}) async-start(s32[384]{0:T(512)} %copy-done.6), calls=%async_computation.4 | async-start | bytes 2048 | tf_op jit(solution)/shard_map/slice | solution.py:488
  120.6 22.2 %all-to-all-start.3 = ((bf16[32,24,384]{2,1,0:T(8,128)(2,1)}), bf16[32,24,384]{2,1,0:T(8,128)(2,1)S(1)}, u32[]{:S(2)}, u32[]{:S(2)}) async-start(bf16[32,24,384]{2,1,0:T(8,128)(2,1)} %bitcast.23), calls=%async_computation.3 | async-start | bytes 1179648 | tf_op jit(solution)/shard_map/all_to_all | solution.py:787
  142.8 5.6 %copy-start.2 = (bf16[32,24,384]{2,1,0:T(8,128)(2,1)}, bf16[32,24,384]{2,1,0:T(8,128)(2,1)S(1)}, u32[]{:S(2)}) copy-start(bf16[32,24,384]{2,1,0:T(8,128)(2,1)S(1)} %all-to-all-done.3.kept_ref) | copy-start | bytes 1769476
  142.8 72.9 %all-to-all-start.2 = ((bf16[32,120,384]{2,1,0:T(8,128)(2,1)}), bf16[32,120,384]{2,1,0:T(8,128)(2,1)S(1)}, u32[]{:S(2)}, u32[]{:S(2)}) async-start(bf16[32,120,384]{2,1,0:T(8,128)(2,1)} %bitcast.22), calls=%async_computation.2 | async-start | bytes 5898240 | tf_op jit(solution)/shard_map/all_to_all | solution.py:787
  148.5 1.6 collective-permute-start.2
  150.2 0.7 copy-start.4
  215.7 3.6 %copy-start = (bf16[32,120,384]{2,1,0:T(8,128)(2,1)}, bf16[32,120,384]{2,1,0:T(8,128)(2,1)S(1)}, u32[]{:S(2)}) copy-start(bf16[32,120,384]{2,1,0:T(8,128)(2,1)S(1)} %all-to-all-done.2.kept_ref) | copy-start | bytes 8847364
  215.9 3.5 %collective-permute-start.3 = (bf16[16,120,384]{2,1,0:T(8,128)(2,1)S(1)}, bf16[16,120,384]{2,1,0:T(8,128)(2,1)}, u32[]{:S(2)}, u32[]{:S(2)}) collective-permute-start(bf16[16,120,384]{2,1,0:T(8,128)(2,1)S(1)} %constant_dynamic-slice_fusion), channel_id=1, source_target_pairs={{0,16},{16,0},{1,17},{17,1},{2,18},{18,2},{3,19},{19,3},{4,20},{20... | collective-permute-start | bytes 4423688 | tf_op jit(solution)/shard_map/ppermute | solution.py:694

commit v5 on v4

--- a/solution.py
+++ b/solution.py
@@ -299,12 +299,8 @@
 
 
 def stem_kernel(kind, place_ref, x_ref, above_ref, *refs):
-    if kind == "first":
-        sources = refs[:7]
-        normed_ref, feat_ref, w1_ref, w2_ref, w3_ref, gain_ref, field = refs[7:]
-    else:
-        w1_ref, w2_ref, w3_ref, gain_ref = refs[:4]
-        normed_ref, feat_ref, field = refs[-3:]
+    sources = refs[:7]
+    normed_ref, feat_ref, w1_ref, w2_ref, w3_ref, gain_ref, field = refs[-7:]
     step = pl.program_id(0)
     rows, cols, depth = x_ref.shape
     bands = depth // 256
@@ -313,11 +309,9 @@
     group = normed_ref.shape[2] // rows
     cells = rows * cols
 
-    if kind == "first":
-
-        @pl.when(step == 0)
-        def _():
-            build_weights(sources, (w1_ref, w2_ref, w3_ref, gain_ref))
+    @pl.when(step == 0)
+    def _():
+        build_weights(sources, (w1_ref, w2_ref, w3_ref, gain_ref))
 
     w1 = w1_ref[...]
     w2 = w2_ref[...]
@@ -359,7 +353,7 @@
         keep = 1.0
         if kind == "last":
             keep = place_ref[1].astype(jnp.float32)
-            above = jnp.where(place_ref[2] > 0, refs[4][...], above)
+            above = jnp.where(place_ref[2] > 0, refs[7][...], above)
         turned = above.T
         upper, lower = (
             layer_one(turned, [128 * b + 64 * a for b in range(bands)]) for a in range(2)
@@ -419,7 +413,7 @@
 def stem(kind, image, place, weights, first, steps, devices, extra=()):
     cols, depth = image.shape[1:]
     rows = 2 * steps
-    shapes = weight_shapes(weights) if kind == "first" else weights
+    shapes = weight_shapes(weights)
     channels, third_depth = shapes[2].shape
     merged = shapes[1].shape[0]
     group = channels // devices
@@ -437,11 +431,7 @@
         jax.ShapeDtypeStruct((devices, steps, 2 * group, cols), jnp.bfloat16),
         jax.ShapeDtypeStruct((rows, channels, cols), jnp.bfloat16),
     ]
-    if kind == "first":
-        out_specs += [whole(a) for a in shapes]
-        out_shape += shapes
-    if kind == "last":
-        in_specs += [whole(extra[0])]
+    in_specs += [whole(a) for a in extra]
     macs = rows * cols * (16 * 208 * 96 + 4 * 400 * merged + third_depth * channels)
     return pl.pallas_call(
         functools.partial(stem_kernel, kind),
@@ -457,7 +447,8 @@
             ]
             + in_specs,
             out_specs=out_specs,
-            scratch_shapes=[pltpu.VMEM((third_depth, 2 * cols), jnp.bfloat16)],
+            scratch_shapes=[pltpu.VMEM(a.shape, a.dtype) for a in shapes]
+            + [pltpu.VMEM((third_depth, 2 * cols), jnp.bfloat16)],
         ),
         out_shape=out_shape,
         compiler_params=pltpu.CompilerParams(vmem_limit_bytes=VMEM_BYTES),
@@ -477,7 +468,8 @@
             turn_u_ref[...], across.astype(jnp.bfloat16), preferred_element_type=jnp.float32
         )
         own = block[:, :width].astype(jnp.float32)
-        g_ref[0, part] = 0.5 * (own + turned if part == 0 else own - turned)
+        both = own + turned if part == 0 else own - turned
+        g_ref[0, part] = (0.5 * both).astype(jnp.bfloat16)
 
 
 def symmetric_filter(spectral_filter, place, group, width):
@@ -500,7 +492,7 @@
             ],
             out_specs=pl.BlockSpec((1, 2, full_rows, width), lambda i, place: (i, 0, 0, 0)),
         ),
-        out_shape=jax.ShapeDtypeStruct((group, 2, full_rows, width), jnp.float32),
+        out_shape=jax.ShapeDtypeStruct((group, 2, full_rows, width), jnp.bfloat16),
         compiler_params=pltpu.CompilerParams(vmem_limit_bytes=VMEM_BYTES),
         cost_estimate=pl.CostEstimate(
             flops=8 * group * full_rows * full_cols * width,
@@ -520,65 +512,140 @@
     return jnp.concatenate([source[j, rows, :] for j in range(source.shape[0])], axis=1)
 
 
+RADIX = 3
+HALF_ROOT = math.sqrt(3.0) / 2.0
+
+
+def repack_kernel(devices, early_ref, out_ref, held):
+    group, length = out_ref.shape[:2]
+    rows = length // devices
+    to_lane_tiles(held, slice(None), early_ref[...].astype(jnp.float32))
+    for k in range(group):
+        for r in range(rows):
+            values = from_lane_tiles(held, pl.ds(r * group + k, devices, stride=rows * group))
+            out_ref[k, r * devices : (r + 1) * devices] = values.astype(jnp.bfloat16)
+
+
+def repack(early, group, devices):
+    length, cols = early.shape
+    return pl.pallas_call(
+        functools.partial(repack_kernel, devices),
+        out_shape=jax.ShapeDtypeStruct((group, length // group, cols), jnp.bfloat16),
+        scratch_shapes=[pltpu.VMEM((cols // 128, length, 128), jnp.float32)],
+        compiler_params=pltpu.CompilerParams(vmem_limit_bytes=VMEM_BYTES // 4),
+        cost_estimate=pl.CostEstimate(
+            flops=length * cols, bytes_accessed=4 * length * cols, transcendentals=0
+        ),
+        name="repack",
+    )(early)
+
+
+def thirds(values, sign):
+    (re0, im0), (re1, im1), (re2, im2) = values
+    sum_re, sum_im = re1 + re2, im1 + im2
+    turn_re, turn_im = HALF_ROOT * sign * (im1 - im2), HALF_ROOT * sign * (re2 - re1)
+    rest_re, rest_im = re0 - 0.5 * sum_re, im0 - 0.5 * sum_im
+    return (
+        (re0 + sum_re, im0 + sum_im),
+        (rest_re + turn_re, rest_im + turn_im),
+        (rest_re - turn_re, rest_im - turn_im),
+    )
+
+
 def filter_kernel(
-    first, norm_scale, *refs
+    first, devices, norm_scale, late_ref, early_ref, g_ref, row_table_ref, fwd_ref, inv_ref,
+    back_ref, twiddle_ref, out_ref, held, made,
 ):
-    *pieces, g_ref, row_table_ref, fwd_ref, inv_ref, back_ref, out_ref, held, made = refs
     step = pl.program_id(0)
-    full_rows = fwd_ref.shape[0] // 2
+    third = fwd_ref.shape[0] // 2
+    full_rows = RADIX * third
     width = g_ref.shape[3]
-    group = held.shape[1] // full_rows
     count = made.shape[1] // full_rows
     per_step = g_ref.shape[0]
+    early = early_ref.shape[1] // devices
+    late = full_rows // devices - early
+    group = held.shape[1] // (late * devices)
 
     @pl.when(step == 0)
     def _():
-        begin = 0
-        for piece in pieces:
-            end = begin + piece.shape[0]
-            to_lane_tiles(held, slice(begin, end), piece[...].astype(jnp.float32))
-            begin = end
-
-    blocks = []
+        to_lane_tiles(held, slice(None), late_ref[...].astype(jnp.float32))
+
+    def source_rows(k, row):
+        if row >= late:
+            begin = (row - late) * devices
+            return early_ref[k, begin : begin + devices]
+        begin = row * group + first + step * per_step + k
+        values = from_lane_tiles(held, pl.ds(begin, devices, stride=late * group))
+        return values.astype(jnp.bfloat16)
+
+    def twiddles(r):
+        cos, sin = twiddle_ref[2 * r - 2], twiddle_ref[2 * r - 1]
+        times = per_step * width // 128
+        return jnp.concatenate([cos] * times, axis=1), jnp.concatenate([sin] * times, axis=1)
+
+    fields = []
     for k in range(per_step):
-        rows = pl.ds(first + step * per_step + k, full_rows, stride=group)
-        field = from_lane_tiles(held, rows)
+        rows = [
+            source_rows(k, r + RADIX * q)
+            for r in range(RADIX)
+            for q in range((late + early) // RADIX)
+        ]
         spread = jnp.dot(
-            field.astype(jnp.bfloat16), row_table_ref[...], preferred_element_type=jnp.float32
-        ).astype(jnp.bfloat16)
-        blocks.append(jnp.concatenate([spread[:, :width], spread[:, width:]], axis=0))
-    spectrum = jnp.dot(
-        fwd_ref[...], jnp.concatenate(blocks, axis=1), preferred_element_type=jnp.float32
-    )
-    blocks = []
-    for k in range(per_step):
-        real = spectrum[:full_rows, k * width : (k + 1) * width]
-        imag = spectrum[full_rows:, k * width : (k + 1) * width]
-        g_real = g_ref[k, 0]
-        g_imag = g_ref[k, 1]
-        blocks.append(
-            jnp.concatenate(
-                [g_real * real - g_imag * imag, g_real * imag + g_imag * real], axis=0
-            ).astype(jnp.bfloat16)
-        )
-    back = jnp.dot(
-        inv_ref[...], jnp.concatenate(blocks, axis=1), preferred_element_type=jnp.float32
-    ).astype(jnp.bfloat16)
-    for k in range(per_step):
-        lanes = slice(k * width, (k + 1) * width)
-        both = jnp.concatenate([back[:full_rows, lanes], back[full_rows:, lanes]], axis=1)
-        result = jnp.dot(both, back_ref[...], preferred_element_type=jnp.float32)
-        rows = pl.ds(step * per_step + k, full_rows, stride=count)
-        to_lane_tiles(made, rows, result * norm_scale)
+            jnp.concatenate(rows, axis=0), row_table_ref[...], preferred_element_type=jnp.float32
+        )
+        fields.append(spread.astype(jnp.bfloat16))
+    parts = []
+    for r in range(RADIX):
+        span = slice(r * third, (r + 1) * third)
+        block = jnp.concatenate(
+            [
+                jnp.concatenate([f[span, :width], f[span, width:]], axis=0)
+                for f in fields
+            ],
+            axis=1,
+        )
+        short = jnp.dot(fwd_ref[...], block, preferred_element_type=jnp.float32)
+        real, imag = short[:third], short[third:]
+        if r > 0:
+            cos, sin = twiddles(r)
+            real, imag = real * cos + imag * sin, imag * cos - real * sin
+        parts.append((real, imag))
+    weighted = []
+    for r, (real, imag) in enumerate(thirds(parts, 1.0)):
+        span = slice(r * third, (r + 1) * third)
+        g_real, g_imag = (
+            jnp.concatenate([g_ref[k, p, span] for k in range(per_step)], axis=1).astype(
+                jnp.float32
+            )
+            for p in range(2)
+        )
+        weighted.append((g_real * real - g_imag * imag, g_real * imag + g_imag * real))
+    for r, (real, imag) in enumerate(thirds(weighted, -1.0)):
+        if r > 0:
+            cos, sin = twiddles(r)
+            real, imag = real * cos - imag * sin, imag * cos + real * sin
+        block = jnp.concatenate([real, imag], axis=0).astype(jnp.bfloat16)
+        back = jnp.dot(inv_ref[...], block, preferred_element_type=jnp.float32).astype(
+            jnp.bfloat16
+        )
+        for k in range(per_step):
+            lanes = slice(k * width, (k + 1) * width)
+            both = jnp.concatenate([back[:third, lanes], back[third:, lanes]], axis=1)
+            result = jnp.dot(both, back_ref[...], preferred_element_type=jnp.float32)
+            rows = pl.ds(r * count + step * per_step + k, third, stride=RADIX * count)
+            to_lane_tiles(made, rows, result * norm_scale)
 
     @pl.when(step == pl.num_programs(0) - 1)
     def _():
         out_ref[...] = from_lane_tiles(made, slice(None)).astype(jnp.bfloat16)
 
 
-def filter_tables(full_rows, field_cols, width, row_order):
-    cos_h, sin_h = fourier_tables(full_rows)
-    cos_f, sin_f = fourier_tables(full_rows, row_order)
+def filter_tables(full_rows, field_cols, width, devices):
+    third = full_rows // RADIX
+    per_device = third // devices
+    order = (per_device * np.arange(devices)[None, :] + np.arange(per_device)[:, None]).reshape(-1)
+    cos_h, sin_h = fourier_tables(third)
+    cos_f, sin_f = fourier_tables(third, order.astype(np.int32))
     cos_w, sin_w = fourier_tables(field_cols)
     fwd = jnp.concatenate(
         [jnp.concatenate([cos_f, sin_f], 1), jnp.concatenate([-sin_f, cos_f], 1)], 0
@@ -594,37 +661,37 @@
     back_table = jnp.concatenate(
         [cos_w[:width] * times[:, None], -sin_w[:width] * times[:, None]], 0
     )
-    return row_table, fwd, inv, back_table
-
-
-def filter_channels(pieces, symmetric, tables, first, count, per_step, devices):
-    row_table, fwd, inv, back_table = tables
-    full_rows = fwd.shape[0] // 2
-    cols = pieces[0].shape[1]
-    group = sum(piece.shape[0] for piece in pieces) // full_rows
-    width = symmetric.shape[3]
+    turns = jnp.arange(1, RADIX)[:, None] * jnp.arange(third)[None, :]
+    angles = turns.astype(jnp.float32) * (2.0 * math.pi / full_rows)
+    twiddle = jnp.stack([jnp.cos(angles), jnp.sin(angles)], axis=1)
+    twiddle = jnp.broadcast_to(twiddle.reshape(-1, third, 1), (2 * RADIX - 2, third, 128))
+    return row_table, fwd, inv, back_table, twiddle
+
+
+def filter_channels(late, early, symmetric, tables, first, count, per_step, devices):
+    full_rows, width = symmetric.shape[2:]
+    group, early_rows = early.shape[:2]
+    cols = late.shape[1]
 
     def whole(array):
         return pl.BlockSpec(array.shape, lambda i: (0,) * array.ndim)
 
-    macs = count * (2 * 4 * full_rows * full_rows * width + 4 * full_rows * cols * width)
+    macs = count * (4 * full_rows * full_rows * width + 4 * full_rows * cols * width)
     made = pl.pallas_call(
-        functools.partial(filter_kernel, first, 1.0 / (full_rows * cols)),
+        functools.partial(filter_kernel, first, devices, 1.0 / (full_rows * cols)),
         grid=(count // per_step,),
         in_specs=[
-            *[whole(piece) for piece in pieces],
+            whole(late),
+            pl.BlockSpec((per_step, early_rows, cols), lambda i: (first // per_step + i, 0, 0)),
             pl.BlockSpec(
                 (per_step, 2, full_rows, width), lambda i: (first // per_step + i, 0, 0, 0)
             ),
-            whole(row_table),
-            whole(fwd),
-            whole(inv),
-            whole(back_table),
-        ],
+        ]
+        + [whole(table) for table in tables],
         out_specs=pl.BlockSpec((full_rows * count, cols), lambda i: (0, 0)),
         out_shape=jax.ShapeDtypeStruct((full_rows * count, cols), jnp.bfloat16),
         scratch_shapes=[
-            pltpu.VMEM((cols // 128, full_rows * group, 128), jnp.float32),
+            pltpu.VMEM((cols // 128, late.shape[0], 128), jnp.float32),
             pltpu.VMEM((cols // 128, full_rows * count, 128), jnp.float32),
         ],
         compiler_params=pltpu.CompilerParams(vmem_limit_bytes=VMEM_BYTES),
@@ -632,7 +699,7 @@
             flops=2 * macs, bytes_accessed=count * full_rows * cols * 8, transcendentals=0
         ),
         name="spectral_filter",
-    )(*pieces, symmetric, row_table, fwd, inv, back_table)
+    )(late, early, symmetric, *tables)
     return made.reshape(devices, full_rows // devices * count, cols)
 
 
@@ -711,12 +778,15 @@
     full_rows = spectral_filter.shape[2]
     sections = lax.axis_size("section")
     devices = sections * lax.axis_size("tile")
+    rows = tile_rows // 2
     suits = (
         sections == 2
         and tile_rows % 8 == 0
         and tile_rows >= 16
         and field_cols % 128 == 0
-        and full_rows % 128 == 0
+        and full_rows % (128 * RADIX) == 0
+        and rows % RADIX == 0
+        and devices % 8 == 0
         and tile_channels % 8 == 0
     )
     arguments = (
@@ -734,7 +804,6 @@
         return general_local(*arguments)
     section = lax.axis_index("section")
     tile = lax.axis_index("tile")
-    rows = tile_rows // 2
     group = tile_channels // 2
     half_channels = channels // 2
     width = -(-(field_cols // 2 + 1) // 128) * 128
@@ -746,27 +815,26 @@
     pairs = rows // 2
     early = max(pairs // 3, 1)
     late = pairs - early
-    normed_early, feat_early, *weights = stem(
+    normed_early, feat_early = stem(
         "first", aerial_patch_grid, place, sources, late, early, devices
     )
     normed_early, arriving = lax.optimization_barrier((normed_early, arriving))
     normed_late, feat_late = stem(
-        "last", aerial_patch_grid, place, weights, 0, late, devices, (arriving,)
-    )
-    pieces = []
-    row_order = []
-    for normed, first, count in ((normed_early, late, early), (normed_late, 0, late)):
-        normed = lax.all_to_all(normed, DEVICES, split_axis=0, concat_axis=0, tiled=True)
-        pieces.append(normed.reshape(2 * count * devices * group, field_cols))
-        own_rows = np.arange(2 * first, 2 * (first + count))
-        row_order.append((rows * np.arange(devices)[:, None] + own_rows).reshape(-1))
-    features = [feat_late, feat_early]
-    features = jnp.concatenate(features, axis=0)
-    row_order = np.concatenate(row_order).astype(np.int32)
+        "last", aerial_patch_grid, place, sources, 0, late, devices, (arriving,)
+    )
+    spread = [
+        lax.all_to_all(normed, DEVICES, split_axis=0, concat_axis=0, tiled=True).reshape(
+            -1, field_cols
+        )
+        for normed in (normed_early, normed_late)
+    ]
+    early_fields = repack(spread[0], group, devices)
+    late_fields = spread[1]
+    features = jnp.concatenate([feat_late, feat_early], axis=0)
 
     channel_place = jnp.reshape(section * group, (1,)).astype(jnp.int32)
     symmetric = symmetric_filter(spectral_filter, channel_place, group, width)
-    tables = filter_tables(full_rows, field_cols, width, row_order)
+    tables = filter_tables(full_rows, field_cols, width, devices)
 
     own = lax.dynamic_slice_in_dim(features, section * half_channels, half_channels, 1)
     sent = lax.dynamic_slice_in_dim(features, (1 - section) * half_channels, half_channels, 1)
@@ -775,15 +843,17 @@
     high = jnp.where(section == 0, arrived, own)
     residual = jnp.transpose(jnp.concatenate([low, high], axis=0), (1, 0, 2))
     residual = residual.reshape(half_channels // group, group, tile_rows, field_cols)
-    pieces, residual, symmetric, tables = lax.optimization_barrier(
-        (pieces, residual, symmetric, tables)
+    late_fields, early_fields, residual, symmetric, tables = lax.optimization_barrier(
+        (late_fields, early_fields, residual, symmetric, tables)
     )
 
     section_place = jnp.reshape(section, (1,)).astype(jnp.int32)
     halves = devices // 2
     output = None
     for first, count in ((group - 2, 2), (0, group - 2)):
-        made = filter_channels(pieces, symmetric, tables, first, count, 2, devices)
+        made = filter_channels(
+            late_fields, early_fields, symmetric, tables, first, count, 2, devices
+        )
         returned = lax.all_to_all(made, DEVICES, split_axis=0, concat_axis=0, tiled=True)
         if output is not None:
             returned, output = lax.optimization_barrier((returned, output))

time: 225 us -> 224 us (level)
  other arithmetic: 19.1 us -> 12.7 us
  waiting for transfers between devices: 88 us -> 92.5 us
    all_to_all x2, waiting for transfers between devices: 21.9 us -> 26.3 us  [local(): lax.all_to_all(normed, DEVICES, split_axis=0, concat_axis=0, tiled=True)]
    convert_element_type x2 -> x3, other arithmetic: 5.1 us -> 3.11 us  [fourier_tables(): jnp.sin(angles).astype(jnp.bfloat16)]
    pallas_call x2 -> x3, Pallas kernels: 24.9 us -> 24.5 us  [the longest x2 23.6 us: filter_channels(): pl.pallas_call(functools.partial(filter_kernel, first, devices, 1.0 / (fu...]
  transfers between devices with their start and end apart: 8 -> 8, of which waited for: 5 -> 5; matrix products, arithmetic and copies ran while one was open for 12% -> 9% of each run, Pallas kernels for 31% -> 31%
where the time goes in v5:
time: 224 us; the launch traced here: 223 us
  waiting for transfers between devices  92.5 us (41%)
  Pallas kernels  81 us (36%)
  starting transfers between devices  23.9 us (11%)
  other arithmetic  12.7 us (6%)
  local copies, waits for them, and re-layouts  12.4 us (6%)
    all_to_all x2, waiting for transfers between devices, local(): lax.all_to_all(made, DEVICES, split_axis=0, concat_axis=0, tiled=True)  61.4 us
    pallas_call x2, Pallas kernels, stem(): pl.pallas_call(functools.partial(stem_kernel, kind), grid_spec=pltpu.Pref...  33.8 us
    all_to_all x2, waiting for transfers between devices, local(): lax.all_to_all(normed, DEVICES, split_axis=0, concat_axis=0, tiled=True)  26.3 us
    pallas_call x2, Pallas kernels, filter_channels(): pl.pallas_call(functools.partial(filter_kernel, first, devices, 1.0 / (fu...  23.6 us
    pallas_call x1, Pallas kernels, symmetric_filter(): pl.pallas_call(symmetric_kernel, grid_spec=pltpu.PrefetchScalarGridSpec(n...  14.2 us
    all_to_all x2, starting transfers between devices, local(): lax.all_to_all(made, DEVICES, split_axis=0, concat_axis=0, tiled=True)  9.79 us
    all_to_all x2, starting transfers between devices, local(): lax.all_to_all(normed, DEVICES, split_axis=0, concat_axis=0, tiled=True)  8.75 us
    pallas_call x2, Pallas kernels, add_residual(): pl.pallas_call(functools.partial(residual_kernel, count), grid_spec=pltpu...  8.52 us
  transfers between devices with their start and end apart: 8, of which 5 were waited for; matrix products, arithmetic and copies ran while one was open for 9% of the time, Pallas kernels for 31%

profile of v5, /device:TPU:0, one launch (start us, length us, event | category | flops | bytes accessed | tf_op | source)
XLA Modules:
  0.0 222.7 jit_solution(9049591174605510604)
XLA Ops:
  0.0 1.1 slice_bitcast_fusion
  1.1 0.1 fusion.36
  1.2 4.9 %collective-permute-start = (bf16[384,384]{1,0:T(8,128)(2,1)S(1)}, bf16[384,384]{1,0:T(8,128)(2,1)S(1)}, u32[]{:S(2)}, u32[]{:S(2)}) collective-permute-start(bf16[384,384]{1,0:T(8,128)(2,1)S(1)} %pad_maximum_fusion.2), channel_id=1, source_target_pairs={{0,1},{1,2},{2,3},{3,4},{4,5},{5,6},{6,7},{7,8},{8,9},{9,10},{10,1... | collective-permute-start | bytes 884744 | tf_op jit(solution)/shard_map/ppermute | solution.py:18
  6.1 0.6 pad_add_fusion.place_ref
  6.7 12.9 %stem.2 = (bf16[32,2,24,384]{3,2,1,0:T(8,128)(2,1)}, bf16[4,384,384]{2,1,0:T(8,128)(2,1)}) custom-call(s32[3]{0:T(128)} %pad_add_fusion.place_ref, bf16[24,384,768]{2,1,0:T(8,128)(2,1)} %above_ref.3, bf16[24,384,768]{2,1,0:T(8,128)(2,1)} %above_ref.3, bf16[48,96]{1,0:T(8,128)(2,1)} %bitcast.31, f32[96]{0:T(128)} %refs_1_.3, bf16[384,192]{1,0:T(8,128)(2,1)} %bitcast.29, ...), custom_call_target="tpu_custom_call" | custom-call | flops 8078229504 | bytes 4608000 | tf_op jit(solution)/shard_map/stem/pallas_call | solution.py:436
  19.5 0.0 collective-permute-done.refs_7_
  19.5 0.0 copy-start.9
  19.6 4.9 %all-to-all-start.1 = ((bf16[32,2,24,384]{3,2,1,0:T(8,128)(2,1)}), bf16[32,2,24,384]{3,2,1,0:T(8,128)(2,1)S(1)}, u32[]{:S(2)}, u32[]{:S(2)}) async-start(bf16[32,2,24,384]{3,2,1,0:T(8,128)(2,1)} %get-tuple-element.25), calls=%async_computation.1 | async-start | bytes 2359296 | tf_op jit(solution)/shard_map/all_to_all | solution.py:826
  24.5 0.0 copy-done.9
  24.5 20.9 %stem.3 = (bf16[32,4,24,384]{3,2,1,0:T(8,128)(2,1)}, bf16[8,384,384]{2,1,0:T(8,128)(2,1)}) custom-call(s32[3]{0:T(128)} %pad_add_fusion.place_ref, bf16[24,384,768]{2,1,0:T(8,128)(2,1)} %above_ref.3, bf16[24,384,768]{2,1,0:T(8,128)(2,1)} %above_ref.3, bf16[48,96]{1,0:T(8,128)(2,1)} %bitcast.32, f32[96]{0:T(128)} %refs_1_.3, bf16[384,192]{1,0:T(8,128)(2,1)} %bitcast.30, ...), custom_call_target="tpu_custom_call" | custom-call | flops 16156459008 | bytes 9216000 | tf_op jit(solution)/shard_map/stem/pallas_call | solution.py:436
  45.4 8.2 %all-to-all-done.1 = bf16[32,2,24,384]{3,2,1,0:T(8,128)(2,1)S(1)} async-done(((bf16[32,2,24,384]{3,2,1,0:T(8,128)(2,1)}), bf16[32,2,24,384]{3,2,1,0:T(8,128)(2,1)S(1)}, u32[]{:S(2)}, u32[]{:S(2)}) %all-to-all-start.1) | async-done | bytes 1179680 | tf_op jit(solution)/shard_map/all_to_all | solution.py:826
  53.6 0.0 copy-start.8
  53.6 3.8 %all-to-all-start = ((bf16[32,4,24,384]{3,2,1,0:T(8,128)(2,1)}), bf16[32,4,24,384]{3,2,1,0:T(8,128)(2,1)S(1)}, u32[]{:S(2)}, u32[]{:S(2)}) async-start(bf16[32,4,24,384]{3,2,1,0:T(8,128)(2,1)} %get-tuple-element.24), calls=%async_computation | async-start | bytes 4718592 | tf_op jit(solution)/shard_map/all_to_all | solution.py:826
  57.4 0.0 copy-start.7
  57.5 0.1 fusion.35
  57.6 0.3 fusion.29
  57.9 0.3 sine_convert_fusion.1
  58.1 0.0 copy-done.8
  58.2 0.3 fusion.30
  58.4 0.3 sine_convert_fusion.2
  58.7 0.7 maximum_maximum_fusion.fwd_ref
  59.4 2.0 constant_dynamic-update-slice_fusion.1
  61.4 0.0 copy-done.7
  61.4 0.0 copy-done.5
  61.4 0.2 constant_dynamic-update-slice_fusion
  61.6 0.0 copy-start.2
  61.6 1.7 constant_dynamic-slice_fusion.2
  63.3 0.1 collective-permute-start.1
  63.4 0.7 maximum_maximum_fusion.1.inv_ref
  64.1 1.0 fusion.8.turn_u_ref
  65.1 2.5 %sine_convert_fusion = (bf16[384,384]{1,0:T(8,128)(2,1)S(1)}, bf16[384,384]{1,0:T(8,128)(2,1)S(1)}) fusion(), kind=kLoop, calls=%fused_computation.9 | loop fusion | flops 1622016 | bytes 589824 | tf_op jit(solution)/shard_map/convert_element_type | solution.py:26
  67.7 0.0 copy-done.2
  67.7 0.8 pad_maximum_fusion.row_table_ref
  68.5 0.1 slice_multiply_fusion
  68.6 0.8 pad_maximum_fusion.1.back_ref
  69.4 0.0 slice-done
  69.4 0.9 fusion.14.turn_w_ref
  70.3 14.2 %symmetric_filter.1.g_ref = bf16[12,2,384,256]{3,2,1,0:T(8,128)(2,1)} custom-call(s32[1]{0:T(128)} %bitcast.12.place_ref, bf16[24,2,384,384]{3,2,1,0:T(8,128)(2,1)} %f_ref.1, bf16[384,256]{1,0:T(8,128)(2,1)} %fusion.14.turn_w_ref, bf16[384,384]{1,0:T(8,128)(2,1)} %fusion.8.turn_u_ref), custom_call_target="tpu_custom_call" | custom-call | flops 3623878656 | bytes 16515072 | tf_op jit(solution)/shard_map/symmetric_filter/pallas_call | solution.py:481
  84.5 0.0 collective-permute-done.1
  84.5 2.9 %broadcast_select_fusion.1 = (bf16[12,192,384]{2,1,0:T(8,128)(2,1)S(1)}, bf16[12,192,384]{2,1,0:T(8,128)(2,1)S(1)}) fusion(bf16[12,192,384]{2,1,0:T(8,128)(2,1)} %collective-permute-done.1, pred[]{:T(512)S(6)} %eq.42, bf16[12,384,384]{2,1,0:T(8,128)(2,1)} %copy-done.2, s32[]{:T(128)S(6)} %select_n.72), kind=kLoop, calls=%fused_computation.2 | loop fusion | flops 1769472 | bytes 7077893 | tf_op jit(solution)/shard_map/jit(_where)/select_n | solution.py:842
  87.4 0.4 maximum_bitcast_fusion
  87.8 3.9 %copy.12 = bf16[192,24,384]{2,1,0:T(8,128)(2,1)} copy(bf16[192,24,384]{2,0,1:T(8,128)(2,1)S(1)} %maximum_bitcast_fusion) | data formatting | bytes 7077888 | tf_op jit(solution)/shard_map/transpose | solution.py:844
  91.7 0.9 repack.1.early_ref
  92.6 0.0 copy-start
  92.6 1.0 copy-done
  93.6 18.2 %all-to-all-done = bf16[32,4,24,384]{3,2,1,0:T(8,128)(2,1)S(1)} async-done(((bf16[32,4,24,384]{3,2,1,0:T(8,128)(2,1)}), bf16[32,4,24,384]{3,2,1,0:T(8,128)(2,1)S(1)}, u32[]{:S(2)}, u32[]{:S(2)}) %all-to-all-start) | async-done | bytes 2359328 | tf_op jit(solution)/shard_map/all_to_all | solution.py:826
  111.8 1.0 broadcast_in_dim.15.twiddle_ref
  112.8 0.5 copy-done.3
  113.3 6.2 %spectral_filter.3 = bf16[768,384]{1,0:T(8,128)(2,1)} custom-call(bf16[3072,384]{1,0:T(8,128)(2,1)} %bitcast.22, bf16[12,128,384]{2,1,0:T(8,128)(2,1)} %copy-done, bf16[12,2,384,256]{3,2,1,0:T(8,128)(2,1)} %symmetric_filter.1.g_ref, bf16[384,512]{1,0:T(8,128)(2,1)} %pad_maximum_fusion.row_table_ref, bf16[256,256]{1,0:T(8,128)(2,1)} %maximum_maximum_fusion.fwd_ref, ...), custom_call_target="tpu_custom_call" | custom-call | flops 1207959552 | bytes 2359296 | tf_op jit(solution)/shard_map/spectral_filter/pallas_call | solution.py:680
  119.5 4.2 %all-to-all-start.3 = ((bf16[32,24,384]{2,1,0:T(8,128)(2,1)}), bf16[32,24,384]{2,1,0:T(8,128)(2,1)S(1)}, u32[]{:S(2)}, u32[]{:S(2)}) async-start(bf16[32,24,384]{2,1,0:T(8,128)(2,1)} %bitcast.25), calls=%async_computation.3 | async-start | bytes 1179648 | tf_op jit(solution)/shard_map/all_to_all | solution.py:857
  123.6 17.4 %spectral_filter.2 = bf16[3840,384]{1,0:T(8,128)(2,1)} custom-call(bf16[3072,384]{1,0:T(8,128)(2,1)} %bitcast.23, bf16[12,128,384]{2,1,0:T(8,128)(2,1)} %copy-done, bf16[12,2,384,256]{3,2,1,0:T(8,128)(2,1)} %symmetric_filter.1.g_ref, bf16[384,512]{1,0:T(8,128)(2,1)} %pad_maximum_fusion.row_table_ref, bf16[256,256]{1,0:T(8,128)(2,1)} %maximum_maximum_fusion.fwd_ref, ...), custom_call_target="tpu_custom_call" | custom-call | flops 6039797760 | bytes 11796480 | tf_op jit(solution)/shard_map/spectral_filter/pallas_call | solution.py:680
  141.1 0.0 all-to-all-done.3.kept_ref
  141.1 5.6 %all-to-all-start.2 = ((bf16[32,120,384]{2,1,0:T(8,128)(2,1)}), bf16[32,120,384]{2,1,0:T(8,128)(2,1)S(1)}, u32[]{:S(2)}, u32[]{:S(2)}) async-start(bf16[32,120,384]{2,1,0:T(8,128)(2,1)} %bitcast.24), calls=%async_computation.2 | async-start | bytes 5898240 | tf_op jit(solution)/shard_map/all_to_all | solution.py:857
  146.7 0.0 copy-done.4
  146.8 0.3 collective-permute-start.2
  147.1 1.3 collective-permute-done.2.other_ref
  148.4 0.7 copy-done.6
  149.1 3.4 %residual.2.refs_0_ = bf16[16,12,24,384]{3,2,1,0:T(8,128)(2,1)} custom-call(s32[1]{0:T(128)} %bitcast.place_ref, bf16[32,24,384]{2,1,0:T(8,128)(2,1)} %copy-done.4, bf16[16,24,384]{2,1,0:T(8,128)(2,1)} %copy-done.6, bf16[16,12,24,384]{3,2,1,0:T(8,128)(2,1)} %bitcast.20), custom_call_target="tpu_custom_call" | custom-call | flops 294912 | bytes 2359296 | tf_op jit(solution)/shard_map/residual/pallas_call | solution.py:739
  152.6 61.4 %all-to-all-done.2.kept_ref = bf16[32,120,384]{2,1,0:T(8,128)(2,1)S(1)} async-done(((bf16[32,120,384]{2,1,0:T(8,128)(2,1)}), bf16[32,120,384]{2,1,0:T(8,128)(2,1)S(1)}, u32[]{:S(2)}, u32[]{:S(2)}) %all-to-all-start.2) | async-done | bytes 2949152 | tf_op jit(solution)/shard_map/all_to_all | solution.py:857
  214.0 0.1 constant_dynamic-slice_fusion
  214.1 0.1 collective-permute-start.3
  214.2 3.4 %collective-permute-done.3.other_ref = bf16[16,120,384]{2,1,0:T(8,128)(2,1)} collective-permute-done((bf16[16,120,384]{2,1,0:T(8,128)(2,1)S(1)}, bf16[16,120,384]{2,1,0:T(8,128)(2,1)}, u32[]{:S(2)}, u32[]{:S(2)}) %collective-permute-start.3) | collective-permute-done | bytes 1474592 | tf_op jit(solution)/shard_map/ppermute | solution.py:761
  217.6 0.0 copy-done.1
  217.6 5.1 %residual.3 = bf16[16,12,24,384]{3,2,1,0:T(8,128)(2,1)} custom-call(s32[1]{0:T(128)} %bitcast.place_ref, bf16[32,120,384]{2,1,0:T(8,128)(2,1)} %copy-done.1, bf16[16,120,384]{2,1,0:T(8,128)(2,1)} %collective-permute-done.3.other_ref, bf16[16,12,24,384]{3,2,1,0:T(8,128)(2,1)} %bitcast.21, ...), custom_call_target="tpu_custom_call", output_to_operand_aliasing={{}: (4, {})} | custom-call | flops 1474560 | bytes 11796480 | tf_op jit(solution)/shard_map/residual/pallas_call | solution.py:739
  (14 shorter events, 0.1 us)
Async XLA Ops:
  1.2 18.3 %collective-permute-start = (bf16[384,384]{1,0:T(8,128)(2,1)S(1)}, bf16[384,384]{1,0:T(8,128)(2,1)S(1)}, u32[]{:S(2)}, u32[]{:S(2)}) collective-permute-start(bf16[384,384]{1,0:T(8,128)(2,1)S(1)} %pad_maximum_fusion.2), channel_id=1, source_target_pairs={{0,1},{1,2},{2,3},{3,4},{4,5},{5,6},{6,7},{7,8},{8,9},{9,10},{10,1... | collective-permute-start | bytes 884744 | tf_op jit(solution)/shard_map/ppermute | solution.py:18
  19.5 4.9 %copy-start.9 = (bf16[384,384]{1,0:T(8,128)(2,1)}, bf16[384,384]{1,0:T(8,128)(2,1)S(1)}, u32[]{:S(2)}) copy-start(bf16[384,384]{1,0:T(8,128)(2,1)S(1)} %collective-permute-done.refs_7_) | copy-start | bytes 884740
  19.6 34.0 %all-to-all-start.1 = ((bf16[32,2,24,384]{3,2,1,0:T(8,128)(2,1)}), bf16[32,2,24,384]{3,2,1,0:T(8,128)(2,1)S(1)}, u32[]{:S(2)}, u32[]{:S(2)}) async-start(bf16[32,2,24,384]{3,2,1,0:T(8,128)(2,1)} %get-tuple-element.25), calls=%async_computation.1 | async-start | bytes 2359296 | tf_op jit(solution)/shard_map/all_to_all | solution.py:826
  53.6 4.6 %copy-start.8 = (s32[128]{0:T(128)S(1)}, s32[128]{0:T(128)}, u32[]{:S(2)}) copy-start(s32[128]{0:T(128)} %constant.80.clone) | copy-start | bytes 1540
  53.6 58.3 %all-to-all-start = ((bf16[32,4,24,384]{3,2,1,0:T(8,128)(2,1)}), bf16[32,4,24,384]{3,2,1,0:T(8,128)(2,1)S(1)}, u32[]{:S(2)}, u32[]{:S(2)}) async-start(bf16[32,4,24,384]{3,2,1,0:T(8,128)(2,1)} %get-tuple-element.24), calls=%async_computation | async-start | bytes 4718592 | tf_op jit(solution)/shard_map/all_to_all | solution.py:826
  57.4 4.0 %copy-start.7 = (s32[384]{0:T(512)}, s32[384]{0:T(512)S(1)}, u32[]{:S(2)}) copy-start(s32[384]{0:T(512)S(1)} %iota.51) | copy-start | bytes 4612
  59.4 2.0 copy-start.5
  61.6 6.0 %copy-start.2 = (bf16[12,384,384]{2,1,0:T(8,128)(2,1)}, bf16[12,384,384]{2,1,0:T(8,128)(2,1)S(1)}, u32[]{:S(2)}) copy-start(bf16[12,384,384]{2,1,0:T(8,128)(2,1)S(1)} %constant_dynamic-update-slice_fusion) | copy-start | bytes 10616836
  63.3 6.1 %slice-start = ((s32[384]{0:T(512)}), s32[256]{0:T(256)S(1)}, s32[]{:S(2)}) async-start(s32[384]{0:T(512)} %copy-done.7), calls=%async_computation.4 | async-start | bytes 2048 | tf_op jit(solution)/shard_map/slice | solution.py:480
  63.3 21.2 %collective-permute-start.1 = (bf16[12,192,384]{2,1,0:T(8,128)(2,1)}, bf16[12,192,384]{2,1,0:T(8,128)(2,1)}, u32[]{:S(2)}, u32[]{:S(2)}) collective-permute-start(bf16[12,192,384]{2,1,0:T(8,128)(2,1)} %constant_dynamic-slice_fusion.2), channel_id=1, source_target_pairs={{0,16},{16,0},{1,17},{17,1},{2,18},{18,2},{3,19},{19,3},{4,20},{20... | collective-permute-start | bytes 5308424 | tf_op jit(solution)/shard_map/ppermute | solution.py:761
  92.6 1.0 copy-start
  111.8 1.5 copy-start.3
  119.5 21.6 %all-to-all-start.3 = ((bf16[32,24,384]{2,1,0:T(8,128)(2,1)}), bf16[32,24,384]{2,1,0:T(8,128)(2,1)S(1)}, u32[]{:S(2)}, u32[]{:S(2)}) async-start(bf16[32,24,384]{2,1,0:T(8,128)(2,1)} %bitcast.25), calls=%async_computation.3 | async-start | bytes 1179648 | tf_op jit(solution)/shard_map/all_to_all | solution.py:857
  141.1 5.6 %copy-start.4 = (bf16[32,24,384]{2,1,0:T(8,128)(2,1)}, bf16[32,24,384]{2,1,0:T(8,128)(2,1)S(1)}, u32[]{:S(2)}) copy-start(bf16[32,24,384]{2,1,0:T(8,128)(2,1)S(1)} %all-to-all-done.3.kept_ref) | copy-start | bytes 1769476
  141.1 72.9 %all-to-all-start.2 = ((bf16[32,120,384]{2,1,0:T(8,128)(2,1)}), bf16[32,120,384]{2,1,0:T(8,128)(2,1)S(1)}, u32[]{:S(2)}, u32[]{:S(2)}) async-start(bf16[32,120,384]{2,1,0:T(8,128)(2,1)} %bitcast.24), calls=%async_computation.2 | async-start | bytes 5898240 | tf_op jit(solution)/shard_map/all_to_all | solution.py:857
  146.8 1.6 collective-permute-start.2
  148.4 0.7 copy-start.6
  214.0 3.6 %copy-start.1 = (bf16[32,120,384]{2,1,0:T(8,128)(2,1)}, bf16[32,120,384]{2,1,0:T(8,128)(2,1)S(1)}, u32[]{:S(2)}) copy-start(bf16[32,120,384]{2,1,0:T(8,128)(2,1)S(1)} %all-to-all-done.2.kept_ref) | copy-start | bytes 8847364
  214.1 3.5 %collective-permute-start.3 = (bf16[16,120,384]{2,1,0:T(8,128)(2,1)S(1)}, bf16[16,120,384]{2,1,0:T(8,128)(2,1)}, u32[]{:S(2)}, u32[]{:S(2)}) collective-permute-start(bf16[16,120,384]{2,1,0:T(8,128)(2,1)S(1)} %constant_dynamic-slice_fusion), channel_id=1, source_target_pairs={{0,16},{16,0},{1,17},{17,1},{2,18},{18,2},{3,19},{19,3},{4,20},{20... | collective-permute-start | bytes 4423688 | tf_op jit(solution)/shard_map/ppermute | solution.py:761

commit v6 on v5

--- a/solution.py
+++ b/solution.py
@@ -298,7 +298,7 @@
     )
 
 
-def stem_kernel(kind, place_ref, x_ref, above_ref, *refs):
+def stem_kernel(kind, x_ref, above_ref, *refs):
     sources = refs[:7]
     normed_ref, feat_ref, w1_ref, w2_ref, w3_ref, gain_ref, field = refs[-7:]
     step = pl.program_id(0)
@@ -352,8 +352,10 @@
         above = lower_half(above_ref[0])
         keep = 1.0
         if kind == "last":
-            keep = place_ref[1].astype(jnp.float32)
-            above = jnp.where(place_ref[2] > 0, refs[7][...], above)
+            lower_section = lax.axis_index("section") > 0
+            inside = lower_section | (lax.axis_index("tile") > 0)
+            keep = jnp.where(inside, 1.0, 0.0)
+            above = jnp.where(lower_section, above, refs[7][...])
         turned = above.T
         upper, lower = (
             layer_one(turned, [128 * b + 64 * a for b in range(bands)]) for a in range(2)
@@ -410,7 +412,7 @@
         ).astype(jnp.bfloat16)
 
 
-def stem(kind, image, place, weights, first, steps, devices, extra=()):
+def stem(kind, image, weights, first, steps, devices, extra=()):
     cols, depth = image.shape[1:]
     rows = 2 * steps
     shapes = weight_shapes(weights)
@@ -418,14 +420,17 @@
     merged = shapes[1].shape[0]
     group = channels // devices
 
+    def section_pairs():
+        return lax.axis_index("section") * (image.shape[0] // 4)
+
     def whole(array):
-        return pl.BlockSpec(array.shape, lambda i, place: (0,) * len(array.shape))
+        return pl.BlockSpec(array.shape, lambda i: (0,) * len(array.shape))
 
     operands = list(weights) + list(extra)
     in_specs = [whole(a) for a in weights]
     out_specs = [
-        pl.BlockSpec((devices, 1, 2 * group, cols), lambda i, place: (0, i, 0, 0)),
-        pl.BlockSpec((2, channels, cols), lambda i, place: (i, 0, 0)),
+        pl.BlockSpec((devices, 1, 2 * group, cols), lambda i: (0, i, 0, 0)),
+        pl.BlockSpec((2, channels, cols), lambda i: (i, 0, 0)),
     ]
     out_shape = [
         jax.ShapeDtypeStruct((devices, steps, 2 * group, cols), jnp.bfloat16),
@@ -435,28 +440,25 @@
     macs = rows * cols * (16 * 208 * 96 + 4 * 400 * merged + third_depth * channels)
     return pl.pallas_call(
         functools.partial(stem_kernel, kind),
-        grid_spec=pltpu.PrefetchScalarGridSpec(
-            num_scalar_prefetch=1,
-            grid=(steps,),
-            in_specs=[
-                pl.BlockSpec((2, cols, depth), lambda i, place: (place[0] + first + i, 0, 0)),
-                pl.BlockSpec(
-                    (1, cols, depth),
-                    lambda i, place: (jnp.maximum(2 * (place[0] + first) - 1, 0), 0, 0),
-                ),
-            ]
-            + in_specs,
-            out_specs=out_specs,
-            scratch_shapes=[pltpu.VMEM(a.shape, a.dtype) for a in shapes]
-            + [pltpu.VMEM((third_depth, 2 * cols), jnp.bfloat16)],
-        ),
+        grid=(steps,),
+        in_specs=[
+            pl.BlockSpec((2, cols, depth), lambda i: (section_pairs() + first + i, 0, 0)),
+            pl.BlockSpec(
+                (1, cols, depth),
+                lambda i: (jnp.maximum(2 * (section_pairs() + first) - 1, 0), 0, 0),
+            ),
+        ]
+        + in_specs,
+        out_specs=out_specs,
+        scratch_shapes=[pltpu.VMEM(a.shape, a.dtype) for a in shapes]
+        + [pltpu.VMEM((third_depth, 2 * cols), jnp.bfloat16)],
         out_shape=out_shape,
         compiler_params=pltpu.CompilerParams(vmem_limit_bytes=VMEM_BYTES),
         cost_estimate=pl.CostEstimate(
             flops=4 * macs, bytes_accessed=rows * cols * 3000, transcendentals=0
         ),
         name="stem",
-    )(place, image, image, *operands)
+    )(image, image, *operands)
 
 
 def symmetric_kernel(place_ref, f_ref, turn_w_ref, turn_u_ref, g_ref):
@@ -661,10 +663,11 @@
     back_table = jnp.concatenate(
         [cos_w[:width] * times[:, None], -sin_w[:width] * times[:, None]], 0
     )
-    turns = jnp.arange(1, RADIX)[:, None] * jnp.arange(third)[None, :]
-    angles = turns.astype(jnp.float32) * (2.0 * math.pi / full_rows)
-    twiddle = jnp.stack([jnp.cos(angles), jnp.sin(angles)], axis=1)
-    twiddle = jnp.broadcast_to(twiddle.reshape(-1, third, 1), (2 * RADIX - 2, third, 128))
+    turns = np.arange(1, RADIX)[:, None] * np.arange(third)[None, :]
+    angles = turns * (2.0 * math.pi / full_rows)
+    twiddle = np.stack([np.cos(angles), np.sin(angles)], axis=1).reshape(-1, third, 1)
+    twiddle = np.broadcast_to(twiddle.astype(np.float32), (2 * RADIX - 2, third, 128))
+    twiddle = jnp.asarray(twiddle)
     return row_table, fwd, inv, back_table, twiddle
 
 
@@ -694,7 +697,7 @@
             pltpu.VMEM((cols // 128, late.shape[0], 128), jnp.float32),
             pltpu.VMEM((cols // 128, full_rows * count, 128), jnp.float32),
         ],
-        compiler_params=pltpu.CompilerParams(vmem_limit_bytes=VMEM_BYTES),
+        compiler_params=pltpu.CompilerParams(vmem_limit_bytes=VMEM_BYTES * (2 if count == per_step else 4) // 5),
         cost_estimate=pl.CostEstimate(
             flops=2 * macs, bytes_accessed=count * full_rows * cols * 8, transcendentals=0
         ),
@@ -720,7 +723,7 @@
 def add_residual(place, returned, other, features, previous, first, count):
     halves, span, cols = other.shape
     group, rows = features.shape[1:3]
-    groups = 4 if halves % 4 == 0 else 1
+    groups = 2 if halves % 2 == 0 else 1
     steps = halves // groups
     operands = [returned, other, features]
     in_specs = [
@@ -747,7 +750,7 @@
         ),
         out_shape=jax.ShapeDtypeStruct(features.shape, jnp.bfloat16),
         input_output_aliases=aliases,
-        compiler_params=pltpu.CompilerParams(vmem_limit_bytes=VMEM_BYTES),
+        compiler_params=pltpu.CompilerParams(vmem_limit_bytes=VMEM_BYTES // 6),
         cost_estimate=pl.CostEstimate(
             flops=halves * count * rows * cols,
             bytes_accessed=halves * count * rows * cols * 8,
@@ -803,24 +806,21 @@
     if not suits:
         return general_local(*arguments)
     section = lax.axis_index("section")
-    tile = lax.axis_index("tile")
     group = tile_channels // 2
     half_channels = channels // 2
     width = -(-(field_cols // 2 + 1) // 128) * 128
 
     arriving = from_behind(lower_half(aerial_patch_grid[-1]), "tile", 1)
-    inside = (section > 0) | (tile > 0)
-    place = jnp.stack([section * (rows // 2), inside, section == 0]).astype(jnp.int32)
     sources = weight_sources(*arguments[1:8])
     pairs = rows // 2
     early = max(pairs // 3, 1)
     late = pairs - early
     normed_early, feat_early = stem(
-        "first", aerial_patch_grid, place, sources, late, early, devices
+        "first", aerial_patch_grid, sources, late, early, devices
     )
     normed_early, arriving = lax.optimization_barrier((normed_early, arriving))
     normed_late, feat_late = stem(
-        "last", aerial_patch_grid, place, sources, 0, late, devices, (arriving,)
+        "last", aerial_patch_grid, sources, 0, late, devices, (arriving,)
     )
     spread = [
         lax.all_to_all(normed, DEVICES, split_axis=0, concat_axis=0, tiled=True).reshape(
@@ -843,16 +843,16 @@
     high = jnp.where(section == 0, arrived, own)
     residual = jnp.transpose(jnp.concatenate([low, high], axis=0), (1, 0, 2))
     residual = residual.reshape(half_channels // group, group, tile_rows, field_cols)
-    late_fields, early_fields, residual, symmetric, tables = lax.optimization_barrier(
-        (late_fields, early_fields, residual, symmetric, tables)
-    )
+    late_fields, residual = lax.optimization_barrier((late_fields, residual))
 
     section_place = jnp.reshape(section, (1,)).astype(jnp.int32)
     halves = devices // 2
     output = None
-    for first, count in ((group - 2, 2), (0, group - 2)):
+    rest = group - 2
+    per_step = 5 if rest % 5 == 0 else 2
+    for first, count, per_step in ((rest, 2, 2), (0, rest, per_step)):
         made = filter_channels(
-            late_fields, early_fields, symmetric, tables, first, count, 2, devices
+            late_fields, early_fields, symmetric, tables, first, count, per_step, devices
         )
         returned = lax.all_to_all(made, DEVICES, split_axis=0, concat_axis=0, tiled=True)
         if output is not None:

time: 224 us -> 237 us (1.058)
  local copies, waits for them, and re-layouts: 12.4 us -> 25.9 us
    unnamed x21 -> x45, local copies, waits for them, and re-layouts: 4.29 us -> 18.3 us
    pallas_call x2, Pallas kernels: 23.6 us -> 20.4 us  [filter_channels(): pl.pallas_call(functools.partial(filter_kernel, first, devices, 1.0 / (fu...]
    all_to_all x2, waiting for transfers between devices: 26.3 us -> 29.5 us  [local(): lax.all_to_all(normed, DEVICES, split_axis=0, concat_axis=0, tiled=True)]
  transfers between devices with their start and end apart: 8 -> 8, of which waited for: 5 -> 5; matrix products, arithmetic and copies ran while one was open for 9% -> 8% of each run, Pallas kernels for 31% -> 29%
where the time goes in v6:
time: 237 us; the launch traced here: 235 us
  waiting for transfers between devices  94.2 us (40%)
  Pallas kernels  78.8 us (33%)
  local copies, waits for them, and re-layouts  25.9 us (11%)
  starting transfers between devices  24 us (10%)
  other arithmetic  11.5 us (5%)
    all_to_all x2, waiting for transfers between devices, local(): lax.all_to_all(made, DEVICES, split_axis=0, concat_axis=0, tiled=True)  60 us
    pallas_call x2, Pallas kernels, stem(): pl.pallas_call(functools.partial(stem_kernel, kind), grid=(steps,), in_sp...  32.7 us
    all_to_all x2, waiting for transfers between devices, local(): lax.all_to_all(normed, DEVICES, split_axis=0, concat_axis=0, tiled=True)  29.5 us
    pallas_call x2, Pallas kernels, filter_channels(): pl.pallas_call(functools.partial(filter_kernel, first, devices, 1.0 / (fu...  20.4 us
    unnamed x45, local copies, waits for them, and re-layouts  18.3 us
    pallas_call x1, Pallas kernels, symmetric_filter(): pl.pallas_call(symmetric_kernel, grid_spec=pltpu.PrefetchScalarGridSpec(n...  14.2 us
    pallas_call x2, Pallas kernels, add_residual(): pl.pallas_call(functools.partial(residual_kernel, count), grid_spec=pltpu...  10.7 us
    all_to_all x2, starting transfers between devices, local(): lax.all_to_all(made, DEVICES, split_axis=0, concat_axis=0, tiled=True)  9.95 us
  transfers between devices with their start and end apart: 8, of which 5 were waited for; matrix products, arithmetic and copies ran while one was open for 8% of the time, Pallas kernels for 29%

profile of v6, /device:TPU:0, one launch (start us, length us, event | category | flops | bytes accessed | tf_op | source)
XLA Modules:
  0.0 234.7 jit_solution(1271805611332453399)
XLA Ops:
  0.0 1.1 slice_bitcast_fusion
  1.1 0.1 fusion.34
  1.2 4.9 %collective-permute-start = (bf16[384,384]{1,0:T(8,128)(2,1)S(1)}, bf16[384,384]{1,0:T(8,128)(2,1)S(1)}, u32[]{:S(2)}, u32[]{:S(2)}) collective-permute-start(bf16[384,384]{1,0:T(8,128)(2,1)S(1)} %pad_maximum_fusion.2), channel_id=1, source_target_pairs={{0,1},{1,2},{2,3},{3,4},{4,5},{5,6},{6,7},{7,8},{8,9},{9,10},{10,1... | collective-permute-start | bytes 884744 | tf_op jit(solution)/shard_map/ppermute | solution.py:18
  6.1 12.3 %stem.2 = (bf16[32,2,24,384]{3,2,1,0:T(8,128)(2,1)}, bf16[4,384,384]{2,1,0:T(8,128)(2,1)}) custom-call(bf16[24,384,768]{2,1,0:T(8,128)(2,1)} %above_ref.3, bf16[24,384,768]{2,1,0:T(8,128)(2,1)} %above_ref.3, bf16[48,96]{1,0:T(8,128)(2,1)} %bitcast.24, f32[96]{0:T(128)} %refs_1_.3, bf16[384,192]{1,0:T(8,128)(2,1)} %bitcast.22, f32[192]{0:T(256)} %refs_3_.3, ...), custom_call_target="tpu_custom_call" | custom-call | flops 8078229504 | bytes 4608000 | tf_op jit(solution)/shard_map/stem/pallas_call | solution.py:441
  18.4 0.0 collective-permute-done.refs_7_
  18.4 4.9 %all-to-all-start.1 = ((bf16[32,2,24,384]{3,2,1,0:T(8,128)(2,1)}), bf16[32,2,24,384]{3,2,1,0:T(8,128)(2,1)S(1)}, u32[]{:S(2)}, u32[]{:S(2)}) async-start(bf16[32,2,24,384]{3,2,1,0:T(8,128)(2,1)} %get-tuple-element.21), calls=%async_computation.1 | async-start | bytes 2359296 | tf_op jit(solution)/shard_map/all_to_all | solution.py:826
  23.3 20.4 %stem.3 = (bf16[32,4,24,384]{3,2,1,0:T(8,128)(2,1)}, bf16[8,384,384]{2,1,0:T(8,128)(2,1)}) custom-call(bf16[24,384,768]{2,1,0:T(8,128)(2,1)} %above_ref.3, bf16[24,384,768]{2,1,0:T(8,128)(2,1)} %above_ref.3, bf16[48,96]{1,0:T(8,128)(2,1)} %bitcast.25, f32[96]{0:T(128)} %refs_1_.3, bf16[384,192]{1,0:T(8,128)(2,1)} %bitcast.23, f32[192]{0:T(256)} %refs_3_.3, ...), custom_call_target="tpu_custom_call" | custom-call | flops 16156459008 | bytes 9216000 | tf_op jit(solution)/shard_map/stem/pallas_call | solution.py:441
  43.7 8.7 %all-to-all-done.1 = bf16[32,2,24,384]{3,2,1,0:T(8,128)(2,1)S(1)} async-done(((bf16[32,2,24,384]{3,2,1,0:T(8,128)(2,1)}), bf16[32,2,24,384]{3,2,1,0:T(8,128)(2,1)S(1)}, u32[]{:S(2)}, u32[]{:S(2)}) %all-to-all-start.1) | async-done | bytes 1179680 | tf_op jit(solution)/shard_map/all_to_all | solution.py:826
  52.4 1.0 copy-done.4
  53.4 3.9 %all-to-all-start = ((bf16[32,4,24,384]{3,2,1,0:T(8,128)(2,1)}), bf16[32,4,24,384]{3,2,1,0:T(8,128)(2,1)}, u32[]{:S(2)}, u32[]{:S(2)}) async-start(bf16[32,4,24,384]{3,2,1,0:T(8,128)(2,1)} %get-tuple-element.17), calls=%async_computation | async-start | bytes 4718592 | tf_op jit(solution)/shard_map/all_to_all | solution.py:826
  57.4 0.3 fusion.29
  57.7 0.3 sine_convert_fusion.1
  58.0 0.3 fusion.30
  58.2 0.3 sine_convert_fusion.2
  58.5 0.7 maximum_maximum_fusion.fwd_ref
  59.2 2.0 constant_dynamic-update-slice_fusion.1
  61.2 0.2 constant_dynamic-update-slice_fusion
  61.5 1.5 constant_dynamic-slice_fusion.2
  62.9 0.0 collective-permute-start.1
  63.0 0.7 maximum_maximum_fusion.1.inv_ref
  63.6 1.0 fusion.8.turn_u_ref
  64.6 2.5 %sine_convert_fusion = (bf16[384,384]{1,0:T(8,128)(2,1)S(1)}, bf16[384,384]{1,0:T(8,128)(2,1)S(1)}) fusion(), kind=kLoop, calls=%fused_computation.9 | loop fusion | flops 1622016 | bytes 589824 | tf_op jit(solution)/shard_map/convert_element_type | solution.py:26
  67.2 0.8 pad_maximum_fusion.row_table_ref
  68.0 0.1 slice_multiply_fusion
  68.2 0.8 pad_maximum_fusion.1.back_ref
  69.0 0.9 fusion.14.turn_w_ref
  69.9 14.2 %symmetric_filter.1.g_ref = bf16[12,2,384,256]{3,2,1,0:T(8,128)(2,1)} custom-call(s32[1]{0:T(128)} %bitcast.9.place_ref, bf16[24,2,384,384]{3,2,1,0:T(8,128)(2,1)} %f_ref.1, bf16[384,256]{1,0:T(8,128)(2,1)} %fusion.14.turn_w_ref, bf16[384,384]{1,0:T(8,128)(2,1)} %fusion.8.turn_u_ref), custom_call_target="tpu_custom_call" | custom-call | flops 3623878656 | bytes 16515072 | tf_op jit(solution)/shard_map/symmetric_filter/pallas_call | solution.py:483
  84.1 0.0 collective-permute-done.1
  84.1 2.3 broadcast_select_fusion.1
  86.4 0.4 maximum_bitcast_fusion
  86.8 2.1 copy.13
  89.0 0.0 copy-start.19
  89.0 0.9 repack.1.early_ref
  89.9 1.0 copy-done.1
  90.9 20.9 %all-to-all-done = bf16[32,4,24,384]{3,2,1,0:T(8,128)(2,1)} async-done(((bf16[32,4,24,384]{3,2,1,0:T(8,128)(2,1)}), bf16[32,4,24,384]{3,2,1,0:T(8,128)(2,1)}, u32[]{:S(2)}, u32[]{:S(2)}) %all-to-all-start) | async-done | bytes 2359328 | tf_op jit(solution)/shard_map/all_to_all | solution.py:826
  111.8 0.1 jit_solution_.3.twiddle_ref
  111.9 2.3 copy-done
  114.3 1.3 copy-done.2
  115.5 1.0 copy-done.7
  116.5 1.0 copy-done.9
  117.5 0.9 copy-done.13
  118.4 0.9 copy-done.15
  119.3 4.7 %spectral_filter.3 = bf16[768,384]{1,0:T(8,128)(2,1)S(1)} custom-call(bf16[3072,384]{1,0:T(8,128)(2,1)} %bitcast.5.late_ref, bf16[12,128,384]{2,1,0:T(8,128)(2,1)S(1)} %copy-done.2, bf16[12,2,384,256]{3,2,1,0:T(8,128)(2,1)S(1)} %copy-done, bf16[384,512]{1,0:T(8,128)(2,1)S(1)} %copy-done.7, bf16[256,256]{1,0:T(8,128)(2,1)S(1)} %copy-done.13, ...), custom_call_target="tpu_custom_call" | custom-call | flops 1207959552 | bytes 2359296 | tf_op jit(solution)/shard_map/spectral_filter/pallas_call | solution.py:683
  124.0 0.0 copy-start.6
  124.1 0.8 copy-done.6
  124.9 4.3 %all-to-all-start.3 = ((bf16[32,24,384]{2,1,0:T(8,128)(2,1)}), bf16[32,24,384]{2,1,0:T(8,128)(2,1)}, u32[]{:S(2)}, u32[]{:S(2)}) async-start(bf16[32,24,384]{2,1,0:T(8,128)(2,1)} %bitcast.18), calls=%async_computation.3 | async-start | bytes 1179648 | tf_op jit(solution)/shard_map/all_to_all | solution.py:857
  129.2 1.3 copy-done.3
  130.4 1.0 copy-done.8
  131.4 1.0 copy-done.10
  132.4 0.9 copy-done.12
  133.4 0.9 copy-done.14
  134.3 0.9 copy-done.16
  135.2 15.7 %spectral_filter.2 = bf16[3840,384]{1,0:T(8,128)(2,1)} custom-call(bf16[3072,384]{1,0:T(8,128)(2,1)} %bitcast.5.late_ref, bf16[12,128,384]{2,1,0:T(8,128)(2,1)S(1)} %copy-done.3, bf16[12,2,384,256]{3,2,1,0:T(8,128)(2,1)} %symmetric_filter.1.g_ref, bf16[384,512]{1,0:T(8,128)(2,1)S(1)} %copy-done.8, bf16[256,256]{1,0:T(8,128)(2,1)S(1)} %copy-done.14, ...), custom_call_target="tpu_custom_call" | custom-call | flops 6039797760 | bytes 11796480 | tf_op jit(solution)/shard_map/spectral_filter/pallas_call | solution.py:683
  150.8 0.0 all-to-all-done.3.kept_ref
  150.8 5.7 %all-to-all-start.2 = ((bf16[32,120,384]{2,1,0:T(8,128)(2,1)}), bf16[32,120,384]{2,1,0:T(8,128)(2,1)}, u32[]{:S(2)}, u32[]{:S(2)}) async-start(bf16[32,120,384]{2,1,0:T(8,128)(2,1)} %bitcast.19), calls=%async_computation.2 | async-start | bytes 5898240 | tf_op jit(solution)/shard_map/all_to_all | solution.py:857
  156.5 1.0 constant_dynamic-slice_fusion.1
  157.5 0.3 collective-permute-start.2
  157.8 1.4 collective-permute-done.2.other_ref
  159.2 4.6 %residual.2.refs_0_ = bf16[16,12,24,384]{3,2,1,0:T(8,128)(2,1)} custom-call(s32[1]{0:T(128)} %bitcast.place_ref, bf16[32,24,384]{2,1,0:T(8,128)(2,1)} %all-to-all-done.3.kept_ref, bf16[16,24,384]{2,1,0:T(8,128)(2,1)S(1)} %collective-permute-done.2.other_ref, bf16[16,12,24,384]{3,2,1,0:T(8,128)(2,1)S(1)} %bitcast.15), custom_call_target="tpu_custom_call" | custom-call | flops 294912 | bytes 2359296 | tf_op jit(solution)/shard_map/residual/pallas_call | solution.py:742
  163.7 60.0 %all-to-all-done.2.kept_ref = bf16[32,120,384]{2,1,0:T(8,128)(2,1)} async-done(((bf16[32,120,384]{2,1,0:T(8,128)(2,1)}), bf16[32,120,384]{2,1,0:T(8,128)(2,1)}, u32[]{:S(2)}, u32[]{:S(2)}) %all-to-all-start.2) | async-done | bytes 2949152 | tf_op jit(solution)/shard_map/all_to_all | solution.py:857
  223.8 1.5 constant_dynamic-slice_fusion
  225.3 0.1 collective-permute-start.3
  225.4 3.3 %collective-permute-done.3.other_ref = bf16[16,120,384]{2,1,0:T(8,128)(2,1)S(1)} collective-permute-done((bf16[16,120,384]{2,1,0:T(8,128)(2,1)S(1)}, bf16[16,120,384]{2,1,0:T(8,128)(2,1)S(1)}, u32[]{:S(2)}, u32[]{:S(2)}) %collective-permute-start.3) | collective-permute-done | bytes 1474592 | tf_op jit(solution)/shard_map/ppermute | solution.py:764
  228.6 6.1 %residual.3 = bf16[16,12,24,384]{3,2,1,0:T(8,128)(2,1)} custom-call(s32[1]{0:T(128)} %bitcast.place_ref, bf16[32,120,384]{2,1,0:T(8,128)(2,1)} %all-to-all-done.2.kept_ref, bf16[16,120,384]{2,1,0:T(8,128)(2,1)S(1)} %collective-permute-done.3.other_ref, bf16[16,12,24,384]{3,2,1,0:T(8,128)(2,1)S(1)} %bitcast.16, ...), custom_call_target="tpu_custom_call", output_to_operand_aliasing={{}: (4, {})} | custom-call | flops 1474560 | bytes 11796480 | tf_op jit(solution)/shard_map/residual/pallas_call | solution.py:742
  (34 shorter events, 0.1 us)
Async XLA Ops:
  1.2 17.2 %collective-permute-start = (bf16[384,384]{1,0:T(8,128)(2,1)S(1)}, bf16[384,384]{1,0:T(8,128)(2,1)S(1)}, u32[]{:S(2)}, u32[]{:S(2)}) collective-permute-start(bf16[384,384]{1,0:T(8,128)(2,1)S(1)} %pad_maximum_fusion.2), channel_id=1, source_target_pairs={{0,1},{1,2},{2,3},{3,4},{4,5},{5,6},{6,7},{7,8},{8,9},{9,10},{10,1... | collective-permute-start | bytes 884744 | tf_op jit(solution)/shard_map/ppermute | solution.py:18
  18.4 4.9 %copy-start.21 = (bf16[384,384]{1,0:T(8,128)(2,1)}, bf16[384,384]{1,0:T(8,128)(2,1)S(1)}, u32[]{:S(2)}) copy-start(bf16[384,384]{1,0:T(8,128)(2,1)S(1)} %collective-permute-done.refs_7_) | copy-start | bytes 884740
  18.4 34.0 %all-to-all-start.1 = ((bf16[32,2,24,384]{3,2,1,0:T(8,128)(2,1)}), bf16[32,2,24,384]{3,2,1,0:T(8,128)(2,1)S(1)}, u32[]{:S(2)}, u32[]{:S(2)}) async-start(bf16[32,2,24,384]{3,2,1,0:T(8,128)(2,1)} %get-tuple-element.21), calls=%async_computation.1 | async-start | bytes 2359296 | tf_op jit(solution)/shard_map/all_to_all | solution.py:826
  52.4 1.0 copy-start.4
  52.4 5.6 %copy-start.20 = (s32[128]{0:T(128)S(1)}, s32[128]{0:T(128)}, u32[]{:S(2)}) copy-start(s32[128]{0:T(128)} %constant.75.clone) | copy-start | bytes 1540
  53.4 58.4 %all-to-all-start = ((bf16[32,4,24,384]{3,2,1,0:T(8,128)(2,1)}), bf16[32,4,24,384]{3,2,1,0:T(8,128)(2,1)}, u32[]{:S(2)}, u32[]{:S(2)}) async-start(bf16[32,4,24,384]{3,2,1,0:T(8,128)(2,1)} %get-tuple-element.17), calls=%async_computation | async-start | bytes 4718592 | tf_op jit(solution)/shard_map/all_to_all | solution.py:826
  57.4 3.8 %copy-start.18 = (s32[384]{0:T(512)}, s32[384]{0:T(512)S(1)}, u32[]{:S(2)}) copy-start(s32[384]{0:T(512)S(1)} %iota.37) | copy-start | bytes 4612
  59.2 2.0 copy-start.17
  62.9 6.0 %slice-start = ((s32[384]{0:T(512)}), s32[256]{0:T(256)S(1)}, s32[]{:S(2)}) async-start(s32[384]{0:T(512)} %copy-done.18), calls=%async_computation.4 | async-start | bytes 2048 | tf_op jit(solution)/shard_map/slice | solution.py:482
  62.9 21.2 %collective-permute-start.1 = (bf16[12,192,384]{2,1,0:T(8,128)(2,1)}, bf16[12,192,384]{2,1,0:T(8,128)(2,1)}, u32[]{:S(2)}, u32[]{:S(2)}) collective-permute-start(bf16[12,192,384]{2,1,0:T(8,128)(2,1)} %constant_dynamic-slice_fusion.2), channel_id=1, source_target_pairs={{0,16},{16,0},{1,17},{17,1},{2,18},{18,2},{3,19},{19,3},{4,20},{20... | collective-permute-start | bytes 5308424 | tf_op jit(solution)/shard_map/ppermute | solution.py:764
  86.8 2.1 copy-start.5
  89.0 22.8 %copy-start.19 = (f32[4,128]{1,0:T(4,128)S(1)}, f32[4,128]{1,0:T(4,128)}, u32[]{:S(2)}) copy-start(f32[4,128]{1,0:T(4,128)} %constant.76.clone) | copy-start | bytes 6148
  89.8 1.1 copy-start.1
  111.9 2.3 copy-start
  114.2 1.3 copy-start.2
  115.5 1.0 copy-start.7
  116.5 1.0 copy-start.9
  117.5 0.9 copy-start.13
  118.4 0.9 copy-start.15
  119.3 4.7 %copy-start.11 = (f32[4,128,128]{2,1,0:T(8,128)}, f32[4,128,128]{2,1,0:T(8,128)S(1)}, u32[]{:S(2)}) copy-start(f32[4,128,128]{2,1,0:T(8,128)S(1)} %jit_solution_.3.twiddle_ref) | copy-start | bytes 786436
  124.0 0.8 copy-start.6
  124.9 26.0 %all-to-all-start.3 = ((bf16[32,24,384]{2,1,0:T(8,128)(2,1)}), bf16[32,24,384]{2,1,0:T(8,128)(2,1)}, u32[]{:S(2)}, u32[]{:S(2)}) async-start(bf16[32,24,384]{2,1,0:T(8,128)(2,1)} %bitcast.18), calls=%async_computation.3 | async-start | bytes 1179648 | tf_op jit(solution)/shard_map/all_to_all | solution.py:857
  129.1 1.3 copy-start.3
  130.4 1.0 copy-start.8
  131.4 1.0 copy-start.10
  132.4 0.9 copy-start.12
  133.4 0.9 copy-start.14
  134.3 0.9 copy-start.16
  150.8 72.9 %all-to-all-start.2 = ((bf16[32,120,384]{2,1,0:T(8,128)(2,1)}), bf16[32,120,384]{2,1,0:T(8,128)(2,1)}, u32[]{:S(2)}, u32[]{:S(2)}) async-start(bf16[32,120,384]{2,1,0:T(8,128)(2,1)} %bitcast.19), calls=%async_computation.2 | async-start | bytes 5898240 | tf_op jit(solution)/shard_map/all_to_all | solution.py:857
  157.5 1.6 collective-permute-start.2
  225.3 3.3 %collective-permute-start.3 = (bf16[16,120,384]{2,1,0:T(8,128)(2,1)S(1)}, bf16[16,120,384]{2,1,0:T(8,128)(2,1)S(1)}, u32[]{:S(2)}, u32[]{:S(2)}) collective-permute-start(bf16[16,120,384]{2,1,0:T(8,128)(2,1)S(1)} %constant_dynamic-slice_fusion), channel_id=1, source_target_pairs={{0,16},{16,0},{1,17},{17,1},{2,18},{18,2},{3,19},{19,3},{4,20},{20... | collective-permute-start | bytes 4423688 | tf_op jit(solution)/shard_map/ppermute | solution.py:764

commit v7 on v6

--- a/solution.py
+++ b/solution.py
@@ -453,7 +453,7 @@
         scratch_shapes=[pltpu.VMEM(a.shape, a.dtype) for a in shapes]
         + [pltpu.VMEM((third_depth, 2 * cols), jnp.bfloat16)],
         out_shape=out_shape,
-        compiler_params=pltpu.CompilerParams(vmem_limit_bytes=VMEM_BYTES),
+        compiler_params=pltpu.CompilerParams(vmem_limit_bytes=VMEM_BYTES + 3 * 1024 * 1024),
         cost_estimate=pl.CostEstimate(
             flops=4 * macs, bytes_accessed=rows * cols * 3000, transcendentals=0
         ),
@@ -697,7 +697,7 @@
             pltpu.VMEM((cols // 128, late.shape[0], 128), jnp.float32),
             pltpu.VMEM((cols // 128, full_rows * count, 128), jnp.float32),
         ],
-        compiler_params=pltpu.CompilerParams(vmem_limit_bytes=VMEM_BYTES * (2 if count == per_step else 4) // 5),
+        compiler_params=pltpu.CompilerParams(vmem_limit_bytes=VMEM_BYTES),
         cost_estimate=pl.CostEstimate(
             flops=2 * macs, bytes_accessed=count * full_rows * cols * 8, transcendentals=0
         ),
@@ -723,7 +723,7 @@
 def add_residual(place, returned, other, features, previous, first, count):
     halves, span, cols = other.shape
     group, rows = features.shape[1:3]
-    groups = 2 if halves % 2 == 0 else 1
+    groups = 4 if halves % 4 == 0 else 1
     steps = halves // groups
     operands = [returned, other, features]
     in_specs = [
@@ -750,7 +750,7 @@
         ),
         out_shape=jax.ShapeDtypeStruct(features.shape, jnp.bfloat16),
         input_output_aliases=aliases,
-        compiler_params=pltpu.CompilerParams(vmem_limit_bytes=VMEM_BYTES // 6),
+        compiler_params=pltpu.CompilerParams(vmem_limit_bytes=VMEM_BYTES),
         cost_estimate=pl.CostEstimate(
             flops=halves * count * rows * cols,
             bytes_accessed=halves * count * rows * cols * 8,

time: 237 us -> 221 us (0.932)
  local copies, waits for them, and re-layouts: 25.9 us -> 11.6 us
    unnamed x45 -> x19, local copies, waits for them, and re-layouts: 18.3 us -> 3.73 us
    all_to_all x2, waiting for transfers between devices: 29.5 us -> 26.5 us  [local(): lax.all_to_all(normed, DEVICES, split_axis=0, concat_axis=0, tiled=True)]
  transfers between devices with their start and end apart: 8 -> 8, of which waited for: 5 -> 6; matrix products, arithmetic and copies ran while one was open for 8% -> 9% of each run, Pallas kernels for 29% -> 31%
where the time goes in v7:
time: 221 us; the launch traced here: 220 us
  waiting for transfers between devices  92.9 us (42%)
  Pallas kernels  79.9 us (36%)
  starting transfers between devices  23.7 us (11%)
  local copies, waits for them, and re-layouts  11.6 us (5%)
  other arithmetic  11.4 us (5%)
    all_to_all x2, waiting for transfers between devices, local(): lax.all_to_all(made, DEVICES, split_axis=0, concat_axis=0, tiled=True)  61.7 us
    pallas_call x2, Pallas kernels, stem(): pl.pallas_call(functools.partial(stem_kernel, kind), grid=(steps,), in_sp...  32.7 us
    all_to_all x2, waiting for transfers between devices, local(): lax.all_to_all(normed, DEVICES, split_axis=0, concat_axis=0, tiled=True)  26.5 us
    pallas_call x2, Pallas kernels, filter_channels(): pl.pallas_call(functools.partial(filter_kernel, first, devices, 1.0 / (fu...  22.3 us
    pallas_call x1, Pallas kernels, symmetric_filter(): pl.pallas_call(symmetric_kernel, grid_spec=pltpu.PrefetchScalarGridSpec(n...  14.2 us
    all_to_all x2, starting transfers between devices, local(): lax.all_to_all(made, DEVICES, split_axis=0, concat_axis=0, tiled=True)  9.49 us
    all_to_all x2, starting transfers between devices, local(): lax.all_to_all(normed, DEVICES, split_axis=0, concat_axis=0, tiled=True)  8.97 us
    pallas_call x2, Pallas kernels, add_residual(): pl.pallas_call(functools.partial(residual_kernel, count), grid_spec=pltpu...  8.52 us
  transfers between devices with their start and end apart: 8, of which 6 were waited for; matrix products, arithmetic and copies ran while one was open for 9% of the time, Pallas kernels for 31%

profile of v7, /device:TPU:0, one launch (start us, length us, event | category | flops | bytes accessed | tf_op | source)
XLA Modules:
  0.0 219.8 jit_solution(5345835596812247976)
XLA Ops:
  0.0 1.1 slice_bitcast_fusion
  1.1 0.1 fusion.34
  1.2 4.9 %collective-permute-start = (bf16[384,384]{1,0:T(8,128)(2,1)S(1)}, bf16[384,384]{1,0:T(8,128)(2,1)S(1)}, u32[]{:S(2)}, u32[]{:S(2)}) collective-permute-start(bf16[384,384]{1,0:T(8,128)(2,1)S(1)} %pad_maximum_fusion.2), channel_id=1, source_target_pairs={{0,1},{1,2},{2,3},{3,4},{4,5},{5,6},{6,7},{7,8},{8,9},{9,10},{10,1... | collective-permute-start | bytes 884744 | tf_op jit(solution)/shard_map/ppermute | solution.py:18
  6.1 12.3 %stem.2 = (bf16[32,2,24,384]{3,2,1,0:T(8,128)(2,1)}, bf16[4,384,384]{2,1,0:T(8,128)(2,1)}) custom-call(bf16[24,384,768]{2,1,0:T(8,128)(2,1)} %above_ref.3, bf16[24,384,768]{2,1,0:T(8,128)(2,1)} %above_ref.3, bf16[48,96]{1,0:T(8,128)(2,1)} %bitcast.23, f32[96]{0:T(128)} %refs_1_.3, bf16[384,192]{1,0:T(8,128)(2,1)} %bitcast.21, f32[192]{0:T(256)} %refs_3_.3, ...), custom_call_target="tpu_custom_call" | custom-call | flops 8078229504 | bytes 4608000 | tf_op jit(solution)/shard_map/stem/pallas_call | solution.py:441
  18.4 0.0 collective-permute-done.refs_7_
  18.4 0.0 copy-start.8
  18.4 5.0 %all-to-all-start.1 = ((bf16[32,2,24,384]{3,2,1,0:T(8,128)(2,1)}), bf16[32,2,24,384]{3,2,1,0:T(8,128)(2,1)}, u32[]{:S(2)}, u32[]{:S(2)}) async-start(bf16[32,2,24,384]{3,2,1,0:T(8,128)(2,1)} %get-tuple-element.21), calls=%async_computation.1 | async-start | bytes 2359296 | tf_op jit(solution)/shard_map/all_to_all | solution.py:826
  23.4 0.0 copy-done.8
  23.4 20.4 %stem.3 = (bf16[32,4,24,384]{3,2,1,0:T(8,128)(2,1)}, bf16[8,384,384]{2,1,0:T(8,128)(2,1)}) custom-call(bf16[24,384,768]{2,1,0:T(8,128)(2,1)} %above_ref.3, bf16[24,384,768]{2,1,0:T(8,128)(2,1)} %above_ref.3, bf16[48,96]{1,0:T(8,128)(2,1)} %bitcast.24, f32[96]{0:T(128)} %refs_1_.3, bf16[384,192]{1,0:T(8,128)(2,1)} %bitcast.22, f32[192]{0:T(256)} %refs_3_.3, ...), custom_call_target="tpu_custom_call" | custom-call | flops 16156459008 | bytes 9216000 | tf_op jit(solution)/shard_map/stem/pallas_call | solution.py:441
  43.9 8.6 %all-to-all-done.1 = bf16[32,2,24,384]{3,2,1,0:T(8,128)(2,1)} async-done(((bf16[32,2,24,384]{3,2,1,0:T(8,128)(2,1)}), bf16[32,2,24,384]{3,2,1,0:T(8,128)(2,1)}, u32[]{:S(2)}, u32[]{:S(2)}) %all-to-all-start.1) | async-done | bytes 1179680 | tf_op jit(solution)/shard_map/all_to_all | solution.py:826
  52.5 0.0 copy-start.7
  52.5 3.9 %all-to-all-start = ((bf16[32,4,24,384]{3,2,1,0:T(8,128)(2,1)}), bf16[32,4,24,384]{3,2,1,0:T(8,128)(2,1)}, u32[]{:S(2)}, u32[]{:S(2)}) async-start(bf16[32,4,24,384]{3,2,1,0:T(8,128)(2,1)} %get-tuple-element.17), calls=%async_computation | async-start | bytes 4718592 | tf_op jit(solution)/shard_map/all_to_all | solution.py:826
  56.5 0.0 copy-start.5
  56.5 0.3 fusion.29
  56.8 0.3 sine_convert_fusion.1
  57.0 0.0 copy-done.7
  57.1 0.3 fusion.30
  57.3 0.3 sine_convert_fusion.2
  57.6 0.7 maximum_maximum_fusion.fwd_ref
  58.3 0.0 copy-start.3
  58.3 2.0 constant_dynamic-update-slice_fusion.1
  60.3 0.0 copy-done.5
  60.3 0.0 copy-done.3
  60.3 0.2 constant_dynamic-update-slice_fusion
  60.6 1.5 constant_dynamic-slice_fusion.2
  62.0 0.0 slice-start
  62.0 0.0 collective-permute-start.1
  62.1 0.7 maximum_maximum_fusion.1.inv_ref
  62.7 1.0 fusion.8.turn_u_ref
  63.7 2.5 %sine_convert_fusion = (bf16[384,384]{1,0:T(8,128)(2,1)S(1)}, bf16[384,384]{1,0:T(8,128)(2,1)S(1)}) fusion(), kind=kLoop, calls=%fused_computation.9 | loop fusion | flops 1622016 | bytes 589824 | tf_op jit(solution)/shard_map/convert_element_type | solution.py:26
  66.3 0.8 pad_maximum_fusion.row_table_ref
  67.1 0.1 slice_multiply_fusion
  67.2 0.8 pad_maximum_fusion.1.back_ref
  68.0 0.0 slice-done
  68.0 0.9 fusion.14.turn_w_ref
  69.0 14.2 %symmetric_filter.1.g_ref = bf16[12,2,384,256]{3,2,1,0:T(8,128)(2,1)} custom-call(s32[1]{0:T(128)} %bitcast.9.place_ref, bf16[24,2,384,384]{3,2,1,0:T(8,128)(2,1)} %f_ref.1, bf16[384,256]{1,0:T(8,128)(2,1)} %fusion.14.turn_w_ref, bf16[384,384]{1,0:T(8,128)(2,1)} %fusion.8.turn_u_ref), custom_call_target="tpu_custom_call" | custom-call | flops 3623878656 | bytes 16515072 | tf_op jit(solution)/shard_map/symmetric_filter/pallas_call | solution.py:483
  83.2 0.0 collective-permute-done.1
  83.2 2.3 %broadcast_select_fusion.1 = (bf16[12,192,384]{2,1,0:T(8,128)(2,1)S(1)}, bf16[12,192,384]{2,1,0:T(8,128)(2,1)S(1)}) fusion(bf16[12,192,384]{2,1,0:T(8,128)(2,1)} %collective-permute-done.1, pred[]{:T(512)S(6)} %eq.41, bf16[12,384,384]{2,1,0:T(8,128)(2,1)S(1)} %constant_dynamic-update-slice_fusion, s32[]{:T(128)S(6)} %select_n.72), kind=kLoop, calls=%fused_computation.2 | loop fusion | flops 1769472 | bytes 7077893 | tf_op jit(solution)/shard_map/jit(_where)/select_n | solution.py:842
  85.5 0.4 maximum_bitcast_fusion
  85.9 3.9 %copy.13 = bf16[192,24,384]{2,1,0:T(8,128)(2,1)} copy(bf16[192,24,384]{2,0,1:T(8,128)(2,1)S(1)} %maximum_bitcast_fusion) | data formatting | bytes 7077888 | tf_op jit(solution)/shard_map/transpose | solution.py:844
  89.8 0.0 copy-start.6
  89.8 2.1 repack.1.early_ref
  92.0 0.0 copy-start
  92.0 1.0 copy-done
  93.0 17.9 %all-to-all-done = bf16[32,4,24,384]{3,2,1,0:T(8,128)(2,1)} async-done(((bf16[32,4,24,384]{3,2,1,0:T(8,128)(2,1)}), bf16[32,4,24,384]{3,2,1,0:T(8,128)(2,1)}, u32[]{:S(2)}, u32[]{:S(2)}) %all-to-all-start) | async-done | bytes 2359328 | tf_op jit(solution)/shard_map/all_to_all | solution.py:826
  110.9 0.0 copy-done.6
  110.9 0.8 jit_solution_.3.twiddle_ref
  111.7 6.1 %spectral_filter.3 = bf16[768,384]{1,0:T(8,128)(2,1)} custom-call(bf16[3072,384]{1,0:T(8,128)(2,1)} %bitcast.5.late_ref, bf16[12,128,384]{2,1,0:T(8,128)(2,1)} %copy-done, bf16[12,2,384,256]{3,2,1,0:T(8,128)(2,1)} %symmetric_filter.1.g_ref, bf16[384,512]{1,0:T(8,128)(2,1)} %pad_maximum_fusion.row_table_ref, bf16[256,256]{1,0:T(8,128)(2,1)} %maximum_maximum_fusion.fwd_ref, ...), custom_call_target="tpu_custom_call" | custom-call | flops 1207959552 | bytes 2359296 | tf_op jit(solution)/shard_map/spectral_filter/pallas_call | solution.py:683
  117.8 4.2 %all-to-all-start.3 = ((bf16[32,24,384]{2,1,0:T(8,128)(2,1)}), bf16[32,24,384]{2,1,0:T(8,128)(2,1)S(1)}, u32[]{:S(2)}, u32[]{:S(2)}) async-start(bf16[32,24,384]{2,1,0:T(8,128)(2,1)} %bitcast.18), calls=%async_computation.3 | async-start | bytes 1179648 | tf_op jit(solution)/shard_map/all_to_all | solution.py:857
  122.0 16.2 %spectral_filter.2 = bf16[3840,384]{1,0:T(8,128)(2,1)} custom-call(bf16[3072,384]{1,0:T(8,128)(2,1)} %bitcast.5.late_ref, bf16[12,128,384]{2,1,0:T(8,128)(2,1)} %copy-done, bf16[12,2,384,256]{3,2,1,0:T(8,128)(2,1)} %symmetric_filter.1.g_ref, bf16[384,512]{1,0:T(8,128)(2,1)} %pad_maximum_fusion.row_table_ref, bf16[256,256]{1,0:T(8,128)(2,1)} %maximum_maximum_fusion.fwd_ref, ...), custom_call_target="tpu_custom_call" | custom-call | flops 6039797760 | bytes 11796480 | tf_op jit(solution)/shard_map/spectral_filter/pallas_call | solution.py:683
  138.2 0.3 all-to-all-done.3.kept_ref
  138.5 0.0 copy-start.2
  138.5 5.3 %all-to-all-start.2 = ((bf16[32,120,384]{2,1,0:T(8,128)(2,1)}), bf16[32,120,384]{2,1,0:T(8,128)(2,1)S(1)}, u32[]{:S(2)}, u32[]{:S(2)}) async-start(bf16[32,120,384]{2,1,0:T(8,128)(2,1)} %bitcast.17), calls=%async_computation.2 | async-start | bytes 5898240 | tf_op jit(solution)/shard_map/all_to_all | solution.py:857
  143.8 0.0 copy-done.2
  143.9 0.3 collective-permute-start.2
  144.2 1.3 collective-permute-done.2.other_ref
  145.5 0.7 copy-done.4
  146.2 3.4 %residual.2.refs_0_ = bf16[16,12,24,384]{3,2,1,0:T(8,128)(2,1)} custom-call(s32[1]{0:T(128)} %bitcast.place_ref, bf16[32,24,384]{2,1,0:T(8,128)(2,1)} %copy-done.2, bf16[16,24,384]{2,1,0:T(8,128)(2,1)} %copy-done.4, bf16[16,12,24,384]{3,2,1,0:T(8,128)(2,1)} %bitcast.15), custom_call_target="tpu_custom_call" | custom-call | flops 294912 | bytes 2359296 | tf_op jit(solution)/shard_map/residual/pallas_call | solution.py:742
  149.7 61.4 %all-to-all-done.2.kept_ref = bf16[32,120,384]{2,1,0:T(8,128)(2,1)S(1)} async-done(((bf16[32,120,384]{2,1,0:T(8,128)(2,1)}), bf16[32,120,384]{2,1,0:T(8,128)(2,1)S(1)}, u32[]{:S(2)}, u32[]{:S(2)}) %all-to-all-start.2) | async-done | bytes 2949152 | tf_op jit(solution)/shard_map/all_to_all | solution.py:857
  211.1 0.1 constant_dynamic-slice_fusion
  211.2 0.1 collective-permute-start.3
  211.3 3.4 %collective-permute-done.3.other_ref = bf16[16,120,384]{2,1,0:T(8,128)(2,1)} collective-permute-done((bf16[16,120,384]{2,1,0:T(8,128)(2,1)S(1)}, bf16[16,120,384]{2,1,0:T(8,128)(2,1)}, u32[]{:S(2)}, u32[]{:S(2)}) %collective-permute-start.3) | collective-permute-done | bytes 1474592 | tf_op jit(solution)/shard_map/ppermute | solution.py:764
  214.7 0.0 copy-done.1
  214.7 5.1 %residual.3 = bf16[16,12,24,384]{3,2,1,0:T(8,128)(2,1)} custom-call(s32[1]{0:T(128)} %bitcast.place_ref, bf16[32,120,384]{2,1,0:T(8,128)(2,1)} %copy-done.1, bf16[16,120,384]{2,1,0:T(8,128)(2,1)} %collective-permute-done.3.other_ref, bf16[16,12,24,384]{3,2,1,0:T(8,128)(2,1)} %bitcast.16, ...), custom_call_target="tpu_custom_call", output_to_operand_aliasing={{}: (4, {})} | custom-call | flops 1474560 | bytes 11796480 | tf_op jit(solution)/shard_map/residual/pallas_call | solution.py:742
  (8 shorter events, 0.1 us)
Async XLA Ops:
  1.2 17.2 %collective-permute-start = (bf16[384,384]{1,0:T(8,128)(2,1)S(1)}, bf16[384,384]{1,0:T(8,128)(2,1)S(1)}, u32[]{:S(2)}, u32[]{:S(2)}) collective-permute-start(bf16[384,384]{1,0:T(8,128)(2,1)S(1)} %pad_maximum_fusion.2), channel_id=1, source_target_pairs={{0,1},{1,2},{2,3},{3,4},{4,5},{5,6},{6,7},{7,8},{8,9},{9,10},{10,1... | collective-permute-start | bytes 884744 | tf_op jit(solution)/shard_map/ppermute | solution.py:18
  18.4 5.0 %copy-start.8 = (bf16[384,384]{1,0:T(8,128)(2,1)}, bf16[384,384]{1,0:T(8,128)(2,1)S(1)}, u32[]{:S(2)}) copy-start(bf16[384,384]{1,0:T(8,128)(2,1)S(1)} %collective-permute-done.refs_7_) | copy-start | bytes 884740
  18.4 34.1 %all-to-all-start.1 = ((bf16[32,2,24,384]{3,2,1,0:T(8,128)(2,1)}), bf16[32,2,24,384]{3,2,1,0:T(8,128)(2,1)}, u32[]{:S(2)}, u32[]{:S(2)}) async-start(bf16[32,2,24,384]{3,2,1,0:T(8,128)(2,1)} %get-tuple-element.21), calls=%async_computation.1 | async-start | bytes 2359296 | tf_op jit(solution)/shard_map/all_to_all | solution.py:826
  52.5 4.6 %copy-start.7 = (s32[128]{0:T(128)S(1)}, s32[128]{0:T(128)}, u32[]{:S(2)}) copy-start(s32[128]{0:T(128)} %constant.75.clone) | copy-start | bytes 1540
  52.5 58.4 %all-to-all-start = ((bf16[32,4,24,384]{3,2,1,0:T(8,128)(2,1)}), bf16[32,4,24,384]{3,2,1,0:T(8,128)(2,1)}, u32[]{:S(2)}, u32[]{:S(2)}) async-start(bf16[32,4,24,384]{3,2,1,0:T(8,128)(2,1)} %get-tuple-element.17), calls=%async_computation | async-start | bytes 4718592 | tf_op jit(solution)/shard_map/all_to_all | solution.py:826
  56.5 3.8 %copy-start.5 = (s32[384]{0:T(512)}, s32[384]{0:T(512)S(1)}, u32[]{:S(2)}) copy-start(s32[384]{0:T(512)S(1)} %iota.37) | copy-start | bytes 4612
  58.3 2.0 copy-start.3
  62.0 6.0 %slice-start = ((s32[384]{0:T(512)}), s32[256]{0:T(256)S(1)}, s32[]{:S(2)}) async-start(s32[384]{0:T(512)} %copy-done.5), calls=%async_computation.4 | async-start | bytes 2048 | tf_op jit(solution)/shard_map/slice | solution.py:482
  62.0 21.2 %collective-permute-start.1 = (bf16[12,192,384]{2,1,0:T(8,128)(2,1)}, bf16[12,192,384]{2,1,0:T(8,128)(2,1)}, u32[]{:S(2)}, u32[]{:S(2)}) collective-permute-start(bf16[12,192,384]{2,1,0:T(8,128)(2,1)} %constant_dynamic-slice_fusion.2), channel_id=1, source_target_pairs={{0,16},{16,0},{1,17},{17,1},{2,18},{18,2},{3,19},{19,3},{4,20},{20... | collective-permute-start | bytes 5308424 | tf_op jit(solution)/shard_map/ppermute | solution.py:764
  89.8 21.0 %copy-start.6 = (f32[4,128]{1,0:T(4,128)S(1)}, f32[4,128]{1,0:T(4,128)}, u32[]{:S(2)}) copy-start(f32[4,128]{1,0:T(4,128)} %constant.76.clone) | copy-start | bytes 6148
  92.0 1.0 copy-start
  117.8 20.7 %all-to-all-start.3 = ((bf16[32,24,384]{2,1,0:T(8,128)(2,1)}), bf16[32,24,384]{2,1,0:T(8,128)(2,1)S(1)}, u32[]{:S(2)}, u32[]{:S(2)}) async-start(bf16[32,24,384]{2,1,0:T(8,128)(2,1)} %bitcast.18), calls=%async_computation.3 | async-start | bytes 1179648 | tf_op jit(solution)/shard_map/all_to_all | solution.py:857
  138.5 5.3 %copy-start.2 = (bf16[32,24,384]{2,1,0:T(8,128)(2,1)}, bf16[32,24,384]{2,1,0:T(8,128)(2,1)S(1)}, u32[]{:S(2)}) copy-start(bf16[32,24,384]{2,1,0:T(8,128)(2,1)S(1)} %all-to-all-done.3.kept_ref) | copy-start | bytes 1769476
  138.5 72.6 %all-to-all-start.2 = ((bf16[32,120,384]{2,1,0:T(8,128)(2,1)}), bf16[32,120,384]{2,1,0:T(8,128)(2,1)S(1)}, u32[]{:S(2)}, u32[]{:S(2)}) async-start(bf16[32,120,384]{2,1,0:T(8,128)(2,1)} %bitcast.17), calls=%async_computation.2 | async-start | bytes 5898240 | tf_op jit(solution)/shard_map/all_to_all | solution.py:857
  143.9 1.6 collective-permute-start.2
  145.5 0.7 copy-start.4
  211.1 3.6 %copy-start.1 = (bf16[32,120,384]{2,1,0:T(8,128)(2,1)}, bf16[32,120,384]{2,1,0:T(8,128)(2,1)S(1)}, u32[]{:S(2)}) copy-start(bf16[32,120,384]{2,1,0:T(8,128)(2,1)S(1)} %all-to-all-done.2.kept_ref) | copy-start | bytes 8847364
  211.2 3.5 %collective-permute-start.3 = (bf16[16,120,384]{2,1,0:T(8,128)(2,1)S(1)}, bf16[16,120,384]{2,1,0:T(8,128)(2,1)}, u32[]{:S(2)}, u32[]{:S(2)}) collective-permute-start(bf16[16,120,384]{2,1,0:T(8,128)(2,1)S(1)} %constant_dynamic-slice_fusion), channel_id=1, source_target_pairs={{0,16},{16,0},{1,17},{17,1},{2,18},{18,2},{3,19},{19,3},{4,20},{20... | collective-permute-start | bytes 4423688 | tf_op jit(solution)/shard_map/ppermute | solution.py:764

commit v8 on v7

--- a/solution.py
+++ b/solution.py
@@ -518,8 +518,9 @@
 HALF_ROOT = math.sqrt(3.0) / 2.0
 
 
-def repack_kernel(devices, early_ref, out_ref, held):
+def repack_kernel(devices, early_ref, twiddle_ref, out_ref, turn_ref, held):
     group, length = out_ref.shape[:2]
+    turn_ref[...] = twiddle_ref[...]
     rows = length // devices
     to_lane_tiles(held, slice(None), early_ref[...].astype(jnp.float32))
     for k in range(group):
@@ -528,18 +529,21 @@
             out_ref[k, r * devices : (r + 1) * devices] = values.astype(jnp.bfloat16)
 
 
-def repack(early, group, devices):
+def repack(early, twiddle, group, devices):
     length, cols = early.shape
     return pl.pallas_call(
         functools.partial(repack_kernel, devices),
-        out_shape=jax.ShapeDtypeStruct((group, length // group, cols), jnp.bfloat16),
+        out_shape=[
+            jax.ShapeDtypeStruct((group, length // group, cols), jnp.bfloat16),
+            jax.ShapeDtypeStruct(twiddle.shape, twiddle.dtype),
+        ],
         scratch_shapes=[pltpu.VMEM((cols // 128, length, 128), jnp.float32)],
-        compiler_params=pltpu.CompilerParams(vmem_limit_bytes=VMEM_BYTES // 4),
+        compiler_params=pltpu.CompilerParams(vmem_limit_bytes=VMEM_BYTES),
         cost_estimate=pl.CostEstimate(
             flops=length * cols, bytes_accessed=4 * length * cols, transcendentals=0
         ),
         name="repack",
-    )(early)
+    )(early, twiddle)
 
 
 def thirds(values, sign):
@@ -723,7 +727,7 @@
 def add_residual(place, returned, other, features, previous, first, count):
     halves, span, cols = other.shape
     group, rows = features.shape[1:3]
-    groups = 4 if halves % 4 == 0 else 1
+    groups = 8 if halves % 8 == 0 else 1
     steps = halves // groups
     operands = [returned, other, features]
     in_specs = [
@@ -810,7 +814,11 @@
     half_channels = channels // 2
     width = -(-(field_cols // 2 + 1) // 128) * 128
 
-    arriving = from_behind(lower_half(aerial_patch_grid[-1]), "tile", 1)
+    arriving = lax.ppermute(
+        lower_half(aerial_patch_grid[-1]),
+        ("section", "tile"),
+        [(i, i + 1) for i in range(lax.axis_size("tile") - 1)],
+    )
     sources = weight_sources(*arguments[1:8])
     pairs = rows // 2
     early = max(pairs // 3, 1)
@@ -828,13 +836,14 @@
         )
         for normed in (normed_early, normed_late)
     ]
-    early_fields = repack(spread[0], group, devices)
     late_fields = spread[1]
     features = jnp.concatenate([feat_late, feat_early], axis=0)
 
     channel_place = jnp.reshape(section * group, (1,)).astype(jnp.int32)
     symmetric = symmetric_filter(spectral_filter, channel_place, group, width)
-    tables = filter_tables(full_rows, field_cols, width, devices)
+    *tables, twiddle = filter_tables(full_rows, field_cols, width, devices)
+    early_fields, twiddle = repack(spread[0], twiddle, group, devices)
+    tables.append(twiddle)
 
     own = lax.dynamic_slice_in_dim(features, section * half_channels, half_channels, 1)
     sent = lax.dynamic_slice_in_dim(features, (1 - section) * half_channels, half_channels, 1)

time: 221 us -> 219 us (level)
  no operation moved by 1% of the time
where the time goes in v8:
time: 219 us; the launch traced here: 218 us
  waiting for transfers between devices  93.3 us (43%)
  Pallas kernels  78.9 us (36%)
  starting transfers between devices  23.7 us (11%)
  other arithmetic  11.4 us (5%)
  local copies, waits for them, and re-layouts  10.6 us (5%)
    all_to_all x2, waiting for transfers between devices, local(): lax.all_to_all(made, DEVICES, split_axis=0, concat_axis=0, tiled=True)  63 us
    pallas_call x2, Pallas kernels, stem(): pl.pallas_call(functools.partial(stem_kernel, kind), grid=(steps,), in_sp...  32.7 us
    all_to_all x2, waiting for transfers between devices, local(): lax.all_to_all(normed, DEVICES, split_axis=0, concat_axis=0, tiled=True)  25.6 us
    pallas_call x2, Pallas kernels, filter_channels(): pl.pallas_call(functools.partial(filter_kernel, first, devices, 1.0 / (fu...  22.3 us
    pallas_call x1, Pallas kernels, symmetric_filter(): pl.pallas_call(symmetric_kernel, grid_spec=pltpu.PrefetchScalarGridSpec(n...  14.2 us
    all_to_all x2, starting transfers between devices, local(): lax.all_to_all(made, DEVICES, split_axis=0, concat_axis=0, tiled=True)  9.48 us
    all_to_all x2, starting transfers between devices, local(): lax.all_to_all(normed, DEVICES, split_axis=0, concat_axis=0, tiled=True)  8.97 us
    pallas_call x2, Pallas kernels, add_residual(): pl.pallas_call(functools.partial(residual_kernel, count), grid_spec=pltpu...  6.43 us
  transfers between devices with their start and end apart: 8, of which 6 were waited for; matrix products, arithmetic and copies ran while one was open for 9% of the time, Pallas kernels for 31%

profile of v8, /device:TPU:0, one launch (start us, length us, event | category | flops | bytes accessed | tf_op | source)
XLA Modules:
  0.0 218.1 jit_solution(4855994139298104554)
XLA Ops:
  0.0 1.1 slice_bitcast_fusion
  1.1 0.1 fusion.34
  1.2 4.9 %collective-permute-start = (bf16[384,384]{1,0:T(8,128)(2,1)S(1)}, bf16[384,384]{1,0:T(8,128)(2,1)S(1)}, u32[]{:S(2)}, u32[]{:S(2)}) collective-permute-start(bf16[384,384]{1,0:T(8,128)(2,1)S(1)} %pad_maximum_fusion.2), channel_id=1, source_target_pairs={{0,1},{1,2},{2,3},{3,4},{4,5},{5,6},{6,7},{7,8},{8,9},{9,10},{10,1... | collective-permute-start | bytes 884744 | tf_op jit(solution)/shard_map/ppermute | solution.py:817
  6.1 12.3 %stem.2 = (bf16[32,2,24,384]{3,2,1,0:T(8,128)(2,1)}, bf16[4,384,384]{2,1,0:T(8,128)(2,1)}) custom-call(bf16[24,384,768]{2,1,0:T(8,128)(2,1)} %above_ref.3, bf16[24,384,768]{2,1,0:T(8,128)(2,1)} %above_ref.3, bf16[48,96]{1,0:T(8,128)(2,1)} %bitcast.23, f32[96]{0:T(128)} %refs_1_.3, bf16[384,192]{1,0:T(8,128)(2,1)} %bitcast.21, f32[192]{0:T(256)} %refs_3_.3, ...), custom_call_target="tpu_custom_call" | custom-call | flops 8078229504 | bytes 4608000 | tf_op jit(solution)/shard_map/stem/pallas_call | solution.py:441
  18.4 0.0 collective-permute-done.refs_7_
  18.4 0.0 copy-start.7
  18.4 5.0 %all-to-all-start.1 = ((bf16[32,2,24,384]{3,2,1,0:T(8,128)(2,1)}), bf16[32,2,24,384]{3,2,1,0:T(8,128)(2,1)}, u32[]{:S(2)}, u32[]{:S(2)}) async-start(bf16[32,2,24,384]{3,2,1,0:T(8,128)(2,1)} %get-tuple-element.23), calls=%async_computation.1 | async-start | bytes 2359296 | tf_op jit(solution)/shard_map/all_to_all | solution.py:834
  23.4 0.0 copy-done.7
  23.4 20.4 %stem.3 = (bf16[32,4,24,384]{3,2,1,0:T(8,128)(2,1)}, bf16[8,384,384]{2,1,0:T(8,128)(2,1)}) custom-call(bf16[24,384,768]{2,1,0:T(8,128)(2,1)} %above_ref.3, bf16[24,384,768]{2,1,0:T(8,128)(2,1)} %above_ref.3, bf16[48,96]{1,0:T(8,128)(2,1)} %bitcast.24, f32[96]{0:T(128)} %refs_1_.3, bf16[384,192]{1,0:T(8,128)(2,1)} %bitcast.22, f32[192]{0:T(256)} %refs_3_.3, ...), custom_call_target="tpu_custom_call" | custom-call | flops 16156459008 | bytes 9216000 | tf_op jit(solution)/shard_map/stem/pallas_call | solution.py:441
  43.9 8.6 %all-to-all-done.1 = bf16[32,2,24,384]{3,2,1,0:T(8,128)(2,1)} async-done(((bf16[32,2,24,384]{3,2,1,0:T(8,128)(2,1)}), bf16[32,2,24,384]{3,2,1,0:T(8,128)(2,1)}, u32[]{:S(2)}, u32[]{:S(2)}) %all-to-all-start.1) | async-done | bytes 1179680 | tf_op jit(solution)/shard_map/all_to_all | solution.py:834
  52.5 0.0 copy-start.6
  52.5 3.9 %all-to-all-start = ((bf16[32,4,24,384]{3,2,1,0:T(8,128)(2,1)}), bf16[32,4,24,384]{3,2,1,0:T(8,128)(2,1)}, u32[]{:S(2)}, u32[]{:S(2)}) async-start(bf16[32,4,24,384]{3,2,1,0:T(8,128)(2,1)} %get-tuple-element.19), calls=%async_computation | async-start | bytes 4718592 | tf_op jit(solution)/shard_map/all_to_all | solution.py:834
  56.5 0.0 copy-start.4
  56.5 0.3 fusion.29
  56.8 0.3 sine_convert_fusion.1
  57.0 0.0 copy-done.6
  57.1 0.3 fusion.30
  57.3 0.3 sine_convert_fusion.2
  57.6 0.7 maximum_maximum_fusion.fwd_ref
  58.3 0.0 copy-start.2
  58.3 2.0 constant_dynamic-update-slice_fusion.1
  60.3 0.0 copy-done.4
  60.3 0.0 copy-done.2
  60.3 0.2 constant_dynamic-update-slice_fusion
  60.6 1.5 constant_dynamic-slice_fusion.2
  62.0 0.0 slice-start
  62.0 0.0 collective-permute-start.1
  62.1 0.7 maximum_maximum_fusion.1.inv_ref
  62.7 1.0 fusion.8.turn_u_ref
  63.7 2.5 %sine_convert_fusion = (bf16[384,384]{1,0:T(8,128)(2,1)S(1)}, bf16[384,384]{1,0:T(8,128)(2,1)S(1)}) fusion(), kind=kLoop, calls=%fused_computation.9 | loop fusion | flops 1622016 | bytes 589824 | tf_op jit(solution)/shard_map/convert_element_type | solution.py:26
  66.3 0.8 pad_maximum_fusion.row_table_ref
  67.1 0.1 slice_multiply_fusion
  67.2 0.8 pad_maximum_fusion.1.back_ref
  68.0 0.0 slice-done
  68.0 0.9 fusion.14.turn_w_ref
  69.0 14.2 %symmetric_filter.1.g_ref = bf16[12,2,384,256]{3,2,1,0:T(8,128)(2,1)} custom-call(s32[1]{0:T(128)} %bitcast.9.place_ref, bf16[24,2,384,384]{3,2,1,0:T(8,128)(2,1)} %f_ref.1, bf16[384,256]{1,0:T(8,128)(2,1)} %fusion.14.turn_w_ref, bf16[384,384]{1,0:T(8,128)(2,1)} %fusion.8.turn_u_ref), custom_call_target="tpu_custom_call" | custom-call | flops 3623878656 | bytes 16515072 | tf_op jit(solution)/shard_map/symmetric_filter/pallas_call | solution.py:483
  83.2 0.0 collective-permute-done.1
  83.2 2.3 %broadcast_select_fusion.1 = (bf16[12,192,384]{2,1,0:T(8,128)(2,1)S(1)}, bf16[12,192,384]{2,1,0:T(8,128)(2,1)S(1)}) fusion(bf16[12,192,384]{2,1,0:T(8,128)(2,1)} %collective-permute-done.1, pred[]{:T(512)S(6)} %eq.41, bf16[12,384,384]{2,1,0:T(8,128)(2,1)S(1)} %constant_dynamic-update-slice_fusion, s32[]{:T(128)S(6)} %select_n.72), kind=kLoop, calls=%fused_computation.2 | loop fusion | flops 1769472 | bytes 7077893 | tf_op jit(solution)/shard_map/jit(_where)/select_n | solution.py:851
  85.5 0.4 maximum_bitcast_fusion
  85.9 0.0 copy-start.5
  85.9 3.9 %copy.13 = bf16[192,24,384]{2,1,0:T(8,128)(2,1)} copy(bf16[192,24,384]{2,0,1:T(8,128)(2,1)S(1)} %maximum_bitcast_fusion) | data formatting | bytes 7077888 | tf_op jit(solution)/shard_map/transpose | solution.py:853
  89.9 0.0 copy-done.5
  89.9 0.8 jit_solution_.3.twiddle_ref
  90.7 3.2 %repack.1 = (bf16[12,128,384]{2,1,0:T(8,128)(2,1)}, f32[4,128,128]{2,1,0:T(8,128)}) custom-call(bf16[1536,384]{1,0:T(8,128)(2,1)} %bitcast.8.early_ref, f32[4,128,128]{2,1,0:T(8,128)} %jit_solution_.3.twiddle_ref), custom_call_target="tpu_custom_call" | custom-call | flops 589824 | bytes 2359296 | tf_op jit(solution)/shard_map/repack/pallas_call | solution.py:534
  93.9 17.0 %all-to-all-done = bf16[32,4,24,384]{3,2,1,0:T(8,128)(2,1)} async-done(((bf16[32,4,24,384]{3,2,1,0:T(8,128)(2,1)}), bf16[32,4,24,384]{3,2,1,0:T(8,128)(2,1)}, u32[]{:S(2)}, u32[]{:S(2)}) %all-to-all-start) | async-done | bytes 2359328 | tf_op jit(solution)/shard_map/all_to_all | solution.py:834
  110.9 6.1 %spectral_filter.3 = bf16[768,384]{1,0:T(8,128)(2,1)} custom-call(bf16[3072,384]{1,0:T(8,128)(2,1)} %bitcast.5.late_ref, bf16[12,128,384]{2,1,0:T(8,128)(2,1)} %get-tuple-element.24.early_ref, bf16[12,2,384,256]{3,2,1,0:T(8,128)(2,1)} %symmetric_filter.1.g_ref, bf16[384,512]{1,0:T(8,128)(2,1)} %pad_maximum_fusion.row_table_ref, ...), custom_call_target="tpu_custom_call" | custom-call | flops 1207959552 | bytes 2359296 | tf_op jit(solution)/shard_map/spectral_filter/pallas_call | solution.py:687
  116.9 4.2 %all-to-all-start.3 = ((bf16[32,24,384]{2,1,0:T(8,128)(2,1)}), bf16[32,24,384]{2,1,0:T(8,128)(2,1)S(1)}, u32[]{:S(2)}, u32[]{:S(2)}) async-start(bf16[32,24,384]{2,1,0:T(8,128)(2,1)} %bitcast.18), calls=%async_computation.3 | async-start | bytes 1179648 | tf_op jit(solution)/shard_map/all_to_all | solution.py:866
  121.1 16.2 %spectral_filter.2 = bf16[3840,384]{1,0:T(8,128)(2,1)} custom-call(bf16[3072,384]{1,0:T(8,128)(2,1)} %bitcast.5.late_ref, bf16[12,128,384]{2,1,0:T(8,128)(2,1)} %get-tuple-element.24.early_ref, bf16[12,2,384,256]{3,2,1,0:T(8,128)(2,1)} %symmetric_filter.1.g_ref, bf16[384,512]{1,0:T(8,128)(2,1)} %pad_maximum_fusion.row_table_ref, ...), custom_call_target="tpu_custom_call" | custom-call | flops 6039797760 | bytes 11796480 | tf_op jit(solution)/shard_map/spectral_filter/pallas_call | solution.py:687
  137.3 0.3 all-to-all-done.3.kept_ref
  137.6 0.0 copy-start.1
  137.6 5.3 %all-to-all-start.2 = ((bf16[32,120,384]{2,1,0:T(8,128)(2,1)}), bf16[32,120,384]{2,1,0:T(8,128)(2,1)S(1)}, u32[]{:S(2)}, u32[]{:S(2)}) async-start(bf16[32,120,384]{2,1,0:T(8,128)(2,1)} %bitcast.17), calls=%async_computation.2 | async-start | bytes 5898240 | tf_op jit(solution)/shard_map/all_to_all | solution.py:866
  143.0 0.0 copy-done.1
  143.0 0.3 collective-permute-start.2
  143.3 1.3 collective-permute-done.2.other_ref
  144.7 0.0 copy-start.3
  144.7 0.7 copy-done.3
  145.4 2.1 residual.2.refs_0_
  147.5 62.7 %all-to-all-done.2.kept_ref = bf16[32,120,384]{2,1,0:T(8,128)(2,1)S(1)} async-done(((bf16[32,120,384]{2,1,0:T(8,128)(2,1)}), bf16[32,120,384]{2,1,0:T(8,128)(2,1)S(1)}, u32[]{:S(2)}, u32[]{:S(2)}) %all-to-all-start.2) | async-done | bytes 2949152 | tf_op jit(solution)/shard_map/all_to_all | solution.py:866
  210.2 0.0 copy-start
  210.2 0.1 constant_dynamic-slice_fusion
  210.4 0.1 collective-permute-start.3
  210.4 3.4 %collective-permute-done.3.other_ref = bf16[16,120,384]{2,1,0:T(8,128)(2,1)} collective-permute-done((bf16[16,120,384]{2,1,0:T(8,128)(2,1)S(1)}, bf16[16,120,384]{2,1,0:T(8,128)(2,1)}, u32[]{:S(2)}, u32[]{:S(2)}) %collective-permute-start.3) | collective-permute-done | bytes 1474592 | tf_op jit(solution)/shard_map/ppermute | solution.py:768
  213.8 0.0 copy-done
  213.8 4.3 %residual.3 = bf16[16,12,24,384]{3,2,1,0:T(8,128)(2,1)} custom-call(s32[1]{0:T(128)} %bitcast.place_ref, bf16[32,120,384]{2,1,0:T(8,128)(2,1)} %copy-done, bf16[16,120,384]{2,1,0:T(8,128)(2,1)} %collective-permute-done.3.other_ref, bf16[16,12,24,384]{3,2,1,0:T(8,128)(2,1)} %bitcast.16, ...), custom_call_target="tpu_custom_call", output_to_operand_aliasing={{}: (4, {})} | custom-call | flops 1474560 | bytes 11796480 | tf_op jit(solution)/shard_map/residual/pallas_call | solution.py:746
  (6 shorter events, 0.1 us)
Async XLA Ops:
  1.2 17.2 %collective-permute-start = (bf16[384,384]{1,0:T(8,128)(2,1)S(1)}, bf16[384,384]{1,0:T(8,128)(2,1)S(1)}, u32[]{:S(2)}, u32[]{:S(2)}) collective-permute-start(bf16[384,384]{1,0:T(8,128)(2,1)S(1)} %pad_maximum_fusion.2), channel_id=1, source_target_pairs={{0,1},{1,2},{2,3},{3,4},{4,5},{5,6},{6,7},{7,8},{8,9},{9,10},{10,1... | collective-permute-start | bytes 884744 | tf_op jit(solution)/shard_map/ppermute | solution.py:817
  18.4 5.0 %copy-start.7 = (bf16[384,384]{1,0:T(8,128)(2,1)}, bf16[384,384]{1,0:T(8,128)(2,1)S(1)}, u32[]{:S(2)}) copy-start(bf16[384,384]{1,0:T(8,128)(2,1)S(1)} %collective-permute-done.refs_7_) | copy-start | bytes 884740
  18.4 34.1 %all-to-all-start.1 = ((bf16[32,2,24,384]{3,2,1,0:T(8,128)(2,1)}), bf16[32,2,24,384]{3,2,1,0:T(8,128)(2,1)}, u32[]{:S(2)}, u32[]{:S(2)}) async-start(bf16[32,2,24,384]{3,2,1,0:T(8,128)(2,1)} %get-tuple-element.23), calls=%async_computation.1 | async-start | bytes 2359296 | tf_op jit(solution)/shard_map/all_to_all | solution.py:834
  52.5 4.6 %copy-start.6 = (s32[128]{0:T(128)S(1)}, s32[128]{0:T(128)}, u32[]{:S(2)}) copy-start(s32[128]{0:T(128)} %constant.75.clone) | copy-start | bytes 1540
  52.5 58.4 %all-to-all-start = ((bf16[32,4,24,384]{3,2,1,0:T(8,128)(2,1)}), bf16[32,4,24,384]{3,2,1,0:T(8,128)(2,1)}, u32[]{:S(2)}, u32[]{:S(2)}) async-start(bf16[32,4,24,384]{3,2,1,0:T(8,128)(2,1)} %get-tuple-element.19), calls=%async_computation | async-start | bytes 4718592 | tf_op jit(solution)/shard_map/all_to_all | solution.py:834
  56.5 3.8 %copy-start.4 = (s32[384]{0:T(512)}, s32[384]{0:T(512)S(1)}, u32[]{:S(2)}) copy-start(s32[384]{0:T(512)S(1)} %iota.37) | copy-start | bytes 4612
  58.3 2.0 copy-start.2
  62.0 6.0 %slice-start = ((s32[384]{0:T(512)}), s32[256]{0:T(256)S(1)}, s32[]{:S(2)}) async-start(s32[384]{0:T(512)} %copy-done.4), calls=%async_computation.4 | async-start | bytes 2048 | tf_op jit(solution)/shard_map/slice | solution.py:482
  62.0 21.2 %collective-permute-start.1 = (bf16[12,192,384]{2,1,0:T(8,128)(2,1)}, bf16[12,192,384]{2,1,0:T(8,128)(2,1)}, u32[]{:S(2)}, u32[]{:S(2)}) collective-permute-start(bf16[12,192,384]{2,1,0:T(8,128)(2,1)} %constant_dynamic-slice_fusion.2), channel_id=1, source_target_pairs={{0,16},{16,0},{1,17},{17,1},{2,18},{18,2},{3,19},{19,3},{4,20},{20... | collective-permute-start | bytes 5308424 | tf_op jit(solution)/shard_map/ppermute | solution.py:768
  85.9 3.9 %copy-start.5 = (f32[4,128]{1,0:T(4,128)S(1)}, f32[4,128]{1,0:T(4,128)}, u32[]{:S(2)}) copy-start(f32[4,128]{1,0:T(4,128)} %constant.76.clone) | copy-start | bytes 6148
  116.9 20.7 %all-to-all-start.3 = ((bf16[32,24,384]{2,1,0:T(8,128)(2,1)}), bf16[32,24,384]{2,1,0:T(8,128)(2,1)S(1)}, u32[]{:S(2)}, u32[]{:S(2)}) async-start(bf16[32,24,384]{2,1,0:T(8,128)(2,1)} %bitcast.18), calls=%async_computation.3 | async-start | bytes 1179648 | tf_op jit(solution)/shard_map/all_to_all | solution.py:866
  137.6 5.3 %copy-start.1 = (bf16[32,24,384]{2,1,0:T(8,128)(2,1)}, bf16[32,24,384]{2,1,0:T(8,128)(2,1)S(1)}, u32[]{:S(2)}) copy-start(bf16[32,24,384]{2,1,0:T(8,128)(2,1)S(1)} %all-to-all-done.3.kept_ref) | copy-start | bytes 1769476
  137.6 72.6 %all-to-all-start.2 = ((bf16[32,120,384]{2,1,0:T(8,128)(2,1)}), bf16[32,120,384]{2,1,0:T(8,128)(2,1)S(1)}, u32[]{:S(2)}, u32[]{:S(2)}) async-start(bf16[32,120,384]{2,1,0:T(8,128)(2,1)} %bitcast.17), calls=%async_computation.2 | async-start | bytes 5898240 | tf_op jit(solution)/shard_map/all_to_all | solution.py:866
  143.0 1.6 collective-permute-start.2
  144.7 0.7 copy-start.3
  210.2 3.6 %copy-start = (bf16[32,120,384]{2,1,0:T(8,128)(2,1)}, bf16[32,120,384]{2,1,0:T(8,128)(2,1)S(1)}, u32[]{:S(2)}) copy-start(bf16[32,120,384]{2,1,0:T(8,128)(2,1)S(1)} %all-to-all-done.2.kept_ref) | copy-start | bytes 8847364
  210.4 3.5 %collective-permute-start.3 = (bf16[16,120,384]{2,1,0:T(8,128)(2,1)S(1)}, bf16[16,120,384]{2,1,0:T(8,128)(2,1)}, u32[]{:S(2)}, u32[]{:S(2)}) collective-permute-start(bf16[16,120,384]{2,1,0:T(8,128)(2,1)S(1)} %constant_dynamic-slice_fusion), channel_id=1, source_target_pairs={{0,16},{16,0},{1,17},{17,1},{2,18},{18,2},{3,19},{19,3},{4,20},{20... | collective-permute-start | bytes 4423688 | tf_op jit(solution)/shard_map/ppermute | solution.py:768

commit v9 on v8

--- a/solution.py
+++ b/solution.py
@@ -306,7 +306,7 @@
     bands = depth // 256
     channels = w3_ref.shape[0]
     merged = w2_ref.shape[0]
-    group = normed_ref.shape[2] // rows
+    group = normed_ref.shape[2] // 2
     cells = rows * cols
 
     @pl.when(step == 0)
@@ -402,19 +402,26 @@
     pair = 2 * group
     index = lax.broadcasted_iota(jnp.int32, (pair, cols), 0)
     for t in range(channels // pair):
-        one = normed[pair * t : pair * (t + 1), :cols]
-        two = normed[pair * t : pair * (t + 1), cols:]
-        normed_ref[2 * t, 0] = jnp.where(index < group, one, pltpu.roll(two, group, 0)).astype(
-            jnp.bfloat16
-        )
-        normed_ref[2 * t + 1, 0] = jnp.where(
-            index < group, pltpu.roll(one, group, 0), two
-        ).astype(jnp.bfloat16)
-
-
-def stem(kind, image, weights, first, steps, devices, extra=()):
+        for p in range(rows // 2):
+            span = slice(pair * t, pair * (t + 1))
+            one = normed[span, 2 * p * cols : (2 * p + 1) * cols]
+            two = normed[span, (2 * p + 1) * cols : (2 * p + 2) * cols]
+            normed_ref[2 * t, p] = jnp.where(
+                index < group, one, pltpu.roll(two, group, 0)
+            ).astype(jnp.bfloat16)
+            normed_ref[2 * t + 1, p] = jnp.where(
+                index < group, pltpu.roll(one, group, 0), two
+            ).astype(jnp.bfloat16)
+
+
+def stem(kind, image, weights, first, pairs, devices, extra=()):
     cols, depth = image.shape[1:]
-    rows = 2 * steps
+    rows = 2 * pairs
+    per_step = 1
+    if kind == "first" and all(n % 2 == 0 for n in (pairs, first, image.shape[0] // 4)):
+        per_step = 2
+    steps = pairs // per_step
+    span = 2 * per_step
     shapes = weight_shapes(weights)
     channels, third_depth = shapes[2].shape
     merged = shapes[1].shape[0]
@@ -429,11 +436,11 @@
     operands = list(weights) + list(extra)
     in_specs = [whole(a) for a in weights]
     out_specs = [
-        pl.BlockSpec((devices, 1, 2 * group, cols), lambda i: (0, i, 0, 0)),
-        pl.BlockSpec((2, channels, cols), lambda i: (i, 0, 0)),
+        pl.BlockSpec((devices, per_step, 2 * group, cols), lambda i: (0, i, 0, 0)),
+        pl.BlockSpec((span, channels, cols), lambda i: (i, 0, 0)),
     ]
     out_shape = [
-        jax.ShapeDtypeStruct((devices, steps, 2 * group, cols), jnp.bfloat16),
+        jax.ShapeDtypeStruct((devices, pairs, 2 * group, cols), jnp.bfloat16),
         jax.ShapeDtypeStruct((rows, channels, cols), jnp.bfloat16),
     ]
     in_specs += [whole(a) for a in extra]
@@ -442,7 +449,10 @@
         functools.partial(stem_kernel, kind),
         grid=(steps,),
         in_specs=[
-            pl.BlockSpec((2, cols, depth), lambda i: (section_pairs() + first + i, 0, 0)),
+            pl.BlockSpec(
+                (span, cols, depth),
+                lambda i: ((section_pairs() + first) // per_step + i, 0, 0),
+            ),
             pl.BlockSpec(
                 (1, cols, depth),
                 lambda i: (jnp.maximum(2 * (section_pairs() + first) - 1, 0), 0, 0),
@@ -451,7 +461,7 @@
         + in_specs,
         out_specs=out_specs,
         scratch_shapes=[pltpu.VMEM(a.shape, a.dtype) for a in shapes]
-        + [pltpu.VMEM((third_depth, 2 * cols), jnp.bfloat16)],
+        + [pltpu.VMEM((third_depth, span * cols), jnp.bfloat16)],
         out_shape=out_shape,
         compiler_params=pltpu.CompilerParams(vmem_limit_bytes=VMEM_BYTES + 3 * 1024 * 1024),
         cost_estimate=pl.CostEstimate(
@@ -522,7 +532,7 @@
     group, length = out_ref.shape[:2]
     turn_ref[...] = twiddle_ref[...]
     rows = length // devices
-    to_lane_tiles(held, slice(None), early_ref[...].astype(jnp.float32))
+    to_lane_tiles(held, slice(0, early_ref.shape[0]), early_ref[...].astype(jnp.float32))
     for k in range(group):
         for r in range(rows):
             values = from_lane_tiles(held, pl.ds(r * group + k, devices, stride=rows * group))
@@ -537,7 +547,7 @@
             jax.ShapeDtypeStruct((group, length // group, cols), jnp.bfloat16),
             jax.ShapeDtypeStruct(twiddle.shape, twiddle.dtype),
         ],
-        scratch_shapes=[pltpu.VMEM((cols // 128, length, 128), jnp.float32)],
+        scratch_shapes=[pltpu.VMEM((cols // 128, length + length // devices, 128), jnp.float32)],
         compiler_params=pltpu.CompilerParams(vmem_limit_bytes=VMEM_BYTES),
         cost_estimate=pl.CostEstimate(
             flops=length * cols, bytes_accessed=4 * length * cols, transcendentals=0
@@ -566,15 +576,15 @@
     third = fwd_ref.shape[0] // 2
     full_rows = RADIX * third
     width = g_ref.shape[3]
-    count = made.shape[1] // full_rows
+    count = out_ref.shape[0] // full_rows
     per_step = g_ref.shape[0]
     early = early_ref.shape[1] // devices
     late = full_rows // devices - early
-    group = held.shape[1] // (late * devices)
+    group = late_ref.shape[0] // (late * devices)
 
     @pl.when(step == 0)
     def _():
-        to_lane_tiles(held, slice(None), late_ref[...].astype(jnp.float32))
+        to_lane_tiles(held, slice(0, late_ref.shape[0]), late_ref[...].astype(jnp.float32))
 
     def source_rows(k, row):
         if row >= late:
@@ -643,7 +653,7 @@
 
     @pl.when(step == pl.num_programs(0) - 1)
     def _():
-        out_ref[...] = from_lane_tiles(made, slice(None)).astype(jnp.bfloat16)
+        out_ref[...] = from_lane_tiles(made, slice(0, out_ref.shape[0])).astype(jnp.bfloat16)
 
 
 def filter_tables(full_rows, field_cols, width, devices):
@@ -698,8 +708,8 @@
         out_specs=pl.BlockSpec((full_rows * count, cols), lambda i: (0, 0)),
         out_shape=jax.ShapeDtypeStruct((full_rows * count, cols), jnp.bfloat16),
         scratch_shapes=[
-            pltpu.VMEM((cols // 128, late.shape[0], 128), jnp.float32),
-            pltpu.VMEM((cols // 128, full_rows * count, 128), jnp.float32),
+            pltpu.VMEM((cols // 128, late.shape[0] + late.shape[0] // devices, 128), jnp.float32),
+            pltpu.VMEM((cols // 128, (full_rows + 8) * count, 128), jnp.float32),
         ],
         compiler_params=pltpu.CompilerParams(vmem_limit_bytes=VMEM_BYTES),
         cost_estimate=pl.CostEstimate(
@@ -713,7 +723,7 @@
 def residual_kernel(count, place_ref, kept_ref, other_ref, feat_ref, *refs):
     out_ref, held = refs[-2:]
     groups, span, cols = kept_ref.shape
-    rows = held.shape[1] // count
+    rows = 2 * span // count
     own = pl.multiple_of(place_ref[0] * span, 8)
     far = pl.multiple_of((1 - place_ref[0]) * span, 8)
     for g in range(groups):
@@ -750,7 +760,7 @@
             grid=(steps,),
             in_specs=in_specs,
             out_specs=in_specs[2],
-            scratch_shapes=[pltpu.VMEM((cols // 128, rows * count, 128), jnp.float32)],
+            scratch_shapes=[pltpu.VMEM((cols // 128, (rows + 8) * count, 128), jnp.float32)],
         ),
         out_shape=jax.ShapeDtypeStruct(features.shape, jnp.bfloat16),
         input_output_aliases=aliases,

time: 219 us -> 218 us (level)
  no operation moved by 1% of the time
where the time goes in v9:
time: 218 us; the launch traced here: 217 us
  waiting for transfers between devices  93.1 us (43%)
  Pallas kernels  78 us (36%)
  starting transfers between devices  23.9 us (11%)
  other arithmetic  11.4 us (5%)
  local copies, waits for them, and re-layouts  10.6 us (5%)
    all_to_all x2, waiting for transfers between devices, local(): lax.all_to_all(made, DEVICES, split_axis=0, concat_axis=0, tiled=True)  63 us
    pallas_call x2, Pallas kernels, stem(): pl.pallas_call(functools.partial(stem_kernel, kind), grid=(steps,), in_sp...  31.9 us
    all_to_all x2, waiting for transfers between devices, local(): lax.all_to_all(normed, DEVICES, split_axis=0, concat_axis=0, tiled=True)  25.4 us
    pallas_call x2, Pallas kernels, filter_channels(): pl.pallas_call(functools.partial(filter_kernel, first, devices, 1.0 / (fu...  22.3 us
    pallas_call x1, Pallas kernels, symmetric_filter(): pl.pallas_call(symmetric_kernel, grid_spec=pltpu.PrefetchScalarGridSpec(n...  14.2 us
    all_to_all x2, starting transfers between devices, local(): lax.all_to_all(made, DEVICES, split_axis=0, concat_axis=0, tiled=True)  9.5 us
    all_to_all x2, starting transfers between devices, local(): lax.all_to_all(normed, DEVICES, split_axis=0, concat_axis=0, tiled=True)  9.19 us
    pallas_call x2, Pallas kernels, add_residual(): pl.pallas_call(functools.partial(residual_kernel, count), grid_spec=pltpu...  6.44 us
  transfers between devices with their start and end apart: 8, of which 6 were waited for; matrix products, arithmetic and copies ran while one was open for 9% of the time, Pallas kernels for 31%

profile of v9, /device:TPU:0, one launch (start us, length us, event | category | flops | bytes accessed | tf_op | source)
XLA Modules:
  0.0 217.3 jit_solution(7827669514634676139)
XLA Ops:
  0.0 1.1 slice_bitcast_fusion
  1.1 0.1 fusion.34
  1.2 4.9 %collective-permute-start = (bf16[384,384]{1,0:T(8,128)(2,1)S(1)}, bf16[384,384]{1,0:T(8,128)(2,1)S(1)}, u32[]{:S(2)}, u32[]{:S(2)}) collective-permute-start(bf16[384,384]{1,0:T(8,128)(2,1)S(1)} %pad_maximum_fusion.2), channel_id=1, source_target_pairs={{0,1},{1,2},{2,3},{3,4},{4,5},{5,6},{6,7},{7,8},{8,9},{9,10},{10,1... | collective-permute-start | bytes 884744 | tf_op jit(solution)/shard_map/ppermute | solution.py:827
  6.1 11.4 %stem.2 = (bf16[32,2,24,384]{3,2,1,0:T(8,128)(2,1)}, bf16[4,384,384]{2,1,0:T(8,128)(2,1)}) custom-call(bf16[24,384,768]{2,1,0:T(8,128)(2,1)} %above_ref.3, bf16[24,384,768]{2,1,0:T(8,128)(2,1)} %above_ref.3, bf16[48,96]{1,0:T(8,128)(2,1)} %bitcast.23, f32[96]{0:T(128)} %refs_1_.3, bf16[384,192]{1,0:T(8,128)(2,1)} %bitcast.21, f32[192]{0:T(256)} %refs_3_.3, ...), custom_call_target="tpu_custom_call" | custom-call | flops 8078229504 | bytes 4608000 | tf_op jit(solution)/shard_map/stem/pallas_call | solution.py:448
  17.5 0.0 collective-permute-done.refs_7_
  17.5 0.0 copy-start.7
  17.5 5.2 %all-to-all-start.1 = ((bf16[32,2,24,384]{3,2,1,0:T(8,128)(2,1)}), bf16[32,2,24,384]{3,2,1,0:T(8,128)(2,1)}, u32[]{:S(2)}, u32[]{:S(2)}) async-start(bf16[32,2,24,384]{3,2,1,0:T(8,128)(2,1)} %get-tuple-element.23), calls=%async_computation.1 | async-start | bytes 2359296 | tf_op jit(solution)/shard_map/all_to_all | solution.py:844
  22.8 0.0 copy-done.7
  22.8 20.4 %stem.3 = (bf16[32,4,24,384]{3,2,1,0:T(8,128)(2,1)}, bf16[8,384,384]{2,1,0:T(8,128)(2,1)}) custom-call(bf16[24,384,768]{2,1,0:T(8,128)(2,1)} %above_ref.3, bf16[24,384,768]{2,1,0:T(8,128)(2,1)} %above_ref.3, bf16[48,96]{1,0:T(8,128)(2,1)} %bitcast.24, f32[96]{0:T(128)} %refs_1_.3, bf16[384,192]{1,0:T(8,128)(2,1)} %bitcast.22, f32[192]{0:T(256)} %refs_3_.3, ...), custom_call_target="tpu_custom_call" | custom-call | flops 16156459008 | bytes 9216000 | tf_op jit(solution)/shard_map/stem/pallas_call | solution.py:448
  43.2 8.4 %all-to-all-done.1 = bf16[32,2,24,384]{3,2,1,0:T(8,128)(2,1)} async-done(((bf16[32,2,24,384]{3,2,1,0:T(8,128)(2,1)}), bf16[32,2,24,384]{3,2,1,0:T(8,128)(2,1)}, u32[]{:S(2)}, u32[]{:S(2)}) %all-to-all-start.1) | async-done | bytes 1179680 | tf_op jit(solution)/shard_map/all_to_all | solution.py:844
  51.6 0.0 copy-start.6
  51.7 4.0 %all-to-all-start = ((bf16[32,4,24,384]{3,2,1,0:T(8,128)(2,1)}), bf16[32,4,24,384]{3,2,1,0:T(8,128)(2,1)}, u32[]{:S(2)}, u32[]{:S(2)}) async-start(bf16[32,4,24,384]{3,2,1,0:T(8,128)(2,1)} %get-tuple-element.19), calls=%async_computation | async-start | bytes 4718592 | tf_op jit(solution)/shard_map/all_to_all | solution.py:844
  55.7 0.0 copy-start.4
  55.7 0.3 fusion.29
  56.0 0.3 sine_convert_fusion.1
  56.2 0.0 copy-done.6
  56.2 0.3 fusion.30
  56.5 0.3 sine_convert_fusion.2
  56.8 0.7 maximum_maximum_fusion.fwd_ref
  57.5 0.0 copy-start.2
  57.5 2.0 constant_dynamic-update-slice_fusion.1
  59.5 0.0 copy-done.4
  59.5 0.0 copy-done.2
  59.5 0.2 constant_dynamic-update-slice_fusion
  59.7 1.5 constant_dynamic-slice_fusion.2
  61.2 0.0 slice-start
  61.2 0.0 collective-permute-start.1
  61.3 0.7 maximum_maximum_fusion.1.inv_ref
  61.9 1.0 fusion.8.turn_u_ref
  62.9 2.5 %sine_convert_fusion = (bf16[384,384]{1,0:T(8,128)(2,1)S(1)}, bf16[384,384]{1,0:T(8,128)(2,1)S(1)}) fusion(), kind=kLoop, calls=%fused_computation.9 | loop fusion | flops 1622016 | bytes 589824 | tf_op jit(solution)/shard_map/convert_element_type | solution.py:26
  65.5 0.8 pad_maximum_fusion.row_table_ref
  66.3 0.1 slice_multiply_fusion
  66.4 0.8 pad_maximum_fusion.1.back_ref
  67.2 0.0 slice-done
  67.2 0.9 fusion.14.turn_w_ref
  68.2 14.2 %symmetric_filter.1.g_ref = bf16[12,2,384,256]{3,2,1,0:T(8,128)(2,1)} custom-call(s32[1]{0:T(128)} %bitcast.9.place_ref, bf16[24,2,384,384]{3,2,1,0:T(8,128)(2,1)} %f_ref.1, bf16[384,256]{1,0:T(8,128)(2,1)} %fusion.14.turn_w_ref, bf16[384,384]{1,0:T(8,128)(2,1)} %fusion.8.turn_u_ref), custom_call_target="tpu_custom_call" | custom-call | flops 3623878656 | bytes 16515072 | tf_op jit(solution)/shard_map/symmetric_filter/pallas_call | solution.py:493
  82.4 0.0 collective-permute-done.1
  82.4 2.3 %broadcast_select_fusion.1 = (bf16[12,192,384]{2,1,0:T(8,128)(2,1)S(1)}, bf16[12,192,384]{2,1,0:T(8,128)(2,1)S(1)}) fusion(bf16[12,192,384]{2,1,0:T(8,128)(2,1)} %collective-permute-done.1, pred[]{:T(512)S(6)} %eq.41, bf16[12,384,384]{2,1,0:T(8,128)(2,1)S(1)} %constant_dynamic-update-slice_fusion, s32[]{:T(128)S(6)} %select_n.72), kind=kLoop, calls=%fused_computation.2 | loop fusion | flops 1769472 | bytes 7077893 | tf_op jit(solution)/shard_map/jit(_where)/select_n | solution.py:861
  84.7 0.4 maximum_bitcast_fusion
  85.1 0.0 copy-start.5
  85.1 3.9 %copy.13 = bf16[192,24,384]{2,1,0:T(8,128)(2,1)} copy(bf16[192,24,384]{2,0,1:T(8,128)(2,1)S(1)} %maximum_bitcast_fusion) | data formatting | bytes 7077888 | tf_op jit(solution)/shard_map/transpose | solution.py:863
  89.0 0.0 copy-done.5
  89.0 0.8 jit_solution_.3.twiddle_ref
  89.9 3.2 %repack.1 = (bf16[12,128,384]{2,1,0:T(8,128)(2,1)}, f32[4,128,128]{2,1,0:T(8,128)}) custom-call(bf16[1536,384]{1,0:T(8,128)(2,1)} %bitcast.8.early_ref, f32[4,128,128]{2,1,0:T(8,128)} %jit_solution_.3.twiddle_ref), custom_call_target="tpu_custom_call" | custom-call | flops 589824 | bytes 2359296 | tf_op jit(solution)/shard_map/repack/pallas_call | solution.py:544
  93.1 16.9 %all-to-all-done = bf16[32,4,24,384]{3,2,1,0:T(8,128)(2,1)} async-done(((bf16[32,4,24,384]{3,2,1,0:T(8,128)(2,1)}), bf16[32,4,24,384]{3,2,1,0:T(8,128)(2,1)}, u32[]{:S(2)}, u32[]{:S(2)}) %all-to-all-start) | async-done | bytes 2359328 | tf_op jit(solution)/shard_map/all_to_all | solution.py:844
  110.0 6.1 %spectral_filter.3 = bf16[768,384]{1,0:T(8,128)(2,1)} custom-call(bf16[3072,384]{1,0:T(8,128)(2,1)} %bitcast.5.late_ref, bf16[12,128,384]{2,1,0:T(8,128)(2,1)} %get-tuple-element.24.early_ref, bf16[12,2,384,256]{3,2,1,0:T(8,128)(2,1)} %symmetric_filter.1.g_ref, bf16[384,512]{1,0:T(8,128)(2,1)} %pad_maximum_fusion.row_table_ref, ...), custom_call_target="tpu_custom_call" | custom-call | flops 1207959552 | bytes 2359296 | tf_op jit(solution)/shard_map/spectral_filter/pallas_call | solution.py:697
  116.1 4.2 %all-to-all-start.3 = ((bf16[32,24,384]{2,1,0:T(8,128)(2,1)}), bf16[32,24,384]{2,1,0:T(8,128)(2,1)S(1)}, u32[]{:S(2)}, u32[]{:S(2)}) async-start(bf16[32,24,384]{2,1,0:T(8,128)(2,1)} %bitcast.18), calls=%async_computation.3 | async-start | bytes 1179648 | tf_op jit(solution)/shard_map/all_to_all | solution.py:876
  120.3 16.2 %spectral_filter.2 = bf16[3840,384]{1,0:T(8,128)(2,1)} custom-call(bf16[3072,384]{1,0:T(8,128)(2,1)} %bitcast.5.late_ref, bf16[12,128,384]{2,1,0:T(8,128)(2,1)} %get-tuple-element.24.early_ref, bf16[12,2,384,256]{3,2,1,0:T(8,128)(2,1)} %symmetric_filter.1.g_ref, bf16[384,512]{1,0:T(8,128)(2,1)} %pad_maximum_fusion.row_table_ref, ...), custom_call_target="tpu_custom_call" | custom-call | flops 6039797760 | bytes 11796480 | tf_op jit(solution)/shard_map/spectral_filter/pallas_call | solution.py:697
  136.5 0.3 all-to-all-done.3.kept_ref
  136.8 0.0 copy-start.1
  136.8 5.3 %all-to-all-start.2 = ((bf16[32,120,384]{2,1,0:T(8,128)(2,1)}), bf16[32,120,384]{2,1,0:T(8,128)(2,1)S(1)}, u32[]{:S(2)}, u32[]{:S(2)}) async-start(bf16[32,120,384]{2,1,0:T(8,128)(2,1)} %bitcast.17), calls=%async_computation.2 | async-start | bytes 5898240 | tf_op jit(solution)/shard_map/all_to_all | solution.py:876
  142.1 0.0 copy-done.1
  142.2 0.3 collective-permute-start.2
  142.5 1.3 collective-permute-done.2.other_ref
  143.8 0.0 copy-start.3
  143.8 0.7 copy-done.3
  144.5 2.1 residual.2.refs_0_
  146.6 62.7 %all-to-all-done.2.kept_ref = bf16[32,120,384]{2,1,0:T(8,128)(2,1)S(1)} async-done(((bf16[32,120,384]{2,1,0:T(8,128)(2,1)}), bf16[32,120,384]{2,1,0:T(8,128)(2,1)S(1)}, u32[]{:S(2)}, u32[]{:S(2)}) %all-to-all-start.2) | async-done | bytes 2949152 | tf_op jit(solution)/shard_map/all_to_all | solution.py:876
  209.3 0.0 copy-start
  209.3 0.1 constant_dynamic-slice_fusion
  209.5 0.1 collective-permute-start.3
  209.6 3.4 %collective-permute-done.3.other_ref = bf16[16,120,384]{2,1,0:T(8,128)(2,1)} collective-permute-done((bf16[16,120,384]{2,1,0:T(8,128)(2,1)S(1)}, bf16[16,120,384]{2,1,0:T(8,128)(2,1)}, u32[]{:S(2)}, u32[]{:S(2)}) %collective-permute-start.3) | collective-permute-done | bytes 1474592 | tf_op jit(solution)/shard_map/ppermute | solution.py:778
  213.0 0.0 copy-done
  213.0 4.3 %residual.3 = bf16[16,12,24,384]{3,2,1,0:T(8,128)(2,1)} custom-call(s32[1]{0:T(128)} %bitcast.place_ref, bf16[32,120,384]{2,1,0:T(8,128)(2,1)} %copy-done, bf16[16,120,384]{2,1,0:T(8,128)(2,1)} %collective-permute-done.3.other_ref, bf16[16,12,24,384]{3,2,1,0:T(8,128)(2,1)} %bitcast.16, ...), custom_call_target="tpu_custom_call", output_to_operand_aliasing={{}: (4, {})} | custom-call | flops 1474560 | bytes 11796480 | tf_op jit(solution)/shard_map/residual/pallas_call | solution.py:756
  (6 shorter events, 0.1 us)
Async XLA Ops:
  1.2 16.3 %collective-permute-start = (bf16[384,384]{1,0:T(8,128)(2,1)S(1)}, bf16[384,384]{1,0:T(8,128)(2,1)S(1)}, u32[]{:S(2)}, u32[]{:S(2)}) collective-permute-start(bf16[384,384]{1,0:T(8,128)(2,1)S(1)} %pad_maximum_fusion.2), channel_id=1, source_target_pairs={{0,1},{1,2},{2,3},{3,4},{4,5},{5,6},{6,7},{7,8},{8,9},{9,10},{10,1... | collective-permute-start | bytes 884744 | tf_op jit(solution)/shard_map/ppermute | solution.py:827
  17.5 5.2 %copy-start.7 = (bf16[384,384]{1,0:T(8,128)(2,1)}, bf16[384,384]{1,0:T(8,128)(2,1)S(1)}, u32[]{:S(2)}) copy-start(bf16[384,384]{1,0:T(8,128)(2,1)S(1)} %collective-permute-done.refs_7_) | copy-start | bytes 884740
  17.5 34.1 %all-to-all-start.1 = ((bf16[32,2,24,384]{3,2,1,0:T(8,128)(2,1)}), bf16[32,2,24,384]{3,2,1,0:T(8,128)(2,1)}, u32[]{:S(2)}, u32[]{:S(2)}) async-start(bf16[32,2,24,384]{3,2,1,0:T(8,128)(2,1)} %get-tuple-element.23), calls=%async_computation.1 | async-start | bytes 2359296 | tf_op jit(solution)/shard_map/all_to_all | solution.py:844
  51.6 4.6 %copy-start.6 = (s32[128]{0:T(128)S(1)}, s32[128]{0:T(128)}, u32[]{:S(2)}) copy-start(s32[128]{0:T(128)} %constant.75.clone) | copy-start | bytes 1540
  51.7 58.4 %all-to-all-start = ((bf16[32,4,24,384]{3,2,1,0:T(8,128)(2,1)}), bf16[32,4,24,384]{3,2,1,0:T(8,128)(2,1)}, u32[]{:S(2)}, u32[]{:S(2)}) async-start(bf16[32,4,24,384]{3,2,1,0:T(8,128)(2,1)} %get-tuple-element.19), calls=%async_computation | async-start | bytes 4718592 | tf_op jit(solution)/shard_map/all_to_all | solution.py:844
  55.7 3.8 %copy-start.4 = (s32[384]{0:T(512)}, s32[384]{0:T(512)S(1)}, u32[]{:S(2)}) copy-start(s32[384]{0:T(512)S(1)} %iota.37) | copy-start | bytes 4612
  57.5 2.0 copy-start.2
  61.2 6.0 %slice-start = ((s32[384]{0:T(512)}), s32[256]{0:T(256)S(1)}, s32[]{:S(2)}) async-start(s32[384]{0:T(512)} %copy-done.4), calls=%async_computation.4 | async-start | bytes 2048 | tf_op jit(solution)/shard_map/slice | solution.py:492
  61.2 21.2 %collective-permute-start.1 = (bf16[12,192,384]{2,1,0:T(8,128)(2,1)}, bf16[12,192,384]{2,1,0:T(8,128)(2,1)}, u32[]{:S(2)}, u32[]{:S(2)}) collective-permute-start(bf16[12,192,384]{2,1,0:T(8,128)(2,1)} %constant_dynamic-slice_fusion.2), channel_id=1, source_target_pairs={{0,16},{16,0},{1,17},{17,1},{2,18},{18,2},{3,19},{19,3},{4,20},{20... | collective-permute-start | bytes 5308424 | tf_op jit(solution)/shard_map/ppermute | solution.py:778
  85.1 3.9 %copy-start.5 = (f32[4,128]{1,0:T(4,128)S(1)}, f32[4,128]{1,0:T(4,128)}, u32[]{:S(2)}) copy-start(f32[4,128]{1,0:T(4,128)} %constant.76.clone) | copy-start | bytes 6148
  116.1 20.7 %all-to-all-start.3 = ((bf16[32,24,384]{2,1,0:T(8,128)(2,1)}), bf16[32,24,384]{2,1,0:T(8,128)(2,1)S(1)}, u32[]{:S(2)}, u32[]{:S(2)}) async-start(bf16[32,24,384]{2,1,0:T(8,128)(2,1)} %bitcast.18), calls=%async_computation.3 | async-start | bytes 1179648 | tf_op jit(solution)/shard_map/all_to_all | solution.py:876
  136.8 5.3 %copy-start.1 = (bf16[32,24,384]{2,1,0:T(8,128)(2,1)}, bf16[32,24,384]{2,1,0:T(8,128)(2,1)S(1)}, u32[]{:S(2)}) copy-start(bf16[32,24,384]{2,1,0:T(8,128)(2,1)S(1)} %all-to-all-done.3.kept_ref) | copy-start | bytes 1769476
  136.8 72.6 %all-to-all-start.2 = ((bf16[32,120,384]{2,1,0:T(8,128)(2,1)}), bf16[32,120,384]{2,1,0:T(8,128)(2,1)S(1)}, u32[]{:S(2)}, u32[]{:S(2)}) async-start(bf16[32,120,384]{2,1,0:T(8,128)(2,1)} %bitcast.17), calls=%async_computation.2 | async-start | bytes 5898240 | tf_op jit(solution)/shard_map/all_to_all | solution.py:876
  142.2 1.6 collective-permute-start.2
  143.8 0.7 copy-start.3
  209.3 3.6 %copy-start = (bf16[32,120,384]{2,1,0:T(8,128)(2,1)}, bf16[32,120,384]{2,1,0:T(8,128)(2,1)S(1)}, u32[]{:S(2)}) copy-start(bf16[32,120,384]{2,1,0:T(8,128)(2,1)S(1)} %all-to-all-done.2.kept_ref) | copy-start | bytes 8847364
  209.5 3.5 %collective-permute-start.3 = (bf16[16,120,384]{2,1,0:T(8,128)(2,1)S(1)}, bf16[16,120,384]{2,1,0:T(8,128)(2,1)}, u32[]{:S(2)}, u32[]{:S(2)}) collective-permute-start(bf16[16,120,384]{2,1,0:T(8,128)(2,1)S(1)} %constant_dynamic-slice_fusion), channel_id=1, source_target_pairs={{0,16},{16,0},{1,17},{17,1},{2,18},{18,2},{3,19},{19,3},{4,20},{20... | collective-permute-start | bytes 4423688 | tf_op jit(solution)/shard_map/ppermute | solution.py:778

commit v10 on v9

--- a/solution.py
+++ b/solution.py
@@ -720,58 +720,83 @@
     return made.reshape(devices, full_rows // devices * count, cols)
 
 
-def residual_kernel(count, place_ref, kept_ref, other_ref, feat_ref, *refs):
-    out_ref, held = refs[-2:]
-    groups, span, cols = kept_ref.shape
+def residual_kernel(first, count, chunks, kept_hbm, other_hbm, feat_hbm, *refs):
+    out_hbm, kept, other, feat, out, held, done = refs[-7:]
+    halves, span = other.shape[:2]
     rows = 2 * span // count
-    own = pl.multiple_of(place_ref[0] * span, 8)
-    far = pl.multiple_of((1 - place_ref[0]) * span, 8)
-    for g in range(groups):
-        to_lane_tiles(held, pl.ds(own, span), kept_ref[g].astype(jnp.float32))
-        to_lane_tiles(held, pl.ds(far, span), other_ref[g].astype(jnp.float32))
-        for k in range(count):
-            filtered = from_lane_tiles(held, pl.ds(k, rows, stride=count))
-            out_ref[g, k] = (feat_ref[g, k].astype(jnp.float32) + filtered).astype(jnp.bfloat16)
-
-
-def add_residual(place, returned, other, features, previous, first, count):
+    groups = halves // chunks
+    section = lax.axis_index("section")
+
+    def block(c):
+        return pl.ds(c * groups, groups)
+
+    def copies(c):
+        source = pl.ds(section * halves + c * groups, groups)
+        channels = pl.ds(first, count)
+        return [
+            pltpu.make_async_copy(kept_hbm.at[source], kept.at[block(c)], done.at[0, c]),
+            pltpu.make_async_copy(other_hbm.at[block(c)], other.at[block(c)], done.at[1, c]),
+            pltpu.make_async_copy(
+                feat_hbm.at[block(c), channels], feat.at[block(c)], done.at[2, c]
+            ),
+        ]
+
+    def result(c):
+        channels = pl.ds(first, count)
+        return pltpu.make_async_copy(
+            out.at[block(c)], out_hbm.at[block(c), channels], done.at[3, c]
+        )
+
+    for c in range(chunks):
+        for copy in copies(c):
+            copy.start()
+    own = pl.multiple_of(section * span, 8)
+    far = pl.multiple_of((1 - section) * span, 8)
+    for c in range(chunks):
+        for copy in copies(c):
+            copy.wait()
+        for g in range(c * groups, (c + 1) * groups):
+            to_lane_tiles(held, pl.ds(own, span), kept[g].astype(jnp.float32))
+            to_lane_tiles(held, pl.ds(far, span), other[g].astype(jnp.float32))
+            for k in range(count):
+                filtered = from_lane_tiles(held, pl.ds(k, rows, stride=count))
+                out[g, k] = (feat[g, k].astype(jnp.float32) + filtered).astype(jnp.bfloat16)
+        result(c).start()
+    for c in range(chunks):
+        result(c).wait()
+
+
+def add_residual(returned, other, features, previous, first, count):
     halves, span, cols = other.shape
     group, rows = features.shape[1:3]
-    groups = 8 if halves % 8 == 0 else 1
-    steps = halves // groups
+    chunks = 4 if halves % 4 == 0 else 1
     operands = [returned, other, features]
-    in_specs = [
-        pl.BlockSpec((groups, span, cols), lambda i, place: (place[0] * steps + i, 0, 0)),
-        pl.BlockSpec((groups, span, cols), lambda i, place: (i, 0, 0)),
-        pl.BlockSpec(
-            (groups, count, rows, cols),
-            lambda i, place: (i, first // count, 0, 0),
-        ),
-    ]
     aliases = {}
     if previous is not None:
         operands.append(previous)
-        in_specs.append(pl.BlockSpec(memory_space=pl.ANY))
-        aliases = {4: 0}
+        aliases = {3: 0}
     return pl.pallas_call(
-        functools.partial(residual_kernel, count),
-        grid_spec=pltpu.PrefetchScalarGridSpec(
-            num_scalar_prefetch=1,
-            grid=(steps,),
-            in_specs=in_specs,
-            out_specs=in_specs[2],
-            scratch_shapes=[pltpu.VMEM((cols // 128, (rows + 8) * count, 128), jnp.float32)],
-        ),
+        functools.partial(residual_kernel, first, count, chunks),
+        in_specs=[pl.BlockSpec(memory_space=pl.ANY)] * len(operands),
+        out_specs=pl.BlockSpec(memory_space=pl.ANY),
+        scratch_shapes=[
+            pltpu.VMEM((halves, span, cols), jnp.bfloat16),
+            pltpu.VMEM((halves, span, cols), jnp.bfloat16),
+            pltpu.VMEM((halves, count, rows, cols), jnp.bfloat16),
+            pltpu.VMEM((halves, count, rows, cols), jnp.bfloat16),
+            pltpu.VMEM((cols // 128, (rows + 8) * count, 128), jnp.float32),
+            pltpu.SemaphoreType.DMA((4, chunks)),
+        ],
         out_shape=jax.ShapeDtypeStruct(features.shape, jnp.bfloat16),
         input_output_aliases=aliases,
-        compiler_params=pltpu.CompilerParams(vmem_limit_bytes=VMEM_BYTES),
+        compiler_params=pltpu.CompilerParams(vmem_limit_bytes=VMEM_BYTES // 4),
         cost_estimate=pl.CostEstimate(
             flops=halves * count * rows * cols,
             bytes_accessed=halves * count * rows * cols * 8,
             transcendentals=0,
         ),
         name="residual",
-    )(place, *operands)
+    )(*operands)
 
 
 def swap(block):
@@ -864,7 +889,6 @@
     residual = residual.reshape(half_channels // group, group, tile_rows, field_cols)
     late_fields, residual = lax.optimization_barrier((late_fields, residual))
 
-    section_place = jnp.reshape(section, (1,)).astype(jnp.int32)
     halves = devices // 2
     output = None
     rest = group - 2
@@ -877,7 +901,7 @@
         if output is not None:
             returned, output = lax.optimization_barrier((returned, output))
         other = swap(lax.dynamic_slice_in_dim(returned, (1 - section) * halves, halves, 0))
-        output = add_residual(section_place, returned, other, residual, output, first, count)
+        output = add_residual(returned, other, residual, output, first, count)
     return output.reshape(half_channels, tile_rows, field_cols)
 
 

time: 218 us -> 219 us (level)
    dynamic_slice x2, local copies, waits for them, and re-layouts: 0.19 us -> 2.52 us  [local(): lax.dynamic_slice_in_dim(returned, (1 - section) * halves, halves, 0)]
where the time goes in v10:
time: 219 us; the launch traced here: 218 us
  waiting for transfers between devices  94.7 us (43%)
  Pallas kernels  76.7 us (35%)
  starting transfers between devices  24 us (11%)
  other arithmetic  11.4 us (5%)
  local copies, waits for them, and re-layouts  10.4 us (5%)
    all_to_all x2, waiting for transfers between devices, local(): lax.all_to_all(made, DEVICES, split_axis=0, concat_axis=0, tiled=True)  62.7 us
    pallas_call x2, Pallas kernels, stem(): pl.pallas_call(functools.partial(stem_kernel, kind), grid=(steps,), in_sp...  31.8 us
    all_to_all x2, waiting for transfers between devices, local(): lax.all_to_all(normed, DEVICES, split_axis=0, concat_axis=0, tiled=True)  27.3 us
    pallas_call x2, Pallas kernels, filter_channels(): pl.pallas_call(functools.partial(filter_kernel, first, devices, 1.0 / (fu...  22.2 us
    pallas_call x1, Pallas kernels, symmetric_filter(): pl.pallas_call(symmetric_kernel, grid_spec=pltpu.PrefetchScalarGridSpec(n...  14.2 us
    all_to_all x2, starting transfers between devices, local(): lax.all_to_all(made, DEVICES, split_axis=0, concat_axis=0, tiled=True)  9.58 us
    all_to_all x2, starting transfers between devices, local(): lax.all_to_all(normed, DEVICES, split_axis=0, concat_axis=0, tiled=True)  9.19 us
    pallas_call x2, Pallas kernels, add_residual(): pl.pallas_call(functools.partial(residual_kernel, first, count, chunks),...  5.27 us
  transfers between devices with their start and end apart: 8, of which 6 were waited for; matrix products, arithmetic and copies ran while one was open for 9% of the time, Pallas kernels for 31%

profile of v10, /device:TPU:0, one launch (start us, length us, event | category | flops | bytes accessed | tf_op | source)
XLA Modules:
  0.0 217.6 jit_solution(7668236486244675690)
XLA Ops:
  0.0 1.1 slice_bitcast_fusion
  1.1 0.1 fusion.34
  1.2 4.9 %collective-permute-start = (bf16[384,384]{1,0:T(8,128)(2,1)S(1)}, bf16[384,384]{1,0:T(8,128)(2,1)S(1)}, u32[]{:S(2)}, u32[]{:S(2)}) collective-permute-start(bf16[384,384]{1,0:T(8,128)(2,1)S(1)} %pad_maximum_fusion.2), channel_id=1, source_target_pairs={{0,1},{1,2},{2,3},{3,4},{4,5},{5,6},{6,7},{7,8},{8,9},{9,10},{10,1... | collective-permute-start | bytes 884744 | tf_op jit(solution)/shard_map/ppermute | solution.py:852
  6.1 11.5 %stem.2 = (bf16[32,2,24,384]{3,2,1,0:T(8,128)(2,1)}, bf16[4,384,384]{2,1,0:T(8,128)(2,1)}) custom-call(bf16[24,384,768]{2,1,0:T(8,128)(2,1)} %above_ref.3, bf16[24,384,768]{2,1,0:T(8,128)(2,1)} %above_ref.3, bf16[48,96]{1,0:T(8,128)(2,1)} %bitcast.22, f32[96]{0:T(128)} %refs_1_.3, bf16[384,192]{1,0:T(8,128)(2,1)} %bitcast.20, f32[192]{0:T(256)} %refs_3_.3, ...), custom_call_target="tpu_custom_call" | custom-call | flops 8078229504 | bytes 4608000 | tf_op jit(solution)/shard_map/stem/pallas_call | solution.py:448
  17.6 0.0 collective-permute-done.refs_7_
  17.6 0.0 copy-start.4
  17.6 5.2 %all-to-all-start.1 = ((bf16[32,2,24,384]{3,2,1,0:T(8,128)(2,1)}), bf16[32,2,24,384]{3,2,1,0:T(8,128)(2,1)}, u32[]{:S(2)}, u32[]{:S(2)}) async-start(bf16[32,2,24,384]{3,2,1,0:T(8,128)(2,1)} %get-tuple-element.23), calls=%async_computation.1 | async-start | bytes 2359296 | tf_op jit(solution)/shard_map/all_to_all | solution.py:869
  22.8 0.0 copy-done.4
  22.8 20.4 %stem.3 = (bf16[32,4,24,384]{3,2,1,0:T(8,128)(2,1)}, bf16[8,384,384]{2,1,0:T(8,128)(2,1)}) custom-call(bf16[24,384,768]{2,1,0:T(8,128)(2,1)} %above_ref.3, bf16[24,384,768]{2,1,0:T(8,128)(2,1)} %above_ref.3, bf16[48,96]{1,0:T(8,128)(2,1)} %bitcast.23, f32[96]{0:T(128)} %refs_1_.3, bf16[384,192]{1,0:T(8,128)(2,1)} %bitcast.21, f32[192]{0:T(256)} %refs_3_.3, ...), custom_call_target="tpu_custom_call" | custom-call | flops 16156459008 | bytes 9216000 | tf_op jit(solution)/shard_map/stem/pallas_call | solution.py:448
  43.1 8.5 %all-to-all-done.1 = bf16[32,2,24,384]{3,2,1,0:T(8,128)(2,1)} async-done(((bf16[32,2,24,384]{3,2,1,0:T(8,128)(2,1)}), bf16[32,2,24,384]{3,2,1,0:T(8,128)(2,1)}, u32[]{:S(2)}, u32[]{:S(2)}) %all-to-all-start.1) | async-done | bytes 1179680 | tf_op jit(solution)/shard_map/all_to_all | solution.py:869
  51.7 0.0 copy-start.3
  51.7 4.0 %all-to-all-start = ((bf16[32,4,24,384]{3,2,1,0:T(8,128)(2,1)}), bf16[32,4,24,384]{3,2,1,0:T(8,128)(2,1)}, u32[]{:S(2)}, u32[]{:S(2)}) async-start(bf16[32,4,24,384]{3,2,1,0:T(8,128)(2,1)} %get-tuple-element.19), calls=%async_computation | async-start | bytes 4718592 | tf_op jit(solution)/shard_map/all_to_all | solution.py:869
  55.7 0.0 copy-start.1
  55.7 0.3 fusion.29
  56.0 0.3 sine_convert_fusion.1
  56.3 0.0 copy-done.3
  56.3 0.3 fusion.30
  56.5 0.3 sine_convert_fusion.2
  56.8 0.7 maximum_maximum_fusion.fwd_ref
  57.5 0.0 copy-start
  57.5 2.0 constant_dynamic-update-slice_fusion.1
  59.5 0.0 copy-done.1
  59.5 0.0 copy-done
  59.5 0.2 constant_dynamic-update-slice_fusion
  59.8 1.5 constant_dynamic-slice_fusion.2
  61.3 0.0 slice-start
  61.3 0.0 collective-permute-start.1
  61.3 0.7 maximum_maximum_fusion.1.inv_ref
  61.9 1.0 fusion.8.turn_u_ref
  63.0 2.5 %sine_convert_fusion = (bf16[384,384]{1,0:T(8,128)(2,1)S(1)}, bf16[384,384]{1,0:T(8,128)(2,1)S(1)}) fusion(), kind=kLoop, calls=%fused_computation.9 | loop fusion | flops 1622016 | bytes 589824 | tf_op jit(solution)/shard_map/convert_element_type | solution.py:26
  65.6 0.8 pad_maximum_fusion.row_table_ref
  66.3 0.1 slice_multiply_fusion
  66.5 0.8 pad_maximum_fusion.1.back_ref
  67.2 0.0 slice-done
  67.2 0.9 fusion.14.turn_w_ref
  68.2 14.2 %symmetric_filter.1.g_ref = bf16[12,2,384,256]{3,2,1,0:T(8,128)(2,1)} custom-call(s32[1]{0:T(128)} %bitcast.8.place_ref, bf16[24,2,384,384]{3,2,1,0:T(8,128)(2,1)} %f_ref.1, bf16[384,256]{1,0:T(8,128)(2,1)} %fusion.14.turn_w_ref, bf16[384,384]{1,0:T(8,128)(2,1)} %fusion.8.turn_u_ref), custom_call_target="tpu_custom_call" | custom-call | flops 3623878656 | bytes 16515072 | tf_op jit(solution)/shard_map/symmetric_filter/pallas_call | solution.py:493
  82.4 0.0 collective-permute-done.1
  82.4 2.3 %broadcast_select_fusion.1 = (bf16[12,192,384]{2,1,0:T(8,128)(2,1)S(1)}, bf16[12,192,384]{2,1,0:T(8,128)(2,1)S(1)}) fusion(bf16[12,192,384]{2,1,0:T(8,128)(2,1)} %collective-permute-done.1, pred[]{:T(512)S(6)} %eq.41, bf16[12,384,384]{2,1,0:T(8,128)(2,1)S(1)} %constant_dynamic-update-slice_fusion, s32[]{:T(128)S(6)} %select_n.72), kind=kLoop, calls=%fused_computation.2 | loop fusion | flops 1769472 | bytes 7077893 | tf_op jit(solution)/shard_map/jit(_where)/select_n | solution.py:886
  84.7 0.4 maximum_bitcast_fusion
  85.1 0.0 copy-start.2
  85.2 2.1 copy.13
  87.3 0.0 copy-done.2
  87.3 0.8 jit_solution_.3.twiddle_ref
  88.1 3.2 %repack.1 = (bf16[12,128,384]{2,1,0:T(8,128)(2,1)}, f32[4,128,128]{2,1,0:T(8,128)}) custom-call(bf16[1536,384]{1,0:T(8,128)(2,1)} %bitcast.7.early_ref, f32[4,128,128]{2,1,0:T(8,128)} %jit_solution_.3.twiddle_ref), custom_call_target="tpu_custom_call" | custom-call | flops 589824 | bytes 2359296 | tf_op jit(solution)/shard_map/repack/pallas_call | solution.py:544
  91.3 18.7 %all-to-all-done = bf16[32,4,24,384]{3,2,1,0:T(8,128)(2,1)} async-done(((bf16[32,4,24,384]{3,2,1,0:T(8,128)(2,1)}), bf16[32,4,24,384]{3,2,1,0:T(8,128)(2,1)}, u32[]{:S(2)}, u32[]{:S(2)}) %all-to-all-start) | async-done | bytes 2359328 | tf_op jit(solution)/shard_map/all_to_all | solution.py:869
  110.1 6.1 %spectral_filter.3 = bf16[768,384]{1,0:T(8,128)(2,1)} custom-call(bf16[3072,384]{1,0:T(8,128)(2,1)} %bitcast.4.late_ref, bf16[12,128,384]{2,1,0:T(8,128)(2,1)} %get-tuple-element.24.early_ref, bf16[12,2,384,256]{3,2,1,0:T(8,128)(2,1)} %symmetric_filter.1.g_ref, bf16[384,512]{1,0:T(8,128)(2,1)} %pad_maximum_fusion.row_table_ref, ...), custom_call_target="tpu_custom_call" | custom-call | flops 1207959552 | bytes 2359296 | tf_op jit(solution)/shard_map/spectral_filter/pallas_call | solution.py:697
  116.1 4.3 %all-to-all-start.3 = ((bf16[32,24,384]{2,1,0:T(8,128)(2,1)}), bf16[32,24,384]{2,1,0:T(8,128)(2,1)}, u32[]{:S(2)}, u32[]{:S(2)}) async-start(bf16[32,24,384]{2,1,0:T(8,128)(2,1)} %bitcast.17), calls=%async_computation.3 | async-start | bytes 1179648 | tf_op jit(solution)/shard_map/all_to_all | solution.py:900
  120.4 16.1 %spectral_filter.2 = bf16[3840,384]{1,0:T(8,128)(2,1)} custom-call(bf16[3072,384]{1,0:T(8,128)(2,1)} %bitcast.4.late_ref, bf16[12,128,384]{2,1,0:T(8,128)(2,1)} %get-tuple-element.24.early_ref, bf16[12,2,384,256]{3,2,1,0:T(8,128)(2,1)} %symmetric_filter.1.g_ref, bf16[384,512]{1,0:T(8,128)(2,1)} %pad_maximum_fusion.row_table_ref, ...), custom_call_target="tpu_custom_call" | custom-call | flops 6039797760 | bytes 11796480 | tf_op jit(solution)/shard_map/spectral_filter/pallas_call | solution.py:697
  136.5 0.3 all-to-all-done.3.kept_hbm
  136.9 5.3 %all-to-all-start.2 = ((bf16[32,120,384]{2,1,0:T(8,128)(2,1)}), bf16[32,120,384]{2,1,0:T(8,128)(2,1)}, u32[]{:S(2)}, u32[]{:S(2)}) async-start(bf16[32,120,384]{2,1,0:T(8,128)(2,1)} %bitcast.16), calls=%async_computation.2 | async-start | bytes 5898240 | tf_op jit(solution)/shard_map/all_to_all | solution.py:900
  142.2 1.0 constant_dynamic-slice_fusion.1
  143.2 0.3 collective-permute-start.2
  143.4 1.4 collective-permute-done.2.other_hbm
  144.8 2.2 %residual.2.refs_0_ = bf16[16,12,24,384]{3,2,1,0:T(8,128)(2,1)} custom-call(bf16[32,24,384]{2,1,0:T(8,128)(2,1)} %all-to-all-done.3.kept_hbm, bf16[16,24,384]{2,1,0:T(8,128)(2,1)S(1)} %collective-permute-done.2.other_hbm, bf16[16,12,24,384]{3,2,1,0:T(8,128)(2,1)S(1)} %bitcast.14), custom_call_target="tpu_custom_call" | custom-call | flops 294912 | bytes 2359296 | tf_op jit(solution)/shard_map/residual/pallas_call | solution.py:778
  147.0 62.4 %all-to-all-done.2.kept_hbm = bf16[32,120,384]{2,1,0:T(8,128)(2,1)} async-done(((bf16[32,120,384]{2,1,0:T(8,128)(2,1)}), bf16[32,120,384]{2,1,0:T(8,128)(2,1)}, u32[]{:S(2)}, u32[]{:S(2)}) %all-to-all-start.2) | async-done | bytes 2949152 | tf_op jit(solution)/shard_map/all_to_all | solution.py:900
  209.4 1.5 constant_dynamic-slice_fusion
  210.9 0.1 collective-permute-start.3
  211.0 3.3 %collective-permute-done.3.other_hbm = bf16[16,120,384]{2,1,0:T(8,128)(2,1)S(1)} collective-permute-done((bf16[16,120,384]{2,1,0:T(8,128)(2,1)S(1)}, bf16[16,120,384]{2,1,0:T(8,128)(2,1)S(1)}, u32[]{:S(2)}, u32[]{:S(2)}) %collective-permute-start.3) | collective-permute-done | bytes 1474592 | tf_op jit(solution)/shard_map/ppermute | solution.py:803
  214.3 3.1 %residual.3 = bf16[16,12,24,384]{3,2,1,0:T(8,128)(2,1)} custom-call(bf16[32,120,384]{2,1,0:T(8,128)(2,1)} %all-to-all-done.2.kept_hbm, bf16[16,120,384]{2,1,0:T(8,128)(2,1)S(1)} %collective-permute-done.3.other_hbm, bf16[16,12,24,384]{3,2,1,0:T(8,128)(2,1)S(1)} %bitcast.15, bf16[16,12,24,384]{3,2,1,0:T(8,128)(2,1)} %residual.2.refs_0_), custom_call_target="tpu_custom_call", output_to_operand_aliasing={{}: (3, {})} | custom-call | flops 1474560 | bytes 11796480 | tf_op jit(solution)/shard_map/residual/pallas_call | solution.py:778
  (5 shorter events, 0.1 us)
Async XLA Ops:
  1.2 16.3 %collective-permute-start = (bf16[384,384]{1,0:T(8,128)(2,1)S(1)}, bf16[384,384]{1,0:T(8,128)(2,1)S(1)}, u32[]{:S(2)}, u32[]{:S(2)}) collective-permute-start(bf16[384,384]{1,0:T(8,128)(2,1)S(1)} %pad_maximum_fusion.2), channel_id=1, source_target_pairs={{0,1},{1,2},{2,3},{3,4},{4,5},{5,6},{6,7},{7,8},{8,9},{9,10},{10,1... | collective-permute-start | bytes 884744 | tf_op jit(solution)/shard_map/ppermute | solution.py:852
  17.6 5.2 %copy-start.4 = (bf16[384,384]{1,0:T(8,128)(2,1)}, bf16[384,384]{1,0:T(8,128)(2,1)S(1)}, u32[]{:S(2)}) copy-start(bf16[384,384]{1,0:T(8,128)(2,1)S(1)} %collective-permute-done.refs_7_) | copy-start | bytes 884740
  17.6 34.1 %all-to-all-start.1 = ((bf16[32,2,24,384]{3,2,1,0:T(8,128)(2,1)}), bf16[32,2,24,384]{3,2,1,0:T(8,128)(2,1)}, u32[]{:S(2)}, u32[]{:S(2)}) async-start(bf16[32,2,24,384]{3,2,1,0:T(8,128)(2,1)} %get-tuple-element.23), calls=%async_computation.1 | async-start | bytes 2359296 | tf_op jit(solution)/shard_map/all_to_all | solution.py:869
  51.7 4.6 %copy-start.3 = (s32[128]{0:T(128)S(1)}, s32[128]{0:T(128)}, u32[]{:S(2)}) copy-start(s32[128]{0:T(128)} %constant.75.clone) | copy-start | bytes 1540
  51.7 58.4 %all-to-all-start = ((bf16[32,4,24,384]{3,2,1,0:T(8,128)(2,1)}), bf16[32,4,24,384]{3,2,1,0:T(8,128)(2,1)}, u32[]{:S(2)}, u32[]{:S(2)}) async-start(bf16[32,4,24,384]{3,2,1,0:T(8,128)(2,1)} %get-tuple-element.19), calls=%async_computation | async-start | bytes 4718592 | tf_op jit(solution)/shard_map/all_to_all | solution.py:869
  55.7 3.8 %copy-start.1 = (s32[384]{0:T(512)}, s32[384]{0:T(512)S(1)}, u32[]{:S(2)}) copy-start(s32[384]{0:T(512)S(1)} %iota.37) | copy-start | bytes 4612
  57.5 2.0 copy-start
  61.3 6.0 %slice-start = ((s32[384]{0:T(512)}), s32[256]{0:T(256)S(1)}, s32[]{:S(2)}) async-start(s32[384]{0:T(512)} %copy-done.1), calls=%async_computation.4 | async-start | bytes 2048 | tf_op jit(solution)/shard_map/slice | solution.py:492
  61.3 21.2 %collective-permute-start.1 = (bf16[12,192,384]{2,1,0:T(8,128)(2,1)}, bf16[12,192,384]{2,1,0:T(8,128)(2,1)}, u32[]{:S(2)}, u32[]{:S(2)}) collective-permute-start(bf16[12,192,384]{2,1,0:T(8,128)(2,1)} %constant_dynamic-slice_fusion.2), channel_id=1, source_target_pairs={{0,16},{16,0},{1,17},{17,1},{2,18},{18,2},{3,19},{19,3},{4,20},{20... | collective-permute-start | bytes 5308424 | tf_op jit(solution)/shard_map/ppermute | solution.py:803
  85.1 2.1 copy-start.2
  116.1 20.8 %all-to-all-start.3 = ((bf16[32,24,384]{2,1,0:T(8,128)(2,1)}), bf16[32,24,384]{2,1,0:T(8,128)(2,1)}, u32[]{:S(2)}, u32[]{:S(2)}) async-start(bf16[32,24,384]{2,1,0:T(8,128)(2,1)} %bitcast.17), calls=%async_computation.3 | async-start | bytes 1179648 | tf_op jit(solution)/shard_map/all_to_all | solution.py:900
  136.9 72.5 %all-to-all-start.2 = ((bf16[32,120,384]{2,1,0:T(8,128)(2,1)}), bf16[32,120,384]{2,1,0:T(8,128)(2,1)}, u32[]{:S(2)}, u32[]{:S(2)}) async-start(bf16[32,120,384]{2,1,0:T(8,128)(2,1)} %bitcast.16), calls=%async_computation.2 | async-start | bytes 5898240 | tf_op jit(solution)/shard_map/all_to_all | solution.py:900
  143.2 1.6 collective-permute-start.2
  210.9 3.3 %collective-permute-start.3 = (bf16[16,120,384]{2,1,0:T(8,128)(2,1)S(1)}, bf16[16,120,384]{2,1,0:T(8,128)(2,1)S(1)}, u32[]{:S(2)}, u32[]{:S(2)}) collective-permute-start(bf16[16,120,384]{2,1,0:T(8,128)(2,1)S(1)} %constant_dynamic-slice_fusion), channel_id=1, source_target_pairs={{0,16},{16,0},{1,17},{17,1},{2,18},{18,2},{3,19},{19,3},{4,20},{20... | collective-permute-start | bytes 4423688 | tf_op jit(solution)/shard_map/ppermute | solution.py:803

commit v11 on v10

--- a/solution.py
+++ b/solution.py
@@ -789,7 +789,7 @@
         ],
         out_shape=jax.ShapeDtypeStruct(features.shape, jnp.bfloat16),
         input_output_aliases=aliases,
-        compiler_params=pltpu.CompilerParams(vmem_limit_bytes=VMEM_BYTES // 4),
+        compiler_params=pltpu.CompilerParams(vmem_limit_bytes=VMEM_BYTES if previous is None else VMEM_BYTES // 4),
         cost_estimate=pl.CostEstimate(
             flops=halves * count * rows * cols,
             bytes_accessed=halves * count * rows * cols * 8,

time: 219 us -> 218 us (level)
  no operation moved by 1% of the time
where the time goes in v11:
time: 218 us
  waiting for transfers between devices  92.8 us (43%)
  Pallas kernels  77 us (35%)
  starting transfers between devices  24 us (11%)
  local copies, waits for them, and re-layouts  11.9 us (5%)
  other arithmetic  11.4 us (5%)
    all_to_all x2, waiting for transfers between devices, local(): lax.all_to_all(made, DEVICES, split_axis=0, concat_axis=0, tiled=True)  62.8 us
    pallas_call x2, Pallas kernels, stem(): pl.pallas_call(functools.partial(stem_kernel, kind), grid=(steps,), in_sp...  31.9 us
    all_to_all x2, waiting for transfers between devices, local(): lax.all_to_all(normed, DEVICES, split_axis=0, concat_axis=0, tiled=True)  25.4 us
    pallas_call x2, Pallas kernels, filter_channels(): pl.pallas_call(functools.partial(filter_kernel, first, devices, 1.0 / (fu...  22.3 us
    pallas_call x1, Pallas kernels, symmetric_filter(): pl.pallas_call(symmetric_kernel, grid_spec=pltpu.PrefetchScalarGridSpec(n...  14.2 us
    all_to_all x2, starting transfers between devices, local(): lax.all_to_all(made, DEVICES, split_axis=0, concat_axis=0, tiled=True)  9.61 us
    all_to_all x2, starting transfers between devices, local(): lax.all_to_all(normed, DEVICES, split_axis=0, concat_axis=0, tiled=True)  9.19 us
    pallas_call x2, Pallas kernels, add_residual(): pl.pallas_call(functools.partial(residual_kernel, first, count, chunks),...  5.43 us
  transfers between devices with their start and end apart: 8, of which 6 were waited for; matrix products, arithmetic and copies ran while one was open for 9% of the time, Pallas kernels for 31%

profile of v11, /device:TPU:0, one launch (start us, length us, event | category | flops | bytes accessed | tf_op | source)
XLA Modules:
  0.0 217.6 jit_solution(8936153398741119766)
XLA Ops:
  0.0 1.1 slice_bitcast_fusion
  1.1 0.1 fusion.34
  1.2 4.9 %collective-permute-start = (bf16[384,384]{1,0:T(8,128)(2,1)S(1)}, bf16[384,384]{1,0:T(8,128)(2,1)S(1)}, u32[]{:S(2)}, u32[]{:S(2)}) collective-permute-start(bf16[384,384]{1,0:T(8,128)(2,1)S(1)} %pad_maximum_fusion.2), channel_id=1, source_target_pairs={{0,1},{1,2},{2,3},{3,4},{4,5},{5,6},{6,7},{7,8},{8,9},{9,10},{10,1... | collective-permute-start | bytes 884744 | tf_op jit(solution)/shard_map/ppermute | solution.py:852
  6.1 11.4 %stem.2 = (bf16[32,2,24,384]{3,2,1,0:T(8,128)(2,1)}, bf16[4,384,384]{2,1,0:T(8,128)(2,1)}) custom-call(bf16[24,384,768]{2,1,0:T(8,128)(2,1)} %above_ref.3, bf16[24,384,768]{2,1,0:T(8,128)(2,1)} %above_ref.3, bf16[48,96]{1,0:T(8,128)(2,1)} %bitcast.22, f32[96]{0:T(128)} %refs_1_.3, bf16[384,192]{1,0:T(8,128)(2,1)} %bitcast.20, f32[192]{0:T(256)} %refs_3_.3, ...), custom_call_target="tpu_custom_call" | custom-call | flops 8078229504 | bytes 4608000 | tf_op jit(solution)/shard_map/stem/pallas_call | solution.py:448
  17.5 0.0 collective-permute-done.refs_7_
  17.5 0.0 copy-start.7
  17.5 5.2 %all-to-all-start.1 = ((bf16[32,2,24,384]{3,2,1,0:T(8,128)(2,1)}), bf16[32,2,24,384]{3,2,1,0:T(8,128)(2,1)}, u32[]{:S(2)}, u32[]{:S(2)}) async-start(bf16[32,2,24,384]{3,2,1,0:T(8,128)(2,1)} %get-tuple-element.23), calls=%async_computation.1 | async-start | bytes 2359296 | tf_op jit(solution)/shard_map/all_to_all | solution.py:869
  22.8 0.0 copy-done.7
  22.8 20.4 %stem.3 = (bf16[32,4,24,384]{3,2,1,0:T(8,128)(2,1)}, bf16[8,384,384]{2,1,0:T(8,128)(2,1)}) custom-call(bf16[24,384,768]{2,1,0:T(8,128)(2,1)} %above_ref.3, bf16[24,384,768]{2,1,0:T(8,128)(2,1)} %above_ref.3, bf16[48,96]{1,0:T(8,128)(2,1)} %bitcast.23, f32[96]{0:T(128)} %refs_1_.3, bf16[384,192]{1,0:T(8,128)(2,1)} %bitcast.21, f32[192]{0:T(256)} %refs_3_.3, ...), custom_call_target="tpu_custom_call" | custom-call | flops 16156459008 | bytes 9216000 | tf_op jit(solution)/shard_map/stem/pallas_call | solution.py:448
  43.2 8.4 %all-to-all-done.1 = bf16[32,2,24,384]{3,2,1,0:T(8,128)(2,1)} async-done(((bf16[32,2,24,384]{3,2,1,0:T(8,128)(2,1)}), bf16[32,2,24,384]{3,2,1,0:T(8,128)(2,1)}, u32[]{:S(2)}, u32[]{:S(2)}) %all-to-all-start.1) | async-done | bytes 1179680 | tf_op jit(solution)/shard_map/all_to_all | solution.py:869
  51.6 0.0 copy-start.6
  51.7 4.0 %all-to-all-start = ((bf16[32,4,24,384]{3,2,1,0:T(8,128)(2,1)}), bf16[32,4,24,384]{3,2,1,0:T(8,128)(2,1)}, u32[]{:S(2)}, u32[]{:S(2)}) async-start(bf16[32,4,24,384]{3,2,1,0:T(8,128)(2,1)} %get-tuple-element.19), calls=%async_computation | async-start | bytes 4718592 | tf_op jit(solution)/shard_map/all_to_all | solution.py:869
  55.7 0.0 copy-start.4
  55.7 0.3 fusion.29
  56.0 0.3 sine_convert_fusion.1
  56.2 0.0 copy-done.6
  56.2 0.3 fusion.30
  56.5 0.3 sine_convert_fusion.2
  56.8 0.7 maximum_maximum_fusion.fwd_ref
  57.5 0.0 copy-start.2
  57.5 2.0 constant_dynamic-update-slice_fusion.1
  59.5 0.0 copy-done.4
  59.5 0.0 copy-done.2
  59.5 0.2 constant_dynamic-update-slice_fusion
  59.7 1.5 constant_dynamic-slice_fusion.2
  61.2 0.0 slice-start
  61.2 0.0 collective-permute-start.1
  61.3 0.7 maximum_maximum_fusion.1.inv_ref
  61.9 1.0 fusion.8.turn_u_ref
  62.9 2.5 %sine_convert_fusion = (bf16[384,384]{1,0:T(8,128)(2,1)S(1)}, bf16[384,384]{1,0:T(8,128)(2,1)S(1)}) fusion(), kind=kLoop, calls=%fused_computation.9 | loop fusion | flops 1622016 | bytes 589824 | tf_op jit(solution)/shard_map/convert_element_type | solution.py:26
  65.5 0.8 pad_maximum_fusion.row_table_ref
  66.3 0.1 slice_multiply_fusion
  66.4 0.8 pad_maximum_fusion.1.back_ref
  67.2 0.0 slice-done
  67.2 0.9 fusion.14.turn_w_ref
  68.2 14.2 %symmetric_filter.1.g_ref = bf16[12,2,384,256]{3,2,1,0:T(8,128)(2,1)} custom-call(s32[1]{0:T(128)} %bitcast.8.place_ref, bf16[24,2,384,384]{3,2,1,0:T(8,128)(2,1)} %f_ref.1, bf16[384,256]{1,0:T(8,128)(2,1)} %fusion.14.turn_w_ref, bf16[384,384]{1,0:T(8,128)(2,1)} %fusion.8.turn_u_ref), custom_call_target="tpu_custom_call" | custom-call | flops 3623878656 | bytes 16515072 | tf_op jit(solution)/shard_map/symmetric_filter/pallas_call | solution.py:493
  82.4 0.0 collective-permute-done.1
  82.4 2.3 %broadcast_select_fusion.1 = (bf16[12,192,384]{2,1,0:T(8,128)(2,1)S(1)}, bf16[12,192,384]{2,1,0:T(8,128)(2,1)S(1)}) fusion(bf16[12,192,384]{2,1,0:T(8,128)(2,1)} %collective-permute-done.1, pred[]{:T(512)S(6)} %eq.41, bf16[12,384,384]{2,1,0:T(8,128)(2,1)S(1)} %constant_dynamic-update-slice_fusion, s32[]{:T(128)S(6)} %select_n.72), kind=kLoop, calls=%fused_computation.2 | loop fusion | flops 1769472 | bytes 7077893 | tf_op jit(solution)/shard_map/jit(_where)/select_n | solution.py:886
  84.7 0.4 maximum_bitcast_fusion
  85.1 0.0 copy-start.5
  85.1 3.9 %copy.13 = bf16[192,24,384]{2,1,0:T(8,128)(2,1)} copy(bf16[192,24,384]{2,0,1:T(8,128)(2,1)S(1)} %maximum_bitcast_fusion) | data formatting | bytes 7077888 | tf_op jit(solution)/shard_map/transpose | solution.py:888
  89.0 0.0 copy-done.5
  89.0 0.8 jit_solution_.3.twiddle_ref
  89.9 3.2 %repack.1 = (bf16[12,128,384]{2,1,0:T(8,128)(2,1)}, f32[4,128,128]{2,1,0:T(8,128)}) custom-call(bf16[1536,384]{1,0:T(8,128)(2,1)} %bitcast.7.early_ref, f32[4,128,128]{2,1,0:T(8,128)} %jit_solution_.3.twiddle_ref), custom_call_target="tpu_custom_call" | custom-call | flops 589824 | bytes 2359296 | tf_op jit(solution)/shard_map/repack/pallas_call | solution.py:544
  93.1 16.9 %all-to-all-done = bf16[32,4,24,384]{3,2,1,0:T(8,128)(2,1)} async-done(((bf16[32,4,24,384]{3,2,1,0:T(8,128)(2,1)}), bf16[32,4,24,384]{3,2,1,0:T(8,128)(2,1)}, u32[]{:S(2)}, u32[]{:S(2)}) %all-to-all-start) | async-done | bytes 2359328 | tf_op jit(solution)/shard_map/all_to_all | solution.py:869
  110.0 6.1 %spectral_filter.3 = bf16[768,384]{1,0:T(8,128)(2,1)} custom-call(bf16[3072,384]{1,0:T(8,128)(2,1)} %bitcast.4.late_ref, bf16[12,128,384]{2,1,0:T(8,128)(2,1)} %get-tuple-element.24.early_ref, bf16[12,2,384,256]{3,2,1,0:T(8,128)(2,1)} %symmetric_filter.1.g_ref, bf16[384,512]{1,0:T(8,128)(2,1)} %pad_maximum_fusion.row_table_ref, ...), custom_call_target="tpu_custom_call" | custom-call | flops 1207959552 | bytes 2359296 | tf_op jit(solution)/shard_map/spectral_filter/pallas_call | solution.py:697
  116.1 4.2 %all-to-all-start.3 = ((bf16[32,24,384]{2,1,0:T(8,128)(2,1)}), bf16[32,24,384]{2,1,0:T(8,128)(2,1)S(1)}, u32[]{:S(2)}, u32[]{:S(2)}) async-start(bf16[32,24,384]{2,1,0:T(8,128)(2,1)} %bitcast.17), calls=%async_computation.3 | async-start | bytes 1179648 | tf_op jit(solution)/shard_map/all_to_all | solution.py:900
  120.3 16.2 %spectral_filter.2 = bf16[3840,384]{1,0:T(8,128)(2,1)} custom-call(bf16[3072,384]{1,0:T(8,128)(2,1)} %bitcast.4.late_ref, bf16[12,128,384]{2,1,0:T(8,128)(2,1)} %get-tuple-element.24.early_ref, bf16[12,2,384,256]{3,2,1,0:T(8,128)(2,1)} %symmetric_filter.1.g_ref, bf16[384,512]{1,0:T(8,128)(2,1)} %pad_maximum_fusion.row_table_ref, ...), custom_call_target="tpu_custom_call" | custom-call | flops 6039797760 | bytes 11796480 | tf_op jit(solution)/shard_map/spectral_filter/pallas_call | solution.py:697
  136.5 0.3 all-to-all-done.3.kept_hbm
  136.8 0.0 copy-start.1
  136.8 5.4 %all-to-all-start.2 = ((bf16[32,120,384]{2,1,0:T(8,128)(2,1)}), bf16[32,120,384]{2,1,0:T(8,128)(2,1)}, u32[]{:S(2)}, u32[]{:S(2)}) async-start(bf16[32,120,384]{2,1,0:T(8,128)(2,1)} %bitcast.16), calls=%async_computation.2 | async-start | bytes 5898240 | tf_op jit(solution)/shard_map/all_to_all | solution.py:900
  142.2 0.0 copy-done.1
  142.3 0.3 collective-permute-start.2
  142.5 1.4 collective-permute-done.2.other_hbm
  143.9 0.0 copy-start.3
  143.9 0.7 copy-done.3
  144.6 0.0 copy-start
  144.6 2.3 %residual.2.refs_0_ = bf16[16,12,24,384]{3,2,1,0:T(8,128)(2,1)} custom-call(bf16[32,24,384]{2,1,0:T(8,128)(2,1)} %copy-done.1, bf16[16,24,384]{2,1,0:T(8,128)(2,1)} %copy-done.3, bf16[16,12,24,384]{3,2,1,0:T(8,128)(2,1)} %bitcast.14), custom_call_target="tpu_custom_call" | custom-call | flops 294912 | bytes 2359296 | tf_op jit(solution)/shard_map/residual/pallas_call | solution.py:778
  147.0 62.5 %all-to-all-done.2.kept_hbm = bf16[32,120,384]{2,1,0:T(8,128)(2,1)} async-done(((bf16[32,120,384]{2,1,0:T(8,128)(2,1)}), bf16[32,120,384]{2,1,0:T(8,128)(2,1)}, u32[]{:S(2)}, u32[]{:S(2)}) %all-to-all-start.2) | async-done | bytes 2949152 | tf_op jit(solution)/shard_map/all_to_all | solution.py:900
  209.4 1.5 constant_dynamic-slice_fusion
  211.0 0.1 collective-permute-start.3
  211.1 3.3 %collective-permute-done.3.other_hbm = bf16[16,120,384]{2,1,0:T(8,128)(2,1)S(1)} collective-permute-done((bf16[16,120,384]{2,1,0:T(8,128)(2,1)S(1)}, bf16[16,120,384]{2,1,0:T(8,128)(2,1)S(1)}, u32[]{:S(2)}, u32[]{:S(2)}) %collective-permute-start.3) | collective-permute-done | bytes 1474592 | tf_op jit(solution)/shard_map/ppermute | solution.py:803
  214.3 0.0 copy-done
  214.3 3.1 %residual.3 = bf16[16,12,24,384]{3,2,1,0:T(8,128)(2,1)} custom-call(bf16[32,120,384]{2,1,0:T(8,128)(2,1)} %all-to-all-done.2.kept_hbm, bf16[16,120,384]{2,1,0:T(8,128)(2,1)S(1)} %collective-permute-done.3.other_hbm, bf16[16,12,24,384]{3,2,1,0:T(8,128)(2,1)S(1)} %bitcast.15, bf16[16,12,24,384]{3,2,1,0:T(8,128)(2,1)} %residual.2.refs_0_), custom_call_target="tpu_custom_call", output_to_operand_aliasing={{}: (3, {})} | custom-call | flops 1474560 | bytes 11796480 | tf_op jit(solution)/shard_map/residual/pallas_call | solution.py:778
  (6 shorter events, 0.1 us)
Async XLA Ops:
  1.2 16.3 %collective-permute-start = (bf16[384,384]{1,0:T(8,128)(2,1)S(1)}, bf16[384,384]{1,0:T(8,128)(2,1)S(1)}, u32[]{:S(2)}, u32[]{:S(2)}) collective-permute-start(bf16[384,384]{1,0:T(8,128)(2,1)S(1)} %pad_maximum_fusion.2), channel_id=1, source_target_pairs={{0,1},{1,2},{2,3},{3,4},{4,5},{5,6},{6,7},{7,8},{8,9},{9,10},{10,1... | collective-permute-start | bytes 884744 | tf_op jit(solution)/shard_map/ppermute | solution.py:852
  17.5 5.2 %copy-start.7 = (bf16[384,384]{1,0:T(8,128)(2,1)}, bf16[384,384]{1,0:T(8,128)(2,1)S(1)}, u32[]{:S(2)}) copy-start(bf16[384,384]{1,0:T(8,128)(2,1)S(1)} %collective-permute-done.refs_7_) | copy-start | bytes 884740
  17.5 34.1 %all-to-all-start.1 = ((bf16[32,2,24,384]{3,2,1,0:T(8,128)(2,1)}), bf16[32,2,24,384]{3,2,1,0:T(8,128)(2,1)}, u32[]{:S(2)}, u32[]{:S(2)}) async-start(bf16[32,2,24,384]{3,2,1,0:T(8,128)(2,1)} %get-tuple-element.23), calls=%async_computation.1 | async-start | bytes 2359296 | tf_op jit(solution)/shard_map/all_to_all | solution.py:869
  51.6 4.6 %copy-start.6 = (s32[128]{0:T(128)S(1)}, s32[128]{0:T(128)}, u32[]{:S(2)}) copy-start(s32[128]{0:T(128)} %constant.75.clone) | copy-start | bytes 1540
  51.7 58.4 %all-to-all-start = ((bf16[32,4,24,384]{3,2,1,0:T(8,128)(2,1)}), bf16[32,4,24,384]{3,2,1,0:T(8,128)(2,1)}, u32[]{:S(2)}, u32[]{:S(2)}) async-start(bf16[32,4,24,384]{3,2,1,0:T(8,128)(2,1)} %get-tuple-element.19), calls=%async_computation | async-start | bytes 4718592 | tf_op jit(solution)/shard_map/all_to_all | solution.py:869
  55.7 3.8 %copy-start.4 = (s32[384]{0:T(512)}, s32[384]{0:T(512)S(1)}, u32[]{:S(2)}) copy-start(s32[384]{0:T(512)S(1)} %iota.37) | copy-start | bytes 4612
  57.5 2.0 copy-start.2
  61.2 6.0 %slice-start = ((s32[384]{0:T(512)}), s32[256]{0:T(256)S(1)}, s32[]{:S(2)}) async-start(s32[384]{0:T(512)} %copy-done.4), calls=%async_computation.4 | async-start | bytes 2048 | tf_op jit(solution)/shard_map/slice | solution.py:492
  61.2 21.2 %collective-permute-start.1 = (bf16[12,192,384]{2,1,0:T(8,128)(2,1)}, bf16[12,192,384]{2,1,0:T(8,128)(2,1)}, u32[]{:S(2)}, u32[]{:S(2)}) collective-permute-start(bf16[12,192,384]{2,1,0:T(8,128)(2,1)} %constant_dynamic-slice_fusion.2), channel_id=1, source_target_pairs={{0,16},{16,0},{1,17},{17,1},{2,18},{18,2},{3,19},{19,3},{4,20},{20... | collective-permute-start | bytes 5308424 | tf_op jit(solution)/shard_map/ppermute | solution.py:803
  85.1 3.9 %copy-start.5 = (f32[4,128]{1,0:T(4,128)S(1)}, f32[4,128]{1,0:T(4,128)}, u32[]{:S(2)}) copy-start(f32[4,128]{1,0:T(4,128)} %constant.76.clone) | copy-start | bytes 6148
  116.1 20.7 %all-to-all-start.3 = ((bf16[32,24,384]{2,1,0:T(8,128)(2,1)}), bf16[32,24,384]{2,1,0:T(8,128)(2,1)S(1)}, u32[]{:S(2)}, u32[]{:S(2)}) async-start(bf16[32,24,384]{2,1,0:T(8,128)(2,1)} %bitcast.17), calls=%async_computation.3 | async-start | bytes 1179648 | tf_op jit(solution)/shard_map/all_to_all | solution.py:900
  136.8 5.4 %copy-start.1 = (bf16[32,24,384]{2,1,0:T(8,128)(2,1)}, bf16[32,24,384]{2,1,0:T(8,128)(2,1)S(1)}, u32[]{:S(2)}) copy-start(bf16[32,24,384]{2,1,0:T(8,128)(2,1)S(1)} %all-to-all-done.3.kept_hbm) | copy-start | bytes 1769476
  136.8 72.7 %all-to-all-start.2 = ((bf16[32,120,384]{2,1,0:T(8,128)(2,1)}), bf16[32,120,384]{2,1,0:T(8,128)(2,1)}, u32[]{:S(2)}, u32[]{:S(2)}) async-start(bf16[32,120,384]{2,1,0:T(8,128)(2,1)} %bitcast.16), calls=%async_computation.2 | async-start | bytes 5898240 | tf_op jit(solution)/shard_map/all_to_all | solution.py:900
  142.3 1.6 collective-permute-start.2
  143.9 0.7 copy-start.3
  144.6 69.7 %copy-start = (bf16[192,24,384]{2,1,0:T(8,128)(2,1)S(1)}, bf16[192,24,384]{2,1,0:T(8,128)(2,1)}, u32[]{:S(2)}) copy-start(bf16[192,24,384]{2,1,0:T(8,128)(2,1)} %copy.13) | copy-start | bytes 10616836
  211.0 3.3 %collective-permute-start.3 = (bf16[16,120,384]{2,1,0:T(8,128)(2,1)S(1)}, bf16[16,120,384]{2,1,0:T(8,128)(2,1)S(1)}, u32[]{:S(2)}, u32[]{:S(2)}) collective-permute-start(bf16[16,120,384]{2,1,0:T(8,128)(2,1)S(1)} %constant_dynamic-slice_fusion), channel_id=1, source_target_pairs={{0,16},{16,0},{1,17},{17,1},{2,18},{18,2},{3,19},{19,3},{4,20},{20... | collective-permute-start | bytes 4423688 | tf_op jit(solution)/shard_map/ppermute | solution.py:803

commit v12 on v11

--- a/solution.py
+++ b/solution.py
@@ -355,7 +355,7 @@
             lower_section = lax.axis_index("section") > 0
             inside = lower_section | (lax.axis_index("tile") > 0)
             keep = jnp.where(inside, 1.0, 0.0)
-            above = jnp.where(lower_section, above, refs[7][...])
+            above = jnp.where(lower_section, above, lower_half(refs[7][...]))
         turned = above.T
         upper, lower = (
             layer_one(turned, [128 * b + 64 * a for b in range(bands)]) for a in range(2)
@@ -789,7 +789,7 @@
         ],
         out_shape=jax.ShapeDtypeStruct(features.shape, jnp.bfloat16),
         input_output_aliases=aliases,
-        compiler_params=pltpu.CompilerParams(vmem_limit_bytes=VMEM_BYTES if previous is None else VMEM_BYTES // 4),
+        compiler_params=pltpu.CompilerParams(vmem_limit_bytes=VMEM_BYTES),
         cost_estimate=pl.CostEstimate(
             flops=halves * count * rows * cols,
             bytes_accessed=halves * count * rows * cols * 8,
@@ -850,7 +850,7 @@
     width = -(-(field_cols // 2 + 1) // 128) * 128
 
     arriving = lax.ppermute(
-        lower_half(aerial_patch_grid[-1]),
+        aerial_patch_grid[-1],
         ("section", "tile"),
         [(i, i + 1) for i in range(lax.axis_size("tile") - 1)],
     )

time: 218 us -> 218 us (level)
  no operation moved by 1% of the time
where the time goes in v12:
time: 218 us; the launch traced here: 217 us
  waiting for transfers between devices  92.9 us (43%)
  Pallas kernels  78.1 us (36%)
  starting transfers between devices  24 us (11%)
  other arithmetic  11.3 us (5%)
  local copies, waits for them, and re-layouts  10.5 us (5%)
    all_to_all x2, waiting for transfers between devices, local(): lax.all_to_all(made, DEVICES, split_axis=0, concat_axis=0, tiled=True)  62.9 us
    pallas_call x2, Pallas kernels, stem(): pl.pallas_call(functools.partial(stem_kernel, kind), grid=(steps,), in_sp...  32 us
    all_to_all x2, waiting for transfers between devices, local(): lax.all_to_all(normed, DEVICES, split_axis=0, concat_axis=0, tiled=True)  25.3 us
    pallas_call x2, Pallas kernels, filter_channels(): pl.pallas_call(functools.partial(filter_kernel, first, devices, 1.0 / (fu...  22.3 us
    pallas_call x1, Pallas kernels, symmetric_filter(): pl.pallas_call(symmetric_kernel, grid_spec=pltpu.PrefetchScalarGridSpec(n...  14.2 us
    all_to_all x2, starting transfers between devices, local(): lax.all_to_all(made, DEVICES, split_axis=0, concat_axis=0, tiled=True)  9.51 us
    all_to_all x2, starting transfers between devices, local(): lax.all_to_all(normed, DEVICES, split_axis=0, concat_axis=0, tiled=True)  8.41 us
    pallas_call x2, Pallas kernels, add_residual(): pl.pallas_call(functools.partial(residual_kernel, first, count, chunks),...  6.38 us
  transfers between devices with their start and end apart: 8, of which 6 were waited for; matrix products, arithmetic and copies ran while one was open for 9% of the time, Pallas kernels for 31%

profile of v12, /device:TPU:0, one launch (start us, length us, event | category | flops | bytes accessed | tf_op | source)
XLA Modules:
  0.0 217.2 jit_solution(7987935201485066354)
XLA Ops:
  0.0 1.1 slice_bitcast_fusion
  1.1 5.7 %collective-permute-start = (bf16[384,768]{1,0:T(8,128)(2,1)S(1)}, bf16[384,768]{1,0:T(8,128)(2,1)}, u32[]{:S(2)}, u32[]{:S(2)}) collective-permute-start(bf16[384,768]{1,0:T(8,128)(2,1)S(1)} %slice_bitcast_fusion), channel_id=1, source_target_pairs={{0,1},{1,2},{2,3},{3,4},{4,5},{5,6},{6,7},{7,8},{8,9},{9,10},{10,1... | collective-permute-start | bytes 1769480 | tf_op jit(solution)/shard_map/ppermute | solution.py:852
  6.8 11.4 %stem.2 = (bf16[32,2,24,384]{3,2,1,0:T(8,128)(2,1)}, bf16[4,384,384]{2,1,0:T(8,128)(2,1)}) custom-call(bf16[24,384,768]{2,1,0:T(8,128)(2,1)} %above_ref.3, bf16[24,384,768]{2,1,0:T(8,128)(2,1)} %above_ref.3, bf16[48,96]{1,0:T(8,128)(2,1)} %bitcast.22, f32[96]{0:T(128)} %refs_1_.3, bf16[384,192]{1,0:T(8,128)(2,1)} %bitcast.20, f32[192]{0:T(256)} %refs_3_.3, ...), custom_call_target="tpu_custom_call" | custom-call | flops 8078229504 | bytes 4608000 | tf_op jit(solution)/shard_map/stem/pallas_call | solution.py:448
  18.2 0.0 collective-permute-done.refs_7_
  18.2 4.4 %all-to-all-start.1 = ((bf16[32,2,24,384]{3,2,1,0:T(8,128)(2,1)}), bf16[32,2,24,384]{3,2,1,0:T(8,128)(2,1)}, u32[]{:S(2)}, u32[]{:S(2)}) async-start(bf16[32,2,24,384]{3,2,1,0:T(8,128)(2,1)} %get-tuple-element.23), calls=%async_computation.1 | async-start | bytes 2359296 | tf_op jit(solution)/shard_map/all_to_all | solution.py:869
  22.6 20.5 %stem.3 = (bf16[32,4,24,384]{3,2,1,0:T(8,128)(2,1)}, bf16[8,384,384]{2,1,0:T(8,128)(2,1)}) custom-call(bf16[24,384,768]{2,1,0:T(8,128)(2,1)} %above_ref.3, bf16[24,384,768]{2,1,0:T(8,128)(2,1)} %above_ref.3, bf16[48,96]{1,0:T(8,128)(2,1)} %bitcast.23, f32[96]{0:T(128)} %refs_1_.3, bf16[384,192]{1,0:T(8,128)(2,1)} %bitcast.21, f32[192]{0:T(256)} %refs_3_.3, ...), custom_call_target="tpu_custom_call" | custom-call | flops 16156459008 | bytes 9216000 | tf_op jit(solution)/shard_map/stem/pallas_call | solution.py:448
  43.2 8.4 %all-to-all-done.1 = bf16[32,2,24,384]{3,2,1,0:T(8,128)(2,1)} async-done(((bf16[32,2,24,384]{3,2,1,0:T(8,128)(2,1)}), bf16[32,2,24,384]{3,2,1,0:T(8,128)(2,1)}, u32[]{:S(2)}, u32[]{:S(2)}) %all-to-all-start.1) | async-done | bytes 1179680 | tf_op jit(solution)/shard_map/all_to_all | solution.py:869
  51.5 0.0 copy-start.6
  51.5 4.0 %all-to-all-start = ((bf16[32,4,24,384]{3,2,1,0:T(8,128)(2,1)}), bf16[32,4,24,384]{3,2,1,0:T(8,128)(2,1)}, u32[]{:S(2)}, u32[]{:S(2)}) async-start(bf16[32,4,24,384]{3,2,1,0:T(8,128)(2,1)} %get-tuple-element.19), calls=%async_computation | async-start | bytes 4718592 | tf_op jit(solution)/shard_map/all_to_all | solution.py:869
  55.6 0.0 copy-start.4
  55.6 0.3 fusion.29
  55.8 0.3 sine_convert_fusion.1
  56.1 0.0 copy-done.6
  56.1 0.3 fusion.30
  56.4 0.3 sine_convert_fusion.2
  56.7 0.7 maximum_maximum_fusion.fwd_ref
  57.3 0.0 copy-start.2
  57.3 2.0 constant_dynamic-update-slice_fusion.1
  59.4 0.0 copy-done.4
  59.4 0.0 copy-done.2
  59.4 0.2 constant_dynamic-update-slice_fusion
  59.6 1.5 constant_dynamic-slice_fusion.2
  61.1 0.0 slice-start
  61.1 0.0 collective-permute-start.1
  61.1 0.7 maximum_maximum_fusion.1.inv_ref
  61.8 1.0 fusion.8.turn_u_ref
  62.8 2.5 %sine_convert_fusion = (bf16[384,384]{1,0:T(8,128)(2,1)S(1)}, bf16[384,384]{1,0:T(8,128)(2,1)S(1)}) fusion(), kind=kLoop, calls=%fused_computation.9 | loop fusion | flops 1622016 | bytes 589824 | tf_op jit(solution)/shard_map/convert_element_type | solution.py:26
  65.4 0.8 pad_maximum_fusion.row_table_ref
  66.2 0.1 slice_multiply_fusion
  66.3 0.8 pad_maximum_fusion.1.back_ref
  67.1 0.0 slice-done
  67.1 0.9 fusion.14.turn_w_ref
  68.0 14.2 %symmetric_filter.1.g_ref = bf16[12,2,384,256]{3,2,1,0:T(8,128)(2,1)} custom-call(s32[1]{0:T(128)} %bitcast.8.place_ref, bf16[24,2,384,384]{3,2,1,0:T(8,128)(2,1)} %f_ref.1, bf16[384,256]{1,0:T(8,128)(2,1)} %fusion.14.turn_w_ref, bf16[384,384]{1,0:T(8,128)(2,1)} %fusion.8.turn_u_ref), custom_call_target="tpu_custom_call" | custom-call | flops 3623878656 | bytes 16515072 | tf_op jit(solution)/shard_map/symmetric_filter/pallas_call | solution.py:493
  82.3 0.0 collective-permute-done.1
  82.3 2.3 %broadcast_select_fusion.1 = (bf16[12,192,384]{2,1,0:T(8,128)(2,1)S(1)}, bf16[12,192,384]{2,1,0:T(8,128)(2,1)S(1)}) fusion(bf16[12,192,384]{2,1,0:T(8,128)(2,1)} %collective-permute-done.1, pred[]{:T(512)S(6)} %eq.41, bf16[12,384,384]{2,1,0:T(8,128)(2,1)S(1)} %constant_dynamic-update-slice_fusion, s32[]{:T(128)S(6)} %select_n.72), kind=kLoop, calls=%fused_computation.2 | loop fusion | flops 1769472 | bytes 7077893 | tf_op jit(solution)/shard_map/jit(_where)/select_n | solution.py:886
  84.6 0.4 maximum_bitcast_fusion
  85.0 0.0 copy-start.5
  85.0 3.9 %copy.13 = bf16[192,24,384]{2,1,0:T(8,128)(2,1)} copy(bf16[192,24,384]{2,0,1:T(8,128)(2,1)S(1)} %maximum_bitcast_fusion) | data formatting | bytes 7077888 | tf_op jit(solution)/shard_map/transpose | solution.py:888
  88.9 0.0 copy-done.5
  88.9 0.8 jit_solution_.3.twiddle_ref
  89.7 3.2 %repack.1 = (bf16[12,128,384]{2,1,0:T(8,128)(2,1)}, f32[4,128,128]{2,1,0:T(8,128)}) custom-call(bf16[1536,384]{1,0:T(8,128)(2,1)} %bitcast.7.early_ref, f32[4,128,128]{2,1,0:T(8,128)} %jit_solution_.3.twiddle_ref), custom_call_target="tpu_custom_call" | custom-call | flops 589824 | bytes 2359296 | tf_op jit(solution)/shard_map/repack/pallas_call | solution.py:544
  93.0 17.0 %all-to-all-done = bf16[32,4,24,384]{3,2,1,0:T(8,128)(2,1)} async-done(((bf16[32,4,24,384]{3,2,1,0:T(8,128)(2,1)}), bf16[32,4,24,384]{3,2,1,0:T(8,128)(2,1)}, u32[]{:S(2)}, u32[]{:S(2)}) %all-to-all-start) | async-done | bytes 2359328 | tf_op jit(solution)/shard_map/all_to_all | solution.py:869
  109.9 6.1 %spectral_filter.3 = bf16[768,384]{1,0:T(8,128)(2,1)} custom-call(bf16[3072,384]{1,0:T(8,128)(2,1)} %bitcast.4.late_ref, bf16[12,128,384]{2,1,0:T(8,128)(2,1)} %get-tuple-element.24.early_ref, bf16[12,2,384,256]{3,2,1,0:T(8,128)(2,1)} %symmetric_filter.1.g_ref, bf16[384,512]{1,0:T(8,128)(2,1)} %pad_maximum_fusion.row_table_ref, ...), custom_call_target="tpu_custom_call" | custom-call | flops 1207959552 | bytes 2359296 | tf_op jit(solution)/shard_map/spectral_filter/pallas_call | solution.py:697
  116.0 4.2 %all-to-all-start.3 = ((bf16[32,24,384]{2,1,0:T(8,128)(2,1)}), bf16[32,24,384]{2,1,0:T(8,128)(2,1)S(1)}, u32[]{:S(2)}, u32[]{:S(2)}) async-start(bf16[32,24,384]{2,1,0:T(8,128)(2,1)} %bitcast.17), calls=%async_computation.3 | async-start | bytes 1179648 | tf_op jit(solution)/shard_map/all_to_all | solution.py:900
  120.2 16.2 %spectral_filter.2 = bf16[3840,384]{1,0:T(8,128)(2,1)} custom-call(bf16[3072,384]{1,0:T(8,128)(2,1)} %bitcast.4.late_ref, bf16[12,128,384]{2,1,0:T(8,128)(2,1)} %get-tuple-element.24.early_ref, bf16[12,2,384,256]{3,2,1,0:T(8,128)(2,1)} %symmetric_filter.1.g_ref, bf16[384,512]{1,0:T(8,128)(2,1)} %pad_maximum_fusion.row_table_ref, ...), custom_call_target="tpu_custom_call" | custom-call | flops 6039797760 | bytes 11796480 | tf_op jit(solution)/shard_map/spectral_filter/pallas_call | solution.py:697
  136.4 0.3 all-to-all-done.3.kept_hbm
  136.7 0.0 copy-start.1
  136.7 5.3 %all-to-all-start.2 = ((bf16[32,120,384]{2,1,0:T(8,128)(2,1)}), bf16[32,120,384]{2,1,0:T(8,128)(2,1)S(1)}, u32[]{:S(2)}, u32[]{:S(2)}) async-start(bf16[32,120,384]{2,1,0:T(8,128)(2,1)} %bitcast.16), calls=%async_computation.2 | async-start | bytes 5898240 | tf_op jit(solution)/shard_map/all_to_all | solution.py:900
  142.0 0.0 copy-done.1
  142.1 0.3 collective-permute-start.2
  142.4 1.3 collective-permute-done.2.other_hbm
  143.7 0.0 copy-start.3
  143.7 0.7 copy-done.3
  144.4 2.2 %residual.2.refs_0_ = bf16[16,12,24,384]{3,2,1,0:T(8,128)(2,1)} custom-call(bf16[32,24,384]{2,1,0:T(8,128)(2,1)} %copy-done.1, bf16[16,24,384]{2,1,0:T(8,128)(2,1)} %copy-done.3, bf16[16,12,24,384]{3,2,1,0:T(8,128)(2,1)} %bitcast.14), custom_call_target="tpu_custom_call" | custom-call | flops 294912 | bytes 2359296 | tf_op jit(solution)/shard_map/residual/pallas_call | solution.py:778
  146.6 62.6 %all-to-all-done.2.kept_hbm = bf16[32,120,384]{2,1,0:T(8,128)(2,1)S(1)} async-done(((bf16[32,120,384]{2,1,0:T(8,128)(2,1)}), bf16[32,120,384]{2,1,0:T(8,128)(2,1)S(1)}, u32[]{:S(2)}, u32[]{:S(2)}) %all-to-all-start.2) | async-done | bytes 2949152 | tf_op jit(solution)/shard_map/all_to_all | solution.py:900
  209.2 0.0 copy-start
  209.2 0.1 constant_dynamic-slice_fusion
  209.4 0.1 collective-permute-start.3
  209.5 3.4 %collective-permute-done.3.other_hbm = bf16[16,120,384]{2,1,0:T(8,128)(2,1)} collective-permute-done((bf16[16,120,384]{2,1,0:T(8,128)(2,1)S(1)}, bf16[16,120,384]{2,1,0:T(8,128)(2,1)}, u32[]{:S(2)}, u32[]{:S(2)}) %collective-permute-start.3) | collective-permute-done | bytes 1474592 | tf_op jit(solution)/shard_map/ppermute | solution.py:803
  212.9 0.0 copy-done
  212.9 4.2 %residual.3 = bf16[16,12,24,384]{3,2,1,0:T(8,128)(2,1)} custom-call(bf16[32,120,384]{2,1,0:T(8,128)(2,1)} %copy-done, bf16[16,120,384]{2,1,0:T(8,128)(2,1)} %collective-permute-done.3.other_hbm, bf16[16,12,24,384]{3,2,1,0:T(8,128)(2,1)} %bitcast.15, bf16[16,12,24,384]{3,2,1,0:T(8,128)(2,1)} %residual.2.refs_0_), custom_call_target="tpu_custom_call", output_to_operand_aliasing={{}: (3, {})} | custom-call | flops 1474560 | bytes 11796480 | tf_op jit(solution)/shard_map/residual/pallas_call | solution.py:778
  (5 shorter events, 0.1 us)
Async XLA Ops:
  1.1 17.1 %collective-permute-start = (bf16[384,768]{1,0:T(8,128)(2,1)S(1)}, bf16[384,768]{1,0:T(8,128)(2,1)}, u32[]{:S(2)}, u32[]{:S(2)}) collective-permute-start(bf16[384,768]{1,0:T(8,128)(2,1)S(1)} %slice_bitcast_fusion), channel_id=1, source_target_pairs={{0,1},{1,2},{2,3},{3,4},{4,5},{5,6},{6,7},{7,8},{8,9},{9,10},{10,1... | collective-permute-start | bytes 1769480 | tf_op jit(solution)/shard_map/ppermute | solution.py:852
  18.2 33.3 %all-to-all-start.1 = ((bf16[32,2,24,384]{3,2,1,0:T(8,128)(2,1)}), bf16[32,2,24,384]{3,2,1,0:T(8,128)(2,1)}, u32[]{:S(2)}, u32[]{:S(2)}) async-start(bf16[32,2,24,384]{3,2,1,0:T(8,128)(2,1)} %get-tuple-element.23), calls=%async_computation.1 | async-start | bytes 2359296 | tf_op jit(solution)/shard_map/all_to_all | solution.py:869
  51.5 4.6 %copy-start.6 = (s32[128]{0:T(128)S(1)}, s32[128]{0:T(128)}, u32[]{:S(2)}) copy-start(s32[128]{0:T(128)} %constant.75.clone) | copy-start | bytes 1540
  51.5 58.4 %all-to-all-start = ((bf16[32,4,24,384]{3,2,1,0:T(8,128)(2,1)}), bf16[32,4,24,384]{3,2,1,0:T(8,128)(2,1)}, u32[]{:S(2)}, u32[]{:S(2)}) async-start(bf16[32,4,24,384]{3,2,1,0:T(8,128)(2,1)} %get-tuple-element.19), calls=%async_computation | async-start | bytes 4718592 | tf_op jit(solution)/shard_map/all_to_all | solution.py:869
  55.6 3.8 %copy-start.4 = (s32[384]{0:T(512)}, s32[384]{0:T(512)S(1)}, u32[]{:S(2)}) copy-start(s32[384]{0:T(512)S(1)} %iota.37) | copy-start | bytes 4612
  57.3 2.0 copy-start.2
  61.1 6.0 %slice-start = ((s32[384]{0:T(512)}), s32[256]{0:T(256)S(1)}, s32[]{:S(2)}) async-start(s32[384]{0:T(512)} %copy-done.4), calls=%async_computation.4 | async-start | bytes 2048 | tf_op jit(solution)/shard_map/slice | solution.py:492
  61.1 21.2 %collective-permute-start.1 = (bf16[12,192,384]{2,1,0:T(8,128)(2,1)}, bf16[12,192,384]{2,1,0:T(8,128)(2,1)}, u32[]{:S(2)}, u32[]{:S(2)}) collective-permute-start(bf16[12,192,384]{2,1,0:T(8,128)(2,1)} %constant_dynamic-slice_fusion.2), channel_id=1, source_target_pairs={{0,16},{16,0},{1,17},{17,1},{2,18},{18,2},{3,19},{19,3},{4,20},{20... | collective-permute-start | bytes 5308424 | tf_op jit(solution)/shard_map/ppermute | solution.py:803
  85.0 3.9 %copy-start.5 = (f32[4,128]{1,0:T(4,128)S(1)}, f32[4,128]{1,0:T(4,128)}, u32[]{:S(2)}) copy-start(f32[4,128]{1,0:T(4,128)} %constant.76.clone) | copy-start | bytes 6148
  116.0 20.7 %all-to-all-start.3 = ((bf16[32,24,384]{2,1,0:T(8,128)(2,1)}), bf16[32,24,384]{2,1,0:T(8,128)(2,1)S(1)}, u32[]{:S(2)}, u32[]{:S(2)}) async-start(bf16[32,24,384]{2,1,0:T(8,128)(2,1)} %bitcast.17), calls=%async_computation.3 | async-start | bytes 1179648 | tf_op jit(solution)/shard_map/all_to_all | solution.py:900
  136.7 5.3 %copy-start.1 = (bf16[32,24,384]{2,1,0:T(8,128)(2,1)}, bf16[32,24,384]{2,1,0:T(8,128)(2,1)S(1)}, u32[]{:S(2)}) copy-start(bf16[32,24,384]{2,1,0:T(8,128)(2,1)S(1)} %all-to-all-done.3.kept_hbm) | copy-start | bytes 1769476
  136.7 72.6 %all-to-all-start.2 = ((bf16[32,120,384]{2,1,0:T(8,128)(2,1)}), bf16[32,120,384]{2,1,0:T(8,128)(2,1)S(1)}, u32[]{:S(2)}, u32[]{:S(2)}) async-start(bf16[32,120,384]{2,1,0:T(8,128)(2,1)} %bitcast.16), calls=%async_computation.2 | async-start | bytes 5898240 | tf_op jit(solution)/shard_map/all_to_all | solution.py:900
  142.1 1.6 collective-permute-start.2
  143.7 0.7 copy-start.3
  209.2 3.6 %copy-start = (bf16[32,120,384]{2,1,0:T(8,128)(2,1)}, bf16[32,120,384]{2,1,0:T(8,128)(2,1)S(1)}, u32[]{:S(2)}) copy-start(bf16[32,120,384]{2,1,0:T(8,128)(2,1)S(1)} %all-to-all-done.2.kept_hbm) | copy-start | bytes 8847364
  209.4 3.5 %collective-permute-start.3 = (bf16[16,120,384]{2,1,0:T(8,128)(2,1)S(1)}, bf16[16,120,384]{2,1,0:T(8,128)(2,1)}, u32[]{:S(2)}, u32[]{:S(2)}) collective-permute-start(bf16[16,120,384]{2,1,0:T(8,128)(2,1)S(1)} %constant_dynamic-slice_fusion), channel_id=1, source_target_pairs={{0,16},{16,0},{1,17},{17,1},{2,18},{18,2},{3,19},{19,3},{4,20},{20... | collective-permute-start | bytes 4423688 | tf_op jit(solution)/shard_map/ppermute | solution.py:803
